TPU v7x, 32 devices: a whole 2x2x4 slice. The times are simulated.
32 devices in a mesh: pos: 8 (over y, x, core), grp: 4 (over z).
Axes of the slice: x: 2, y: 2, z: 4, core: 2. Of those that a mesh axis runs over, the one named last changes fastest.
Arguments:
- inputs: bfloat16 [12544, 1024], P(('pos', 'grp')), may hold values from -9 to 9
- segment_ids: int32 [64], replicated, may hold values from 0 to 15, as said below
- pad_mask: int32 [12544], replicated, may hold values 0 or 1
- time_weight: bfloat16 [3, 1024, 256], replicated, may hold values from -0.109375 to 0.109375
- gain_first: float32 [256], replicated, may hold values from 0.5 to 1.5
- shift_first: float32 [256], replicated, may hold values from -4 to 4
- space_weight: bfloat16 [9, 256, 256], replicated, may hold values from -0.125 to 0.125
- gain_second: float32 [256], replicated, may hold values from 0.5 to 1.5
- shift_second: float32 [256], replicated, may hold values from -4 to 4
- expand_weight: bfloat16 [256, 1024], replicated, may hold values from -0.375 to 0.375
- gain_third: float32 [1024], replicated, may hold values from 0.5 to 1.5
- shift_third: float32 [1024], replicated, may hold values from -4 to 4
- query_weight: bfloat16 [1024, 512], replicated, may hold values from -0.1875 to 0.1875
- key_weight: bfloat16 [1024, 512], replicated, may hold values from -0.1875 to 0.1875
- value_weight: bfloat16 [1024, 512], replicated, may hold values from -0.1875 to 0.1875
- out_weight: bfloat16 [512, 1024], replicated, may hold values from -0.25 to 0.25
- gain_final: float32 [1024], replicated, may hold values from 0.5 to 1.5
- shift_final: float32 [1024], replicated, may hold values from -4 to 4
- cotangent: bfloat16 [12544, 1024], P(('pos', 'grp')), may hold values from -6 to 6
Outputs:
- output: bfloat16 [12544, 1024], P(('pos', 'grp'))
- input_grad: float32 [12544, 1024], P(('pos', 'grp'))
- time_grad: float32 [3, 1024, 256], P(None, 'pos')
- gain_first_grad: float32 [256], replicated
- shift_first_grad: float32 [256], replicated
- space_grad: float32 [9, 256, 256], P(None, 'pos')
- gain_second_grad: float32 [256], replicated
- shift_second_grad: float32 [256], replicated
- expand_grad: float32 [256, 1024], P(None, 'pos')
- gain_third_grad: float32 [1024], replicated
- shift_third_grad: float32 [1024], replicated
- query_grad: float32 [1024, 512], P('pos')
- key_grad: float32 [1024, 512], P('pos')
- value_grad: float32 [1024, 512], P('pos')
- out_weight_grad: float32 [512, 1024], P(None, 'pos')
- gain_final_grad: float32 [1024], replicated
- shift_final_grad: float32 [1024], replicated
Inputs may be any that keep to these rules, and one draw needn't show every extreme that they name: `segment_ids`: ids never fall; the aligned block k of 8 frames holds the id 2k, then possibly 2k + 1, with 2k on half of the block or more.
All inputs are finite; a program needn't handle non-finite values.
Results may differ from a plain program's by a relative error of at most 0.035.
The roundings to bfloat16 on the way count: a program that leaves them out, or rounds other values in their place, can miss the bound.
Values may be sent and summed in bfloat16 or wider, within the bound.
No kernel may reach another device: no remote copies, remote signals or barrier semaphores. Data moves between devices by JAX's collectives and lax.ppermute only.
A program may use at most 128 MiB of HBM per device.

v0:
```python
import jax
import jax.numpy as jnp
from jax import lax
from jax.sharding import PartitionSpec as P

SIDE = 14


EPSILON = 1e-05
TEMPER = 0.2
MASKED_SCORE = -1000000000.0


def padded_2(shard, sides, width):
    for axis, dim in sides:
        count, length = (lax.axis_size(axis), shard.shape[dim])
        up = [(i, (i + 1) % count) for i in range(count - 1)]
        down = [(j, i) for i, j in up]
        last = lax.slice_in_dim(shard, length - width, length, axis=dim)
        first = lax.slice_in_dim(shard, 0, width, axis=dim)
        before = lax.ppermute(last, axis, up)
        after = lax.ppermute(first, axis, down)
        shard = jnp.concatenate([before, shard, after], axis=dim)
    return shard


def silu_grad(pre_act, gradient):
    sigmoid_val = jax.nn.sigmoid(pre_act)
    return gradient * sigmoid_val * (1.0 + pre_act * (1.0 - sigmoid_val))


def contract_rows(left_side, right_side):
    return lax.dot_general(
        left_side, right_side, (((0,), (0,)), ((), ())), preferred_element_type=jnp.float32
    )


def contract_cols(left_side, right_side):
    return lax.dot_general(
        left_side, right_side, (((1,), (1,)), ((), ())), preferred_element_type=jnp.float32
    )


def norm_forward(hidden, valid_rows, valid_total, gain_vec, shift_vec):
    sum_values = jnp.sum(hidden * valid_rows, axis=0)
    sum_squares = jnp.sum(hidden * hidden * valid_rows, axis=0)
    sum_values, sum_squares = lax.psum((sum_values, sum_squares), ("pos", "grp"))
    average = sum_values / valid_total
    spread = sum_squares / valid_total - average * average
    inverse_std = lax.rsqrt(spread + EPSILON)
    normed = (hidden - average) * inverse_std
    return (normed * gain_vec + shift_vec, (normed, inverse_std, average))


def norm_backward(gradient, kept_state, hidden, valid_rows, valid_total, gain_vec):
    normed, inverse_std, average = kept_state
    gain_part = jnp.sum(gradient * normed, axis=0)
    shift_part = jnp.sum(gradient, axis=0)
    gain_part, shift_part = lax.psum((gain_part, shift_part), ("pos", "grp"))
    d_spread = -0.5 * gain_vec * gain_part * inverse_std * inverse_std
    d_average = -gain_vec * shift_part * inverse_std - 2.0 * average * d_spread
    d_hidden = (
        gradient * gain_vec * inverse_std
        + valid_rows * (d_average + 2.0 * hidden * d_spread) / valid_total
    )
    return (d_hidden, gain_part, shift_part)


def pool_keys(values, valid_rows):
    half_side = SIDE // 2
    frame_count = values.shape[0] // (SIDE * SIDE)
    blocks = values.reshape(frame_count, half_side, 2, half_side, 2, values.shape[1])
    weights = valid_rows.reshape(frame_count, half_side, 2, half_side, 2, 1)
    block_sums = jnp.sum(blocks * weights, axis=(2, 4))
    counts = jnp.sum(weights, axis=(2, 4))
    return (block_sums / jnp.maximum(counts, 1.0)).reshape(
        frame_count * half_side * half_side, values.shape[1]
    )


def spread_keys(gradient, valid_rows):
    half_side = SIDE // 2
    frame_count = valid_rows.shape[0] // (SIDE * SIDE)
    weights = valid_rows.reshape(frame_count, half_side, 2, half_side, 2, 1)
    counts = jnp.sum(weights, axis=(2, 4), keepdims=True)
    shaped = gradient.reshape(frame_count, half_side, 1, half_side, 1, gradient.shape[1])
    result = shaped / jnp.maximum(counts, 1.0) * weights
    return result.reshape(frame_count * SIDE * SIDE, gradient.shape[1])


def soft_weights(logits, allowed):
    scores = jnp.where(allowed, logits * TEMPER, MASKED_SCORE)
    row_max = jnp.max(scores, axis=1, keepdims=True)
    exponent = jnp.exp(scores - row_max)
    return exponent / jnp.sum(exponent, axis=1, keepdims=True)


def local(
    inputs,
    segment_ids,
    pad_mask,
    time_weight,
    gain_first,
    shift_first,
    space_weight,
    gain_second,
    shift_second,
    expand_weight,
    gain_third,
    shift_third,
    query_weight,
    key_weight,
    value_weight,
    out_weight,
    gain_final,
    shift_final,
    cotangent,
):
    frame_area = SIDE * SIDE
    half_side = SIDE // 2
    row_count, channels = inputs.shape
    frame_count = row_count // frame_area
    bottleneck = time_weight.shape[2]
    group_size = lax.axis_size("grp")
    group_frames = frame_count * group_size
    group_index = lax.axis_index("grp")
    block_index = lax.axis_index("pos")
    seg_group = lax.dynamic_slice_in_dim(segment_ids, block_index * group_frames, group_frames)
    border = jnp.full((1,), -1, jnp.int32)
    seg_padded = jnp.concatenate([border, seg_group, border])
    seg_own = lax.dynamic_slice_in_dim(seg_padded, group_index * frame_count + 1, frame_count)
    seg_before = lax.dynamic_slice_in_dim(seg_padded, group_index * frame_count, frame_count)
    seg_after = lax.dynamic_slice_in_dim(seg_padded, group_index * frame_count + 2, frame_count)
    prev_ok = (seg_before == seg_own).astype(jnp.float32)[:, None, None]
    next_ok = (seg_after == seg_own).astype(jnp.float32)[:, None, None]
    mask_group = lax.dynamic_slice_in_dim(
        pad_mask, block_index * group_frames * frame_area, group_frames * frame_area
    ).astype(jnp.float32)
    valid_rows = lax.dynamic_slice_in_dim(mask_group, group_index * row_count, row_count)[:, None]
    valid_total = jnp.sum(pad_mask.astype(jnp.float32))
    key_total = group_frames * half_side * half_side
    key_counts = jnp.sum(
        mask_group.reshape(group_frames, half_side, 2, half_side, 2), axis=(2, 4)
    ).reshape(key_total)
    key_ok = key_counts > 0.5
    key_seg = jnp.repeat(seg_group, half_side * half_side, total_repeat_length=key_total)
    query_seg = jnp.repeat(seg_group, frame_area, total_repeat_length=group_frames * frame_area)
    stacked = inputs.reshape(frame_count, frame_area, channels)
    padded = padded_2(stacked, (("grp", 0),), 1)
    previous = padded[:-2]
    following = padded[2:]
    pre_first = jnp.dot(stacked, time_weight[1], preferred_element_type=jnp.float32)
    pre_first = pre_first + prev_ok * jnp.dot(
        previous, time_weight[0], preferred_element_type=jnp.float32
    )
    pre_first = pre_first + next_ok * jnp.dot(
        following, time_weight[2], preferred_element_type=jnp.float32
    )
    pre_first = pre_first.reshape(row_count, bottleneck)
    act_first, kept_first = norm_forward(
        pre_first, valid_rows, valid_total, gain_first, shift_first
    )
    z_first = jax.nn.silu(act_first).astype(jnp.bfloat16)
    padded_grid = jnp.pad(
        z_first.reshape(frame_count, SIDE, SIDE, bottleneck), ((0, 0), (1, 1), (1, 1), (0, 0))
    )
    pre_second = jnp.zeros((frame_count, SIDE, SIDE, bottleneck), jnp.float32)
    for tap_index in range(9):
        row_off = tap_index // 3
        col_off = tap_index % 3
        window = padded_grid[:, row_off : row_off + SIDE, col_off : col_off + SIDE, :]
        pre_second = pre_second + jnp.dot(
            window, space_weight[tap_index], preferred_element_type=jnp.float32
        )
    pre_second = pre_second.reshape(row_count, bottleneck)
    act_second, kept_second = norm_forward(
        pre_second, valid_rows, valid_total, gain_second, shift_second
    )
    z_second = jax.nn.silu(act_second).astype(jnp.bfloat16)
    pre_third = jnp.dot(z_second, expand_weight, preferred_element_type=jnp.float32)
    act_third, kept_third = norm_forward(
        pre_third, valid_rows, valid_total, gain_third, shift_third
    )
    summed = inputs.astype(jnp.float32) + act_third
    unit = jax.nn.silu(summed).astype(jnp.bfloat16)
    theta = jnp.dot(unit, query_weight, preferred_element_type=jnp.float32).astype(jnp.bfloat16)
    key_full = jnp.dot(unit, key_weight, preferred_element_type=jnp.float32)
    value_full = jnp.dot(unit, value_weight, preferred_element_type=jnp.float32)
    keys_here = pool_keys(key_full, valid_rows).astype(jnp.bfloat16)
    values_here = pool_keys(value_full, valid_rows).astype(jnp.bfloat16)
    query_slice, key_slice, value_slice = (
        lax.all_to_all(theta, "grp", split_axis=1, concat_axis=0, tiled=True),
        lax.all_to_all(keys_here, "grp", split_axis=1, concat_axis=0, tiled=True),
        lax.all_to_all(values_here, "grp", split_axis=1, concat_axis=0, tiled=True),
    )
    allowed = (query_seg[:, None] == key_seg[None, :]) & key_ok[None, :]
    logits = lax.psum(contract_cols(query_slice, key_slice), "grp")
    probs = soft_weights(logits, allowed)
    probs_low = probs.astype(jnp.bfloat16)
    mixed_slice = jnp.dot(probs_low, value_slice, preferred_element_type=jnp.float32).astype(
        jnp.bfloat16
    )
    attended = lax.all_to_all(mixed_slice, "grp", split_axis=0, concat_axis=1, tiled=True)
    pre_final = jnp.dot(attended, out_weight, preferred_element_type=jnp.float32)
    act_final, kept_final = norm_forward(
        pre_final, valid_rows, valid_total, gain_final, shift_final
    )
    output = (unit.astype(jnp.float32) + act_final).astype(jnp.bfloat16)
    grad_out = cotangent.astype(jnp.float32)
    d_final, gain_final_grad, shift_final_grad = norm_backward(
        grad_out, kept_final, pre_final, valid_rows, valid_total, gain_final
    )
    d_final_low = d_final.astype(jnp.bfloat16)
    out_weight_part = contract_rows(attended, d_final_low)
    d_attended = contract_cols(d_final_low, out_weight).astype(jnp.bfloat16)
    d_slice = lax.all_to_all(d_attended, "grp", split_axis=1, concat_axis=0, tiled=True)
    d_probs = lax.psum(contract_cols(d_slice, value_slice), "grp")
    d_value_slice = contract_rows(probs_low, d_slice)
    row_terms = jnp.sum(probs * d_probs, axis=1, keepdims=True)
    d_logits = (TEMPER * probs * (d_probs - row_terms)).astype(jnp.bfloat16)
    d_query_slice = jnp.dot(d_logits, key_slice, preferred_element_type=jnp.float32)
    d_key_slice = contract_rows(d_logits, query_slice)
    d_theta, d_keys, d_values = (
        lax.all_to_all(d_query_slice, "grp", split_axis=0, concat_axis=1, tiled=True),
        lax.all_to_all(d_key_slice, "grp", split_axis=0, concat_axis=1, tiled=True),
        lax.all_to_all(d_value_slice, "grp", split_axis=0, concat_axis=1, tiled=True),
    )
    d_theta_low = d_theta.astype(jnp.bfloat16)
    d_key_low = spread_keys(d_keys, valid_rows).astype(jnp.bfloat16)
    d_value_low = spread_keys(d_values, valid_rows).astype(jnp.bfloat16)
    query_part = contract_rows(unit, d_theta_low)
    key_part = contract_rows(unit, d_key_low)
    value_part = contract_rows(unit, d_value_low)
    d_unit = grad_out + contract_cols(d_theta_low, query_weight)
    d_unit = (
        d_unit + contract_cols(d_key_low, key_weight) + contract_cols(d_value_low, value_weight)
    )
    d_summed = silu_grad(summed, d_unit)
    d_third, gain_third_grad, shift_third_grad = norm_backward(
        d_summed, kept_third, pre_third, valid_rows, valid_total, gain_third
    )
    d_third_low = d_third.astype(jnp.bfloat16)
    expand_part = contract_rows(z_second, d_third_low)
    d_act_second = silu_grad(act_second, contract_cols(d_third_low, expand_weight))
    d_second, gain_second_grad, shift_second_grad = norm_backward(
        d_act_second, kept_second, pre_second, valid_rows, valid_total, gain_second
    )
    d_second_low = d_second.astype(jnp.bfloat16).reshape(frame_count, SIDE, SIDE, bottleneck)
    grad_grid = jnp.zeros((frame_count, SIDE + 2, SIDE + 2, bottleneck), jnp.float32)
    tap_grads = []
    for tap_index in range(9):
        row_off = tap_index // 3
        col_off = tap_index % 3
        window = padded_grid[:, row_off : row_off + SIDE, col_off : col_off + SIDE, :]
        tap_grads.append(
            lax.dot_general(
                window,
                d_second_low,
                (((0, 1, 2), (0, 1, 2)), ((), ())),
                preferred_element_type=jnp.float32,
            )
        )
        back_tap = lax.dot_general(
            d_second_low,
            space_weight[tap_index],
            (((3,), (1,)), ((), ())),
            preferred_element_type=jnp.float32,
        )
        grad_grid = grad_grid.at[:, row_off : row_off + SIDE, col_off : col_off + SIDE, :].add(
            back_tap
        )
    space_part = jnp.stack(tap_grads)
    d_z_first = grad_grid[:, 1:-1, 1:-1, :].reshape(row_count, bottleneck)
    d_act_first = silu_grad(act_first, d_z_first)
    d_first, gain_first_grad, shift_first_grad = norm_backward(
        d_act_first, kept_first, pre_first, valid_rows, valid_total, gain_first
    )
    d_first_low = d_first.astype(jnp.bfloat16).reshape(frame_count, frame_area, bottleneck)
    grad_padded = padded_2(d_first_low, (("grp", 0),), 1)
    contract_last = (((2,), (1,)), ((), ()))
    d_conv = lax.dot_general(
        d_first_low, time_weight[1], contract_last, preferred_element_type=jnp.float32
    )
    d_conv = d_conv + next_ok * lax.dot_general(
        grad_padded[2:], time_weight[0], contract_last, preferred_element_type=jnp.float32
    )
    d_conv = d_conv + prev_ok * lax.dot_general(
        grad_padded[:-2], time_weight[2], contract_last, preferred_element_type=jnp.float32
    )
    input_grad = d_summed + d_conv.reshape(row_count, channels)
    contract_frames = (((0, 1), (0, 1)), ((), ()))
    prev_low = prev_ok.astype(jnp.bfloat16)
    next_low = next_ok.astype(jnp.bfloat16)
    time_part = jnp.stack(
        [
            lax.dot_general(
                previous * prev_low,
                d_first_low,
                contract_frames,
                preferred_element_type=jnp.float32,
            ),
            lax.dot_general(
                stacked, d_first_low, contract_frames, preferred_element_type=jnp.float32
            ),
            lax.dot_general(
                following * next_low,
                d_first_low,
                contract_frames,
                preferred_element_type=jnp.float32,
            ),
        ]
    )
    time_share, space_share, expand_share, query_share, key_share, value_share, out_share = (
        lax.psum_scatter(time_part, "pos", scatter_dimension=1, tiled=True),
        lax.psum_scatter(space_part, "pos", scatter_dimension=1, tiled=True),
        lax.psum_scatter(expand_part, "pos", scatter_dimension=1, tiled=True),
        lax.psum_scatter(query_part, "pos", scatter_dimension=0, tiled=True),
        lax.psum_scatter(key_part, "pos", scatter_dimension=0, tiled=True),
        lax.psum_scatter(value_part, "pos", scatter_dimension=0, tiled=True),
        lax.psum_scatter(out_weight_part, "pos", scatter_dimension=1, tiled=True),
    )
    time_grad, space_grad, expand_grad, query_grad, key_grad, value_grad, out_weight_grad = (
        lax.psum(
            (time_share, space_share, expand_share, query_share, key_share, value_share, out_share),
            "grp",
        )
    )
    return (
        output,
        input_grad,
        time_grad,
        gain_first_grad,
        shift_first_grad,
        space_grad,
        gain_second_grad,
        shift_second_grad,
        expand_grad,
        gain_third_grad,
        shift_third_grad,
        query_grad,
        key_grad,
        value_grad,
        out_weight_grad,
        gain_final_grad,
        shift_final_grad,
    )


def solution(mesh):
    in_specs = (
        P(("pos", "grp"), None),
        P(),
        P(),
        P(),
        P(),
        P(),
        P(),
        P(),
        P(),
        P(),
        P(),
        P(),
        P(),
        P(),
        P(),
        P(),
        P(),
        P(),
        P(("pos", "grp"), None),
    )
    out_specs = (
        P(("pos", "grp"), None),
        P(("pos", "grp"), None),
        P(None, "pos", None),
        P(),
        P(),
        P(None, "pos", None),
        P(),
        P(),
        P(None, "pos"),
        P(),
        P(),
        P("pos", None),
        P("pos", None),
        P("pos", None),
        P(None, "pos"),
        P(),
        P(),
    )
    return jax.shard_map(local, mesh=mesh, in_specs=in_specs, out_specs=out_specs, check_vma=False)
```

profile of v0, /device:TPU:0, one launch (start us, length us, event | category | flops | bytes accessed | tf_op | source)
XLA Modules:
  0.0 990.2 jit_solution(14997750457076087711)
XLA Ops:
  10.8 6.3 collective-permute-start
  21.4 4.0 collective-permute-done
  28.7 41.5 %all-reduce.9 = (f32[256]{0:T(256)S(1)}, f32[256]{0:T(256)S(1)}) all-reduce(f32[256]{0:T(256)S(1)} %get-tuple-element.162, f32[256]{0:T(256)S(1)} %get-tuple-element.161), channel_id=1, replica_groups=mesh['pos'=8,'grp'=4] {'pos','grp'}, use_global_device_ids=true, to_apply=%region_1.0 | all-reduce | flops 512 | bytes 4096 | tf_op jit(solution)/shard_map/psum | solution.py:47
  73.7 40.2 %all-reduce.8 = (f32[256]{0:T(256)S(1)}, f32[256]{0:T(256)S(1)}) all-reduce(f32[256]{0:T(256)S(1)} %get-tuple-element.158, f32[256]{0:T(256)S(1)} %get-tuple-element.157), channel_id=1, replica_groups=mesh['pos'=8,'grp'=4] {'pos','grp'}, use_global_device_ids=true, to_apply=%region_6.7 | all-reduce | flops 512 | bytes 4096 | tf_op jit(solution)/shard_map/psum | solution.py:47
  114.6 2.7 multiply_reduce_fusion.4
  117.3 40.0 %all-reduce.7 = (f32[1024]{0:T(1024)S(1)}, f32[1024]{0:T(1024)S(1)}) all-reduce(f32[1024]{0:T(1024)S(1)} %get-tuple-element.152, f32[1024]{0:T(1024)S(1)} %get-tuple-element.151), channel_id=1, replica_groups=mesh['pos'=8,'grp'=4] {'pos','grp'}, use_global_device_ids=true, to_apply=%region_10.11 | all-reduce | flops 2048 | bytes 16384 | tf_op jit(solution)/shard_map/psum | solution.py:47
  163.2 2.7 fusion.179
  174.2 3.7 all-to-all-start.1
  179.4 4.4 all-to-all-done.1
  183.8 3.6 all-to-all-start
  187.6 9.8 all-to-all-done
  200.8 5.0 select_select_fusion
  206.5 3.3 all-to-all-start.2
  209.9 5.0 select_select_fusion.1
  214.9 3.8 all-to-all-done.2
  218.7 85.9 %all-reduce.15.cloned.1.call-done = f32[1568,392]{0,1:T(8,128)} async-done(((f32[1568,392]{0,1:T(8,128)}), f32[1568,392]{0,1:T(8,128)}) %all-reduce.15.cloned.1.call-update) | async-done | bytes 2458640 | tf_op jit(solution)/shard_map/psum | solution.py:197
  309.9 14.5 %all_to_all.125 = bf16[4,392,128]{2,1,0:T(8,128)(2,1)S(1)} all-to-all(bf16[4,392,128]{2,1,0:T(8,128)(2,1)S(1)} %bitcast.331), channel_id=1, replica_groups=mesh['pos'=8,'grp'=4] {'grp'}, dimensions={0} | all-to-all | bytes 802816 | tf_op jit(solution)/shard_map/all_to_all | solution.py:203
  326.3 39.2 %all-reduce.6 = (f32[1024]{0:T(1024)S(1)}, f32[1024]{0:T(1024)S(1)}) all-reduce(f32[1024]{0:T(1024)S(1)} %get-tuple-element.150, f32[1024]{0:T(1024)S(1)} %get-tuple-element.149), channel_id=1, replica_groups=mesh['pos'=8,'grp'=4] {'pos','grp'}, use_global_device_ids=true, to_apply=%region_21.22 | all-reduce | flops 2048 | bytes 16384 | tf_op jit(solution)/shard_map/psum | solution.py:47
  368.2 40.3 %all-reduce.5 = (f32[1024]{0:T(1024)S(1)}, f32[1024]{0:T(1024)S(1)}) all-reduce(f32[1024]{0:T(1024)S(1)} %get-tuple-element.156, f32[1024]{0:T(1024)S(1)} %get-tuple-element.155), channel_id=1, replica_groups=mesh['pos'=8,'grp'=4] {'pos','grp'}, use_global_device_ids=true, to_apply=%region_27.28 | all-reduce | flops 2048 | bytes 16384 | tf_op jit(solution)/shard_map/psum | solution.py:59
  409.1 4.0 fusion.4
  414.1 13.7 %all_to_all.126 = bf16[392,4,128]{2,0,1:T(8,128)(2,1)S(1)} all-to-all(bf16[392,4,128]{2,0,1:T(8,128)(2,1)S(1)} %bitcast.330), channel_id=1, replica_groups=mesh['pos'=8,'grp'=4] {'grp'}, dimensions={1} | all-to-all | bytes 802816 | tf_op jit(solution)/shard_map/all_to_all | solution.py:216
  432.2 3.1 fusion.54
  435.4 2.8 fusion.185
  438.2 4.2 all-to-all-start.7
  442.4 95.6 %all-reduce.17.cloned.1.call-done = f32[1568,392]{0,1:T(8,128)} async-done(((f32[1568,392]{0,1:T(8,128)}), f32[1568,392]{0,1:T(8,128)}) %all-reduce.17.cloned.1.call-update) | async-done | bytes 2458640 | tf_op jit(solution)/shard_map/psum | solution.py:217
  542.1 2.9 dot_general.208
  545.0 2.7 fusion.184
  547.8 3.4 all-to-all-start.6
  553.4 2.8 fusion.183
  556.2 3.1 all-to-all-done.6
  559.3 3.5 all-to-all-start.5
  566.6 3.0 fusion.166
  569.7 3.6 all-to-all-done.5
  575.3 4.9 fusion.170
  580.2 38.0 %all-reduce.4 = (f32[1024]{0:T(1024)S(1)}, f32[1024]{0:T(1024)S(1)}) all-reduce(f32[1024]{0:T(1024)S(1)} %get-tuple-element.154, f32[1024]{0:T(1024)S(1)} %get-tuple-element.153), channel_id=1, replica_groups=mesh['pos'=8,'grp'=4] {'pos','grp'}, use_global_device_ids=true, to_apply=%region_33.34 | all-reduce | flops 2048 | bytes 16384 | tf_op jit(solution)/shard_map/psum | solution.py:59
  618.9 3.0 add_convert_fusion
  635.4 41.5 %all-reduce.3 = (f32[256]{0:T(256)S(1)}, f32[256]{0:T(256)S(1)}) all-reduce(f32[256]{0:T(256)S(1)} %get-tuple-element.164, f32[256]{0:T(256)S(1)} %get-tuple-element.163), channel_id=1, replica_groups=mesh['pos'=8,'grp'=4] {'pos','grp'}, use_global_device_ids=true, to_apply=%region_37.38 | all-reduce | flops 512 | bytes 4096 | tf_op jit(solution)/shard_map/psum | solution.py:59
  684.2 2.8 scatter-add.31
  687.0 3.0 fusion.11
  690.0 2.7 scatter-add.34
  717.1 39.3 %all-reduce.2 = (f32[256]{0:T(256)S(1)}, f32[256]{0:T(256)S(1)}) all-reduce(f32[256]{0:T(256)S(1)} %get-tuple-element.160, f32[256]{0:T(256)S(1)} %get-tuple-element.159), channel_id=1, replica_groups=mesh['pos'=8,'grp'=4] {'pos','grp'}, use_global_device_ids=true, to_apply=%region_42.43 | all-reduce | flops 512 | bytes 4096 | tf_op jit(solution)/shard_map/psum | solution.py:59
  763.8 31.3 %reduce-scatter.14.cloned.1.call-done = f32[128,512]{1,0:T(8,128)} async-done(((f32[1024,512]{1,0:T(8,128)}), f32[128,512]{1,0:T(8,128)}) %reduce-scatter.14.cloned.1.call-update) | async-done | bytes 262160 | tf_op jit(solution)/shard_map/reduce_scatter | solution.py:317
  795.1 45.9 %reduce-scatter.10.cloned.1.call-done = f32[9,32,256]{2,1,0:T(8,128)} async-done(((f32[9,256,256]{2,1,0:T(8,128)}), f32[9,32,256]{2,1,0:T(8,128)}) %reduce-scatter.10.cloned.1.call-update) | async-done | bytes 294928 | tf_op jit(solution)/shard_map/reduce_scatter | solution.py:315
  841.0 50.0 %reduce-scatter.8.cloned.1.call-done = f32[3,128,256]{2,1,0:T(8,128)} async-done(((f32[3,1024,256]{2,1,0:T(8,128)}), f32[3,128,256]{2,1,0:T(8,128)}) %reduce-scatter.8.cloned.1.call-update) | async-done | bytes 393232 | tf_op jit(solution)/shard_map/reduce_scatter | solution.py:314
  892.9 4.6 collective-permute-start.3
  898.1 2.7 collective-permute-done.3
  902.4 2.8 add.459
  905.2 69.7 %all-reduce.19.cloned.1.call-done = (f32[3,128,256]{2,1,0:T(8,128)}, f32[9,32,256]{2,1,0:T(8,128)}, f32[256,128]{1,0:T(8,128)}, f32[128,512]{1,0:T(8,128)}, f32[...) async-done(((f32[3,128,256]{2,1,0:T(8,128)}, f32[9,32,256]{2,1,0:T(8,128)}, f32[256,128]{1,0:T(8,128)}, f32[128,512]{1,0:T(8,128)}, f32[128,512]{1,0:T(8,128)}, ...) | async-done | bytes 1867792 | tf_op jit(solution)/shard_map/psum | solution.py:323
  (384 shorter events, 127.4 us)
Async XLA Ops:
  7.2 317.2 %copy-start = (bf16[512,1024]{1,0:T(8,128)(2,1)S(1)}, bf16[512,1024]{1,0:T(8,128)(2,1)}, u32[]{:S(2)}) copy-start(bf16[512,1024]{1,0:T(8,128)(2,1)} %param.56) | copy-start | bytes 3145732
  7.2 11.3 %copy-start.7 = (bf16[392,1024]{1,0:T(8,128)(2,1)S(1)}, bf16[392,1024]{1,0:T(8,128)(2,1)}, u32[]{:S(2)}) copy-start(bf16[392,1024]{1,0:T(8,128)(2,1)} %param.41) | copy-start | bytes 2408452
  7.2 9.9 copy-start.44
  7.2 10.3 %copy-start.104 = (s32[64]{0:T(128)S(1)}, s32[64]{0:T(128)}, u32[]{:S(2)}) copy-start(s32[64]{0:T(128)} %param.42) | copy-start | bytes 772
  9.5 17.5 %collective-permute-start.1 = (bf16[1,196,1024]{2,1,0:T(8,128)(2,1)}, bf16[1,196,1024]{2,1,0:T(8,128)(2,1)S(1)}, u32[]{:S(2)}, u32[]{:S(2)}) collective-permute-start(bf16[1,196,1024]{2,1,0:T(8,128)(2,1)} %get-tuple-element.208), channel_id=1, source_target_pairs={{1,0},{2,1},{3,2},{5,4},{6,5},{7,6},{9,8},{10,9},{11,10},{13,12},{... | collective-permute-start | bytes 1204232 | tf_op jit(solution)/shard_map/ppermute | solution.py:22
  10.8 14.6 %collective-permute-start = (bf16[1,196,1024]{2,1,0:T(8,128)(2,1)}, bf16[1,196,1024]{2,1,0:T(8,128)(2,1)}, u32[]{:S(2)}, u32[]{:S(2)}) collective-permute-start(bf16[1,196,1024]{2,1,0:T(8,128)(2,1)} %get-tuple-element.209), channel_id=1, source_target_pairs={{0,1},{1,2},{2,3},{4,5},{5,6},{6,7},{8,9},{9,10},{10,11},{12,13},{... | collective-permute-start | bytes 1204232 | tf_op jit(solution)/shard_map/ppermute | solution.py:21
  27.7 43.3 %copy-start.45 = (f32[256]{0:T(256)S(1)}, f32[256]{0:T(256)}, u32[]{:S(2)}) copy-start(f32[256]{0:T(256)} %param.45) | copy-start | bytes 3076
  27.7 43.3 %copy-start.55 = (f32[256]{0:T(256)S(1)}, f32[256]{0:T(256)}, u32[]{:S(2)}) copy-start(f32[256]{0:T(256)} %param.46) | copy-start | bytes 3076
  28.1 43.6 %copy-start.11 = (f32[2,196,256]{2,1,0:T(8,128)}, f32[2,196,256]{2,1,0:T(8,128)S(1)}, u32[]{:S(2)}) copy-start(f32[2,196,256]{2,1,0:T(8,128)S(1)} %get-tuple-element.240) | copy-start | bytes 1204228
  28.7 43.2 %copy-start.13 = (f32[2,196,256]{2,0,1:T(2,128)}, f32[2,196,256]{2,0,1:T(2,128)S(1)}, u32[]{:S(2)}) copy-start(f32[2,196,256]{2,0,1:T(2,128)S(1)} %copy.56) | copy-start | bytes 1204228
  73.1 41.5 %copy-start.69 = (f32[256]{0:T(256)S(1)}, f32[256]{0:T(256)}, u32[]{:S(2)}) copy-start(f32[256]{0:T(256)} %param.48) | copy-start | bytes 3076
  73.1 41.5 %copy-start.102 = (f32[256]{0:T(256)S(1)}, f32[256]{0:T(256)}, u32[]{:S(2)}) copy-start(f32[256]{0:T(256)} %param.49) | copy-start | bytes 3076
  73.7 43.5 %copy-start.29 = (f32[392,256]{1,0:T(8,128)}, f32[392,256]{1,0:T(8,128)S(1)}, u32[]{:S(2)}) copy-start(f32[392,256]{1,0:T(8,128)S(1)} %reshape.771) | copy-start | bytes 1204228
  114.6 43.3 %copy-start.49 = (f32[1024]{0:T(1024)S(1)}, f32[1024]{0:T(1024)}, u32[]{:S(2)}) copy-start(f32[1024]{0:T(1024)} %param.51) | copy-start | bytes 12292
  114.6 43.3 %copy-start.67 = (f32[1024]{0:T(1024)S(1)}, f32[1024]{0:T(1024)}, u32[]{:S(2)}) copy-start(f32[1024]{0:T(1024)} %param.52) | copy-start | bytes 12292
  174.2 9.6 all-to-all-start.1
  183.8 13.5 %all-to-all-start = ((bf16[392,4,128]{2,0,1:T(8,128)(2,1)}), bf16[392,4,128]{2,0,1:T(8,128)(2,1)S(1)}, u32[]{:S(2)}, u32[]{:S(2)}) async-start(bf16[392,4,128]{2,0,1:T(8,128)(2,1)} %bitcast.319), calls=%async_computation | async-start | bytes 802816 | tf_op jit(solution)/shard_map/all_to_all | solution.py:192
  187.5 117.2 %all-reduce.15.cloned.1.call-start = ((), (), s32[]{:S(2)}) async-start(), calls=%async_computation.15 | async-start | bytes 5218304 | tf_op jit(solution)/shard_map/psum | solution.py:197
  199.5 10.4 %copy-start.93 = (pred[392]{0:T(512)(128)(4,1)S(1)}, pred[392]{0:T(512)(128)(4,1)}, u32[]{:S(2)}) copy-start(pred[392]{0:T(512)(128)(4,1)} %constant.528) | copy-start | bytes 1180
  199.5 10.4 %copy-start.94 = (pred[392]{0:T(512)(128)(4,1)S(1)}, pred[392]{0:T(512)(128)(4,1)}, u32[]{:S(2)}) copy-start(pred[392]{0:T(512)(128)(4,1)} %constant.527) | copy-start | bytes 1180
  199.5 10.4 %copy-start.95 = (pred[392]{0:T(512)(128)(4,1)S(1)}, pred[392]{0:T(512)(128)(4,1)}, u32[]{:S(2)}) copy-start(pred[392]{0:T(512)(128)(4,1)} %constant.526) | copy-start | bytes 1180
  199.5 10.4 %copy-start.96 = (pred[392]{0:T(512)(128)(4,1)S(1)}, pred[392]{0:T(512)(128)(4,1)}, u32[]{:S(2)}) copy-start(pred[392]{0:T(512)(128)(4,1)} %constant.525) | copy-start | bytes 1180
  199.5 10.4 %copy-start.97 = (pred[392]{0:T(512)(128)(4,1)S(1)}, pred[392]{0:T(512)(128)(4,1)}, u32[]{:S(2)}) copy-start(pred[392]{0:T(512)(128)(4,1)} %constant.524) | copy-start | bytes 1180
  199.5 10.4 %copy-start.98 = (pred[392]{0:T(512)(128)(4,1)S(1)}, pred[392]{0:T(512)(128)(4,1)}, u32[]{:S(2)}) copy-start(pred[392]{0:T(512)(128)(4,1)} %constant.523) | copy-start | bytes 1180
  199.5 10.4 %copy-start.99 = (pred[392]{0:T(512)(128)(4,1)S(1)}, pred[392]{0:T(512)(128)(4,1)}, u32[]{:S(2)}) copy-start(pred[392]{0:T(512)(128)(4,1)} %constant.522) | copy-start | bytes 1180
  206.5 12.2 %all-to-all-start.2 = ((bf16[98,4,128]{2,0,1:T(8,128)(2,1)}), bf16[98,4,128]{2,0,1:T(8,128)(2,1)S(1)}, u32[]{:S(2)}, u32[]{:S(2)}) async-start(bf16[98,4,128]{2,0,1:T(8,128)(2,1)} %copy.62), calls=%async_computation.2 | async-start | bytes 212992 | tf_op jit(solution)/shard_map/all_to_all | solution.py:194
  209.8 328.3 %all-reduce.17.cloned.1.call-start = ((), (), s32[]{:S(2)}) async-start(), calls=%async_computation.16 | async-start | bytes 5218304 | tf_op jit(solution)/shard_map/psum | solution.py:217
  309.2 15.2 %copy-start.2 = (f32[1568,392]{0,1:T(8,128)}, f32[1568,392]{0,1:T(8,128)S(1)}, u32[]{:S(2)}) copy-start(f32[1568,392]{0,1:T(8,128)S(1)} %get-tuple-element.195) | copy-start | bytes 7375876
  326.3 82.1 %copy-start.57 = (f32[1024]{0:T(1024)S(1)}, f32[1024]{0:T(1024)}, u32[]{:S(2)}) copy-start(f32[1024]{0:T(1024)} %param.57) | copy-start | bytes 12292
  326.3 82.8 %copy-start.66 = (f32[1024]{0:T(1024)S(1)}, f32[1024]{0:T(1024)}, u32[]{:S(2)}) copy-start(f32[1024]{0:T(1024)} %param.58) | copy-start | bytes 12292
  430.7 333.0 %reduce-scatter.20.cloned.1.call-start = ((), (), s32[]{:S(2)}) async-start(), calls=%async_computation.23 | async-start | bytes 2359296 | tf_op jit(solution)/shard_map/reduce_scatter | solution.py:320
  435.4 102.7 %copy-start.3 = (f32[1568,392]{0,1:T(8,128)S(1)}, f32[1568,392]{0,1:T(8,128)}, u32[]{:S(2)}) copy-start(f32[1568,392]{0,1:T(8,128)} %copy-done.2) | copy-start | bytes 7375876
  438.2 109.6 %all-to-all-start.7 = ((f32[4,98,128]{2,1,0:T(8,128)}), f32[4,98,128]{2,1,0:T(8,128)}, u32[]{:S(2)}, u32[]{:S(2)}) async-start(f32[4,98,128]{2,1,0:T(8,128)} %fusion.185), calls=%async_computation.7 | async-start | bytes 425984 | tf_op jit(solution)/shard_map/all_to_all | solution.py:226
  547.8 11.5 %all-to-all-start.6 = ((f32[4,98,128]{2,1,0:T(8,128)}), f32[4,98,128]{2,1,0:T(8,128)S(1)}, u32[]{:S(2)}, u32[]{:S(2)}) async-start(f32[4,98,128]{2,1,0:T(8,128)} %fusion.184), calls=%async_computation.6 | async-start | bytes 425984 | tf_op jit(solution)/shard_map/all_to_all | solution.py:225
  559.3 13.9 %all-to-all-start.5 = ((bf16[4,392,128]{2,1,0:T(8,128)(2,1)}), bf16[4,392,128]{2,1,0:T(8,128)(2,1)S(1)}, u32[]{:S(2)}, u32[]{:S(2)}) async-start(bf16[4,392,128]{2,1,0:T(8,128)(2,1)} %fusion.183), calls=%async_computation.5 | async-start | bytes 802816 | tf_op jit(solution)/shard_map/all_to_all | solution.py:224
  562.8 200.9 %reduce-scatter.12.cloned.1.call-start = ((), (), s32[]{:S(2)}) async-start(), calls=%async_computation.19 | async-start | bytes 1179648 | tf_op jit(solution)/shard_map/reduce_scatter | solution.py:316
  575.3 43.0 %copy-start.59 = (f32[1024]{0:T(1024)S(1)}, f32[1024]{0:T(1024)}, u32[]{:S(2)}) copy-start(f32[1024]{0:T(1024)} %copy-done.58) | copy-start | bytes 12292
  624.5 139.3 %reduce-scatter.16.cloned.1.call-start = ((), (), s32[]{:S(2)}) async-start(), calls=%async_computation.21 | async-start | bytes 2359296 | tf_op jit(solution)/shard_map/reduce_scatter | solution.py:318
  626.7 137.1 %reduce-scatter.18.cloned.1.call-start = ((), (), s32[]{:S(2)}) async-start(), calls=%async_computation.22 | async-start | bytes 2359296 | tf_op jit(solution)/shard_map/reduce_scatter | solution.py:319
  630.1 165.1 %reduce-scatter.14.cloned.1.call-start = ((), (), s32[]{:S(2)}) async-start(), calls=%async_computation.20 | async-start | bytes 2359296 | tf_op jit(solution)/shard_map/reduce_scatter | solution.py:317
  679.0 162.0 %reduce-scatter.10.cloned.1.call-start = ((), (), s32[]{:S(2)}) async-start(), calls=%async_computation.18 | async-start | bytes 2654208 | tf_op jit(solution)/shard_map/reduce_scatter | solution.py:315
  701.7 189.3 %reduce-scatter.8.cloned.1.call-start = ((), (), s32[]{:S(2)}) async-start(), calls=%async_computation.17 | async-start | bytes 3538944 | tf_op jit(solution)/shard_map/reduce_scatter | solution.py:314
  715.8 40.6 %copy-start.32 = (f32[392,256]{1,0:T(8,128)S(1)}, f32[392,256]{1,0:T(8,128)}, u32[]{:S(2)}) copy-start(f32[392,256]{1,0:T(8,128)} %reshape.784) | copy-start | bytes 1204228
  717.1 41.8 %copy-start.63 = (f32[2,196]{1,0:T(2,128)S(1)}, f32[2,196]{1,0:T(2,128)}, u32[]{:S(2)}) copy-start(f32[2,196]{1,0:T(2,128)} %copy-done.62) | copy-start | bytes 4708
  763.6 128.8 %copy-start.25 = (bf16[3,1024,256]{2,1,0:T(8,128)(2,1)S(1)}, bf16[3,1024,256]{2,1,0:T(8,128)(2,1)}, u32[]{:S(2)}) copy-start(bf16[3,1024,256]{2,1,0:T(8,128)(2,1)} %param.44) | copy-start | bytes 4718596
  763.6 211.3 %all-reduce.19.cloned.1.call-start = ((), (), s32[]{:S(2)}) async-start(), calls=%async_computation.24 | async-start | bytes 3735552 | tf_op jit(solution)/shard_map/psum | solution.py:323
  891.1 6.6 collective-permute-start.2
  892.9 7.9 collective-permute-start.3
  (77 other events, 261.1 us)
Sparse Core Ops, SparseCore 0:
  199.7 104.9 all-reduce.14
  430.8 107.1 all-reduce.16
  541.3 40.2 reduce-scatter.19
  624.6 36.4 reduce-scatter.11
  664.6 41.1 reduce-scatter.15
  708.9 41.2 reduce-scatter.17
  753.8 41.2 reduce-scatter.13
  798.5 42.4 reduce-scatter.9
  844.8 46.2 reduce-scatter.7
  893.8 81.0 all-reduce.18
where the time goes:
time: 1000 us; the launch traced here: 990 us
  waiting for transfers between devices  410 us (41%)
  blocking collectives  348 us (35%)
  matrix products  75.7 us (8%)
  local copies, waits for them, and re-layouts  54.1 us (5%)
  other arithmetic  50.1 us (5%)
  starting transfers between devices  35.6 us (4%)
  between operations  16.3 us (2%)
    psum x4, blocking collectives, norm_forward(): lax.psum((sum_values, sum_squares), ('pos', 'grp'))  161 us
    psum x4, blocking collectives, norm_backward(): gain_part, shift_part = lax.psum((gain_part, shift_part), ('pos', 'grp'))  159 us
    psum x1, waiting for transfers between devices, local(): d_probs = lax.psum(contract_cols(d_slice, value_slice), 'grp')  95.6 us
    psum x1, waiting for transfers between devices, local(): logits = lax.psum(contract_cols(query_slice, key_slice), 'grp')  85.9 us
    psum x1, waiting for transfers between devices, local(): lax.psum((time_share, space_share, expand_share, query_share, key_share,...  69.7 us
    reduce_scatter x1, waiting for transfers between devices, local(): lax.psum_scatter(time_part, 'pos', scatter_dimension=1, tiled=True)  50 us
    reduce_scatter x1, waiting for transfers between devices, local(): lax.psum_scatter(space_part, 'pos', scatter_dimension=1, tiled=True)  45.9 us
    reduce_scatter x1, waiting for transfers between devices, local(): lax.psum_scatter(query_part, 'pos', scatter_dimension=0, tiled=True)  31.3 us
  transfers between devices with their start and end apart: 20, of which 14 were waited for; matrix products, arithmetic and copies ran while one was open for 12% of the time, Pallas kernels for 0%

commit v1 on v0

v1 whole, which is shorter than its diff:
```python
import functools

import jax
import jax.numpy as jnp
import numpy as np
from jax import lax
from jax.experimental import pallas as pl
from jax.experimental.pallas import tpu as pltpu
from jax.sharding import PartitionSpec as P

SIDE = 14
HALF = SIDE // 2
AREA = SIDE * SIDE
LANE = 128
EDGE = 16
EPSILON = 1e-05
TEMPER = 0.2
MASKED_SCORE = -1000000000.0
PAD_SCORE = -2000000000.0
F32 = jnp.float32
BF16 = jnp.bfloat16
VMEM_BYTES = 24 * 1024 * 1024


def flip(count, bit):
    return [(i, i ^ bit) for i in range(count)]


def dot(left, right):
    return jnp.dot(left, right, preferred_element_type=F32)


def dot_rows(left, right):
    return lax.dot_general(left, right, (((0,), (0,)), ((), ())), preferred_element_type=F32)


def dot_cols(left, right):
    return lax.dot_general(left, right, (((1,), (1,)), ((), ())), preferred_element_type=F32)


def first_count():
    pos_count, grp_count = lax.axis_size("pos"), lax.axis_size("grp")
    return pos_count * grp_count if pos_count * grp_count <= 64 else pos_count


def trade(copies):
    pos_count, grp_count = lax.axis_size("pos"), lax.axis_size("grp")
    if pos_count * grp_count <= 64:
        return lax.all_to_all(copies, ("pos", "grp"), 0, 0, tiled=True)
    part = lax.all_to_all(copies, "pos", 0, 0, tiled=True).sum(0)
    copies = jnp.broadcast_to(part[None], (grp_count,) + part.shape)
    return lax.all_to_all(copies, "grp", 0, 0, tiled=True)


def shrink(part):
    pos_count, grp_count = lax.axis_size("pos"), lax.axis_size("grp")
    place, layer = lax.axis_index("pos"), lax.axis_index("grp")
    bits = pos_count.bit_length() - 1
    held = part.reshape((2,) * bits + part.shape[1:])
    for bit in range(bits):
        axis = bits - 1 - bit
        mine = (place >> bit) & 1
        sent = lax.dynamic_index_in_dim(held, 1 - mine, axis, False).astype(BF16)
        kept = lax.dynamic_index_in_dim(held, mine, axis, False)
        held = kept + lax.ppermute(sent, "pos", flip(pos_count, 1 << bit)).astype(F32)
    levels = grp_count.bit_length() - 1
    for bit in range(levels - 1):
        mine = (layer >> bit) & 1
        pair = held.reshape((2, held.shape[0] // 2) + held.shape[1:])
        sent = lax.dynamic_index_in_dim(pair, 1 - mine, 0, False).astype(BF16)
        kept = lax.dynamic_index_in_dim(pair, mine, 0, False)
        held = kept + lax.ppermute(sent, "grp", flip(grp_count, 1 << bit)).astype(F32)
    low = held.astype(BF16)
    other = lax.ppermute(low, "grp", flip(grp_count, 1 << (levels - 1)))
    held = (low.astype(F32) + other.astype(F32)).astype(BF16)
    for bit in reversed(range(levels - 1)):
        mine = (layer >> bit) & 1
        other = lax.ppermute(held, "grp", flip(grp_count, 1 << bit))
        first = jnp.where(mine == 0, held, other)
        second = jnp.where(mine == 0, other, held)
        held = jnp.concatenate([first, second], axis=0)
    return held.astype(F32)


def call(kernel, outs, scalars, *arrays, scratch=(), flops=0):
    shapes = [jax.ShapeDtypeStruct(shape, kind) for shape, kind in outs]
    moved = sum(int(np.prod(s.shape)) * s.dtype.itemsize for s in shapes)
    moved += sum(a.size * a.dtype.itemsize for a in arrays)
    return pl.pallas_call(
        kernel,
        out_shape=shapes,
        in_specs=[pl.BlockSpec(memory_space=pltpu.SMEM)]
        + [pl.BlockSpec(memory_space=pltpu.VMEM)] * len(arrays),
        out_specs=[pl.BlockSpec(memory_space=pltpu.VMEM)] * len(shapes),
        scratch_shapes=list(scratch),
        compiler_params=pltpu.CompilerParams(vmem_limit_bytes=VMEM_BYTES),
        cost_estimate=pl.CostEstimate(flops=flops, bytes_accessed=moved, transcendentals=0),
    )(scalars, *arrays)


def chunks(width, step=LANE):
    return [slice(start, start + step) for start in range(0, width, step)]


def emit(copies_ref, row, where, value):
    count = copies_ref.shape[0]
    copies_ref[:, row : row + 1, where] = jnp.broadcast_to(
        value[None], (count,) + value.shape
    )


def column_sum(value):
    return jnp.sum(value, axis=0, keepdims=True)


def moments_of(sums, total):
    mean = sums[0:1] / total
    return mean, lax.rsqrt(sums[1:2] / total - mean * mean + EPSILON)


def silu_grad(pre_act, gradient):
    sig = jax.nn.sigmoid(pre_act)
    return gradient * sig * (1.0 + pre_act * (1.0 - sig))


def back_terms(gain, mean, inv, gain_grad, shift_grad, total):
    d_spread = -0.5 * gain * gain_grad * inv * inv
    d_mean = -gain * shift_grad * inv - 2.0 * mean * d_spread
    return gain * inv, d_mean / total, 2.0 * d_spread / total


def border_kernel(sc, x, w, tap_0, tap_2, up, down):
    rows = x.shape[0]
    tap_0[...] = dot(x[...], w[0])
    tap_2[...] = dot(x[...], w[2])
    up[...] = tap_0[rows - AREA : rows, :]
    down[...] = tap_2[0:AREA, :]


def first_kernel(frames, sc, tap_0, tap_1, tap_2, before, after, place, pre, copies, last, first):
    for t in range(frames):
        here = slice(t * AREA, (t + 1) * AREA)
        prev = before[...] if t == 0 else tap_0[(t - 1) * AREA : t * AREA, :]
        following = after[...] if t == frames - 1 else tap_2[(t + 1) * AREA : (t + 2) * AREA, :]
        pre[here, :] = tap_1[here, :] + sc[1 + t] * prev + sc[1 + frames + t] * following
    last[...] = pre[(frames - 1) * AREA : frames * AREA, :]
    first[...] = pre[0:AREA, :]
    valid = place[:, 0:1]
    for c in chunks(pre.shape[1]):
        hidden = pre[:, c]
        masked = hidden * valid
        emit(copies, 0, c, column_sum(masked))
        emit(copies, 1, c, column_sum(masked * hidden))


def inside(place, down, right):
    y = place[:, 2:3] + float(down)
    x = place[:, 1:2] + float(right)
    top = float(SIDE - 1)
    ok = (y >= 0.0) & (y <= top) & (x >= 0.0) & (x <= top)
    return ok.astype(F32)


def fill_padded(padded, value):
    rows, width = value.shape
    padded[0:EDGE, :] = jnp.zeros((EDGE, width), F32)
    padded[EDGE + rows : 2 * EDGE + rows, :] = jnp.zeros((EDGE, width), F32)
    padded[EDGE : EDGE + rows, :] = value


def second_kernel(sc, copies_in, pre_1, gain, shift, w, place, pre_2, windows, copies, stats, padded):
    rows, width = pre_1.shape
    total = sc[0]
    mean, inv = moments_of(jnp.sum(copies_in[...], axis=0), total)
    stats[0:1, :] = mean
    stats[1:2, :] = inv
    act = (pre_1[...] - mean) * inv * gain[...] + shift[...]
    fill_padded(padded, (act * jax.nn.sigmoid(act)).astype(BF16).astype(F32))
    for tap in range(9):
        down, right = tap // 3 - 1, tap % 3 - 1
        start = EDGE + down * SIDE + right
        window = padded[start : start + rows, :]
        if tap != 4:
            window = window * inside(place, down, right)
        windows[:, tap * width : (tap + 1) * width] = window.astype(BF16)
    pre_2[...] = dot(windows[...], w[...])
    valid = place[:, 0:1]
    for c in chunks(width):
        hidden = pre_2[:, c]
        masked = hidden * valid
        emit(copies, 0, c, column_sum(masked))
        emit(copies, 1, c, column_sum(masked * hidden))


def third_kernel(sc, copies_in, pre_2, gain, shift, w, place, cot, z_2, pre_3, copies, stats):
    total = sc[0]
    mean, inv = moments_of(jnp.sum(copies_in[...], axis=0), total)
    stats[0:1, :] = mean
    stats[1:2, :] = inv
    act = (pre_2[...] - mean) * inv * gain[...] + shift[...]
    z_2[...] = (act * jax.nn.sigmoid(act)).astype(BF16)
    valid = place[:, 0:1]
    for c in chunks(w.shape[1], 2 * LANE):
        pre_3[:, c] = dot(z_2[...], w[:, c])
    for c in chunks(w.shape[1]):
        hidden = pre_3[:, c]
        masked = hidden * valid
        emit(copies, 0, c, column_sum(masked))
        emit(copies, 1, c, column_sum(masked * hidden))
        emit(copies, 2, c, column_sum(cot[:, c].astype(F32)))


def unit_kernel(sc, copies_in, pre_3, x, gain, shift, pool, counts, w_key, w_value, unit, pooled, kv, stats):
    total = sc[0]
    sums = jnp.sum(copies_in[...], axis=0)
    mean, inv = moments_of(sums, total)
    stats[0:1, :] = mean
    stats[1:2, :] = inv
    stats[2:3, :] = sums[2:3]
    blocks, inner = pool.shape[0], w_key.shape[1]
    for c in chunks(x.shape[1]):
        scale = inv[:, c] * gain[:, c]
        summed = x[:, c].astype(F32) + (pre_3[:, c] - mean[:, c]) * scale + shift[:, c]
        unit[:, c] = (summed * jax.nn.sigmoid(summed)).astype(BF16)
    for c in chunks(x.shape[1], 2 * LANE):
        sums_here = dot(pool[...], unit[:, c])
        high = sums_here.astype(BF16)
        pooled[0:blocks, c] = high
        pooled[blocks : 2 * blocks, c] = (sums_here - high.astype(F32)).astype(BF16)
    many = jnp.maximum(counts[:, 0:1], 1.0)
    for k, w in enumerate((w_key, w_value)):
        for c in chunks(inner, 2 * LANE):
            both = dot(pooled[...], w[:, c])
            to = slice(k * inner + c.start, k * inner + c.stop)
            kv[:, to] = ((both[:blocks] + both[blocks:]) / many).astype(BF16)


def attend_kernel(slots, sc, theta, w, cot, place, key_row, *refs):
    blocks = refs[:slots]
    kv, probs, attended, pre_4, copies = refs[slots:]
    size, inner = blocks[0].shape[0], theta.shape[1]
    for k in range(slots):
        kv[k * size : (k + 1) * size, :] = blocks[k][...]
    logits = dot_cols(theta[...], kv[:, 0:inner])
    allowed = place[:, 3:4] == key_row[0:1, :]
    scores = jnp.where(allowed, logits * TEMPER, key_row[1:2, :])
    exponent = jnp.exp(scores - jnp.max(scores, axis=1, keepdims=True))
    weights = exponent / jnp.sum(exponent, axis=1, keepdims=True)
    probs[...] = weights
    attended[...] = dot(weights.astype(BF16), kv[:, inner:]).astype(BF16)
    valid = place[:, 0:1]
    for c in chunks(w.shape[1], 2 * LANE):
        pre_4[:, c] = dot(attended[...], w[:, c])
    for c in chunks(w.shape[1]):
        hidden = pre_4[:, c]
        masked = hidden * valid
        emit(copies, 0, c, column_sum(masked))
        emit(copies, 1, c, column_sum(masked * hidden))
        emit(copies, 2, c, column_sum(cot[:, c].astype(F32) * hidden))


def attend_back_kernel(slots, sc, copies_in, stats_3, pre_4, cot, gain, w, probs, kv, theta, place, key_row, *refs):
    d_final, d_logits, stats, own = refs[:4]
    sent = refs[4:]
    total = sc[0]
    size, inner = own.shape[0], theta.shape[1]
    sums = jnp.sum(copies_in[...], axis=0)
    mean, inv = moments_of(sums, total)
    shift_grad = stats_3[2:3, :]
    gain_grad = inv * (sums[2:3] - mean * shift_grad)
    stats[0:1, :] = mean
    stats[1:2, :] = inv
    stats[2:3, :] = gain_grad
    scale, base, slope = back_terms(gain[...], mean, inv, gain_grad, shift_grad, total)
    valid = place[:, 0:1]
    for c in chunks(cot.shape[1]):
        d_final[:, c] = (
            cot[:, c].astype(F32) * scale[:, c]
            + valid * (base[:, c] + pre_4[:, c] * slope[:, c])
        ).astype(BF16)
    d_attended = dot_cols(d_final[...], w[...]).astype(BF16)
    d_probs = dot_cols(d_attended, kv[:, inner:])
    weights = probs[...]
    row_terms = jnp.sum(weights * d_probs, axis=1, keepdims=True)
    allowed = place[:, 3:4] == key_row[0:1, :]
    d_scores = jnp.where(allowed, TEMPER * weights * (d_probs - row_terms), 0.0)
    d_logits[...] = d_scores.astype(BF16)
    d_keys = dot_rows(d_logits[...], theta[...])
    d_values = dot_rows(weights.astype(BF16), d_attended)
    own[:, 0:inner] = d_keys[0:size]
    own[:, inner:] = d_values[0:size]
    for k in range(1, slots):
        here = slice(k * size, (k + 1) * size)
        sent[k - 1][:, 0:inner] = d_keys[here].astype(BF16)
        sent[k - 1][:, inner:] = d_values[here].astype(BF16)


def summed_back_kernel(slots, sc, own, d_unit_part, pre_3, x, stats_3, gain, shift, spread, counts, w_key, w_value, *refs):
    received = refs[: slots - 1]
    d_pooled, d_summed, copies, stacked = refs[slots - 1 :]
    size, inner = own.shape[0], w_key.shape[1]
    many = jnp.maximum(counts[:, 0:1], 1.0)
    whole = own[...]
    for other in received:
        whole = whole + other[...].astype(F32)
    low = (whole / many).astype(BF16)
    d_pooled[0:size, :] = low
    d_pooled[size : 2 * size, :] = low
    for c in chunks(x.shape[1], 2 * LANE):
        part = dot_cols(low[:, 0:inner], w_key[c, :]) + dot_cols(low[:, inner:], w_value[c, :])
        high = part.astype(BF16)
        stacked[0:size, c] = high
        stacked[size : 2 * size, c] = (part - high.astype(F32)).astype(BF16)
    mean, inv = stats_3[0:1, :], stats_3[1:2, :]
    for c in chunks(x.shape[1], 2 * LANE):
        d_unit = d_unit_part[:, c] + dot(spread[...], stacked[:, c])
        normed = (pre_3[:, c] - mean[:, c]) * inv[:, c]
        summed = x[:, c].astype(F32) + normed * gain[:, c] + shift[:, c]
        d_here = silu_grad(summed, d_unit)
        d_summed[:, c] = d_here
        emit(copies, 0, c, column_sum(d_here * normed))
        emit(copies, 1, c, column_sum(d_here))


def third_back_kernel(sc, copies_in, stats_3, gain_3, d_summed, pre_3, w, pre_2, stats_2, gain_2, shift_2, place, d_third, d_act, copies, grads):
    total = sc[0]
    sums = jnp.sum(copies_in[...], axis=0)
    grads[...] = sums
    scale, base, slope = back_terms(
        gain_3[...], stats_3[0:1, :], stats_3[1:2, :], sums[0:1], sums[1:2], total
    )
    valid = place[:, 0:1]
    for c in chunks(d_summed.shape[1]):
        d_third[:, c] = (
            d_summed[:, c] * scale[:, c] + valid * (base[:, c] + pre_3[:, c] * slope[:, c])
        ).astype(BF16)
    d_z = dot_cols(d_third[...], w[...])
    normed = (pre_2[...] - stats_2[0:1, :]) * stats_2[1:2, :]
    d_here = silu_grad(normed * gain_2[...] + shift_2[...], d_z)
    d_act[...] = d_here
    for c in chunks(d_here.shape[1]):
        emit(copies, 0, c, column_sum((d_here * normed)[:, c]))
        emit(copies, 1, c, column_sum(d_here[:, c]))


def second_back_kernel(frames, sc, copies_in, stats_2, gain_2, d_act_2, pre_2, w, pre_1, stats_1, gain_1, shift_1, place, d_second, d_act, copies, grads, last, first, padded):
    total = sc[0]
    rows, width = pre_1.shape
    sums = jnp.sum(copies_in[...], axis=0)
    grads[...] = sums
    scale, base, slope = back_terms(
        gain_2[...], stats_2[0:1, :], stats_2[1:2, :], sums[0:1], sums[1:2], total
    )
    low = (d_act_2[...] * scale + place[:, 0:1] * (base + pre_2[...] * slope)).astype(BF16)
    d_second[...] = low
    fill_padded(padded, low.astype(F32))
    d_z = dot_cols(low, w[4])
    for tap in range(9):
        if tap == 4:
            continue
        down, right = 1 - tap // 3, 1 - tap % 3
        start = EDGE + down * SIDE + right
        window = padded[start : start + rows, :] * inside(place, down, right)
        d_z = d_z + dot_cols(window.astype(BF16), w[tap])
    normed = (pre_1[...] - stats_1[0:1, :]) * stats_1[1:2, :]
    d_here = silu_grad(normed * gain_1[...] + shift_1[...], d_z)
    d_act[...] = d_here
    last[...] = d_act[(frames - 1) * AREA : frames * AREA, :]
    first[...] = d_act[0:AREA, :]
    for c in chunks(width):
        emit(copies, 0, c, column_sum((d_here * normed)[:, c]))
        emit(copies, 1, c, column_sum(d_here[:, c]))


def first_back_kernel(frames, sc, copies_in, stats_1, gain_1, d_act, pre_1, d_before, d_after, pre_before, pre_after, w, d_summed, place, near, input_grad, d_taps, grads, whole, moved):
    total = sc[0]
    width = pre_1.shape[1]
    sums = jnp.sum(copies_in[...], axis=0)
    grads[...] = sums
    scale, base, slope = back_terms(
        gain_1[...], stats_1[0:1, :], stats_1[1:2, :], sums[0:1], sums[1:2], total
    )
    whole[...] = d_act[...] * scale + place[:, 0:1] * (base + pre_1[...] * slope)
    d_taps[:, width : 2 * width] = whole[...].astype(BF16)
    d_prev = d_before[...] * scale + near[:, 0:1] * (base + pre_before[...] * slope)
    d_next = d_after[...] * scale + near[:, 1:2] * (base + pre_after[...] * slope)
    for t in range(frames):
        here = slice(t * AREA, (t + 1) * AREA)
        ahead = d_next if t == frames - 1 else whole[(t + 1) * AREA : (t + 2) * AREA, :]
        moved[here, :] = ahead * sc[1 + frames + t]
    d_taps[:, 0:width] = moved[...].astype(BF16)
    for t in range(frames):
        here = slice(t * AREA, (t + 1) * AREA)
        behind = d_prev if t == 0 else whole[(t - 1) * AREA : t * AREA, :]
        moved[here, :] = behind * sc[1 + t]
    d_taps[:, 2 * width :] = moved[...].astype(BF16)
    for c in chunks(d_summed.shape[1], 2 * LANE):
        value = d_summed[:, c]
        for tap in range(3):
            value = value + dot_cols(d_taps[:, tap * width : (tap + 1) * width], w[tap, c, :])
        input_grad[:, c] = value


def local(
    inputs, segment_ids, pad_mask, time_weight, gain_first, shift_first, space_weight, gain_second,
    shift_second, expand_weight, gain_third, shift_third, query_weight, key_weight, value_weight,
    out_weight, gain_final, shift_final, cotangent,
):
    rows, channels = inputs.shape
    frames = rows // AREA
    narrow = time_weight.shape[2]
    inner = query_weight.shape[1]
    pos_count, grp_count = lax.axis_size("pos"), lax.axis_size("grp")
    group_frames = frames * grp_count
    layer, block = lax.axis_index("grp"), lax.axis_index("pos")
    up = [(i, i + 1) for i in range(grp_count - 1)]
    down = [(i + 1, i) for i in range(grp_count - 1)]
    copies = first_count()
    own_keys = frames * HALF * HALF
    size = -(-own_keys // 16) * 16
    row = lambda v: v.reshape(1, -1)
    gain_1, shift_1, gain_2, shift_2 = map(row, (gain_first, shift_first, gain_second, shift_second))
    gain_3, shift_3, gain_4 = map(row, (gain_third, shift_third, gain_final))

    seg_group = lax.dynamic_slice_in_dim(segment_ids, block * group_frames, group_frames)
    border = jnp.full((1,), -1, jnp.int32)
    seg_padded = jnp.concatenate([border, seg_group, border])
    seg_own = lax.dynamic_slice_in_dim(seg_padded, layer * frames + 1, frames)
    seg_before = lax.dynamic_slice_in_dim(seg_padded, layer * frames, frames)
    seg_after = lax.dynamic_slice_in_dim(seg_padded, layer * frames + 2, frames)
    total = jnp.sum(pad_mask.astype(F32))
    scalars = jnp.concatenate(
        [total[None], (seg_before == seg_own).astype(F32), (seg_after == seg_own).astype(F32)]
    )
    start = (block * grp_count + layer) * rows
    valid = lax.dynamic_slice_in_dim(pad_mask, start, rows).astype(F32)
    spot = np.arange(rows)
    place = jnp.stack(
        [
            valid,
            jnp.asarray(spot % SIDE, F32),
            jnp.asarray(spot % AREA // SIDE, F32),
            jnp.broadcast_to(seg_own[:, None], (frames, AREA)).reshape(rows).astype(F32),
        ],
        axis=1,
    )
    near_start = jnp.stack([jnp.maximum(start - AREA, 0), start + rows])
    near = jnp.stack(
        [lax.dynamic_slice_in_dim(pad_mask, near_start[k], AREA) for k in range(2)], axis=1
    ).astype(F32)
    owner = (spot // AREA) * HALF * HALF + (spot % AREA // SIDE // 2) * HALF + spot % SIDE // 2
    member = np.zeros((size, rows), np.float32)
    member[owner, spot] = 1.0
    pool = (jnp.asarray(member) * valid[None, :]).astype(BF16)
    half_spread = (jnp.asarray(member.T.copy()) * valid[:, None]).astype(BF16)
    spread = jnp.concatenate([half_spread, half_spread], axis=1)
    mask_group = lax.dynamic_slice_in_dim(
        pad_mask, block * group_frames * AREA, group_frames * AREA
    ).astype(F32)
    key_counts = jnp.sum(
        mask_group.reshape(grp_count, frames, HALF, 2, HALF, 2), axis=(3, 5)
    ).reshape(grp_count, own_keys)
    key_seg = jnp.broadcast_to(
        seg_group.reshape(grp_count, frames, 1), (grp_count, frames, HALF * HALF)
    ).reshape(grp_count, own_keys)
    key_seg = jnp.where(key_counts > 0.5, key_seg.astype(F32), -1.0)
    key_seg = jnp.pad(key_seg, ((0, 0), (0, size - own_keys)), constant_values=-1.0)
    order = layer ^ np.arange(grp_count)
    floor = np.full((grp_count, size), MASKED_SCORE, np.float32)
    floor[:, own_keys:] = PAD_SCORE
    key_row = jnp.stack([key_seg[order].reshape(-1), jnp.asarray(floor.reshape(-1))])
    counts = jnp.pad(
        lax.dynamic_index_in_dim(key_counts, layer, 0, False), (0, size - own_keys)
    )[:, None]

    narrow_f32 = ((rows, narrow), F32)
    wide_f32 = ((rows, channels), F32)
    wide_bf16 = ((rows, channels), BF16)
    frame_f32 = ((AREA, narrow), F32)

    tap_0, tap_2, to_next, to_prev = call(
        border_kernel, [narrow_f32, narrow_f32, frame_f32, frame_f32], scalars, inputs, time_weight,
        flops=4 * rows * channels * narrow,
    )
    before = lax.ppermute(to_next, "grp", up)
    after = lax.ppermute(to_prev, "grp", down)
    tap_1 = dot(inputs, time_weight[1])
    pre_1, sums, last, first = call(
        functools.partial(first_kernel, frames),
        [narrow_f32, ((copies, 2, narrow), F32), frame_f32, frame_f32],
        scalars, tap_0, tap_1, tap_2, before, after, place,
    )
    sums = trade(sums)
    pre_before = lax.ppermute(last, "grp", up)
    pre_after = lax.ppermute(first, "grp", down)
    pre_2, windows, sums, stats_1 = call(
        second_kernel,
        [narrow_f32, ((rows, 9 * narrow), BF16), ((copies, 2, narrow), F32), ((2, narrow), F32)],
        scalars, sums, pre_1, gain_1, shift_1, space_weight.reshape(9 * narrow, narrow), place,
        scratch=[pltpu.VMEM((rows + 2 * EDGE, narrow), F32)],
        flops=18 * rows * narrow * narrow,
    )
    sums = trade(sums)
    z_2, pre_3, sums, stats_2 = call(
        third_kernel,
        [((rows, narrow), BF16), wide_f32, ((copies, 3, channels), F32), ((2, narrow), F32)],
        scalars, sums, pre_2, gain_2, shift_2, expand_weight, place, cotangent,
        flops=2 * rows * narrow * channels,
    )
    sums = trade(sums)
    unit, pooled, kv_own, stats_3 = call(
        unit_kernel,
        [wide_bf16, ((2 * size, channels), BF16), ((size, 2 * inner), BF16), ((3, channels), F32)],
        scalars, sums, pre_3, inputs, gain_3, shift_3, pool, counts, key_weight, value_weight,
        flops=2 * size * channels * (rows + 4 * inner),
    )
    kv_blocks = [kv_own] + [
        lax.ppermute(kv_own, "grp", flip(grp_count, step)) for step in range(1, grp_count)
    ]
    theta = dot(unit, query_weight).astype(BF16)
    kv, probs, attended, pre_4, sums = call(
        functools.partial(attend_kernel, grp_count),
        [
            ((grp_count * size, 2 * inner), BF16), ((rows, grp_count * size), F32),
            ((rows, inner), BF16), wide_f32, ((copies, 3, channels), F32),
        ],
        scalars, theta, out_weight, cotangent, place, key_row, *kv_blocks,
        flops=2 * rows * inner * (2 * grp_count * size + channels),
    )
    sums = trade(sums)

    d_final, d_logits, stats_4, d_kv, *d_sent = call(
        functools.partial(attend_back_kernel, grp_count),
        [
            wide_bf16, ((rows, grp_count * size), BF16), ((3, channels), F32),
            ((size, 2 * inner), F32),
        ]
        + [((size, 2 * inner), BF16)] * (grp_count - 1),
        scalars, sums, stats_3, pre_4, cotangent, gain_4, out_weight, probs, kv, theta, place, key_row,
        flops=2 * rows * inner * (3 * grp_count * size + channels),
    )
    d_received = [
        lax.ppermute(d_sent[step - 1], "grp", flip(grp_count, step)) for step in range(1, grp_count)
    ]
    gain_final_grad, shift_final_grad = stats_4[2], stats_3[2]
    output = (
        unit.astype(F32)
        + (pre_4 - stats_4[0]) * stats_4[1] * gain_final
        + shift_final
    ).astype(BF16)
    d_theta = dot(d_logits, kv[:, :inner]).astype(BF16)
    d_unit_part = cotangent.astype(F32) + dot_cols(d_theta, query_weight)
    d_pooled, d_summed, sums = call(
        functools.partial(summed_back_kernel, grp_count),
        [((2 * size, 2 * inner), BF16), wide_f32, ((copies, 2, channels), F32)],
        scalars, d_kv, d_unit_part, pre_3, inputs, stats_3, gain_3, shift_3, spread, counts,
        key_weight, value_weight, *d_received,
        scratch=[pltpu.VMEM((2 * size, channels), BF16)],
        flops=4 * size * channels * (inner + rows),
    )
    sums = trade(sums)
    d_third, d_act_2, sums, grads_3 = call(
        third_back_kernel,
        [wide_bf16, narrow_f32, ((copies, 2, narrow), F32), ((2, channels), F32)],
        scalars, sums, stats_3, gain_3, d_summed, pre_3, expand_weight, pre_2, stats_2, gain_2,
        shift_2, place,
        flops=2 * rows * narrow * channels,
    )
    sums = trade(sums)
    d_second, d_act_1, sums, grads_2, last, first = call(
        functools.partial(second_back_kernel, frames),
        [
            ((rows, narrow), BF16), narrow_f32, ((copies, 2, narrow), F32), ((2, narrow), F32),
            frame_f32, frame_f32,
        ],
        scalars, sums, stats_2, gain_2, d_act_2, pre_2, space_weight, pre_1, stats_1, gain_1,
        shift_1, place,
        scratch=[pltpu.VMEM((rows + 2 * EDGE, narrow), F32)],
        flops=18 * rows * narrow * narrow,
    )
    sums = trade(sums)
    d_before = lax.ppermute(last, "grp", up)
    d_after = lax.ppermute(first, "grp", down)
    input_grad, d_taps, grads_1 = call(
        functools.partial(first_back_kernel, frames),
        [wide_f32, ((rows, 3 * narrow), BF16), ((2, narrow), F32)],
        scalars, sums, stats_1, gain_1, d_act_1, pre_1, d_before, d_after, pre_before, pre_after,
        time_weight, d_summed, place, near,
        scratch=[pltpu.VMEM((rows, narrow), F32), pltpu.VMEM((rows, narrow), F32)],
        flops=6 * rows * narrow * channels,
    )

    def row_shards(part):
        return part.reshape(pos_count, part.shape[0] // pos_count, part.shape[1])

    def col_shards(part):
        wide = part.shape[1] // pos_count
        return part.reshape(part.shape[0], pos_count, wide).transpose(1, 0, 2)

    def bundle(parts):
        return jnp.concatenate([p.reshape(pos_count, -1, LANE) for p in parts], axis=1)

    share_1 = shrink(
        bundle([col_shards(dot_rows(attended, d_final)), row_shards(dot_rows(unit, d_theta))])
    )
    share_2 = shrink(
        bundle(
            [
                row_shards(dot_rows(pooled, d_pooled[:, :inner])),
                row_shards(dot_rows(pooled, d_pooled[:, inner:])),
            ]
        )
    )
    space_part = dot_rows(windows, d_second).reshape(9, narrow, narrow)
    time_part = jnp.stack(
        [dot_rows(inputs, d_taps[:, k * narrow : (k + 1) * narrow]) for k in range(3)]
    )

    def stack_shards(part):
        count, depth, wide = part.shape
        cut = part.reshape(count, pos_count, depth // pos_count, wide)
        return cut.transpose(1, 0, 2, 3)

    share_3 = shrink(
        bundle([col_shards(dot_rows(z_2, d_third)), stack_shards(space_part)])
    )
    share_4 = shrink(bundle([stack_shards(time_part)]))

    def take(share, start, shape):
        extent = int(np.prod(shape)) // LANE
        return share[start : start + extent].reshape(shape)

    deep, wide = channels // pos_count, narrow // pos_count
    half = deep * inner // LANE
    out_grad = take(share_1, 0, (inner, deep))
    query_grad = take(share_1, half, (deep, inner))
    key_grad = take(share_2, 0, (deep, inner))
    value_grad = take(share_2, half, (deep, inner))
    expand_grad = take(share_3, 0, (narrow, deep))
    space_grad = take(share_3, narrow * deep // LANE, (9, wide, narrow))
    time_grad = take(share_4, 0, (3, deep, narrow))
    return (
        output, input_grad, time_grad, grads_1[0], grads_1[1], space_grad,
        grads_2[0], grads_2[1], expand_grad, grads_3[0], grads_3[1],
        query_grad, key_grad, value_grad, out_grad, gain_final_grad, shift_final_grad,
    )


def solution(mesh):
    split = P(("pos", "grp"), None)
    in_specs = (split,) + (P(),) * 17 + (split,)
    out_specs = (
        split, split, P(None, "pos", None), P(), P(), P(None, "pos", None), P(), P(),
        P(None, "pos"), P(), P(), P("pos", None), P("pos", None), P("pos", None),
        P(None, "pos"), P(), P(),
    )
    return jax.shard_map(local, mesh=mesh, in_specs=in_specs, out_specs=out_specs, check_vma=False)
```

time: 1000 us -> 340 us (0.34)
  blocking collectives: 348 us -> 0 us
  waiting for transfers between devices: 410 us -> 89.7 us
  matrix products: 75.7 us -> 15.8 us
  local copies, waits for them, and re-layouts: 54.1 us -> 98.8 us
  starting transfers between devices: 35.6 us -> 78.5 us
  Pallas kernels: 0 us -> 26.4 us
  other arithmetic: 50.1 us -> 26.9 us
  between operations: 16.3 us -> 1.91 us
    psum x8 -> x0, blocking collectives: 320 us -> none  [the longest x4 161 us: norm_forward(): lax.psum((sum_values, sum_squares), ('pos', 'grp'))]
    psum x3 -> x0, waiting for transfers between devices: 251 us -> none  [the longest x1 95.6 us: local(): d_probs = lax.psum(contract_cols(d_slice, value_slice), 'grp')]
    reduce_scatter x7 -> x0, waiting for transfers between devices: 127 us -> none  [the longest x1 50 us: local(): lax.psum_scatter(time_part, 'pos', scatter_dimension=1, tiled=True)]
    dot_general x57 -> x13, matrix products: 75.7 us -> 15.8 us  [the longest x9 11.6 us: dot_rows(): lax.dot_general(left, right, (((0,), (0,)), ((), ())), preferred_element_...]
    ppermute x4 -> x36, waiting for transfers between devices: 6.93 us -> 58.4 us  [the longest x3 18 us: local(): lax.ppermute(kv_own, 'grp', flip(grp_count, step))]
    unnamed x219 -> x236, local copies, waits for them, and re-layouts: 15.5 us -> 57.8 us
    ppermute x4 -> x36, starting transfers between devices: 13.4 us -> 51.5 us  [the longest x12 9.79 us: shrink(): lax.ppermute(sent, 'pos', flip(pos_count, 1 << bit)).astype(F32)]
    all_to_all x2 -> x0, blocking collectives: 28.2 us -> none  [the longest x1 14.5 us: local(): lax.all_to_all(mixed_slice, 'grp', split_axis=0, concat_axis=1, tiled=True)]
  transfers between devices with their start and end apart: 20 -> 43, of which waited for: 14 -> 23; matrix products, arithmetic and copies ran while one was open for 12% -> 24% of each run, Pallas kernels for 0% -> 4%
where the time goes in v1:
time: 340 us; the launch traced here: 338 us
  local copies, waits for them, and re-layouts  98.8 us (29%)
  waiting for transfers between devices  89.7 us (26%)
  starting transfers between devices  78.5 us (23%)
  other arithmetic  26.9 us (8%)
  Pallas kernels  26.4 us (8%)
  matrix products  15.8 us (5%)
    unnamed x236, local copies, waits for them, and re-layouts  57.8 us
    all_to_all x7, waiting for transfers between devices, trade(): return lax.all_to_all(copies, ('pos', 'grp'), 0, 0, tiled=True)  31.3 us
    all_to_all x7, starting transfers between devices, trade(): return lax.all_to_all(copies, ('pos', 'grp'), 0, 0, tiled=True)  27 us
    pallas_call x11, Pallas kernels, call(): pl.pallas_call(kernel, out_shape=shapes, in_specs=[pl.BlockSpec(memory_sp...  26.4 us
    ppermute x3, waiting for transfers between devices, local(): lax.ppermute(kv_own, 'grp', flip(grp_count, step))  18 us
    dot_general x9, matrix products, dot_rows(): lax.dot_general(left, right, (((0,), (0,)), ((), ())), preferred_element_...  11.6 us
    concatenate x6, local copies, waits for them, and re-layouts, bundle(): jnp.concatenate([p.reshape(pos_count, -1, LANE) for p in parts], axis=1)  11.4 us
    ppermute x12, starting transfers between devices, shrink(): lax.ppermute(sent, 'pos', flip(pos_count, 1 << bit)).astype(F32)  9.79 us
  transfers between devices with their start and end apart: 43, of which 23 were waited for; matrix products, arithmetic and copies ran while one was open for 24% of the time, Pallas kernels for 4%

profile of v1, /device:TPU:0, one launch (start us, length us, event | category | flops | bytes accessed | tf_op | source)
XLA Modules:
  0.0 338.0 jit_solution(3489213386610331167)
XLA Ops:
  9.0 5.1 %collective-permute-start = (f32[196,256]{1,0:T(8,128)S(1)}, f32[196,256]{1,0:T(8,128)S(1)}, u32[]{:S(2)}, u32[]{:S(2)}) collective-permute-start(f32[196,256]{1,0:T(8,128)S(1)} %get-tuple-element.67), channel_id=1, source_target_pairs={{0,1},{1,2},{2,3},{4,5},{5,6},{6,7},{8,9},{9,10},{10,11},{12,13},{... | collective-permute-start | bytes 602120 | tf_op jit(solution)/shard_map/ppermute | solution.py:485
  18.4 4.1 %collective-permute-done.1.after = f32[196,256]{1,0:T(8,128)S(1)} collective-permute-done((f32[196,256]{1,0:T(8,128)S(1)}, f32[196,256]{1,0:T(8,128)S(1)}, u32[]{:S(2)}, u32[]{:S(2)}) %collective-permute-start.1) | collective-permute-done | bytes 200736 | tf_op jit(solution)/shard_map/ppermute | solution.py:486
  28.9 4.8 %all-to-all-start = ((f32[32,2,256]{2,1,0:T(2,128)}), f32[32,2,256]{2,1,0:T(2,128)S(1)}, u32[]{:S(2)}, u32[]{:S(2)}) async-start(f32[32,2,256]{2,1,0:T(2,128)} %get-tuple-element.69), calls=%async_computation | async-start | bytes 131072 | tf_op jit(solution)/shard_map/all_to_all | solution.py:49
  34.5 6.7 %all-to-all-done.copies_in = f32[32,2,256]{2,1,0:T(2,128)S(1)} async-done(((f32[32,2,256]{2,1,0:T(2,128)}), f32[32,2,256]{2,1,0:T(2,128)S(1)}, u32[]{:S(2)}, u32[]{:S(2)}) %all-to-all-start) | async-done | bytes 65568 | tf_op jit(solution)/shard_map/all_to_all | solution.py:49
  42.5 3.3 shard_map.370
  48.4 2.6 all-to-all-start.1
  53.5 5.0 %all-to-all-done.1.copies_in = f32[32,2,256]{2,1,0:T(2,128)S(1)} async-done(((f32[32,2,256]{2,1,0:T(2,128)}), f32[32,2,256]{2,1,0:T(2,128)S(1)}, u32[]{:S(2)}, u32[]{:S(2)}) %all-to-all-start.1) | async-done | bytes 65568 | tf_op jit(solution)/shard_map/all_to_all | solution.py:49
  65.2 2.6 all-to-all-start.2
  70.2 12.0 %all-to-all-done.2.copies_in = f32[32,3,1024]{2,1,0:T(4,128)S(1)} async-done(((f32[32,3,1024]{2,1,0:T(4,128)}), f32[32,3,1024]{2,1,0:T(4,128)S(1)}, u32[]{:S(2)}, u32[]{:S(2)}) %all-to-all-start.2) | async-done | bytes 393248 | tf_op jit(solution)/shard_map/all_to_all | solution.py:49
  87.4 2.0 shard_map.372
  89.5 2.8 collective-permute-start.4
  94.6 5.3 %collective-permute-done.4.refs_3_ = bf16[112,1024]{1,0:T(8,128)(2,1)S(1)} collective-permute-done((bf16[112,1024]{1,0:T(8,128)(2,1)S(1)}, bf16[112,1024]{1,0:T(8,128)(2,1)S(1)}, u32[]{:S(2)}, u32[]{:S(2)}) %collective-permute-start.4) | collective-permute-done | bytes 229408 | tf_op jit(solution)/shard_map/ppermute | solution.py:518
  99.9 12.7 %collective-permute-done.3.refs_2_ = bf16[112,1024]{1,0:T(8,128)(2,1)S(1)} collective-permute-done((bf16[112,1024]{1,0:T(8,128)(2,1)S(1)}, bf16[112,1024]{1,0:T(8,128)(2,1)S(1)}, u32[]{:S(2)}, u32[]{:S(2)}) %collective-permute-start.3) | collective-permute-done | bytes 229408 | tf_op jit(solution)/shard_map/ppermute | solution.py:518
  112.6 2.4 shard_map.373
  119.7 3.4 %all-to-all-start.3 = ((f32[32,3,1024]{2,1,0:T(4,128)}), f32[32,3,1024]{2,1,0:T(4,128)S(1)}, u32[]{:S(2)}, u32[]{:S(2)}) async-start(f32[32,3,1024]{2,1,0:T(4,128)} %copy-done.50), calls=%async_computation.3 | async-start | bytes 1048576 | tf_op jit(solution)/shard_map/all_to_all | solution.py:49
  127.2 4.4 %collective-permute-start.10 = (f32[196,256]{1,0:T(8,128)}, f32[196,256]{1,0:T(8,128)}, u32[]{:S(2)}, u32[]{:S(2)}) collective-permute-start(f32[196,256]{1,0:T(8,128)} %copy-done.99), channel_id=1, source_target_pairs={{0,1},{1,2},{2,3},{4,5},{5,6},{6,7},{8,9},{9,10},{10,11},{12,13},{... | collective-permute-start | bytes 602120 | tf_op jit(solution)/shard_map/ppermute | solution.py:494
  133.6 3.8 %all-to-all-done.3.copies_in = f32[32,3,1024]{2,1,0:T(4,128)S(1)} async-done(((f32[32,3,1024]{2,1,0:T(4,128)}), f32[32,3,1024]{2,1,0:T(4,128)S(1)}, u32[]{:S(2)}, u32[]{:S(2)}) %all-to-all-start.3) | async-done | bytes 393248 | tf_op jit(solution)/shard_map/all_to_all | solution.py:49
  145.4 3.5 %shard_map.374 = (bf16[392,1024]{1,0:T(8,128)(2,1)S(1)}, bf16[392,448]{1,0:T(8,128)(2,1)S(1)}, f32[3,1024]{1,0:T(4,128)S(1)}, f32[112,1024]{1,0:T(8,128)S(1)}, b...) custom-call(f32[5]{0:T(128)S(1)} %copy-done.76, ...), custom_call_target="tpu_custom_call" | custom-call | flops 950534144 | bytes 8211072 | tf_op jit(solution)/shard_map/pallas_call | solution.py:89
  149.3 2.1 fusion.46
  153.8 2.5 collective-permute-start.5
  158.7 2.7 concatenate.55
  168.6 7.2 %collective-permute-done.6.refs_1_ = bf16[112,1024]{1,0:T(8,128)(2,1)S(1)} collective-permute-done((bf16[112,1024]{1,0:T(8,128)(2,1)}, bf16[112,1024]{1,0:T(8,128)(2,1)S(1)}, u32[]{:S(2)}, u32[]{:S(2)}) %collective-permute-start.6) | collective-permute-done | bytes 229408 | tf_op jit(solution)/shard_map/ppermute | solution.py:543
  179.1 3.1 shard_map.375
  183.4 5.1 %all-to-all-start.4 = ((f32[32,2,1024]{2,1,0:T(2,128)}), f32[32,2,1024]{2,1,0:T(2,128)S(1)}, u32[]{:S(2)}, u32[]{:S(2)}) async-start(f32[32,2,1024]{2,1,0:T(2,128)} %get-tuple-element.88), calls=%async_computation.4 | async-start | bytes 524288 | tf_op jit(solution)/shard_map/all_to_all | solution.py:49
  192.1 2.6 concatenate.59
  194.7 2.6 concatenate.58
  205.2 2.1 shard_map.376
  208.0 6.0 %all-to-all-start.5 = ((f32[32,2,256]{2,1,0:T(2,128)}), f32[32,2,256]{2,1,0:T(2,128)S(1)}, u32[]{:S(2)}, u32[]{:S(2)}) async-start(f32[32,2,256]{2,1,0:T(2,128)} %get-tuple-element.91), calls=%async_computation.5 | async-start | bytes 131072 | tf_op jit(solution)/shard_map/all_to_all | solution.py:49
  217.5 3.8 %all-to-all-done.5.copies_in = f32[32,2,256]{2,1,0:T(2,128)S(1)} async-done(((f32[32,2,256]{2,1,0:T(2,128)}), f32[32,2,256]{2,1,0:T(2,128)S(1)}, u32[]{:S(2)}, u32[]{:S(2)}) %all-to-all-start.5) | async-done | bytes 65568 | tf_op jit(solution)/shard_map/all_to_all | solution.py:49
  222.3 2.8 shard_map.377
  227.3 2.6 all-to-all-start.6
  229.8 3.6 %collective-permute-start.8 = (f32[196,256]{1,0:T(8,128)S(1)}, f32[196,256]{1,0:T(8,128)S(1)}, u32[]{:S(2)}, u32[]{:S(2)}) collective-permute-start(f32[196,256]{1,0:T(8,128)S(1)} %get-tuple-element.96), channel_id=1, source_target_pairs={{0,1},{1,2},{2,3},{4,5},{5,6},{6,7},{8,9},{9,10},{10,11},{12,13},{... | collective-permute-start | bytes 602120 | tf_op jit(solution)/shard_map/ppermute | solution.py:582
  233.5 2.4 fusion.45
  237.4 3.2 concatenate.51
  240.7 2.5 fusion.7
  245.1 2.1 bitcast_add_fusion.1
  250.3 2.3 collective-permute-done.9.d_after
  255.4 3.2 shard_map.378
  264.0 3.9 %maximum_bitcast_fusion = f32[8,3,128,256]{3,2,1,0:T(8,128)} fusion(f32[1,8,128,256]{3,2,0,1:T(8,128)} %bitcast.181, f32[1,8,128,256]{3,2,0,1:T(8,128)} %bitcast.182, f32[1,8,128,256]{3,2,0,1:T(8,128)} %bitcast.183), kind=kLoop, calls=%fused_computation.5 | loop fusion | flops 1572864 | bytes 6291456 | tf_op jit(solution)/shard_map/transpose | solution.py:622
  267.8 4.4 %reshape_reshape.4 = f32[2,2,2,768,128]{4,3,2,1,0:T(8,128)} reshape(f32[8,3,128,256]{3,2,1,0:T(8,128)} %maximum_bitcast_fusion) | data formatting | bytes 6291456 | tf_op jit(solution)/shard_map/reshape;reshape | solution.py:59
  274.4 2.2 bitcast_add_fusion
  283.4 8.2 %collective-permute-done.31 = bf16[2,1024,128]{2,1,0:T(8,128)(2,1)S(1)} collective-permute-done((bf16[2,1024,128]{2,1,0:T(8,128)(2,1)S(1)}, bf16[2,1024,128]{2,1,0:T(8,128)(2,1)S(1)}, u32[]{:S(2)}, u32[]{:S(2)}) %collective-permute-start.31) | collective-permute-done | bytes 524320 | tf_op jit(solution)/shard_map/ppermute | solution.py:65
  298.4 2.6 collective-permute-start.28
  301.5 4.4 %collective-permute-done.28 = bf16[512,128]{1,0:T(8,128)(2,1)S(1)} collective-permute-done((bf16[512,128]{1,0:T(8,128)(2,1)S(1)}, bf16[512,128]{1,0:T(8,128)(2,1)S(1)}, u32[]{:S(2)}, u32[]{:S(2)}) %collective-permute-start.28) | collective-permute-done | bytes 131104 | tf_op jit(solution)/shard_map/ppermute | solution.py:74
  307.6 2.3 collective-permute-start.34
  322.8 2.2 collective-permute-start.22
  326.7 2.2 collective-permute-done.22
  328.9 2.1 collective-permute-start.23
  (404 shorter events, 150.8 us)
Async XLA Ops:
  0.7 93.3 %copy-start = (bf16[1024,512]{1,0:T(8,128)(2,1)S(1)}, bf16[1024,512]{1,0:T(8,128)(2,1)}, u32[]{:S(2)}) copy-start(bf16[1024,512]{1,0:T(8,128)(2,1)} %param.37) | copy-start | bytes 3145732
  6.4 75.8 %copy-start.74 = (f32[5]{0:T(128)}, f32[5]{0:T(128)S(1)}, u32[]{:S(2)}) copy-start(f32[5]{0:T(128)S(1)} %pad_maximum_fusion.3.sc) | copy-start | bytes 64
  9.0 9.4 %collective-permute-start = (f32[196,256]{1,0:T(8,128)S(1)}, f32[196,256]{1,0:T(8,128)S(1)}, u32[]{:S(2)}, u32[]{:S(2)}) collective-permute-start(f32[196,256]{1,0:T(8,128)S(1)} %get-tuple-element.67), channel_id=1, source_target_pairs={{0,1},{1,2},{2,3},{4,5},{5,6},{6,7},{8,9},{9,10},{10,11},{12,13},{... | collective-permute-start | bytes 602120 | tf_op jit(solution)/shard_map/ppermute | solution.py:485
  14.1 8.4 %collective-permute-start.1 = (f32[196,256]{1,0:T(8,128)S(1)}, f32[196,256]{1,0:T(8,128)S(1)}, u32[]{:S(2)}, u32[]{:S(2)}) collective-permute-start(f32[196,256]{1,0:T(8,128)S(1)} %get-tuple-element.68), channel_id=1, source_target_pairs={{1,0},{2,1},{3,2},{5,4},{6,5},{7,6},{9,8},{10,9},{11,10},{13,12},{... | collective-permute-start | bytes 602120 | tf_op jit(solution)/shard_map/ppermute | solution.py:486
  26.1 32.4 %copy-start.88 = (f32[256]{0:T(256)S(1)}, f32[256]{0:T(256)}, u32[]{:S(2)}) copy-start(f32[256]{0:T(256)} %param.32) | copy-start | bytes 3076
  26.1 32.4 %copy-start.96 = (f32[256]{0:T(256)S(1)}, f32[256]{0:T(256)}, u32[]{:S(2)}) copy-start(f32[256]{0:T(256)} %param.33) | copy-start | bytes 3076
  28.9 33.1 %copy-start.27 = (f32[392,256]{1,0:T(8,128)}, f32[392,256]{1,0:T(8,128)S(1)}, u32[]{:S(2)}) copy-start(f32[392,256]{1,0:T(8,128)S(1)} %get-tuple-element.70.pre_1) | copy-start | bytes 1204228
  28.9 12.3 %all-to-all-start = ((f32[32,2,256]{2,1,0:T(2,128)}), f32[32,2,256]{2,1,0:T(2,128)S(1)}, u32[]{:S(2)}, u32[]{:S(2)}) async-start(f32[32,2,256]{2,1,0:T(2,128)} %get-tuple-element.69), calls=%async_computation | async-start | bytes 131072 | tf_op jit(solution)/shard_map/all_to_all | solution.py:49
  48.4 10.1 %all-to-all-start.1 = ((f32[32,2,256]{2,1,0:T(2,128)}), f32[32,2,256]{2,1,0:T(2,128)S(1)}, u32[]{:S(2)}, u32[]{:S(2)}) async-start(f32[32,2,256]{2,1,0:T(2,128)} %get-tuple-element.71), calls=%async_computation.1 | async-start | bytes 131072 | tf_op jit(solution)/shard_map/all_to_all | solution.py:49
  65.2 17.0 %all-to-all-start.2 = ((f32[32,3,1024]{2,1,0:T(4,128)}), f32[32,3,1024]{2,1,0:T(4,128)S(1)}, u32[]{:S(2)}, u32[]{:S(2)}) async-start(f32[32,3,1024]{2,1,0:T(4,128)} %copy-done.51), calls=%async_computation.2 | async-start | bytes 1048576 | tf_op jit(solution)/shard_map/all_to_all | solution.py:49
  89.5 10.3 %collective-permute-start.4 = (bf16[112,1024]{1,0:T(8,128)(2,1)S(1)}, bf16[112,1024]{1,0:T(8,128)(2,1)S(1)}, u32[]{:S(2)}, u32[]{:S(2)}) collective-permute-start(bf16[112,1024]{1,0:T(8,128)(2,1)S(1)} %get-tuple-element.76.refs_0_), channel_id=1, source_target_pairs={{0,3},{1,2},{2,1},{3,0},{4,7},{5,6},{6,5},{7,4},{8,11},{9,10},{10,... | collective-permute-start | bytes 688136 | tf_op jit(solution)/shard_map/ppermute | solution.py:518
  92.3 20.2 %collective-permute-start.3 = (bf16[112,1024]{1,0:T(8,128)(2,1)S(1)}, bf16[112,1024]{1,0:T(8,128)(2,1)S(1)}, u32[]{:S(2)}, u32[]{:S(2)}) collective-permute-start(bf16[112,1024]{1,0:T(8,128)(2,1)S(1)} %get-tuple-element.76.refs_0_), channel_id=1, source_target_pairs={{0,2},{1,3},{2,0},{3,1},{4,6},{5,7},{6,4},{7,5},{8,10},{9,11},{10,... | collective-permute-start | bytes 688136 | tf_op jit(solution)/shard_map/ppermute | solution.py:518
  93.6 19.0 %collective-permute-start.2 = (bf16[112,1024]{1,0:T(8,128)(2,1)S(1)}, bf16[112,1024]{1,0:T(8,128)(2,1)S(1)}, u32[]{:S(2)}, u32[]{:S(2)}) collective-permute-start(bf16[112,1024]{1,0:T(8,128)(2,1)S(1)} %get-tuple-element.76.refs_0_), channel_id=1, source_target_pairs={{0,1},{1,0},{2,3},{3,2},{4,5},{5,4},{6,7},{7,6},{8,9},{9,8},{10,11... | collective-permute-start | bytes 688136 | tf_op jit(solution)/shard_map/ppermute | solution.py:518
  119.7 17.8 %all-to-all-start.3 = ((f32[32,3,1024]{2,1,0:T(4,128)}), f32[32,3,1024]{2,1,0:T(4,128)S(1)}, u32[]{:S(2)}, u32[]{:S(2)}) async-start(f32[32,3,1024]{2,1,0:T(4,128)} %copy-done.50), calls=%async_computation.3 | async-start | bytes 1048576 | tf_op jit(solution)/shard_map/all_to_all | solution.py:49
  127.2 121.1 %collective-permute-start.10 = (f32[196,256]{1,0:T(8,128)}, f32[196,256]{1,0:T(8,128)}, u32[]{:S(2)}, u32[]{:S(2)}) collective-permute-start(f32[196,256]{1,0:T(8,128)} %copy-done.99), channel_id=1, source_target_pairs={{0,1},{1,2},{2,3},{4,5},{5,6},{6,7},{8,9},{9,10},{10,11},{12,13},{... | collective-permute-start | bytes 602120 | tf_op jit(solution)/shard_map/ppermute | solution.py:494
  131.5 116.7 %collective-permute-start.11 = (f32[196,256]{1,0:T(8,128)}, f32[196,256]{1,0:T(8,128)}, u32[]{:S(2)}, u32[]{:S(2)}) collective-permute-start(f32[196,256]{1,0:T(8,128)} %copy-done.98), channel_id=1, source_target_pairs={{1,0},{2,1},{3,2},{5,4},{6,5},{7,6},{9,8},{10,9},{11,10},{13,12},{... | collective-permute-start | bytes 602120 | tf_op jit(solution)/shard_map/ppermute | solution.py:495
  153.8 14.8 %collective-permute-start.5 = (bf16[112,1024]{1,0:T(8,128)(2,1)}, bf16[112,1024]{1,0:T(8,128)(2,1)S(1)}, u32[]{:S(2)}, u32[]{:S(2)}) collective-permute-start(bf16[112,1024]{1,0:T(8,128)(2,1)} %get-tuple-element.85), channel_id=1, source_target_pairs={{0,1},{1,0},{2,3},{3,2},{4,5},{5,4},{6,7},{7,6},{8,9},{9,8},{10,11... | collective-permute-start | bytes 688136 | tf_op jit(solution)/shard_map/ppermute | solution.py:543
  156.3 19.5 %collective-permute-start.6 = (bf16[112,1024]{1,0:T(8,128)(2,1)}, bf16[112,1024]{1,0:T(8,128)(2,1)S(1)}, u32[]{:S(2)}, u32[]{:S(2)}) collective-permute-start(bf16[112,1024]{1,0:T(8,128)(2,1)} %get-tuple-element.86), channel_id=1, source_target_pairs={{0,2},{1,3},{2,0},{3,1},{4,6},{5,7},{6,4},{7,5},{8,10},{9,11},{10,... | collective-permute-start | bytes 688136 | tf_op jit(solution)/shard_map/ppermute | solution.py:543
  157.2 19.2 %collective-permute-start.7 = (bf16[112,1024]{1,0:T(8,128)(2,1)}, bf16[112,1024]{1,0:T(8,128)(2,1)S(1)}, u32[]{:S(2)}, u32[]{:S(2)}) collective-permute-start(bf16[112,1024]{1,0:T(8,128)(2,1)} %get-tuple-element.87), channel_id=1, source_target_pairs={{0,3},{1,2},{2,1},{3,0},{4,7},{5,6},{6,5},{7,4},{8,11},{9,10},{10,... | collective-permute-start | bytes 688136 | tf_op jit(solution)/shard_map/ppermute | solution.py:543
  168.6 75.1 %collective-permute-start.24 = (bf16[2,2,1024,128]{3,2,1,0:T(8,128)(2,1)}, bf16[2,2,1024,128]{3,2,1,0:T(8,128)(2,1)}, u32[]{:S(2)}, u32[]{:S(2)}) collective-permute-start(bf16[2,2,1024,128]{3,2,1,0:T(8,128)(2,1)} %fusion.5), channel_id=1, source_target_pairs={{0,4},{4,0},{8,12},{12,8},{16,20},{20,16},{24,28},{28,24},{1,5},{5... | collective-permute-start | bytes 3145736 | tf_op jit(solution)/shard_map/ppermute | solution.py:65
  183.4 18.9 %all-to-all-start.4 = ((f32[32,2,1024]{2,1,0:T(2,128)}), f32[32,2,1024]{2,1,0:T(2,128)S(1)}, u32[]{:S(2)}, u32[]{:S(2)}) async-start(f32[32,2,1024]{2,1,0:T(2,128)} %get-tuple-element.88), calls=%async_computation.4 | async-start | bytes 524288 | tf_op jit(solution)/shard_map/all_to_all | solution.py:49
  202.1 72.4 %collective-permute-start.30 = (bf16[2,2,1024,128]{3,2,1,0:T(8,128)(2,1)}, bf16[2,2,1024,128]{3,2,1,0:T(8,128)(2,1)}, u32[]{:S(2)}, u32[]{:S(2)}) collective-permute-start(bf16[2,2,1024,128]{3,2,1,0:T(8,128)(2,1)} %fusion.6), channel_id=1, source_target_pairs={{0,4},{4,0},{8,12},{12,8},{16,20},{20,16},{24,28},{28,24},{1,5},{5... | collective-permute-start | bytes 3145736 | tf_op jit(solution)/shard_map/ppermute | solution.py:65
  208.0 13.3 %all-to-all-start.5 = ((f32[32,2,256]{2,1,0:T(2,128)}), f32[32,2,256]{2,1,0:T(2,128)S(1)}, u32[]{:S(2)}, u32[]{:S(2)}) async-start(f32[32,2,256]{2,1,0:T(2,128)} %get-tuple-element.91), calls=%async_computation.5 | async-start | bytes 131072 | tf_op jit(solution)/shard_map/all_to_all | solution.py:49
  227.3 23.0 %all-to-all-start.6 = ((f32[32,2,256]{2,1,0:T(2,128)}), f32[32,2,256]{2,1,0:T(2,128)S(1)}, u32[]{:S(2)}, u32[]{:S(2)}) async-start(f32[32,2,256]{2,1,0:T(2,128)} %get-tuple-element.94), calls=%async_computation.6 | async-start | bytes 131072 | tf_op jit(solution)/shard_map/all_to_all | solution.py:49
  229.8 20.4 %collective-permute-start.8 = (f32[196,256]{1,0:T(8,128)S(1)}, f32[196,256]{1,0:T(8,128)S(1)}, u32[]{:S(2)}, u32[]{:S(2)}) collective-permute-start(f32[196,256]{1,0:T(8,128)S(1)} %get-tuple-element.96), channel_id=1, source_target_pairs={{0,1},{1,2},{2,3},{4,5},{5,6},{6,7},{8,9},{9,10},{10,11},{12,13},{... | collective-permute-start | bytes 602120 | tf_op jit(solution)/shard_map/ppermute | solution.py:582
  243.7 8.9 %collective-permute-start.9 = (f32[196,256]{1,0:T(8,128)S(1)}, f32[196,256]{1,0:T(8,128)S(1)}, u32[]{:S(2)}, u32[]{:S(2)}) collective-permute-start(f32[196,256]{1,0:T(8,128)S(1)} %copy-done.101), channel_id=1, source_target_pairs={{1,0},{2,1},{3,2},{5,4},{6,5},{7,6},{9,8},{10,9},{11,10},{13,12},{... | collective-permute-start | bytes 602120 | tf_op jit(solution)/shard_map/ppermute | solution.py:583
  248.3 32.8 %collective-permute-start.18 = (bf16[2,2,832,128]{3,2,1,0:T(8,128)(2,1)}, bf16[2,2,832,128]{3,2,1,0:T(8,128)(2,1)}, u32[]{:S(2)}, u32[]{:S(2)}) collective-permute-start(bf16[2,2,832,128]{3,2,1,0:T(8,128)(2,1)} %fusion.7), channel_id=1, source_target_pairs={{0,4},{4,0},{8,12},{12,8},{16,20},{20,16},{24,28},{28,24},{1,5},{5... | collective-permute-start | bytes 2555912 | tf_op jit(solution)/shard_map/ppermute | solution.py:65
  248.8 29.5 %collective-permute-start.25 = (bf16[2,1024,128]{2,1,0:T(8,128)(2,1)}, bf16[2,1024,128]{2,1,0:T(8,128)(2,1)}, u32[]{:S(2)}, u32[]{:S(2)}) collective-permute-start(bf16[2,1024,128]{2,1,0:T(8,128)(2,1)} %fusion.9), channel_id=1, source_target_pairs={{0,8},{4,12},{8,0},{12,4},{16,24},{20,28},{24,16},{28,20},{1,9},{5... | collective-permute-start | bytes 1572872 | tf_op jit(solution)/shard_map/ppermute | solution.py:65
  274.3 20.6 %collective-permute-start.12 = (bf16[2,2,768,128]{3,2,1,0:T(8,128)(2,1)S(1)}, bf16[2,2,768,128]{3,2,1,0:T(8,128)(2,1)S(1)}, u32[]{:S(2)}, u32[]{:S(2)}) collective-permute-start(bf16[2,2,768,128]{3,2,1,0:T(8,128)(2,1)S(1)} %fusion.8), channel_id=1, source_target_pairs={{0,4},{4,0},{8,12},{12,8},{16,20},{20,16},{24,28},{28,24},{1,5},{5... | collective-permute-start | bytes 2359304 | tf_op jit(solution)/shard_map/ppermute | solution.py:65
  276.8 14.8 %collective-permute-start.31 = (bf16[2,1024,128]{2,1,0:T(8,128)(2,1)S(1)}, bf16[2,1024,128]{2,1,0:T(8,128)(2,1)S(1)}, u32[]{:S(2)}, u32[]{:S(2)}) collective-permute-start(bf16[2,1024,128]{2,1,0:T(8,128)(2,1)S(1)} %fusion.10), channel_id=1, source_target_pairs={{0,8},{4,12},{8,0},{12,4},{16,24},{20,28},{24,16},{28,20},{1,9},{5... | collective-permute-start | bytes 1572872 | tf_op jit(solution)/shard_map/ppermute | solution.py:65
  279.5 13.7 %collective-permute-start.26 = (bf16[1024,128]{1,0:T(8,128)(2,1)S(1)}, bf16[1024,128]{1,0:T(8,128)(2,1)S(1)}, u32[]{:S(2)}, u32[]{:S(2)}) collective-permute-start(bf16[1024,128]{1,0:T(8,128)(2,1)S(1)} %fusion.17), channel_id=1, source_target_pairs={{0,16},{4,20},{8,24},{12,28},{16,0},{20,4},{24,8},{28,12},{1,17},{... | collective-permute-start | bytes 786440 | tf_op jit(solution)/shard_map/ppermute | solution.py:65
  282.5 23.6 %collective-permute-start.19 = (bf16[2,832,128]{2,1,0:T(8,128)(2,1)S(1)}, bf16[2,832,128]{2,1,0:T(8,128)(2,1)S(1)}, u32[]{:S(2)}, u32[]{:S(2)}) collective-permute-start(bf16[2,832,128]{2,1,0:T(8,128)(2,1)S(1)} %fusion.15), channel_id=1, source_target_pairs={{0,8},{4,12},{8,0},{12,4},{16,24},{20,28},{24,16},{28,20},{1,9},{5... | collective-permute-start | bytes 1277960 | tf_op jit(solution)/shard_map/ppermute | solution.py:65
  291.7 9.3 %collective-permute-start.32 = (bf16[1024,128]{1,0:T(8,128)(2,1)S(1)}, bf16[1024,128]{1,0:T(8,128)(2,1)S(1)}, u32[]{:S(2)}, u32[]{:S(2)}) collective-permute-start(bf16[1024,128]{1,0:T(8,128)(2,1)S(1)} %fusion.18), channel_id=1, source_target_pairs={{0,16},{4,20},{8,24},{12,28},{16,0},{20,4},{24,8},{28,12},{1,17},{... | collective-permute-start | bytes 786440 | tf_op jit(solution)/shard_map/ppermute | solution.py:65
  293.4 5.0 %collective-permute-start.27 = (bf16[512,128]{1,0:T(8,128)(2,1)S(1)}, bf16[512,128]{1,0:T(8,128)(2,1)S(1)}, u32[]{:S(2)}, u32[]{:S(2)}) collective-permute-start(bf16[512,128]{1,0:T(8,128)(2,1)S(1)} %fusion.32), channel_id=1, source_target_pairs={{0,1},{1,0},{2,3},{3,2},{4,5},{5,4},{6,7},{7,6},{8,9},{9,8},{10,11... | collective-permute-start | bytes 393224 | tf_op jit(solution)/shard_map/ppermute | solution.py:72
  296.0 17.2 %collective-permute-start.13 = (bf16[2,768,128]{2,1,0:T(8,128)(2,1)}, bf16[2,768,128]{2,1,0:T(8,128)(2,1)S(1)}, u32[]{:S(2)}, u32[]{:S(2)}) collective-permute-start(bf16[2,768,128]{2,1,0:T(8,128)(2,1)} %fusion.16), channel_id=1, source_target_pairs={{0,8},{4,12},{8,0},{12,4},{16,24},{20,28},{24,16},{28,20},{1,9},{5... | collective-permute-start | bytes 1179656 | tf_op jit(solution)/shard_map/ppermute | solution.py:65
  298.4 7.4 %collective-permute-start.28 = (bf16[512,128]{1,0:T(8,128)(2,1)S(1)}, bf16[512,128]{1,0:T(8,128)(2,1)S(1)}, u32[]{:S(2)}, u32[]{:S(2)}) collective-permute-start(bf16[512,128]{1,0:T(8,128)(2,1)S(1)} %fusion.20), channel_id=1, source_target_pairs={{0,2},{1,3},{2,0},{3,1},{4,6},{5,7},{6,4},{7,5},{8,10},{9,11},{10,... | collective-permute-start | bytes 393224 | tf_op jit(solution)/shard_map/ppermute | solution.py:74
  301.1 6.5 %collective-permute-start.33 = (bf16[512,128]{1,0:T(8,128)(2,1)S(1)}, bf16[512,128]{1,0:T(8,128)(2,1)S(1)}, u32[]{:S(2)}, u32[]{:S(2)}) collective-permute-start(bf16[512,128]{1,0:T(8,128)(2,1)S(1)} %fusion.33), channel_id=1, source_target_pairs={{0,1},{1,0},{2,3},{3,2},{4,5},{5,4},{6,7},{7,6},{8,9},{9,8},{10,11... | collective-permute-start | bytes 393224 | tf_op jit(solution)/shard_map/ppermute | solution.py:72
  305.9 5.7 %collective-permute-start.29 = (bf16[512,128]{1,0:T(8,128)(2,1)S(1)}, bf16[512,128]{1,0:T(8,128)(2,1)S(1)}, u32[]{:S(2)}, u32[]{:S(2)}) collective-permute-start(bf16[512,128]{1,0:T(8,128)(2,1)S(1)} %add_convert_fusion.2), channel_id=1, source_target_pairs={{0,1},{1,0},{2,3},{3,2},{4,5},{5,4},{6,7},{7,6},{8,9},{9,8},{10,11... | collective-permute-start | bytes 393224 | tf_op jit(solution)/shard_map/ppermute | solution.py:78
  306.9 9.6 %collective-permute-start.20 = (bf16[832,128]{1,0:T(8,128)(2,1)}, bf16[832,128]{1,0:T(8,128)(2,1)S(1)}, u32[]{:S(2)}, u32[]{:S(2)}) collective-permute-start(bf16[832,128]{1,0:T(8,128)(2,1)} %fusion.25), channel_id=1, source_target_pairs={{0,16},{4,20},{8,24},{12,28},{16,0},{20,4},{24,8},{28,12},{1,17},{... | collective-permute-start | bytes 638984 | tf_op jit(solution)/shard_map/ppermute | solution.py:65
  307.6 7.6 %collective-permute-start.34 = (bf16[512,128]{1,0:T(8,128)(2,1)S(1)}, bf16[512,128]{1,0:T(8,128)(2,1)}, u32[]{:S(2)}, u32[]{:S(2)}) collective-permute-start(bf16[512,128]{1,0:T(8,128)(2,1)S(1)} %fusion.19), channel_id=1, source_target_pairs={{0,2},{1,3},{2,0},{3,1},{4,6},{5,7},{6,4},{7,5},{8,10},{9,11},{10,... | collective-permute-start | bytes 393224 | tf_op jit(solution)/shard_map/ppermute | solution.py:74
  313.3 5.7 %collective-permute-start.14 = (bf16[768,128]{1,0:T(8,128)(2,1)S(1)}, bf16[768,128]{1,0:T(8,128)(2,1)S(1)}, u32[]{:S(2)}, u32[]{:S(2)}) collective-permute-start(bf16[768,128]{1,0:T(8,128)(2,1)S(1)} %fusion.30), channel_id=1, source_target_pairs={{0,16},{4,20},{8,24},{12,28},{16,0},{20,4},{24,8},{28,12},{1,17},{... | collective-permute-start | bytes 589832 | tf_op jit(solution)/shard_map/ppermute | solution.py:65
  316.1 5.0 %collective-permute-start.35 = (bf16[512,128]{1,0:T(8,128)(2,1)S(1)}, bf16[512,128]{1,0:T(8,128)(2,1)S(1)}, u32[]{:S(2)}, u32[]{:S(2)}) collective-permute-start(bf16[512,128]{1,0:T(8,128)(2,1)S(1)} %add_convert_fusion.1), channel_id=1, source_target_pairs={{0,1},{1,0},{2,3},{3,2},{4,5},{5,4},{6,7},{7,6},{8,9},{9,8},{10,11... | collective-permute-start | bytes 393224 | tf_op jit(solution)/shard_map/ppermute | solution.py:78
  316.6 6.2 %collective-permute-start.21 = (bf16[416,128]{1,0:T(8,128)(2,1)S(1)}, bf16[416,128]{1,0:T(8,128)(2,1)S(1)}, u32[]{:S(2)}, u32[]{:S(2)}) collective-permute-start(bf16[416,128]{1,0:T(8,128)(2,1)S(1)} %fusion.34), channel_id=1, source_target_pairs={{0,1},{1,0},{2,3},{3,2},{4,5},{5,4},{6,7},{7,6},{8,9},{9,8},{10,11... | collective-permute-start | bytes 319496 | tf_op jit(solution)/shard_map/ppermute | solution.py:72
  319.1 6.6 %collective-permute-start.15 = (bf16[384,128]{1,0:T(8,128)(2,1)S(1)}, bf16[384,128]{1,0:T(8,128)(2,1)S(1)}, u32[]{:S(2)}, u32[]{:S(2)}) collective-permute-start(bf16[384,128]{1,0:T(8,128)(2,1)S(1)} %fusion.35), channel_id=1, source_target_pairs={{0,1},{1,0},{2,3},{3,2},{4,5},{5,4},{6,7},{7,6},{8,9},{9,8},{10,11... | collective-permute-start | bytes 294920 | tf_op jit(solution)/shard_map/ppermute | solution.py:72
  322.8 6.1 %collective-permute-start.22 = (bf16[416,128]{1,0:T(8,128)(2,1)S(1)}, bf16[416,128]{1,0:T(8,128)(2,1)S(1)}, u32[]{:S(2)}, u32[]{:S(2)}) collective-permute-start(bf16[416,128]{1,0:T(8,128)(2,1)S(1)} %fusion.26), channel_id=1, source_target_pairs={{0,2},{1,3},{2,0},{3,1},{4,6},{5,7},{6,4},{7,5},{8,10},{9,11},{10,... | collective-permute-start | bytes 319496 | tf_op jit(solution)/shard_map/ppermute | solution.py:74
  325.7 6.7 %collective-permute-start.16 = (bf16[384,128]{1,0:T(8,128)(2,1)S(1)}, bf16[384,128]{1,0:T(8,128)(2,1)S(1)}, u32[]{:S(2)}, u32[]{:S(2)}) collective-permute-start(bf16[384,128]{1,0:T(8,128)(2,1)S(1)} %fusion.31), channel_id=1, source_target_pairs={{0,2},{1,3},{2,0},{3,1},{4,6},{5,7},{6,4},{7,5},{8,10},{9,11},{10,... | collective-permute-start | bytes 294920 | tf_op jit(solution)/shard_map/ppermute | solution.py:74
  328.9 4.8 %collective-permute-start.23 = (bf16[416,128]{1,0:T(8,128)(2,1)S(1)}, bf16[416,128]{1,0:T(8,128)(2,1)S(1)}, u32[]{:S(2)}, u32[]{:S(2)}) collective-permute-start(bf16[416,128]{1,0:T(8,128)(2,1)S(1)} %add_convert_fusion.3), channel_id=1, source_target_pairs={{0,1},{1,0},{2,3},{3,2},{4,5},{5,4},{6,7},{7,6},{8,9},{9,8},{10,11... | collective-permute-start | bytes 319496 | tf_op jit(solution)/shard_map/ppermute | solution.py:78
  332.4 4.7 %collective-permute-start.17 = (bf16[384,128]{1,0:T(8,128)(2,1)S(1)}, bf16[384,128]{1,0:T(8,128)(2,1)S(1)}, u32[]{:S(2)}, u32[]{:S(2)}) collective-permute-start(bf16[384,128]{1,0:T(8,128)(2,1)S(1)} %add_convert_fusion.4), channel_id=1, source_target_pairs={{0,1},{1,0},{2,3},{3,2},{4,5},{5,4},{6,7},{7,6},{8,9},{9,8},{10,11... | collective-permute-start | bytes 294920 | tf_op jit(solution)/shard_map/ppermute | solution.py:78
  (111 other events, 650.2 us)

commit v2 on v1

--- a/solution.py
+++ b/solution.py
@@ -19,7 +19,7 @@
 PAD_SCORE = -2000000000.0
 F32 = jnp.float32
 BF16 = jnp.bfloat16
-VMEM_BYTES = 24 * 1024 * 1024
+VMEM_BYTES = 60 * 1024 * 1024
 
 
 def flip(count, bit):
@@ -52,34 +52,8 @@
     return lax.all_to_all(copies, "grp", 0, 0, tiled=True)
 
 
-def shrink(part):
-    pos_count, grp_count = lax.axis_size("pos"), lax.axis_size("grp")
-    place, layer = lax.axis_index("pos"), lax.axis_index("grp")
-    bits = pos_count.bit_length() - 1
-    held = part.reshape((2,) * bits + part.shape[1:])
-    for bit in range(bits):
-        axis = bits - 1 - bit
-        mine = (place >> bit) & 1
-        sent = lax.dynamic_index_in_dim(held, 1 - mine, axis, False).astype(BF16)
-        kept = lax.dynamic_index_in_dim(held, mine, axis, False)
-        held = kept + lax.ppermute(sent, "pos", flip(pos_count, 1 << bit)).astype(F32)
-    levels = grp_count.bit_length() - 1
-    for bit in range(levels - 1):
-        mine = (layer >> bit) & 1
-        pair = held.reshape((2, held.shape[0] // 2) + held.shape[1:])
-        sent = lax.dynamic_index_in_dim(pair, 1 - mine, 0, False).astype(BF16)
-        kept = lax.dynamic_index_in_dim(pair, mine, 0, False)
-        held = kept + lax.ppermute(sent, "grp", flip(grp_count, 1 << bit)).astype(F32)
-    low = held.astype(BF16)
-    other = lax.ppermute(low, "grp", flip(grp_count, 1 << (levels - 1)))
-    held = (low.astype(F32) + other.astype(F32)).astype(BF16)
-    for bit in reversed(range(levels - 1)):
-        mine = (layer >> bit) & 1
-        other = lax.ppermute(held, "grp", flip(grp_count, 1 << bit))
-        first = jnp.where(mine == 0, held, other)
-        second = jnp.where(mine == 0, other, held)
-        held = jnp.concatenate([first, second], axis=0)
-    return held.astype(F32)
+def tie(wanted, *others):
+    return lax.optimization_barrier((wanted,) + others)
 
 
 def call(kernel, outs, scalars, *arrays, scratch=(), flops=0):
@@ -89,13 +63,13 @@
     return pl.pallas_call(
         kernel,
         out_shape=shapes,
-        in_specs=[pl.BlockSpec(memory_space=pltpu.SMEM)]
+        in_specs=[pl.BlockSpec(memory_space=pltpu.SMEM)] * len(scalars)
         + [pl.BlockSpec(memory_space=pltpu.VMEM)] * len(arrays),
         out_specs=[pl.BlockSpec(memory_space=pltpu.VMEM)] * len(shapes),
         scratch_shapes=list(scratch),
         compiler_params=pltpu.CompilerParams(vmem_limit_bytes=VMEM_BYTES),
         cost_estimate=pl.CostEstimate(flops=flops, bytes_accessed=moved, transcendentals=0),
-    )(scalars, *arrays)
+    )(*scalars, *arrays)
 
 
 def chunks(width, step=LANE):
@@ -129,7 +103,7 @@
     return gain * inv, d_mean / total, 2.0 * d_spread / total
 
 
-def border_kernel(sc, x, w, tap_0, tap_2, up, down):
+def border_kernel(x, w, tap_0, tap_2, up, down):
     rows = x.shape[0]
     tap_0[...] = dot(x[...], w[0])
     tap_2[...] = dot(x[...], w[2])
@@ -401,6 +375,280 @@
         input_grad[:, c] = value
 
 
+def put(both, part, start, value):
+    rows = value.shape[0]
+    for k, c in enumerate(chunks(value.shape[1])):
+        both[part & 1, part >> 1, start + k * rows : start + (k + 1) * rows, :] = value[:, c]
+
+
+def pack(both, part, start, value):
+    wide = value.shape[1]
+    fold = LANE // wide
+    step = LANE // fold
+    for k in range(fold):
+        both[part & 1, part >> 1, start : start + step, k * wide : (k + 1) * wide] = value[
+            k * step : (k + 1) * step, :
+        ]
+
+
+def split_out(mine, start, both, low, send, keep, sems):
+    rows = low.shape[1]
+    kept = pltpu.make_async_copy(both.at[mine], keep.at[:, start : start + rows], sems.at[0])
+    kept.start()
+    low[...] = both[1 - mine].astype(BF16)
+    sent = pltpu.make_async_copy(low, send.at[:, start : start + rows], sems.at[1])
+    sent.start()
+    kept.wait()
+    sent.wait()
+
+
+def attend_grads_kernel(parts, start, bits, d_logits, kv, cot, w, attended, d_final, unit, send, keep, d_unit_part, d_theta, both, low, sems):
+    inner, channels = attended.shape[1], unit.shape[1]
+    d_theta[...] = dot(d_logits[...], kv[:, 0:inner]).astype(BF16)
+    for c in chunks(channels, 2 * LANE):
+        d_unit_part[:, c] = cot[:, c].astype(F32) + dot_cols(d_theta[...], w[c, :])
+    wide = channels // parts
+    for p in range(parts):
+        here = slice(p * wide, (p + 1) * wide)
+        put(both, p, inner * wide // LANE, dot_rows(unit[:, here], d_theta[...]))
+    for c in chunks(inner):
+        grad = dot_rows(attended[:, c], d_final[...])
+        for p in range(parts):
+            pack(both, p, c.start * wide // LANE, grad[:, p * wide : (p + 1) * wide])
+    split_out(bits[0], start, both, low, send, keep, sems)
+
+
+def pooled_grads_kernel(parts, start, bits, send_in, keep_in, pooled, d_pooled, send, keep, both, low, sems):
+    wide = pooled.shape[1] // parts
+    for p in range(parts):
+        put(both, p, 0, dot_rows(pooled[:, p * wide : (p + 1) * wide], d_pooled[...]))
+    split_out(bits[0], start, both, low, send, keep, sems)
+
+
+def expand_grads_kernel(parts, start, bits, z_2, d_third, send, keep, both, low, sems):
+    wide = d_third.shape[1] // parts
+    for c in chunks(z_2.shape[1]):
+        grad = dot_rows(z_2[:, c], d_third[...])
+        for p in range(parts):
+            pack(both, p, c.start * wide // LANE, grad[:, p * wide : (p + 1) * wide])
+    split_out(bits[0], start, both, low, send, keep, sems)
+
+
+def space_grads_kernel(parts, start, bits, send_in, keep_in, windows, d_second, send, keep, both, low, sems):
+    width = d_second.shape[1]
+    wide = width // parts
+    for tap in range(9):
+        grad = dot_rows(windows[:, tap * width : (tap + 1) * width], d_second[...])
+        for p in range(parts):
+            put(both, p, tap * wide * width // LANE, grad[p * wide : (p + 1) * wide, :])
+    split_out(bits[0], start, both, low, send, keep, sems)
+
+
+def time_grads_kernel(parts, start, bits, send_in, keep_in, x, d_taps, send, keep, both, low, sems):
+    wide = x.shape[1] // parts
+    for p in range(parts):
+        put(both, p, 0, dot_rows(x[:, p * wide : (p + 1) * wide], d_taps[...]))
+    split_out(bits[0], start, both, low, send, keep, sems)
+
+
+def core_stage_kernel(cut, low_bit, high_bit, bits, keep_in, received, send_1, keep_1, send_2, keep_2):
+    count = send_1.shape[0]
+    rows = keep_in.shape[1]
+    for send, keep, bit, here, low in (
+        (send_1, keep_1, low_bit, slice(0, cut), True),
+        (send_2, keep_2, high_bit, slice(cut, rows), False),
+    ):
+        mine = bits[bit]
+        for i in range(count):
+            at = 2 * i + mine if low else i + count * mine
+            off = 2 * i + 1 - mine if low else i + count * (1 - mine)
+            keep[i] = keep_in[at, here, :] + received[at, here, :].astype(F32)
+            send[i] = (keep_in[off, here, :] + received[off, here, :].astype(F32)).astype(BF16)
+
+
+def plane_stage_kernel(low_bit, high_bit, bits, in_1, received_1, in_2, received_2, send_1, keep_1, send_2, keep_2):
+    count = send_1.shape[0]
+    for keep_in, received, send, keep, bit, low in (
+        (in_1, received_1, send_1, keep_1, low_bit, True),
+        (in_2, received_2, send_2, keep_2, high_bit, False),
+    ):
+        mine = bits[bit]
+        for i in range(count):
+            at = 2 * i + mine if low else i + count * mine
+            off = 2 * i + 1 - mine if low else i + count * (1 - mine)
+            keep[i] = keep_in[at] + received[at].astype(F32)
+            send[i] = (keep_in[off] + received[off].astype(F32)).astype(BF16)
+
+
+def layer_stage_kernel(bit, bits, in_1, received_1, in_2, received_2, send, keep):
+    first = in_1[...] + received_1[...].astype(F32)
+    second = in_2[...] + received_2[...].astype(F32)
+    swap = bits[bit] == 1
+    keep[...] = jnp.where(swap, second, first)
+    send[...] = jnp.where(swap, first, second).astype(BF16)
+
+
+def half_stage_kernel(bit, bits, keep_in, received, send, keep):
+    mine = bits[bit]
+    keep[0] = keep_in[mine] + received[mine].astype(F32)
+    send[0] = (keep_in[1 - mine] + received[1 - mine].astype(F32)).astype(BF16)
+
+
+def join_kernel(keep_in, received, low):
+    low[...] = (keep_in[...] + received[...].astype(F32)).astype(BF16)
+
+
+def exchange_kernel(low, received, final):
+    final[...] = (low[...].astype(F32) + received[...].astype(F32)).astype(BF16)
+
+
+def unfold(part, start, out):
+    rows = out.shape[0]
+    for k, c in enumerate(chunks(out.shape[1])):
+        out[:, c] = part[start + k * rows : start + (k + 1) * rows, :]
+
+
+def attend_outs_kernel(bit, bits, mine, other, out_grad, query_grad, key_grad, value_grad, first, second):
+    swap = bits[bit] == 1
+    here, there = mine[0].astype(F32), other[0].astype(F32)
+    first[...] = jnp.where(swap, there, here)
+    second[...] = jnp.where(swap, here, there)
+    unfold(first, 0, out_grad)
+    unfold(first, out_grad.shape[0], query_grad)
+    unfold(second, 0, key_grad)
+    unfold(second, first.shape[0] // 2, value_grad)
+
+
+def bottleneck_outs_kernel(bit, bits, mine, other, expand_grad, space_grad, time_grad, first, second):
+    swap = bits[bit] == 1
+    here, there = mine[0].astype(F32), other[0].astype(F32)
+    first[...] = jnp.where(swap, there, here)
+    second[...] = jnp.where(swap, here, there)
+    unfold(first, 0, expand_grad)
+    taps, deep, width = space_grad.shape
+    for tap in range(taps):
+        start = expand_grad.shape[0] + tap * deep * width // LANE
+        for k, c in enumerate(chunks(width)):
+            space_grad[tap, :, c] = first[start + k * deep : start + (k + 1) * deep, :]
+    taps, deep, width = time_grad.shape
+    for tap in range(taps):
+        for k, c in enumerate(chunks(width)):
+            start = (tap * width // LANE + k) * deep
+            time_grad[tap, :, c] = second[start : start + deep, :]
+
+
+class Bundle:
+    def __init__(self, bits, cut):
+        self.bits, self.cut = bits, cut
+        self.pos_count, self.grp_count = lax.axis_size("pos"), lax.axis_size("grp")
+        self.pos_bits = self.pos_count.bit_length() - 1
+        self.grp_bits = self.grp_count.bit_length() - 1
+        self.send = self.keep = None
+
+    def add(self, kernel, start, rows, *arrays, extra=(), flops=0):
+        whole = (self.pos_count // 2, 2 * self.cut, LANE)
+        half = (self.pos_count // 2, rows, LANE)
+        held = () if self.send is None else (self.send, self.keep)
+        anywhere = pl.BlockSpec(memory_space=pl.ANY)
+        inside_vmem = pl.BlockSpec(memory_space=pltpu.VMEM)
+        shapes = [jax.ShapeDtypeStruct(whole, BF16), jax.ShapeDtypeStruct(whole, F32)]
+        shapes += [jax.ShapeDtypeStruct(shape, kind) for shape, kind in extra]
+        moved = sum(a.size * a.dtype.itemsize for a in arrays) + 6 * int(np.prod(half))
+        self.send, self.keep, *rest = pl.pallas_call(
+            functools.partial(kernel, self.pos_count, start),
+            out_shape=shapes,
+            in_specs=[pl.BlockSpec(memory_space=pltpu.SMEM)]
+            + [anywhere] * len(held)
+            + [inside_vmem] * len(arrays),
+            out_specs=[anywhere, anywhere] + [inside_vmem] * len(extra),
+            scratch_shapes=[
+                pltpu.VMEM((2,) + half, F32), pltpu.VMEM(half, BF16), pltpu.SemaphoreType.DMA((2,)),
+            ],
+            input_output_aliases={1: 0, 2: 1} if held else {},
+            compiler_params=pltpu.CompilerParams(vmem_limit_bytes=VMEM_BYTES),
+            cost_estimate=pl.CostEstimate(flops=flops, bytes_accessed=moved, transcendentals=0),
+        )(self.bits, *held, *arrays)
+        return rest
+
+    def begin(self):
+        self.received = lax.ppermute(self.send, "pos", flip(self.pos_count, 1))
+
+    def plane(self):
+        count = self.pos_count // 4
+        bits = (1, self.pos_bits - 1)
+        outs = []
+        for rows in (self.cut, self.cut):
+            outs += [((count, rows, LANE), BF16), ((count, rows, LANE), F32)]
+        outs = call(
+            functools.partial(core_stage_kernel, self.cut, *bits), outs, (self.bits,),
+            self.keep, self.received,
+        )
+        self.parts = [list(outs[:2]), list(outs[2:])]
+        self.pair = bits
+        self.turn()
+
+    def turn(self):
+        for k in range(2):
+            pairs = flip(self.pos_count, 1 << self.pair[k])
+            self.parts[k].append(lax.ppermute(self.parts[k][0], "pos", pairs))
+
+    def more(self):
+        while self.parts[0][1].shape[0] > 1:
+            count = self.parts[0][1].shape[0] // 2
+            self.pair = (self.pair[0] + 1, self.pair[1] - 1)
+            outs = [((count, self.cut, LANE), BF16), ((count, self.cut, LANE), F32)] * 2
+            (_, keep_1, got_1), (_, keep_2, got_2) = self.parts
+            outs = call(
+                functools.partial(plane_stage_kernel, *self.pair), outs, (self.bits,),
+                keep_1, got_1, keep_2, got_2,
+            )
+            self.parts = [list(outs[:2]), list(outs[2:])]
+            self.turn()
+
+    def layer(self):
+        (_, keep_1, got_1), (_, keep_2, got_2) = self.parts
+        shape = (1, self.cut, LANE)
+        send, keep = call(
+            functools.partial(layer_stage_kernel, self.pos_bits), [(shape, BF16), (shape, F32)],
+            (self.bits,), keep_1, got_1, keep_2, got_2,
+        )
+        got = lax.ppermute(send, "grp", flip(self.grp_count, 1))
+        for bit in range(1, self.grp_bits - 1):
+            shape = (2, keep.shape[1] // 2, LANE)
+            half = (1,) + shape[1:]
+            send, keep = call(
+                functools.partial(half_stage_kernel, self.pos_bits + bit),
+                [(half, BF16), (half, F32)], (self.bits,), keep.reshape(shape), got.reshape(shape),
+            )
+            got = lax.ppermute(send, "grp", flip(self.grp_count, 1 << bit))
+        (self.low,) = call(join_kernel, [(keep.shape, BF16)], (), keep, got)
+        self.other = lax.ppermute(self.low, "grp", flip(self.grp_count, self.grp_count // 2))
+
+    def finish(self):
+        (final,) = call(exchange_kernel, [(self.low.shape, BF16)], (), self.low, self.other)
+        for bit in reversed(range(1, self.grp_bits - 1)):
+            mine = self.bits[self.pos_bits + bit]
+            other = lax.ppermute(final, "grp", flip(self.grp_count, 1 << bit))
+            lower = jnp.where(mine == 0, final, other)
+            upper = jnp.where(mine == 0, other, final)
+            final = jnp.concatenate([lower, upper], axis=1)
+        self.mine = final
+        self.other = lax.ppermute(final, "grp", flip(self.grp_count, 1))
+
+    def outs(self, kernel, shapes):
+        part = pltpu.VMEM((self.cut, LANE), F32)
+        return call(
+            functools.partial(kernel, self.pos_bits), [(shape, F32) for shape in shapes],
+            (self.bits,), self.mine, self.other, scratch=[part, part],
+        )
+
+    def shares(self):
+        swap = self.bits[self.pos_bits] == 1
+        first = jnp.where(swap, self.other, self.mine)[0].astype(F32)
+        second = jnp.where(swap, self.mine, self.other)[0].astype(F32)
+        return first, second
+
+
 def local(
     inputs, segment_ids, pad_mask, time_weight, gain_first, shift_first, space_weight, gain_second,
     shift_second, expand_weight, gain_third, shift_third, query_weight, key_weight, value_weight,
@@ -419,6 +667,11 @@
     own_keys = frames * HALF * HALF
     size = -(-own_keys // 16) * 16
     row = lambda v: v.reshape(1, -1)
+    deep, wide = channels // pos_count, narrow // pos_count
+    bits = jnp.stack(
+        [(block >> k) & 1 for k in range(pos_count.bit_length() - 1)]
+        + [(layer >> k) & 1 for k in range(grp_count.bit_length() - 1)]
+    ).astype(jnp.int32)
     gain_1, shift_1, gain_2, shift_2 = map(row, (gain_first, shift_first, gain_second, shift_second))
     gain_3, shift_3, gain_4 = map(row, (gain_third, shift_third, gain_final))
 
@@ -479,7 +732,7 @@
     frame_f32 = ((AREA, narrow), F32)
 
     tap_0, tap_2, to_next, to_prev = call(
-        border_kernel, [narrow_f32, narrow_f32, frame_f32, frame_f32], scalars, inputs, time_weight,
+        border_kernel, [narrow_f32, narrow_f32, frame_f32, frame_f32], (), inputs, time_weight,
         flops=4 * rows * channels * narrow,
     )
     before = lax.ppermute(to_next, "grp", up)
@@ -488,7 +741,7 @@
     pre_1, sums, last, first = call(
         functools.partial(first_kernel, frames),
         [narrow_f32, ((copies, 2, narrow), F32), frame_f32, frame_f32],
-        scalars, tap_0, tap_1, tap_2, before, after, place,
+        (scalars,), tap_0, tap_1, tap_2, before, after, place,
     )
     sums = trade(sums)
     pre_before = lax.ppermute(last, "grp", up)
@@ -496,7 +749,7 @@
     pre_2, windows, sums, stats_1 = call(
         second_kernel,
         [narrow_f32, ((rows, 9 * narrow), BF16), ((copies, 2, narrow), F32), ((2, narrow), F32)],
-        scalars, sums, pre_1, gain_1, shift_1, space_weight.reshape(9 * narrow, narrow), place,
+        (scalars,), sums, pre_1, gain_1, shift_1, space_weight.reshape(9 * narrow, narrow), place,
         scratch=[pltpu.VMEM((rows + 2 * EDGE, narrow), F32)],
         flops=18 * rows * narrow * narrow,
     )
@@ -504,14 +757,14 @@
     z_2, pre_3, sums, stats_2 = call(
         third_kernel,
         [((rows, narrow), BF16), wide_f32, ((copies, 3, channels), F32), ((2, narrow), F32)],
-        scalars, sums, pre_2, gain_2, shift_2, expand_weight, place, cotangent,
+        (scalars,), sums, pre_2, gain_2, shift_2, expand_weight, place, cotangent,
         flops=2 * rows * narrow * channels,
     )
     sums = trade(sums)
     unit, pooled, kv_own, stats_3 = call(
         unit_kernel,
         [wide_bf16, ((2 * size, channels), BF16), ((size, 2 * inner), BF16), ((3, channels), F32)],
-        scalars, sums, pre_3, inputs, gain_3, shift_3, pool, counts, key_weight, value_weight,
+        (scalars,), sums, pre_3, inputs, gain_3, shift_3, pool, counts, key_weight, value_weight,
         flops=2 * size * channels * (rows + 4 * inner),
     )
     kv_blocks = [kv_own] + [
@@ -524,7 +777,7 @@
             ((grp_count * size, 2 * inner), BF16), ((rows, grp_count * size), F32),
             ((rows, inner), BF16), wide_f32, ((copies, 3, channels), F32),
         ],
-        scalars, theta, out_weight, cotangent, place, key_row, *kv_blocks,
+        (scalars,), theta, out_weight, cotangent, place, key_row, *kv_blocks,
         flops=2 * rows * inner * (2 * grp_count * size + channels),
     )
     sums = trade(sums)
@@ -536,7 +789,7 @@
             ((size, 2 * inner), F32),
         ]
         + [((size, 2 * inner), BF16)] * (grp_count - 1),
-        scalars, sums, stats_3, pre_4, cotangent, gain_4, out_weight, probs, kv, theta, place, key_row,
+        (scalars,), sums, stats_3, pre_4, cotangent, gain_4, out_weight, probs, kv, theta, place, key_row,
         flops=2 * rows * inner * (3 * grp_count * size + channels),
     )
     d_received = [
@@ -548,32 +801,53 @@
         + (pre_4 - stats_4[0]) * stats_4[1] * gain_final
         + shift_final
     ).astype(BF16)
-    d_theta = dot(d_logits, kv[:, :inner]).astype(BF16)
-    d_unit_part = cotangent.astype(F32) + dot_cols(d_theta, query_weight)
+    half = deep * inner // LANE
+    bundle_1 = Bundle(bits, 2 * half)
+    d_unit_part, _ = bundle_1.add(
+        attend_grads_kernel, 0, 2 * half,
+        d_logits, kv, cotangent, query_weight, attended, d_final, unit,
+        extra=[wide_f32, ((rows, inner), BF16)],
+        flops=2 * rows * inner * (grp_count * size + 3 * channels),
+    )
     d_pooled, d_summed, sums = call(
         functools.partial(summed_back_kernel, grp_count),
         [((2 * size, 2 * inner), BF16), wide_f32, ((copies, 2, channels), F32)],
-        scalars, d_kv, d_unit_part, pre_3, inputs, stats_3, gain_3, shift_3, spread, counts,
+        (scalars,), d_kv, d_unit_part, pre_3, inputs, stats_3, gain_3, shift_3, spread, counts,
         key_weight, value_weight, *d_received,
         scratch=[pltpu.VMEM((2 * size, channels), BF16)],
         flops=4 * size * channels * (inner + rows),
     )
     sums = trade(sums)
+    bundle_1.add(
+        pooled_grads_kernel, 2 * half, 2 * half, pooled, d_pooled,
+        flops=8 * size * channels * inner,
+    )
+    bundle_1.begin()
+    sums, bundle_1.send = tie(sums, bundle_1.send)
     d_third, d_act_2, sums, grads_3 = call(
         third_back_kernel,
         [wide_bf16, narrow_f32, ((copies, 2, narrow), F32), ((2, channels), F32)],
-        scalars, sums, stats_3, gain_3, d_summed, pre_3, expand_weight, pre_2, stats_2, gain_2,
+        (scalars,), sums, stats_3, gain_3, d_summed, pre_3, expand_weight, pre_2, stats_2, gain_2,
         shift_2, place,
         flops=2 * rows * narrow * channels,
     )
     sums = trade(sums)
+    tap_rows = wide * narrow // LANE
+    expand_rows = narrow * deep // LANE
+    bundle_2 = Bundle(bits, expand_rows + 9 * tap_rows)
+    bundle_2.add(
+        expand_grads_kernel, 0, expand_rows, z_2, d_third,
+        flops=2 * rows * narrow * channels,
+    )
+    bundle_1.plane()
+    sums, bundle_2.send, bundle_1.parts[0][1] = tie(sums, bundle_2.send, bundle_1.parts[0][1])
     d_second, d_act_1, sums, grads_2, last, first = call(
         functools.partial(second_back_kernel, frames),
         [
             ((rows, narrow), BF16), narrow_f32, ((copies, 2, narrow), F32), ((2, narrow), F32),
             frame_f32, frame_f32,
         ],
-        scalars, sums, stats_2, gain_2, d_act_2, pre_2, space_weight, pre_1, stats_1, gain_1,
+        (scalars,), sums, stats_2, gain_2, d_act_2, pre_2, space_weight, pre_1, stats_1, gain_1,
         shift_1, place,
         scratch=[pltpu.VMEM((rows + 2 * EDGE, narrow), F32)],
         flops=18 * rows * narrow * narrow,
@@ -581,64 +855,62 @@
     sums = trade(sums)
     d_before = lax.ppermute(last, "grp", up)
     d_after = lax.ppermute(first, "grp", down)
+    bundle_2.add(
+        space_grads_kernel, expand_rows, 9 * tap_rows, windows, d_second,
+        flops=18 * rows * narrow * narrow,
+    )
+    bundle_1.more()
+    sums, bundle_2.send, bundle_1.parts[0][1] = tie(sums, bundle_2.send, bundle_1.parts[0][1])
     input_grad, d_taps, grads_1 = call(
         functools.partial(first_back_kernel, frames),
         [wide_f32, ((rows, 3 * narrow), BF16), ((2, narrow), F32)],
-        scalars, sums, stats_1, gain_1, d_act_1, pre_1, d_before, d_after, pre_before, pre_after,
+        (scalars,), sums, stats_1, gain_1, d_act_1, pre_1, d_before, d_after, pre_before, pre_after,
         time_weight, d_summed, place, near,
         scratch=[pltpu.VMEM((rows, narrow), F32), pltpu.VMEM((rows, narrow), F32)],
         flops=6 * rows * narrow * channels,
     )
 
-    def row_shards(part):
-        return part.reshape(pos_count, part.shape[0] // pos_count, part.shape[1])
-
-    def col_shards(part):
-        wide = part.shape[1] // pos_count
-        return part.reshape(part.shape[0], pos_count, wide).transpose(1, 0, 2)
-
-    def bundle(parts):
-        return jnp.concatenate([p.reshape(pos_count, -1, LANE) for p in parts], axis=1)
-
-    share_1 = shrink(
-        bundle([col_shards(dot_rows(attended, d_final)), row_shards(dot_rows(unit, d_theta))])
-    )
-    share_2 = shrink(
-        bundle(
-            [
-                row_shards(dot_rows(pooled, d_pooled[:, :inner])),
-                row_shards(dot_rows(pooled, d_pooled[:, inner:])),
-            ]
+    bundle_2.add(
+        time_grads_kernel, bundle_2.cut, 3 * deep * narrow // LANE, inputs, d_taps,
+        flops=6 * rows * narrow * channels,
+    )
+    bundle_2.begin()
+    bundle_1.layer()
+    bundle_2.plane()
+    bundle_1.finish()
+    bundle_2.more()
+    bundle_2.layer()
+    bundle_2.finish()
+    if deep == LANE:
+        out_grad, query_grad, key_grad, value_grad = bundle_1.outs(
+            attend_outs_kernel, [(inner, deep)] + [(deep, inner)] * 3
         )
-    )
-    space_part = dot_rows(windows, d_second).reshape(9, narrow, narrow)
-    time_part = jnp.stack(
-        [dot_rows(inputs, d_taps[:, k * narrow : (k + 1) * narrow]) for k in range(3)]
-    )
-
-    def stack_shards(part):
-        count, depth, wide = part.shape
-        cut = part.reshape(count, pos_count, depth // pos_count, wide)
-        return cut.transpose(1, 0, 2, 3)
-
-    share_3 = shrink(
-        bundle([col_shards(dot_rows(z_2, d_third)), stack_shards(space_part)])
-    )
-    share_4 = shrink(bundle([stack_shards(time_part)]))
-
-    def take(share, start, shape):
-        extent = int(np.prod(shape)) // LANE
-        return share[start : start + extent].reshape(shape)
-
-    deep, wide = channels // pos_count, narrow // pos_count
-    half = deep * inner // LANE
-    out_grad = take(share_1, 0, (inner, deep))
-    query_grad = take(share_1, half, (deep, inner))
-    key_grad = take(share_2, 0, (deep, inner))
-    value_grad = take(share_2, half, (deep, inner))
-    expand_grad = take(share_3, 0, (narrow, deep))
-    space_grad = take(share_3, narrow * deep // LANE, (9, wide, narrow))
-    time_grad = take(share_4, 0, (3, deep, narrow))
+        expand_grad, space_grad, time_grad = bundle_2.outs(
+            bottleneck_outs_kernel, [(narrow, deep), (9, wide, narrow), (3, deep, narrow)]
+        )
+    else:
+
+        def columns(share, start, height, width):
+            part = share[start : start + height * width // LANE]
+            return part.reshape(width // LANE, height, LANE).transpose(1, 0, 2).reshape(height, width)
+
+        def folded(share, start, height, width):
+            part = share[start : start + height * width // LANE]
+            part = part.reshape(height // LANE, width, LANE // width, width)
+            return part.transpose(0, 2, 1, 3).reshape(height, width)
+
+        first, second = bundle_1.shares()
+        out_grad = folded(first, 0, inner, deep)
+        query_grad = columns(first, half, deep, inner)
+        key_grad = columns(second, 0, deep, inner)
+        value_grad = columns(second, half, deep, inner)
+        first, second = bundle_2.shares()
+        expand_grad = folded(first, 0, narrow, deep)
+        space_grad = jnp.stack(
+            [columns(first, expand_rows + tap * tap_rows, wide, narrow) for tap in range(9)]
+        )
+        time_all = columns(second, 0, deep, 3 * narrow)
+        time_grad = jnp.stack([time_all[:, k * narrow : (k + 1) * narrow] for k in range(3)])
     return (
         output, input_grad, time_grad, grads_1[0], grads_1[1], space_grad,
         grads_2[0], grads_2[1], expand_grad, grads_3[0], grads_3[1],

time: 340 us -> 302 us (0.89)
  Pallas kernels: 26.4 us -> 100 us
  local copies, waits for them, and re-layouts: 98.8 us -> 25.9 us
  other arithmetic: 26.9 us -> 5.91 us
  matrix products: 15.8 us -> 4.71 us
  starting transfers between devices: 78.5 us -> 73.1 us
    pallas_call x11 -> x23, Pallas kernels: 26.4 us -> 79.5 us  [call(): pl.pallas_call(kernel, out_shape=shapes, in_specs=[pl.BlockSpec(memory_sp...]
    unnamed x236 -> x112, local copies, waits for them, and re-layouts: 57.8 us -> 17.8 us
    pallas_call x0 -> x5, Pallas kernels: none -> 20.9 us  [add(): pl.pallas_call(functools.partial(kernel, self.pos_count, start), out_shap...]
    dot_general x10 -> x0, matrix products: 13.4 us -> none  [the longest x9 11.6 us: dot_rows(): lax.dot_general(left, right, (((0,), (0,)), ((), ())), preferred_element_...]
    concatenate x6 -> x0, local copies, waits for them, and re-layouts: 11.4 us -> none  [bundle(): jnp.concatenate([p.reshape(pos_count, -1, LANE) for p in parts], axis=1)]
    another operation x5 -> x1, local copies, waits for them, and re-layouts: 9.98 us -> 0.63 us  [local(): jnp.stack([block >> k & 1 for k in range(pos_count.bit_length() - 1)] + [...]
    all_to_all x7, waiting for transfers between devices: 31.3 us -> 40.1 us  [trade(): return lax.all_to_all(copies, ('pos', 'grp'), 0, 0, tiled=True)]
    ppermute x24 -> x16, starting transfers between devices: 24.9 us -> 16.5 us  [the longest x8 10.5 us: turn(): self.parts[k].append(lax.ppermute(self.parts[k][0], 'pos', pairs))]
  transfers between devices with their start and end apart: 43 -> 35, of which waited for: 23 -> 16; matrix products, arithmetic and copies ran while one was open for 24% -> 6% of each run, Pallas kernels for 4% -> 17%
where the time goes in v2:
time: 302 us; the launch traced here: 301 us
  Pallas kernels  100 us (33%)
  waiting for transfers between devices  89.3 us (30%)
  starting transfers between devices  73.1 us (24%)
  local copies, waits for them, and re-layouts  25.9 us (9%)
  other arithmetic  5.91 us (2%)
  matrix products  4.71 us (2%)
    pallas_call x23, Pallas kernels, call(): pl.pallas_call(kernel, out_shape=shapes, in_specs=[pl.BlockSpec(memory_sp...  79.5 us
    all_to_all x7, waiting for transfers between devices, trade(): return lax.all_to_all(copies, ('pos', 'grp'), 0, 0, tiled=True)  40.1 us
    all_to_all x7, starting transfers between devices, trade(): return lax.all_to_all(copies, ('pos', 'grp'), 0, 0, tiled=True)  29.5 us
    pallas_call x5, Pallas kernels, add(): pl.pallas_call(functools.partial(kernel, self.pos_count, start), out_shap...  20.9 us
    unnamed x112, local copies, waits for them, and re-layouts  17.8 us
    ppermute x3, waiting for transfers between devices, local(): lax.ppermute(kv_own, 'grp', flip(grp_count, step))  14.5 us
    ppermute x8, starting transfers between devices, turn(): self.parts[k].append(lax.ppermute(self.parts[k][0], 'pos', pairs))  10.5 us
    ppermute x3, waiting for transfers between devices, local(): lax.ppermute(d_sent[step - 1], 'grp', flip(grp_count, step))  8.93 us
  transfers between devices with their start and end apart: 35, of which 16 were waited for; matrix products, arithmetic and copies ran while one was open for 6% of the time, Pallas kernels for 17%

profile of v2, /device:TPU:0, one launch (start us, length us, event | category | flops | bytes accessed | tf_op | source)
XLA Modules:
  0.0 300.5 jit_solution(3679798040238730774)
XLA Ops:
  0.7 3.3 %shard_map.368 = (f32[392,256]{1,0:T(8,128)}, f32[392,256]{1,0:T(8,128)}, f32[196,256]{1,0:T(8,128)}, f32[196,256]{1,0:T(8,128)}) custom-call(bf16[392,1024]{1,0:T(8,128)(2,1)} %x.11, bf16[3,1024,256]{2,1,0:T(8,128)(2,1)} %w.15), custom_call_target="tpu_custom_call" | custom-call | flops 411041792 | bytes 3579904 | tf_op jit(solution)/shard_map/pallas_call | solution.py:63
  4.0 4.9 %collective-permute-start = (f32[196,256]{1,0:T(8,128)}, f32[196,256]{1,0:T(8,128)S(1)}, u32[]{:S(2)}, u32[]{:S(2)}) collective-permute-start(f32[196,256]{1,0:T(8,128)} %get-tuple-element.112), channel_id=1, source_target_pairs={{0,1},{1,2},{2,3},{4,5},{5,6},{6,7},{8,9},{9,10},{10,11},{12,13},{... | collective-permute-start | bytes 602120 | tf_op jit(solution)/shard_map/ppermute | solution.py:738
  18.2 2.5 shard_map.369
  20.7 5.1 %all-to-all-start = ((f32[32,2,256]{2,1,0:T(2,128)}), f32[32,2,256]{2,1,0:T(2,128)S(1)}, u32[]{:S(2)}, u32[]{:S(2)}) async-start(f32[32,2,256]{2,1,0:T(2,128)} %get-tuple-element.114), calls=%async_computation | async-start | bytes 131072 | tf_op jit(solution)/shard_map/all_to_all | solution.py:49
  26.4 7.0 %all-to-all-done.copies_in = f32[32,2,256]{2,1,0:T(2,128)S(1)} async-done(((f32[32,2,256]{2,1,0:T(2,128)}), f32[32,2,256]{2,1,0:T(2,128)S(1)}, u32[]{:S(2)}, u32[]{:S(2)}) %all-to-all-start) | async-done | bytes 65568 | tf_op jit(solution)/shard_map/all_to_all | solution.py:49
  34.0 4.8 %shard_map.370 = (f32[392,256]{1,0:T(8,128)}, bf16[392,2304]{1,0:T(8,128)(2,1)}, f32[32,2,256]{2,1,0:T(2,128)}, f32[2,256]{1,0:T(2,128)}) custom-call(f32[5]{0:T(128)} %pad_maximum_fusion.3.sc, f32[32,2,256]{2,1,0:T(2,128)} %copy-done.16, f32[392,256]{1,0:T(8,128)} %get-tuple-element.115.pre_1, f32[1,256]{1,0:T(1,128)} %bitcast.47, f32[1,256]{1,0:T(1,128)} %bitcast.53, ...), custom_call_target="tpu_custom_call" | custom-call | flops 462422016 | bytes 3930240 | tf_op jit(solution)/shard_map/pallas_call | solution.py:63
  38.8 2.6 all-to-all-start.1
  42.4 6.5 %all-to-all-done.1.copies_in = f32[32,2,256]{2,1,0:T(2,128)S(1)} async-done(((f32[32,2,256]{2,1,0:T(2,128)}), f32[32,2,256]{2,1,0:T(2,128)S(1)}, u32[]{:S(2)}, u32[]{:S(2)}) %all-to-all-start.1) | async-done | bytes 65568 | tf_op jit(solution)/shard_map/all_to_all | solution.py:49
  49.5 3.4 %shard_map.371 = (bf16[392,256]{1,0:T(8,128)(2,1)}, f32[392,1024]{1,0:T(8,128)}, f32[32,3,1024]{2,1,0:T(4,128)}, f32[2,256]{1,0:T(2,128)}) custom-call(f32[5]{0:T(128)} %pad_maximum_fusion.3.sc, f32[32,2,256]{2,1,0:T(2,128)} %copy-done.20, f32[392,256]{1,0:T(8,128)} %get-tuple-element.117.pre_2, f32[1,256]{1,0:T(1,128)} %bitcast.50, f32[1,256]{1,0:T(1,128)} %bitcast.61, ...), custom_call_target="tpu_custom_call" | custom-call | flops 205520896 | bytes 4003968 | tf_op jit(solution)/shard_map/pallas_call | solution.py:63
  52.9 2.6 all-to-all-start.2
  57.5 12.4 %all-to-all-done.2.copies_in = f32[32,3,1024]{2,1,0:T(4,128)S(1)} async-done(((f32[32,3,1024]{2,1,0:T(4,128)}), f32[32,3,1024]{2,1,0:T(4,128)S(1)}, u32[]{:S(2)}, u32[]{:S(2)}) %all-to-all-start.2) | async-done | bytes 393248 | tf_op jit(solution)/shard_map/all_to_all | solution.py:49
  70.7 4.7 %shard_map.372 = (bf16[392,1024]{1,0:T(8,128)(2,1)}, bf16[224,1024]{1,0:T(8,128)(2,1)}, bf16[112,1024]{1,0:T(8,128)(2,1)}, f32[3,1024]{1,0:T(4,128)}) custom-call(f32[5]{0:T(128)} %pad_maximum_fusion.3.sc, f32[32,3,1024]{2,1,0:T(4,128)} %copy-done.4, f32[392,1024]{1,0:T(8,128)} %get-tuple-element.119.pre_3, bf16[392,1024]{1,0:T(8,128)(2,1)} %x.11, ...), custom_call_target="tpu_custom_call" | custom-call | flops 559677440 | bytes 6498496 | tf_op jit(solution)/shard_map/pallas_call | solution.py:63
  75.4 2.5 collective-permute-start.2
  80.4 2.5 convolution_convert_fusion.theta
  82.9 5.0 %collective-permute-done.2.refs_1_ = bf16[112,1024]{1,0:T(8,128)(2,1)S(1)} collective-permute-done((bf16[112,1024]{1,0:T(8,128)(2,1)}, bf16[112,1024]{1,0:T(8,128)(2,1)S(1)}, u32[]{:S(2)}, u32[]{:S(2)}) %collective-permute-start.2) | collective-permute-done | bytes 229408 | tf_op jit(solution)/shard_map/ppermute | solution.py:771
  87.9 9.5 %collective-permute-done.3.refs_2_ = bf16[112,1024]{1,0:T(8,128)(2,1)S(1)} collective-permute-done((bf16[112,1024]{1,0:T(8,128)(2,1)}, bf16[112,1024]{1,0:T(8,128)(2,1)S(1)}, u32[]{:S(2)}, u32[]{:S(2)}) %collective-permute-start.3) | collective-permute-done | bytes 229408 | tf_op jit(solution)/shard_map/ppermute | solution.py:771
  98.8 5.0 %shard_map.373 = (bf16[448,1024]{1,0:T(8,128)(2,1)}, f32[392,448]{1,0:T(8,128)}, bf16[392,512]{1,0:T(8,128)(2,1)}, f32[392,1024]{1,0:T(8,128)}, f32[32,3,1024]{2,1,0:T(4,128)}) custom-call(f32[5]{0:T(128)} %pad_maximum_fusion.3.sc, bf16[392,512]{1,0:T(8,128)(2,1)} %convolution_convert_fusion.theta, bf16[512,1024]{1,0:T(8,128)(2,1)} %w.11, ...), custom_call_target="tpu_custom_call" | custom-call | flops 770703360 | bytes 7200384 | tf_op jit(solution)/shard_map/pallas_call | solution.py:63
  103.8 4.4 %all-to-all-start.3 = ((f32[32,3,1024]{2,1,0:T(4,128)}), f32[32,3,1024]{2,1,0:T(4,128)S(1)}, u32[]{:S(2)}, u32[]{:S(2)}) async-start(f32[32,3,1024]{2,1,0:T(4,128)} %get-tuple-element.123), calls=%async_computation.3 | async-start | bytes 1048576 | tf_op jit(solution)/shard_map/all_to_all | solution.py:49
  109.0 13.4 %all-to-all-done.3.copies_in = f32[32,3,1024]{2,1,0:T(4,128)S(1)} async-done(((f32[32,3,1024]{2,1,0:T(4,128)}), f32[32,3,1024]{2,1,0:T(4,128)S(1)}, u32[]{:S(2)}, u32[]{:S(2)}) %all-to-all-start.3) | async-done | bytes 393248 | tf_op jit(solution)/shard_map/all_to_all | solution.py:49
  123.2 5.8 %shard_map.374 = (bf16[392,1024]{1,0:T(8,128)(2,1)}, bf16[392,448]{1,0:T(8,128)(2,1)}, f32[3,1024]{1,0:T(4,128)}, f32[112,1024]{1,0:T(8,128)}, bf16[112,1024]{1,...) custom-call(f32[5]{0:T(128)} %pad_maximum_fusion.3.sc, f32[32,3,1024]{2,1,0:T(4,128)} %copy-done.3, ...), custom_call_target="tpu_custom_call" | custom-call | flops 950534144 | bytes 8211072 | tf_op jit(solution)/shard_map/pallas_call | solution.py:63
  129.1 2.5 collective-permute-start.5
  134.8 7.3 %shard_map.375 = (bf16[4,2048,128]{2,1,0:T(8,128)(2,1)}, f32[4,2048,128]{2,1,0:T(8,128)}, f32[392,1024]{1,0:T(8,128)}, bf16[392,512]{1,0:T(8,128)(2,1)}) custom-call(s32[5]{0:T(128)} %stack.57.bits, bf16[392,448]{1,0:T(8,128)(2,1)} %get-tuple-element.129.d_logits, bf16[448,1024]{1,0:T(8,128)(2,1)} %get-tuple-element.126.kv, bf16[392,1024]{1,0:T(8,128)(2,1)} %cot.7, ...), custom_call_target="tpu_custom_call" | custom-call | flops 1412956160 | bytes 8272896 | tf_op jit(solution)/shard_map/pallas_call | solution.py:557
  142.2 8.9 %collective-permute-done.6.refs_1_ = bf16[112,1024]{1,0:T(8,128)(2,1)S(1)} collective-permute-done((bf16[112,1024]{1,0:T(8,128)(2,1)}, bf16[112,1024]{1,0:T(8,128)(2,1)S(1)}, u32[]{:S(2)}, u32[]{:S(2)}) %collective-permute-start.6) | collective-permute-done | bytes 229408 | tf_op jit(solution)/shard_map/ppermute | solution.py:796
  151.8 6.2 %shard_map.376 = (bf16[224,1024]{1,0:T(8,128)(2,1)}, f32[392,1024]{1,0:T(8,128)}, f32[32,2,1024]{2,1,0:T(2,128)}) custom-call(f32[5]{0:T(128)} %pad_maximum_fusion.3.sc, f32[112,1024]{1,0:T(8,128)} %get-tuple-element.128.own, f32[392,1024]{1,0:T(8,128)} %get-tuple-element.132.d_unit_part, f32[392,1024]{1,0:T(8,128)} %get-tuple-element.119.pre_3, ...), custom_call_target="tpu_custom_call" | custom-call | flops 414711808 | bytes 9781184 | tf_op jit(solution)/shard_map/pallas_call | solution.py:63
  158.0 3.6 %shard_map.377 = (bf16[4,2048,128]{2,1,0:T(8,128)(2,1)}, f32[4,2048,128]{2,1,0:T(8,128)}) custom-call(s32[5]{0:T(128)} %stack.57.bits, bf16[4,2048,128]{2,1,0:T(8,128)(2,1)} %get-tuple-element.137.send_in, f32[4,2048,128]{2,1,0:T(8,128)} %get-tuple-element.138.keep_in, ...), custom_call_target="tpu_custom_call", output_to_operand_aliasing={{0}: (1, {}), {1}: (2, {})} | custom-call | flops 469762048 | bytes 4063232 | tf_op jit(solution)/shard_map/pallas_call | solution.py:557
  161.7 5.0 %all-to-all-start.4 = ((f32[32,2,1024]{2,1,0:T(2,128)}), f32[32,2,1024]{2,1,0:T(2,128)S(1)}, u32[]{:S(2)}, u32[]{:S(2)}) async-start(f32[32,2,1024]{2,1,0:T(2,128)} %get-tuple-element.136), calls=%async_computation.4 | async-start | bytes 524288 | tf_op jit(solution)/shard_map/all_to_all | solution.py:49
  168.0 4.8 %shard_map.380 = (bf16[2,1024,128]{2,1,0:T(8,128)(2,1)}, f32[2,1024,128]{2,1,0:T(8,128)}, bf16[2,1024,128]{2,1,0:T(8,128)(2,1)}, f32[2,1024,128]{2,1,0:T(8,128)}) custom-call(s32[5]{0:T(128)} %stack.57.bits, f32[4,2048,128]{2,1,0:T(8,128)} %get-tuple-element.149.keep_in, bf16[4,2048,128]{2,1,0:T(8,128)(2,1)} %copy-done.2), custom_call_target="tpu_custom_call" | custom-call | bytes 9437184 | tf_op jit(solution)/shard_map/pallas_call | solution.py:63
  177.6 4.0 %shard_map.378 = (bf16[392,1024]{1,0:T(8,128)(2,1)}, f32[392,256]{1,0:T(8,128)}, f32[32,2,256]{2,1,0:T(2,128)}, f32[2,1024]{1,0:T(2,128)}) custom-call(f32[5]{0:T(128)} %pad_maximum_fusion.3.sc, f32[32,2,1024]{2,1,0:T(2,128)} %copy-done.6, f32[3,1024]{1,0:T(4,128)} %get-tuple-element.124.stats_3, f32[1,1024]{1,0:T(1,128)} %bitcast.40, ...), custom_call_target="tpu_custom_call" | custom-call | flops 205520896 | bytes 5703808 | tf_op jit(solution)/shard_map/pallas_call | solution.py:63
  181.5 2.9 all-to-all-start.5
  184.5 3.7 %collective-permute-start.13 = (f32[196,256]{1,0:T(8,128)S(1)}, f32[196,256]{1,0:T(8,128)S(1)}, u32[]{:S(2)}, u32[]{:S(2)}) collective-permute-start(f32[196,256]{1,0:T(8,128)S(1)} %copy-done.55), channel_id=1, source_target_pairs={{0,1},{1,2},{2,3},{4,5},{5,6},{6,7},{8,9},{9,10},{10,11},{12,13},{... | collective-permute-start | bytes 602120 | tf_op jit(solution)/shard_map/ppermute | solution.py:747
  189.5 2.6 shard_map.379
  192.7 4.2 %shard_map.381 = (bf16[392,256]{1,0:T(8,128)(2,1)}, f32[392,256]{1,0:T(8,128)}, f32[32,2,256]{2,1,0:T(2,128)}, f32[2,256]{1,0:T(2,128)}, f32[196,256]{1,0:T(8,128)}, /*index=5*/f32[196,256]{1,0:T(8,128)}) custom-call(f32[5]{0:T(128)} %pad_maximum_fusion.3.sc, f32[32,2,256]{2,1,0:T(2,128)} %copy-done.15, f32[2,256]{1,0:T(2,128)} %get-tuple-element.144.stats_2, ...), custom_call_target="tpu_custom_call" | custom-call | flops 462422016 | bytes 3533952 | tf_op jit(solution)/shard_map/pallas_call | solution.py:63
  196.9 4.6 %collective-permute-start.11 = (f32[196,256]{1,0:T(8,128)}, f32[196,256]{1,0:T(8,128)S(1)}, u32[]{:S(2)}, u32[]{:S(2)}) collective-permute-start(f32[196,256]{1,0:T(8,128)} %get-tuple-element.167), channel_id=1, source_target_pairs={{0,1},{1,2},{2,3},{4,5},{5,6},{6,7},{8,9},{9,10},{10,11},{12,13},{... | collective-permute-start | bytes 602120 | tf_op jit(solution)/shard_map/ppermute | solution.py:856
  202.9 6.9 %all-to-all-start.6 = ((f32[32,2,256]{2,1,0:T(2,128)}), f32[32,2,256]{2,1,0:T(2,128)S(1)}, u32[]{:S(2)}, u32[]{:S(2)}) async-start(f32[32,2,256]{2,1,0:T(2,128)} %get-tuple-element.154), calls=%async_computation.6 | async-start | bytes 131072 | tf_op jit(solution)/shard_map/all_to_all | solution.py:49
  210.6 3.6 %shard_map.382 = (bf16[4,1664,128]{2,1,0:T(8,128)(2,1)}, f32[4,1664,128]{2,1,0:T(8,128)}) custom-call(s32[5]{0:T(128)} %stack.57.bits, bf16[4,1664,128]{2,1,0:T(8,128)(2,1)} %get-tuple-element.155.send_in, f32[4,1664,128]{2,1,0:T(8,128)} %get-tuple-element.156.keep_in, ...), custom_call_target="tpu_custom_call", output_to_operand_aliasing={{0}: (1, {}), {1}: (2, {})} | custom-call | flops 462422016 | bytes 3776512 | tf_op jit(solution)/shard_map/pallas_call | solution.py:557
  215.1 3.1 %shard_map.383 = (bf16[1,1024,128]{2,1,0:T(8,128)(2,1)}, f32[1,1024,128]{2,1,0:T(8,128)}, bf16[1,1024,128]{2,1,0:T(8,128)(2,1)}, f32[1,1024,128]{2,1,0:T(8,128)}) custom-call(s32[5]{0:T(128)} %stack.57.bits, f32[2,1024,128]{2,1,0:T(8,128)} %get-tuple-element.160.in_1, bf16[2,1024,128]{2,1,0:T(8,128)(2,1)} %copy-done.8, ...), custom_call_target="tpu_custom_call" | custom-call | bytes 4718592 | tf_op jit(solution)/shard_map/pallas_call | solution.py:63
  219.1 4.7 %shard_map.384 = (f32[392,1024]{1,0:T(8,128)}, bf16[392,768]{1,0:T(8,128)(2,1)}, f32[2,256]{1,0:T(2,128)}) custom-call(f32[5]{0:T(128)} %pad_maximum_fusion.3.sc, f32[32,2,256]{2,1,0:T(2,128)} %copy-done.12, f32[2,256]{1,0:T(2,128)} %get-tuple-element.153.stats_1, f32[1,256]{1,0:T(1,128)} %bitcast.49, f32[392,256]{1,0:T(8,128)} %get-tuple-element.166.d_act, ...), custom_call_target="tpu_custom_call" | custom-call | flops 616562688 | bytes 7070368 | tf_op jit(solution)/shard_map/pallas_call | solution.py:63
  223.8 3.8 %shard_map.385 = (bf16[4,1664,128]{2,1,0:T(8,128)(2,1)}, f32[4,1664,128]{2,1,0:T(8,128)}) custom-call(s32[5]{0:T(128)} %stack.57.bits, bf16[4,1664,128]{2,1,0:T(8,128)(2,1)} %get-tuple-element.172.send_in, f32[4,1664,128]{2,1,0:T(8,128)} %get-tuple-element.173.keep_in, bf16[392,1024]{1,0:T(8,128)(2,1)} %x.11, ...), custom_call_target="tpu_custom_call", output_to_operand_aliasing={{0}: (1, {}), {1}: (2, {})} | custom-call | flops 616562688 | bytes 3764224 | tf_op jit(solution)/shard_map/pallas_call | solution.py:557
  232.7 4.3 %shard_map.386 = (bf16[2,832,128]{2,1,0:T(8,128)(2,1)}, f32[2,832,128]{2,1,0:T(8,128)}, bf16[2,832,128]{2,1,0:T(8,128)(2,1)}, f32[2,832,128]{2,1,0:T(8,128)}) custom-call(s32[5]{0:T(128)} %stack.57.bits, f32[4,1664,128]{2,1,0:T(8,128)} %get-tuple-element.175.keep_in, bf16[4,1664,128]{2,1,0:T(8,128)(2,1)} %copy-done.5), custom_call_target="tpu_custom_call" | custom-call | bytes 7667712 | tf_op jit(solution)/shard_map/pallas_call | solution.py:63
  240.8 2.3 shard_map.392
  246.5 4.6 %collective-permute-done.25.received = bf16[1,1024,128]{2,1,0:T(8,128)(2,1)S(1)} collective-permute-done((bf16[1,1024,128]{2,1,0:T(8,128)(2,1)}, bf16[1,1024,128]{2,1,0:T(8,128)(2,1)S(1)}, u32[]{:S(2)}, u32[]{:S(2)}) %collective-permute-start.25) | collective-permute-done | bytes 262176 | tf_op jit(solution)/shard_map/ppermute | solution.py:615
  253.8 2.4 collective-permute-start.26
  257.2 2.8 shard_map.387
  262.4 3.7 %collective-permute-done.18.received_1 = bf16[1,832,128]{2,1,0:T(8,128)(2,1)S(1)} collective-permute-done((bf16[1,832,128]{2,1,0:T(8,128)(2,1)}, bf16[1,832,128]{2,1,0:T(8,128)(2,1)S(1)}, u32[]{:S(2)}, u32[]{:S(2)}) %collective-permute-start.18) | collective-permute-done | bytes 213024 | tf_op jit(solution)/shard_map/ppermute | solution.py:593
  267.3 2.2 shard_map.388
  274.6 2.9 collective-permute-done.20.received
  280.6 8.8 %collective-permute-done.21.received = bf16[1,832,128]{2,1,0:T(8,128)(2,1)S(1)} collective-permute-done((bf16[1,832,128]{2,1,0:T(8,128)(2,1)}, bf16[1,832,128]{2,1,0:T(8,128)(2,1)S(1)}, u32[]{:S(2)}, u32[]{:S(2)}) %collective-permute-start.21) | collective-permute-done | bytes 213024 | tf_op jit(solution)/shard_map/ppermute | solution.py:625
  295.2 2.7 collective-permute-done.22.other
  (205 shorter events, 72.1 us)
Async XLA Ops:
  0.7 10.7 %copy-start.48 = (f32[392,1]{0,1:T(1,128)S(1)}, f32[392,1]{0,1:T(1,128)}, u32[]{:S(2)}) copy-start(f32[392,1]{0,1:T(1,128)} %constant.78) | copy-start | bytes 4708
  0.7 10.7 %copy-start.49 = (f32[392,1]{0,1:T(1,128)S(1)}, f32[392,1]{0,1:T(1,128)}, u32[]{:S(2)}) copy-start(f32[392,1]{0,1:T(1,128)} %constant.77) | copy-start | bytes 4708
  0.7 12.8 %copy-start = (bf16[392,1024]{1,0:T(8,128)(2,1)S(1)}, bf16[392,1024]{1,0:T(8,128)(2,1)}, u32[]{:S(2)}) copy-start(bf16[392,1024]{1,0:T(8,128)(2,1)} %x.11) | copy-start | bytes 2408452
  0.7 10.2 %copy-start.50 = (s32[64]{0:T(128)S(1)}, s32[64]{0:T(128)}, u32[]{:S(2)}) copy-start(s32[64]{0:T(128)} %param.26) | copy-start | bytes 772
  4.0 11.7 %collective-permute-start = (f32[196,256]{1,0:T(8,128)}, f32[196,256]{1,0:T(8,128)S(1)}, u32[]{:S(2)}, u32[]{:S(2)}) collective-permute-start(f32[196,256]{1,0:T(8,128)} %get-tuple-element.112), channel_id=1, source_target_pairs={{0,1},{1,2},{2,3},{4,5},{5,6},{6,7},{8,9},{9,10},{10,11},{12,13},{... | collective-permute-start | bytes 602120 | tf_op jit(solution)/shard_map/ppermute | solution.py:738
  8.9 8.6 %collective-permute-start.1 = (f32[196,256]{1,0:T(8,128)}, f32[196,256]{1,0:T(8,128)S(1)}, u32[]{:S(2)}, u32[]{:S(2)}) collective-permute-start(f32[196,256]{1,0:T(8,128)} %get-tuple-element.113), channel_id=1, source_target_pairs={{1,0},{2,1},{3,2},{5,4},{6,5},{7,6},{9,8},{10,9},{11,10},{13,12},{... | collective-permute-start | bytes 602120 | tf_op jit(solution)/shard_map/ppermute | solution.py:739
  20.7 12.6 %all-to-all-start = ((f32[32,2,256]{2,1,0:T(2,128)}), f32[32,2,256]{2,1,0:T(2,128)S(1)}, u32[]{:S(2)}, u32[]{:S(2)}) async-start(f32[32,2,256]{2,1,0:T(2,128)} %get-tuple-element.114), calls=%async_computation | async-start | bytes 131072 | tf_op jit(solution)/shard_map/all_to_all | solution.py:49
  38.8 10.1 %all-to-all-start.1 = ((f32[32,2,256]{2,1,0:T(2,128)}), f32[32,2,256]{2,1,0:T(2,128)S(1)}, u32[]{:S(2)}, u32[]{:S(2)}) async-start(f32[32,2,256]{2,1,0:T(2,128)} %get-tuple-element.116), calls=%async_computation.1 | async-start | bytes 131072 | tf_op jit(solution)/shard_map/all_to_all | solution.py:49
  41.3 14.9 %copy-start.47 = (f32[1,448]{1,0:T(1,128)S(1)}, f32[1,448]{1,0:T(1,128)}, u32[]{:S(2)}) copy-start(f32[1,448]{1,0:T(1,128)} %constant.79) | copy-start | bytes 5380
  41.4 15.5 %copy-start.24 = (f32[112,392]{1,0:T(8,128)S(1)}, f32[112,392]{1,0:T(8,128)}, u32[]{:S(2)}) copy-start(f32[112,392]{1,0:T(8,128)} %constant.68.clone) | copy-start | bytes 526852
  52.9 17.0 %all-to-all-start.2 = ((f32[32,3,1024]{2,1,0:T(4,128)}), f32[32,3,1024]{2,1,0:T(4,128)S(1)}, u32[]{:S(2)}, u32[]{:S(2)}) async-start(f32[32,3,1024]{2,1,0:T(4,128)} %get-tuple-element.118), calls=%async_computation.2 | async-start | bytes 1048576 | tf_op jit(solution)/shard_map/all_to_all | solution.py:49
  75.4 12.5 %collective-permute-start.2 = (bf16[112,1024]{1,0:T(8,128)(2,1)}, bf16[112,1024]{1,0:T(8,128)(2,1)S(1)}, u32[]{:S(2)}, u32[]{:S(2)}) collective-permute-start(bf16[112,1024]{1,0:T(8,128)(2,1)} %get-tuple-element.121.refs_0_), channel_id=1, source_target_pairs={{0,1},{1,0},{2,3},{3,2},{4,5},{5,4},{6,7},{7,6},{8,9},{9,8},{10,11... | collective-permute-start | bytes 688136 | tf_op jit(solution)/shard_map/ppermute | solution.py:771
  78.0 19.5 %collective-permute-start.3 = (bf16[112,1024]{1,0:T(8,128)(2,1)}, bf16[112,1024]{1,0:T(8,128)(2,1)S(1)}, u32[]{:S(2)}, u32[]{:S(2)}) collective-permute-start(bf16[112,1024]{1,0:T(8,128)(2,1)} %get-tuple-element.121.refs_0_), channel_id=1, source_target_pairs={{0,2},{1,3},{2,0},{3,1},{4,6},{5,7},{6,4},{7,5},{8,10},{9,11},{10,... | collective-permute-start | bytes 688136 | tf_op jit(solution)/shard_map/ppermute | solution.py:771
  78.7 18.7 %collective-permute-start.4 = (bf16[112,1024]{1,0:T(8,128)(2,1)}, bf16[112,1024]{1,0:T(8,128)(2,1)S(1)}, u32[]{:S(2)}, u32[]{:S(2)}) collective-permute-start(bf16[112,1024]{1,0:T(8,128)(2,1)} %get-tuple-element.121.refs_0_), channel_id=1, source_target_pairs={{0,3},{1,2},{2,1},{3,0},{4,7},{5,6},{6,5},{7,4},{8,11},{9,10},{10,... | collective-permute-start | bytes 688136 | tf_op jit(solution)/shard_map/ppermute | solution.py:771
  82.9 26.0 %copy-start.39 = (f32[392,112]{1,0:T(8,128)S(1)}, f32[392,112]{1,0:T(8,128)}, u32[]{:S(2)}) copy-start(f32[392,112]{1,0:T(8,128)} %constant.69.clone) | copy-start | bytes 526852
  103.8 18.6 %all-to-all-start.3 = ((f32[32,3,1024]{2,1,0:T(4,128)}), f32[32,3,1024]{2,1,0:T(4,128)S(1)}, u32[]{:S(2)}, u32[]{:S(2)}) async-start(f32[32,3,1024]{2,1,0:T(4,128)} %get-tuple-element.123), calls=%async_computation.3 | async-start | bytes 1048576 | tf_op jit(solution)/shard_map/all_to_all | solution.py:49
  129.1 13.1 %collective-permute-start.5 = (bf16[112,1024]{1,0:T(8,128)(2,1)}, bf16[112,1024]{1,0:T(8,128)(2,1)S(1)}, u32[]{:S(2)}, u32[]{:S(2)}) collective-permute-start(bf16[112,1024]{1,0:T(8,128)(2,1)} %get-tuple-element.133), channel_id=1, source_target_pairs={{0,1},{1,0},{2,3},{3,2},{4,5},{5,4},{6,7},{7,6},{8,9},{9,8},{10,11... | collective-permute-start | bytes 688136 | tf_op jit(solution)/shard_map/ppermute | solution.py:796
  131.6 19.5 %collective-permute-start.6 = (bf16[112,1024]{1,0:T(8,128)(2,1)}, bf16[112,1024]{1,0:T(8,128)(2,1)S(1)}, u32[]{:S(2)}, u32[]{:S(2)}) collective-permute-start(bf16[112,1024]{1,0:T(8,128)(2,1)} %get-tuple-element.134), channel_id=1, source_target_pairs={{0,2},{1,3},{2,0},{3,1},{4,6},{5,7},{6,4},{7,5},{8,10},{9,11},{10,... | collective-permute-start | bytes 688136 | tf_op jit(solution)/shard_map/ppermute | solution.py:796
  132.4 18.7 %collective-permute-start.7 = (bf16[112,1024]{1,0:T(8,128)(2,1)}, bf16[112,1024]{1,0:T(8,128)(2,1)S(1)}, u32[]{:S(2)}, u32[]{:S(2)}) collective-permute-start(bf16[112,1024]{1,0:T(8,128)(2,1)} %get-tuple-element.135), channel_id=1, source_target_pairs={{0,3},{1,2},{2,1},{3,0},{4,7},{5,6},{6,5},{7,4},{8,11},{9,10},{10,... | collective-permute-start | bytes 688136 | tf_op jit(solution)/shard_map/ppermute | solution.py:796
  161.6 5.1 %collective-permute-start.8 = (bf16[4,2048,128]{2,1,0:T(8,128)(2,1)}, bf16[4,2048,128]{2,1,0:T(8,128)(2,1)S(1)}, u32[]{:S(2)}, u32[]{:S(2)}) collective-permute-start(bf16[4,2048,128]{2,1,0:T(8,128)(2,1)} %get-tuple-element.141), channel_id=1, source_target_pairs={{0,4},{4,0},{8,12},{12,8},{16,20},{20,16},{24,28},{28,24},{1,5},{5... | collective-permute-start | bytes 6291464 | tf_op jit(solution)/shard_map/ppermute | solution.py:574
  161.7 15.2 %all-to-all-start.4 = ((f32[32,2,1024]{2,1,0:T(2,128)}), f32[32,2,1024]{2,1,0:T(2,128)S(1)}, u32[]{:S(2)}, u32[]{:S(2)}) async-start(f32[32,2,1024]{2,1,0:T(2,128)} %get-tuple-element.136), calls=%async_computation.4 | async-start | bytes 524288 | tf_op jit(solution)/shard_map/all_to_all | solution.py:49
  172.8 28.7 %collective-permute-start.9 = (bf16[2,1024,128]{2,1,0:T(8,128)(2,1)}, bf16[2,1024,128]{2,1,0:T(8,128)(2,1)S(1)}, u32[]{:S(2)}, u32[]{:S(2)}) collective-permute-start(bf16[2,1024,128]{2,1,0:T(8,128)(2,1)} %get-tuple-element.161), channel_id=1, source_target_pairs={{0,8},{4,12},{8,0},{12,4},{16,24},{20,28},{24,16},{28,20},{1,9},{5... | collective-permute-start | bytes 1572872 | tf_op jit(solution)/shard_map/ppermute | solution.py:593
  174.6 39.7 %collective-permute-start.10 = (bf16[2,1024,128]{2,1,0:T(8,128)(2,1)}, bf16[2,1024,128]{2,1,0:T(8,128)(2,1)S(1)}, u32[]{:S(2)}, u32[]{:S(2)}) collective-permute-start(bf16[2,1024,128]{2,1,0:T(8,128)(2,1)} %get-tuple-element.163), channel_id=1, source_target_pairs={{0,16},{4,20},{8,24},{12,28},{16,0},{20,4},{24,8},{28,12},{1,17},{... | collective-permute-start | bytes 1572872 | tf_op jit(solution)/shard_map/ppermute | solution.py:593
  177.6 10.6 %copy-start.54 = (f32[196,256]{1,0:T(8,128)S(1)}, f32[196,256]{1,0:T(8,128)}, u32[]{:S(2)}) copy-start(f32[196,256]{1,0:T(8,128)} %get-tuple-element.170) | copy-start | bytes 602116
  181.5 10.6 %all-to-all-start.5 = ((f32[32,2,256]{2,1,0:T(2,128)}), f32[32,2,256]{2,1,0:T(2,128)S(1)}, u32[]{:S(2)}, u32[]{:S(2)}) async-start(f32[32,2,256]{2,1,0:T(2,128)} %get-tuple-element.145), calls=%async_computation.5 | async-start | bytes 131072 | tf_op jit(solution)/shard_map/all_to_all | solution.py:49
  184.5 33.7 %collective-permute-start.13 = (f32[196,256]{1,0:T(8,128)S(1)}, f32[196,256]{1,0:T(8,128)S(1)}, u32[]{:S(2)}, u32[]{:S(2)}) collective-permute-start(f32[196,256]{1,0:T(8,128)S(1)} %copy-done.55), channel_id=1, source_target_pairs={{0,1},{1,2},{2,3},{4,5},{5,6},{6,7},{8,9},{9,10},{10,11},{12,13},{... | collective-permute-start | bytes 602120 | tf_op jit(solution)/shard_map/ppermute | solution.py:747
  188.2 30.0 %collective-permute-start.14 = (f32[196,256]{1,0:T(8,128)S(1)}, f32[196,256]{1,0:T(8,128)S(1)}, u32[]{:S(2)}, u32[]{:S(2)}) collective-permute-start(f32[196,256]{1,0:T(8,128)S(1)} %copy-done.54), channel_id=1, source_target_pairs={{1,0},{2,1},{3,2},{5,4},{6,5},{7,6},{9,8},{10,9},{11,10},{13,12},{... | collective-permute-start | bytes 602120 | tf_op jit(solution)/shard_map/ppermute | solution.py:748
  196.9 21.3 %collective-permute-start.11 = (f32[196,256]{1,0:T(8,128)}, f32[196,256]{1,0:T(8,128)S(1)}, u32[]{:S(2)}, u32[]{:S(2)}) collective-permute-start(f32[196,256]{1,0:T(8,128)} %get-tuple-element.167), channel_id=1, source_target_pairs={{0,1},{1,2},{2,3},{4,5},{5,6},{6,7},{8,9},{9,10},{10,11},{12,13},{... | collective-permute-start | bytes 602120 | tf_op jit(solution)/shard_map/ppermute | solution.py:856
  201.5 12.7 %copy-start.8 = (bf16[2,1024,128]{2,1,0:T(8,128)(2,1)}, bf16[2,1024,128]{2,1,0:T(8,128)(2,1)S(1)}, u32[]{:S(2)}) copy-start(bf16[2,1024,128]{2,1,0:T(8,128)(2,1)S(1)} %collective-permute-done.9.received_1) | copy-start | bytes 1572868
  201.5 16.7 %collective-permute-start.12 = (f32[196,256]{1,0:T(8,128)}, f32[196,256]{1,0:T(8,128)S(1)}, u32[]{:S(2)}, u32[]{:S(2)}) collective-permute-start(f32[196,256]{1,0:T(8,128)} %get-tuple-element.168), channel_id=1, source_target_pairs={{1,0},{2,1},{3,2},{5,4},{6,5},{7,6},{9,8},{10,9},{11,10},{13,12},{... | collective-permute-start | bytes 602120 | tf_op jit(solution)/shard_map/ppermute | solution.py:857
  202.9 15.3 %all-to-all-start.6 = ((f32[32,2,256]{2,1,0:T(2,128)}), f32[32,2,256]{2,1,0:T(2,128)S(1)}, u32[]{:S(2)}, u32[]{:S(2)}) async-start(f32[32,2,256]{2,1,0:T(2,128)} %get-tuple-element.154), calls=%async_computation.6 | async-start | bytes 131072 | tf_op jit(solution)/shard_map/all_to_all | solution.py:49
  227.6 3.9 %collective-permute-start.15 = (bf16[4,1664,128]{2,1,0:T(8,128)(2,1)}, bf16[4,1664,128]{2,1,0:T(8,128)(2,1)S(1)}, u32[]{:S(2)}, u32[]{:S(2)}) collective-permute-start(bf16[4,1664,128]{2,1,0:T(8,128)(2,1)} %get-tuple-element.176), channel_id=1, source_target_pairs={{0,4},{4,0},{8,12},{12,8},{16,20},{20,16},{24,28},{28,24},{1,5},{5... | collective-permute-start | bytes 5111816 | tf_op jit(solution)/shard_map/ppermute | solution.py:574
  227.7 12.3 %collective-permute-start.23 = (bf16[1,1024,128]{2,1,0:T(8,128)(2,1)S(1)}, bf16[1,1024,128]{2,1,0:T(8,128)(2,1)S(1)}, u32[]{:S(2)}, u32[]{:S(2)}) collective-permute-start(bf16[1,1024,128]{2,1,0:T(8,128)(2,1)S(1)} %copy-done.53), channel_id=1, source_target_pairs={{0,16},{4,20},{8,24},{12,28},{16,0},{20,4},{24,8},{28,12},{1,17},{... | collective-permute-start | bytes 786440 | tf_op jit(solution)/shard_map/ppermute | solution.py:593
  229.4 10.6 %collective-permute-start.24 = (bf16[1,1024,128]{2,1,0:T(8,128)(2,1)S(1)}, bf16[1,1024,128]{2,1,0:T(8,128)(2,1)S(1)}, u32[]{:S(2)}, u32[]{:S(2)}) collective-permute-start(bf16[1,1024,128]{2,1,0:T(8,128)(2,1)S(1)} %copy-done.52), channel_id=1, source_target_pairs={{0,8},{4,12},{8,0},{12,4},{16,24},{20,28},{24,16},{28,20},{1,9},{5... | collective-permute-start | bytes 786440 | tf_op jit(solution)/shard_map/ppermute | solution.py:593
  232.7 13.2 %copy-start.42 = (f32[3,1024]{1,0:T(4,128)S(1)}, f32[3,1024]{1,0:T(4,128)}, u32[]{:S(2)}) copy-start(f32[3,1024]{1,0:T(4,128)} %get-tuple-element.127) | copy-start | bytes 36868
  237.0 19.3 %collective-permute-start.16 = (bf16[2,832,128]{2,1,0:T(8,128)(2,1)}, bf16[2,832,128]{2,1,0:T(8,128)(2,1)S(1)}, u32[]{:S(2)}, u32[]{:S(2)}) collective-permute-start(bf16[2,832,128]{2,1,0:T(8,128)(2,1)} %get-tuple-element.178), channel_id=1, source_target_pairs={{0,8},{4,12},{8,0},{12,4},{16,24},{20,28},{24,16},{28,20},{1,9},{5... | collective-permute-start | bytes 1277960 | tf_op jit(solution)/shard_map/ppermute | solution.py:593
  238.5 17.7 %collective-permute-start.17 = (bf16[2,832,128]{2,1,0:T(8,128)(2,1)}, bf16[2,832,128]{2,1,0:T(8,128)(2,1)S(1)}, u32[]{:S(2)}, u32[]{:S(2)}) collective-permute-start(bf16[2,832,128]{2,1,0:T(8,128)(2,1)} %get-tuple-element.180), channel_id=1, source_target_pairs={{0,16},{4,20},{8,24},{12,28},{16,0},{20,4},{24,8},{28,12},{1,17},{... | collective-permute-start | bytes 1277960 | tf_op jit(solution)/shard_map/ppermute | solution.py:593
  243.1 8.0 %collective-permute-start.25 = (bf16[1,1024,128]{2,1,0:T(8,128)(2,1)}, bf16[1,1024,128]{2,1,0:T(8,128)(2,1)S(1)}, u32[]{:S(2)}, u32[]{:S(2)}) collective-permute-start(bf16[1,1024,128]{2,1,0:T(8,128)(2,1)} %get-tuple-element.198), channel_id=1, source_target_pairs={{0,1},{1,0},{2,3},{3,2},{4,5},{5,4},{6,7},{7,6},{8,9},{9,8},{10,11... | collective-permute-start | bytes 786440 | tf_op jit(solution)/shard_map/ppermute | solution.py:615
  253.8 17.8 %collective-permute-start.26 = (bf16[1,1024,128]{2,1,0:T(8,128)(2,1)}, bf16[1,1024,128]{2,1,0:T(8,128)(2,1)S(1)}, u32[]{:S(2)}, u32[]{:S(2)}) collective-permute-start(bf16[1,1024,128]{2,1,0:T(8,128)(2,1)} %shard_map.393.low), channel_id=1, source_target_pairs={{0,2},{1,3},{2,0},{3,1},{4,6},{5,7},{6,4},{7,5},{8,10},{9,11},{10,... | collective-permute-start | bytes 786440 | tf_op jit(solution)/shard_map/ppermute | solution.py:625
  260.0 6.1 %collective-permute-start.18 = (bf16[1,832,128]{2,1,0:T(8,128)(2,1)}, bf16[1,832,128]{2,1,0:T(8,128)(2,1)S(1)}, u32[]{:S(2)}, u32[]{:S(2)}) collective-permute-start(bf16[1,832,128]{2,1,0:T(8,128)(2,1)} %get-tuple-element.182), channel_id=1, source_target_pairs={{0,16},{4,20},{8,24},{12,28},{16,0},{20,4},{24,8},{28,12},{1,17},{... | collective-permute-start | bytes 638984 | tf_op jit(solution)/shard_map/ppermute | solution.py:593
  260.5 6.1 %collective-permute-start.19 = (bf16[1,832,128]{2,1,0:T(8,128)(2,1)}, bf16[1,832,128]{2,1,0:T(8,128)(2,1)S(1)}, u32[]{:S(2)}, u32[]{:S(2)}) collective-permute-start(bf16[1,832,128]{2,1,0:T(8,128)(2,1)} %get-tuple-element.184), channel_id=1, source_target_pairs={{0,8},{4,12},{8,0},{12,4},{16,24},{20,28},{24,16},{28,20},{1,9},{5... | collective-permute-start | bytes 638984 | tf_op jit(solution)/shard_map/ppermute | solution.py:593
  261.1 9.9 %copy-start.43 = (f32[2,1024]{1,0:T(2,128)S(1)}, f32[2,1024]{1,0:T(2,128)}, u32[]{:S(2)}) copy-start(f32[2,1024]{1,0:T(2,128)} %get-tuple-element.192) | copy-start | bytes 24580
  262.4 17.7 %copy-start.45 = (f32[2,256]{1,0:T(2,128)S(1)}, f32[2,256]{1,0:T(2,128)}, u32[]{:S(2)}) copy-start(f32[2,256]{1,0:T(2,128)} %get-tuple-element.190) | copy-start | bytes 6148
  267.3 24.6 %copy-start.46 = (f32[2,256]{1,0:T(2,128)S(1)}, f32[2,256]{1,0:T(2,128)}, u32[]{:S(2)}) copy-start(f32[2,256]{1,0:T(2,128)} %get-tuple-element.188) | copy-start | bytes 6148
  269.5 8.1 %collective-permute-start.20 = (bf16[1,832,128]{2,1,0:T(8,128)(2,1)}, bf16[1,832,128]{2,1,0:T(8,128)(2,1)S(1)}, u32[]{:S(2)}, u32[]{:S(2)}) collective-permute-start(bf16[1,832,128]{2,1,0:T(8,128)(2,1)} %get-tuple-element.186), channel_id=1, source_target_pairs={{0,1},{1,0},{2,3},{3,2},{4,5},{5,4},{6,7},{7,6},{8,9},{9,8},{10,11... | collective-permute-start | bytes 638984 | tf_op jit(solution)/shard_map/ppermute | solution.py:615
  274.1 18.3 %collective-permute-start.27 = (bf16[1,1024,128]{2,1,0:T(8,128)(2,1)}, bf16[1,1024,128]{2,1,0:T(8,128)(2,1)S(1)}, u32[]{:S(2)}, u32[]{:S(2)}) collective-permute-start(bf16[1,1024,128]{2,1,0:T(8,128)(2,1)} %shard_map.394.mine), channel_id=1, source_target_pairs={{0,1},{1,0},{2,3},{3,2},{4,5},{5,4},{6,7},{7,6},{8,9},{9,8},{10,11... | collective-permute-start | bytes 786440 | tf_op jit(solution)/shard_map/ppermute | solution.py:636
  280.0 9.3 %collective-permute-start.21 = (bf16[1,832,128]{2,1,0:T(8,128)(2,1)}, bf16[1,832,128]{2,1,0:T(8,128)(2,1)S(1)}, u32[]{:S(2)}, u32[]{:S(2)}) collective-permute-start(bf16[1,832,128]{2,1,0:T(8,128)(2,1)} %shard_map.389.low), channel_id=1, source_target_pairs={{0,2},{1,3},{2,0},{3,1},{4,6},{5,7},{6,4},{7,5},{8,10},{9,11},{10,... | collective-permute-start | bytes 638984 | tf_op jit(solution)/shard_map/ppermute | solution.py:625
  291.8 6.1 %collective-permute-start.22 = (bf16[1,832,128]{2,1,0:T(8,128)(2,1)}, bf16[1,832,128]{2,1,0:T(8,128)(2,1)S(1)}, u32[]{:S(2)}, u32[]{:S(2)}) collective-permute-start(bf16[1,832,128]{2,1,0:T(8,128)(2,1)} %shard_map.390.mine), channel_id=1, source_target_pairs={{0,1},{1,0},{2,3},{3,2},{4,5},{5,4},{6,7},{7,6},{8,9},{9,8},{10,11... | collective-permute-start | bytes 638984 | tf_op jit(solution)/shard_map/ppermute | solution.py:636
  (43 other events, 116.5 us)

commit v3 on v2

--- a/solution.py
+++ b/solution.py
@@ -56,17 +56,51 @@
     return lax.optimization_barrier((wanted,) + others)
 
 
-def call(kernel, outs, scalars, *arrays, scratch=(), flops=0):
+class Stack:
+    def __init__(self, arrays):
+        self.arrays = arrays
+
+
+def call(kernel, outs, scalars, *operands, scratch=(), flops=0):
     shapes = [jax.ShapeDtypeStruct(shape, kind) for shape, kind in outs]
+    arrays, plan, stacks = [], [], []
+    for operand in operands:
+        if isinstance(operand, Stack):
+            plan.append((len(arrays), len(operand.arrays)))
+            arrays += operand.arrays
+            one = operand.arrays[0]
+            stacks.append(pltpu.VMEM((len(operand.arrays) * one.shape[0],) + one.shape[1:], one.dtype))
+        else:
+            plan.append((len(arrays), 0))
+            arrays.append(operand)
+    count_s, count_a = len(scalars), len(arrays)
+
+    def body(*refs):
+        scalar_refs, refs = refs[:count_s], refs[count_s:]
+        in_refs, refs = refs[:count_a], refs[count_a:]
+        out_refs, refs = refs[: len(shapes)], refs[len(shapes) :]
+        user, stack_refs = refs[: len(scratch)], list(refs[len(scratch) :])
+        seen = []
+        for first, count in plan:
+            if count == 0:
+                seen.append(in_refs[first])
+                continue
+            stack = stack_refs.pop(0)
+            size = in_refs[first].shape[0]
+            for k in range(count):
+                stack[k * size : (k + 1) * size, :] = in_refs[first + k][...]
+            seen.append(stack)
+        kernel(*scalar_refs, *seen, *out_refs, *user)
+
     moved = sum(int(np.prod(s.shape)) * s.dtype.itemsize for s in shapes)
     moved += sum(a.size * a.dtype.itemsize for a in arrays)
+    near = pl.BlockSpec(memory_space=pltpu.VMEM)
     return pl.pallas_call(
-        kernel,
+        body,
         out_shape=shapes,
-        in_specs=[pl.BlockSpec(memory_space=pltpu.SMEM)] * len(scalars)
-        + [pl.BlockSpec(memory_space=pltpu.VMEM)] * len(arrays),
-        out_specs=[pl.BlockSpec(memory_space=pltpu.VMEM)] * len(shapes),
-        scratch_shapes=list(scratch),
+        in_specs=[pl.BlockSpec(memory_space=pltpu.SMEM)] * count_s + [near] * count_a,
+        out_specs=[near] * len(shapes),
+        scratch_shapes=list(scratch) + stacks,
         compiler_params=pltpu.CompilerParams(vmem_limit_bytes=VMEM_BYTES),
         cost_estimate=pl.CostEstimate(flops=flops, bytes_accessed=moved, transcendentals=0),
     )(*scalars, *arrays)
@@ -76,20 +110,46 @@
     return [slice(start, start + step) for start in range(0, width, step)]
 
 
-def emit(copies_ref, row, where, value):
-    count = copies_ref.shape[0]
-    copies_ref[:, row : row + 1, where] = jnp.broadcast_to(
-        value[None], (count,) + value.shape
-    )
+def emit(copies_ref, start, value):
+    count, _, width = copies_ref.shape
+    for k in range(0, value.shape[1], LANE):
+        row, lane = divmod(start + k, width)
+        copies_ref[:, row : row + 1, lane : lane + LANE] = jnp.broadcast_to(
+            value[None, :, k : k + LANE], (count, 1, LANE)
+        )
+
+
+def collect(copies_ref):
+    return jnp.sum(copies_ref[...], axis=0)
+
+
+def part(sums, start, size):
+    width = sums.shape[1]
+    pieces, end = [], start + size
+    while start < end:
+        row, lane = divmod(start, width)
+        extent = min(width - lane, end - start)
+        pieces.append(sums[row : row + 1, lane : lane + extent])
+        start += extent
+    return pieces[0] if len(pieces) == 1 else jnp.concatenate(pieces, axis=1)
 
 
 def column_sum(value):
     return jnp.sum(value, axis=0, keepdims=True)
 
 
-def moments_of(sums, total):
-    mean = sums[0:1] / total
-    return mean, lax.rsqrt(sums[1:2] / total - mean * mean + EPSILON)
+def project(vector, w):
+    high = vector.astype(BF16).astype(F32)
+    middle = (vector - high).astype(BF16).astype(F32)
+    low = vector - high - middle
+    blank = jnp.zeros((13, vector.shape[1]), F32)
+    pieces = jnp.concatenate([high, middle, low, blank], axis=0).astype(BF16)
+    return column_sum(dot(pieces, w[...]))
+
+
+def moments_of(values, squares, total):
+    mean = values / total
+    return mean, lax.rsqrt(squares / total - mean * mean + EPSILON)
 
 
 def silu_grad(pre_act, gradient):
@@ -106,25 +166,26 @@
 def border_kernel(x, w, tap_0, tap_2, up, down):
     rows = x.shape[0]
     tap_0[...] = dot(x[...], w[0])
+    up[...] = tap_0[rows - AREA : rows, :]
     tap_2[...] = dot(x[...], w[2])
-    up[...] = tap_0[rows - AREA : rows, :]
     down[...] = tap_2[0:AREA, :]
 
 
-def first_kernel(frames, sc, tap_0, tap_1, tap_2, before, after, place, pre, copies, last, first):
+def first_kernel(frames, sc, tap_0, tap_1, tap_2, place, before, after, pre, copies, last, first):
     for t in range(frames):
         here = slice(t * AREA, (t + 1) * AREA)
         prev = before[...] if t == 0 else tap_0[(t - 1) * AREA : t * AREA, :]
         following = after[...] if t == frames - 1 else tap_2[(t + 1) * AREA : (t + 2) * AREA, :]
         pre[here, :] = tap_1[here, :] + sc[1 + t] * prev + sc[1 + frames + t] * following
-    last[...] = pre[(frames - 1) * AREA : frames * AREA, :]
-    first[...] = pre[0:AREA, :]
+    last[...] = pre[(frames - 1) * AREA : frames * AREA, :].astype(BF16)
+    first[...] = pre[0:AREA, :].astype(BF16)
+    width = pre.shape[1]
     valid = place[:, 0:1]
-    for c in chunks(pre.shape[1]):
+    for c in chunks(width):
         hidden = pre[:, c]
         masked = hidden * valid
-        emit(copies, 0, c, column_sum(masked))
-        emit(copies, 1, c, column_sum(masked * hidden))
+        emit(copies, c.start, column_sum(masked))
+        emit(copies, width + c.start, column_sum(masked * hidden))
 
 
 def inside(place, down, right):
@@ -142,10 +203,11 @@
     padded[EDGE : EDGE + rows, :] = value
 
 
-def second_kernel(sc, copies_in, pre_1, gain, shift, w, place, pre_2, windows, copies, stats, padded):
+def second_kernel(sc, copies_in, pre_1, gain, shift, place, w, pre_2, windows, copies, stats, padded):
     rows, width = pre_1.shape
     total = sc[0]
-    mean, inv = moments_of(jnp.sum(copies_in[...], axis=0), total)
+    sums = collect(copies_in)
+    mean, inv = moments_of(part(sums, 0, width), part(sums, width, width), total)
     stats[0:1, :] = mean
     stats[1:2, :] = inv
     act = (pre_1[...] - mean) * inv * gain[...] + shift[...]
@@ -162,41 +224,41 @@
     for c in chunks(width):
         hidden = pre_2[:, c]
         masked = hidden * valid
-        emit(copies, 0, c, column_sum(masked))
-        emit(copies, 1, c, column_sum(masked * hidden))
-
-
-def third_kernel(sc, copies_in, pre_2, gain, shift, w, place, cot, z_2, pre_3, copies, stats):
+        emit(copies, c.start, column_sum(masked))
+        emit(copies, width + c.start, column_sum(masked * hidden))
+
+
+def third_kernel(sc, copies_in, pre_2, gain, shift, place, w, z_2, pre_3, copies, stats):
+    width = pre_2.shape[1]
     total = sc[0]
-    mean, inv = moments_of(jnp.sum(copies_in[...], axis=0), total)
+    sums = collect(copies_in)
+    mean, inv = moments_of(part(sums, 0, width), part(sums, width, width), total)
     stats[0:1, :] = mean
     stats[1:2, :] = inv
+    valid = place[:, 0:1]
     act = (pre_2[...] - mean) * inv * gain[...] + shift[...]
     z_2[...] = (act * jax.nn.sigmoid(act)).astype(BF16)
-    valid = place[:, 0:1]
+    emit(copies, 0, column_sum(z_2[...].astype(F32) * valid))
     for c in chunks(w.shape[1], 2 * LANE):
-        pre_3[:, c] = dot(z_2[...], w[:, c])
-    for c in chunks(w.shape[1]):
-        hidden = pre_3[:, c]
-        masked = hidden * valid
-        emit(copies, 0, c, column_sum(masked))
-        emit(copies, 1, c, column_sum(masked * hidden))
-        emit(copies, 2, c, column_sum(cot[:, c].astype(F32)))
-
-
-def unit_kernel(sc, copies_in, pre_3, x, gain, shift, pool, counts, w_key, w_value, unit, pooled, kv, stats):
+        hidden = dot(z_2[...], w[:, c])
+        pre_3[:, c] = hidden
+        emit(copies, width + c.start, column_sum(hidden * hidden * valid))
+
+
+def unit_kernel(sc, copies_in, w_expand, gain, shift, pre_3, x, pool, counts, w_key, w_value, unit, pooled, kv, stats):
     total = sc[0]
-    sums = jnp.sum(copies_in[...], axis=0)
-    mean, inv = moments_of(sums, total)
+    narrow, channels = w_expand.shape
+    sums = collect(copies_in)
+    mean, inv = moments_of(
+        project(part(sums, 0, narrow), w_expand), part(sums, narrow, channels), total
+    )
     stats[0:1, :] = mean
     stats[1:2, :] = inv
-    stats[2:3, :] = sums[2:3]
     blocks, inner = pool.shape[0], w_key.shape[1]
-    for c in chunks(x.shape[1]):
+    for c in chunks(channels, 2 * LANE):
         scale = inv[:, c] * gain[:, c]
         summed = x[:, c].astype(F32) + (pre_3[:, c] - mean[:, c]) * scale + shift[:, c]
         unit[:, c] = (summed * jax.nn.sigmoid(summed)).astype(BF16)
-    for c in chunks(x.shape[1], 2 * LANE):
         sums_here = dot(pool[...], unit[:, c])
         high = sums_here.astype(BF16)
         pooled[0:blocks, c] = high
@@ -209,12 +271,8 @@
             kv[:, to] = ((both[:blocks] + both[blocks:]) / many).astype(BF16)
 
 
-def attend_kernel(slots, sc, theta, w, cot, place, key_row, *refs):
-    blocks = refs[:slots]
-    kv, probs, attended, pre_4, copies = refs[slots:]
-    size, inner = blocks[0].shape[0], theta.shape[1]
-    for k in range(slots):
-        kv[k * size : (k + 1) * size, :] = blocks[k][...]
+def attend_kernel(sc, theta, kv, place, key_row, w, cot, probs, attended, pre_4, copies):
+    inner, channels = w.shape
     logits = dot_cols(theta[...], kv[:, 0:inner])
     allowed = place[:, 3:4] == key_row[0:1, :]
     scores = jnp.where(allowed, logits * TEMPER, key_row[1:2, :])
@@ -223,31 +281,31 @@
     probs[...] = weights
     attended[...] = dot(weights.astype(BF16), kv[:, inner:]).astype(BF16)
     valid = place[:, 0:1]
-    for c in chunks(w.shape[1], 2 * LANE):
-        pre_4[:, c] = dot(attended[...], w[:, c])
-    for c in chunks(w.shape[1]):
-        hidden = pre_4[:, c]
-        masked = hidden * valid
-        emit(copies, 0, c, column_sum(masked))
-        emit(copies, 1, c, column_sum(masked * hidden))
-        emit(copies, 2, c, column_sum(cot[:, c].astype(F32) * hidden))
-
-
-def attend_back_kernel(slots, sc, copies_in, stats_3, pre_4, cot, gain, w, probs, kv, theta, place, key_row, *refs):
-    d_final, d_logits, stats, own = refs[:4]
-    sent = refs[4:]
+    emit(copies, 0, column_sum(attended[...].astype(F32) * valid))
+    for c in chunks(channels, 2 * LANE):
+        hidden = dot(attended[...], w[:, c])
+        pre_4[:, c] = hidden
+        emit(copies, inner + c.start, column_sum(hidden * hidden * valid))
+        emit(copies, inner + channels + c.start, column_sum(cot[:, c].astype(F32) * hidden))
+
+
+def attend_back_kernel(slots, sc, copies_in, shift_copies, gain, place, key_row, w, pre_4, cot, kv, probs, theta, d_final, d_logits, mean_out, inv_out, gain_out, shift_out, own, *sent):
     total = sc[0]
-    size, inner = own.shape[0], theta.shape[1]
-    sums = jnp.sum(copies_in[...], axis=0)
-    mean, inv = moments_of(sums, total)
-    shift_grad = stats_3[2:3, :]
-    gain_grad = inv * (sums[2:3] - mean * shift_grad)
-    stats[0:1, :] = mean
-    stats[1:2, :] = inv
-    stats[2:3, :] = gain_grad
+    inner, channels = w.shape
+    size = own.shape[0]
+    sums = collect(copies_in)
+    mean, inv = moments_of(
+        project(part(sums, 0, inner), w), part(sums, inner, channels), total
+    )
+    shift_grad = part(collect(shift_copies), 0, channels)
+    gain_grad = inv * (part(sums, inner + channels, channels) - mean * shift_grad)
+    mean_out[...] = mean
+    inv_out[...] = inv
+    gain_out[...] = gain_grad
+    shift_out[...] = shift_grad
     scale, base, slope = back_terms(gain[...], mean, inv, gain_grad, shift_grad, total)
     valid = place[:, 0:1]
-    for c in chunks(cot.shape[1]):
+    for c in chunks(channels, 2 * LANE):
         d_final[:, c] = (
             cot[:, c].astype(F32) * scale[:, c]
             + valid * (base[:, c] + pre_4[:, c] * slope[:, c])
@@ -259,8 +317,8 @@
     allowed = place[:, 3:4] == key_row[0:1, :]
     d_scores = jnp.where(allowed, TEMPER * weights * (d_probs - row_terms), 0.0)
     d_logits[...] = d_scores.astype(BF16)
+    d_values = dot_rows(weights.astype(BF16), d_attended)
     d_keys = dot_rows(d_logits[...], theta[...])
-    d_values = dot_rows(weights.astype(BF16), d_attended)
     own[:, 0:inner] = d_keys[0:size]
     own[:, inner:] = d_values[0:size]
     for k in range(1, slots):
@@ -269,10 +327,11 @@
         sent[k - 1][:, inner:] = d_values[here].astype(BF16)
 
 
-def summed_back_kernel(slots, sc, own, d_unit_part, pre_3, x, stats_3, gain, shift, spread, counts, w_key, w_value, *refs):
+def summed_back_kernel(slots, sc, own, counts, w_key, w_value, stats_3, gain, shift, spread, d_unit_part, pre_3, x, *refs):
     received = refs[: slots - 1]
     d_pooled, d_summed, copies, stacked = refs[slots - 1 :]
     size, inner = own.shape[0], w_key.shape[1]
+    channels = x.shape[1]
     many = jnp.maximum(counts[:, 0:1], 1.0)
     whole = own[...]
     for other in received:
@@ -280,31 +339,33 @@
     low = (whole / many).astype(BF16)
     d_pooled[0:size, :] = low
     d_pooled[size : 2 * size, :] = low
-    for c in chunks(x.shape[1], 2 * LANE):
-        part = dot_cols(low[:, 0:inner], w_key[c, :]) + dot_cols(low[:, inner:], w_value[c, :])
-        high = part.astype(BF16)
+    mean, inv = stats_3[0:1, :], stats_3[1:2, :]
+    for c in chunks(channels, 2 * LANE):
+        here = dot_cols(low[:, 0:inner], w_key[c, :]) + dot_cols(low[:, inner:], w_value[c, :])
+        high = here.astype(BF16)
         stacked[0:size, c] = high
-        stacked[size : 2 * size, c] = (part - high.astype(F32)).astype(BF16)
-    mean, inv = stats_3[0:1, :], stats_3[1:2, :]
-    for c in chunks(x.shape[1], 2 * LANE):
+        stacked[size : 2 * size, c] = (here - high.astype(F32)).astype(BF16)
         d_unit = d_unit_part[:, c] + dot(spread[...], stacked[:, c])
         normed = (pre_3[:, c] - mean[:, c]) * inv[:, c]
         summed = x[:, c].astype(F32) + normed * gain[:, c] + shift[:, c]
         d_here = silu_grad(summed, d_unit)
         d_summed[:, c] = d_here
-        emit(copies, 0, c, column_sum(d_here * normed))
-        emit(copies, 1, c, column_sum(d_here))
-
-
-def third_back_kernel(sc, copies_in, stats_3, gain_3, d_summed, pre_3, w, pre_2, stats_2, gain_2, shift_2, place, d_third, d_act, copies, grads):
+        emit(copies, c.start, column_sum(d_here * normed))
+        emit(copies, channels + c.start, column_sum(d_here))
+
+
+def third_back_kernel(sc, copies_in, stats_3, gain_3, place, d_summed, pre_3, w, pre_2, stats_2, gain_2, shift_2, d_third, d_act, copies, gain_out, shift_out):
     total = sc[0]
-    sums = jnp.sum(copies_in[...], axis=0)
-    grads[...] = sums
+    channels, width = pre_3.shape[1], pre_2.shape[1]
+    sums = collect(copies_in)
+    gain_grad, shift_grad = part(sums, 0, channels), part(sums, channels, channels)
+    gain_out[...] = gain_grad
+    shift_out[...] = shift_grad
     scale, base, slope = back_terms(
-        gain_3[...], stats_3[0:1, :], stats_3[1:2, :], sums[0:1], sums[1:2], total
+        gain_3[...], stats_3[0:1, :], stats_3[1:2, :], gain_grad, shift_grad, total
     )
     valid = place[:, 0:1]
-    for c in chunks(d_summed.shape[1]):
+    for c in chunks(channels, 2 * LANE):
         d_third[:, c] = (
             d_summed[:, c] * scale[:, c] + valid * (base[:, c] + pre_3[:, c] * slope[:, c])
         ).astype(BF16)
@@ -312,18 +373,19 @@
     normed = (pre_2[...] - stats_2[0:1, :]) * stats_2[1:2, :]
     d_here = silu_grad(normed * gain_2[...] + shift_2[...], d_z)
     d_act[...] = d_here
-    for c in chunks(d_here.shape[1]):
-        emit(copies, 0, c, column_sum((d_here * normed)[:, c]))
-        emit(copies, 1, c, column_sum(d_here[:, c]))
-
-
-def second_back_kernel(frames, sc, copies_in, stats_2, gain_2, d_act_2, pre_2, w, pre_1, stats_1, gain_1, shift_1, place, d_second, d_act, copies, grads, last, first, padded):
+    emit(copies, 0, column_sum(d_here * normed))
+    emit(copies, width, column_sum(d_here))
+
+
+def second_back_kernel(frames, sc, copies_in, stats_2, gain_2, d_act_2, pre_2, place, w, pre_1, stats_1, gain_1, shift_1, d_second, d_act, copies, gain_out, shift_out, last, first, padded):
     total = sc[0]
     rows, width = pre_1.shape
-    sums = jnp.sum(copies_in[...], axis=0)
-    grads[...] = sums
+    sums = collect(copies_in)
+    gain_grad, shift_grad = part(sums, 0, width), part(sums, width, width)
+    gain_out[...] = gain_grad
+    shift_out[...] = shift_grad
     scale, base, slope = back_terms(
-        gain_2[...], stats_2[0:1, :], stats_2[1:2, :], sums[0:1], sums[1:2], total
+        gain_2[...], stats_2[0:1, :], stats_2[1:2, :], gain_grad, shift_grad, total
     )
     low = (d_act_2[...] * scale + place[:, 0:1] * (base + pre_2[...] * slope)).astype(BF16)
     d_second[...] = low
@@ -339,25 +401,30 @@
     normed = (pre_1[...] - stats_1[0:1, :]) * stats_1[1:2, :]
     d_here = silu_grad(normed * gain_1[...] + shift_1[...], d_z)
     d_act[...] = d_here
-    last[...] = d_act[(frames - 1) * AREA : frames * AREA, :]
-    first[...] = d_act[0:AREA, :]
-    for c in chunks(width):
-        emit(copies, 0, c, column_sum((d_here * normed)[:, c]))
-        emit(copies, 1, c, column_sum(d_here[:, c]))
-
-
-def first_back_kernel(frames, sc, copies_in, stats_1, gain_1, d_act, pre_1, d_before, d_after, pre_before, pre_after, w, d_summed, place, near, input_grad, d_taps, grads, whole, moved):
+    last[...] = d_act[(frames - 1) * AREA : frames * AREA, :].astype(BF16)
+    first[...] = d_act[0:AREA, :].astype(BF16)
+    emit(copies, 0, column_sum(d_here * normed))
+    emit(copies, width, column_sum(d_here))
+
+
+def first_back_kernel(frames, sc, copies_in, stats_1, gain_1, d_act, pre_1, place, near, d_before, d_after, pre_before, pre_after, w, d_summed, input_grad, d_taps, gain_out, shift_out, whole, moved):
     total = sc[0]
     width = pre_1.shape[1]
-    sums = jnp.sum(copies_in[...], axis=0)
-    grads[...] = sums
+    sums = collect(copies_in)
+    gain_grad, shift_grad = part(sums, 0, width), part(sums, width, width)
+    gain_out[...] = gain_grad
+    shift_out[...] = shift_grad
     scale, base, slope = back_terms(
-        gain_1[...], stats_1[0:1, :], stats_1[1:2, :], sums[0:1], sums[1:2], total
+        gain_1[...], stats_1[0:1, :], stats_1[1:2, :], gain_grad, shift_grad, total
     )
     whole[...] = d_act[...] * scale + place[:, 0:1] * (base + pre_1[...] * slope)
     d_taps[:, width : 2 * width] = whole[...].astype(BF16)
-    d_prev = d_before[...] * scale + near[:, 0:1] * (base + pre_before[...] * slope)
-    d_next = d_after[...] * scale + near[:, 1:2] * (base + pre_after[...] * slope)
+    d_prev = d_before[...].astype(F32) * scale + near[:, 0:1] * (
+        base + pre_before[...].astype(F32) * slope
+    )
+    d_next = d_after[...].astype(F32) * scale + near[:, 1:2] * (
+        base + pre_after[...].astype(F32) * slope
+    )
     for t in range(frames):
         here = slice(t * AREA, (t + 1) * AREA)
         ahead = d_next if t == frames - 1 else whole[(t + 1) * AREA : (t + 2) * AREA, :]
@@ -392,19 +459,25 @@
 
 
 def split_out(mine, start, both, low, send, keep, sems):
-    rows = low.shape[1]
-    kept = pltpu.make_async_copy(both.at[mine], keep.at[:, start : start + rows], sems.at[0])
+    rows = low.shape[2]
+    low[0] = both[mine].astype(BF16)
+    kept = pltpu.make_async_copy(low.at[0], keep.at[:, start : start + rows], sems.at[0])
     kept.start()
-    low[...] = both[1 - mine].astype(BF16)
-    sent = pltpu.make_async_copy(low, send.at[:, start : start + rows], sems.at[1])
+    low[1] = both[1 - mine].astype(BF16)
+    sent = pltpu.make_async_copy(low.at[1], send.at[:, start : start + rows], sems.at[1])
     sent.start()
     kept.wait()
     sent.wait()
 
 
-def attend_grads_kernel(parts, start, bits, d_logits, kv, cot, w, attended, d_final, unit, send, keep, d_unit_part, d_theta, both, low, sems):
+def attend_grads_kernel(slots, parts, start, bits, d_logits, cot, w, attended, d_final, unit, *refs):
+    blocks = refs[:slots]
+    send, keep, d_unit_part, d_theta, both, low, sems, keys = refs[slots:]
+    size = blocks[0].shape[0]
     inner, channels = attended.shape[1], unit.shape[1]
-    d_theta[...] = dot(d_logits[...], kv[:, 0:inner]).astype(BF16)
+    for k in range(slots):
+        keys[k * size : (k + 1) * size, :] = blocks[k][:, 0:inner]
+    d_theta[...] = dot(d_logits[...], keys[...]).astype(BF16)
     for c in chunks(channels, 2 * LANE):
         d_unit_part[:, c] = cot[:, c].astype(F32) + dot_cols(d_theta[...], w[c, :])
     wide = channels // parts
@@ -462,8 +535,8 @@
         for i in range(count):
             at = 2 * i + mine if low else i + count * mine
             off = 2 * i + 1 - mine if low else i + count * (1 - mine)
-            keep[i] = keep_in[at, here, :] + received[at, here, :].astype(F32)
-            send[i] = (keep_in[off, here, :] + received[off, here, :].astype(F32)).astype(BF16)
+            keep[i] = (keep_in[at, here, :].astype(F32) + received[at, here, :].astype(F32)).astype(BF16)
+            send[i] = (keep_in[off, here, :].astype(F32) + received[off, here, :].astype(F32)).astype(BF16)
 
 
 def plane_stage_kernel(low_bit, high_bit, bits, in_1, received_1, in_2, received_2, send_1, keep_1, send_2, keep_2):
@@ -476,30 +549,14 @@
         for i in range(count):
             at = 2 * i + mine if low else i + count * mine
             off = 2 * i + 1 - mine if low else i + count * (1 - mine)
-            keep[i] = keep_in[at] + received[at].astype(F32)
-            send[i] = (keep_in[off] + received[off].astype(F32)).astype(BF16)
-
-
-def layer_stage_kernel(bit, bits, in_1, received_1, in_2, received_2, send, keep):
-    first = in_1[...] + received_1[...].astype(F32)
-    second = in_2[...] + received_2[...].astype(F32)
-    swap = bits[bit] == 1
-    keep[...] = jnp.where(swap, second, first)
-    send[...] = jnp.where(swap, first, second).astype(BF16)
+            keep[i] = (keep_in[at].astype(F32) + received[at].astype(F32)).astype(BF16)
+            send[i] = (keep_in[off].astype(F32) + received[off].astype(F32)).astype(BF16)
 
 
 def half_stage_kernel(bit, bits, keep_in, received, send, keep):
     mine = bits[bit]
-    keep[0] = keep_in[mine] + received[mine].astype(F32)
-    send[0] = (keep_in[1 - mine] + received[1 - mine].astype(F32)).astype(BF16)
-
-
-def join_kernel(keep_in, received, low):
-    low[...] = (keep_in[...] + received[...].astype(F32)).astype(BF16)
-
-
-def exchange_kernel(low, received, final):
-    final[...] = (low[...].astype(F32) + received[...].astype(F32)).astype(BF16)
+    keep[0] = (keep_in[mine].astype(F32) + received[mine].astype(F32)).astype(BF16)
+    send[0] = (keep_in[1 - mine].astype(F32) + received[1 - mine].astype(F32)).astype(BF16)
 
 
 def unfold(part, start, out):
@@ -545,13 +602,13 @@
         self.grp_bits = self.grp_count.bit_length() - 1
         self.send = self.keep = None
 
-    def add(self, kernel, start, rows, *arrays, extra=(), flops=0):
+    def add(self, kernel, start, rows, *arrays, extra=(), scratch=(), flops=0):
         whole = (self.pos_count // 2, 2 * self.cut, LANE)
         half = (self.pos_count // 2, rows, LANE)
         held = () if self.send is None else (self.send, self.keep)
         anywhere = pl.BlockSpec(memory_space=pl.ANY)
         inside_vmem = pl.BlockSpec(memory_space=pltpu.VMEM)
-        shapes = [jax.ShapeDtypeStruct(whole, BF16), jax.ShapeDtypeStruct(whole, F32)]
+        shapes = [jax.ShapeDtypeStruct(whole, BF16)] * 2
         shapes += [jax.ShapeDtypeStruct(shape, kind) for shape, kind in extra]
         moved = sum(a.size * a.dtype.itemsize for a in arrays) + 6 * int(np.prod(half))
         self.send, self.keep, *rest = pl.pallas_call(
@@ -562,8 +619,10 @@
             + [inside_vmem] * len(arrays),
             out_specs=[anywhere, anywhere] + [inside_vmem] * len(extra),
             scratch_shapes=[
-                pltpu.VMEM((2,) + half, F32), pltpu.VMEM(half, BF16), pltpu.SemaphoreType.DMA((2,)),
-            ],
+                pltpu.VMEM((2,) + half, F32), pltpu.VMEM((2,) + half, BF16),
+                pltpu.SemaphoreType.DMA((2,)),
+            ]
+            + list(scratch),
             input_output_aliases={1: 0, 2: 1} if held else {},
             compiler_params=pltpu.CompilerParams(vmem_limit_bytes=VMEM_BYTES),
             cost_estimate=pl.CostEstimate(flops=flops, bytes_accessed=moved, transcendentals=0),
@@ -578,54 +637,68 @@
         bits = (1, self.pos_bits - 1)
         outs = []
         for rows in (self.cut, self.cut):
-            outs += [((count, rows, LANE), BF16), ((count, rows, LANE), F32)]
+            outs += [((count, rows, LANE), BF16)] * 2
         outs = call(
             functools.partial(core_stage_kernel, self.cut, *bits), outs, (self.bits,),
             self.keep, self.received,
         )
         self.parts = [list(outs[:2]), list(outs[2:])]
         self.pair = bits
-        self.turn()
 
     def turn(self):
         for k in range(2):
             pairs = flip(self.pos_count, 1 << self.pair[k])
             self.parts[k].append(lax.ppermute(self.parts[k][0], "pos", pairs))
 
-    def more(self):
+    def hold(self, value):
+        value, self.parts[0][0], self.parts[1][0] = tie(
+            value, self.parts[0][0], self.parts[1][0]
+        )
+        return value
+
+    def more(self, last=True):
         while self.parts[0][1].shape[0] > 1:
             count = self.parts[0][1].shape[0] // 2
             self.pair = (self.pair[0] + 1, self.pair[1] - 1)
-            outs = [((count, self.cut, LANE), BF16), ((count, self.cut, LANE), F32)] * 2
+            outs = [((count, self.cut, LANE), BF16)] * 4
             (_, keep_1, got_1), (_, keep_2, got_2) = self.parts
             outs = call(
                 functools.partial(plane_stage_kernel, *self.pair), outs, (self.bits,),
                 keep_1, got_1, keep_2, got_2,
             )
             self.parts = [list(outs[:2]), list(outs[2:])]
-            self.turn()
+            if self.parts[0][1].shape[0] > 1 or last:
+                self.turn()
+
+    def after(self, others):
+        for k, other in enumerate(others):
+            self.parts[k][2], _ = tie(self.parts[k][2], other)
 
     def layer(self):
         (_, keep_1, got_1), (_, keep_2, got_2) = self.parts
-        shape = (1, self.cut, LANE)
-        send, keep = call(
-            functools.partial(layer_stage_kernel, self.pos_bits), [(shape, BF16), (shape, F32)],
-            (self.bits,), keep_1, got_1, keep_2, got_2,
-        )
-        got = lax.ppermute(send, "grp", flip(self.grp_count, 1))
+        first = keep_1.astype(F32) + got_1.astype(F32)
+        second = keep_2.astype(F32) + got_2.astype(F32)
+        swap = self.bits[self.pos_bits] == 1
+        keep = jnp.where(swap, second, first).astype(BF16)
+        send = jnp.where(swap, first, second).astype(BF16)
+        self.keep = keep
+        self.got = lax.ppermute(send, "grp", flip(self.grp_count, 1))
+
+    def exchange(self):
+        keep, got = self.keep, self.got
         for bit in range(1, self.grp_bits - 1):
             shape = (2, keep.shape[1] // 2, LANE)
             half = (1,) + shape[1:]
             send, keep = call(
                 functools.partial(half_stage_kernel, self.pos_bits + bit),
-                [(half, BF16), (half, F32)], (self.bits,), keep.reshape(shape), got.reshape(shape),
+                [(half, BF16), (half, BF16)], (self.bits,), keep.reshape(shape), got.reshape(shape),
             )
             got = lax.ppermute(send, "grp", flip(self.grp_count, 1 << bit))
-        (self.low,) = call(join_kernel, [(keep.shape, BF16)], (), keep, got)
+        self.low = (keep.astype(F32) + got.astype(F32)).astype(BF16)
         self.other = lax.ppermute(self.low, "grp", flip(self.grp_count, self.grp_count // 2))
 
     def finish(self):
-        (final,) = call(exchange_kernel, [(self.low.shape, BF16)], (), self.low, self.other)
+        final = (self.low.astype(F32) + self.other.astype(F32)).astype(BF16)
         for bit in reversed(range(1, self.grp_bits - 1)):
             mine = self.bits[self.pos_bits + bit]
             other = lax.ppermute(final, "grp", flip(self.grp_count, 1 << bit))
@@ -730,9 +803,14 @@
     wide_f32 = ((rows, channels), F32)
     wide_bf16 = ((rows, channels), BF16)
     frame_f32 = ((AREA, narrow), F32)
-
+    frame_bf16 = ((AREA, narrow), BF16)
+
+    small = (copies, 2, narrow)
+    shift_sums = jnp.sum(cotangent.astype(F32), axis=0).reshape(1, 2, channels // 2)
+    shift_sums = jnp.broadcast_to(shift_sums, (copies, 2, channels // 2))
     tap_0, tap_2, to_next, to_prev = call(
-        border_kernel, [narrow_f32, narrow_f32, frame_f32, frame_f32], (), inputs, time_weight,
+        border_kernel, [narrow_f32, narrow_f32, frame_f32, frame_f32], (),
+        inputs, time_weight,
         flops=4 * rows * channels * narrow,
     )
     before = lax.ppermute(to_next, "grp", up)
@@ -740,80 +818,90 @@
     tap_1 = dot(inputs, time_weight[1])
     pre_1, sums, last, first = call(
         functools.partial(first_kernel, frames),
-        [narrow_f32, ((copies, 2, narrow), F32), frame_f32, frame_f32],
-        (scalars,), tap_0, tap_1, tap_2, before, after, place,
+        [narrow_f32, (small, F32), frame_bf16, frame_bf16],
+        (scalars,), tap_0, tap_1, tap_2, place, before, after,
     )
     sums = trade(sums)
     pre_before = lax.ppermute(last, "grp", up)
     pre_after = lax.ppermute(first, "grp", down)
     pre_2, windows, sums, stats_1 = call(
         second_kernel,
-        [narrow_f32, ((rows, 9 * narrow), BF16), ((copies, 2, narrow), F32), ((2, narrow), F32)],
-        (scalars,), sums, pre_1, gain_1, shift_1, space_weight.reshape(9 * narrow, narrow), place,
+        [narrow_f32, ((rows, 9 * narrow), BF16), (small, F32), ((2, narrow), F32)],
+        (scalars,), sums, pre_1, gain_1, shift_1, place,
+        space_weight.reshape(9 * narrow, narrow),
         scratch=[pltpu.VMEM((rows + 2 * EDGE, narrow), F32)],
         flops=18 * rows * narrow * narrow,
     )
     sums = trade(sums)
+    sums, pre_before, pre_after = tie(sums, pre_before, pre_after)
     z_2, pre_3, sums, stats_2 = call(
         third_kernel,
-        [((rows, narrow), BF16), wide_f32, ((copies, 3, channels), F32), ((2, narrow), F32)],
-        (scalars,), sums, pre_2, gain_2, shift_2, expand_weight, place, cotangent,
+        [
+            ((rows, narrow), BF16), wide_f32, ((copies, 2, (narrow + channels) // 2), F32),
+            ((2, narrow), F32),
+        ],
+        (scalars,), sums, pre_2, gain_2, shift_2, place, expand_weight,
         flops=2 * rows * narrow * channels,
     )
     sums = trade(sums)
     unit, pooled, kv_own, stats_3 = call(
         unit_kernel,
-        [wide_bf16, ((2 * size, channels), BF16), ((size, 2 * inner), BF16), ((3, channels), F32)],
-        (scalars,), sums, pre_3, inputs, gain_3, shift_3, pool, counts, key_weight, value_weight,
+        [wide_bf16, ((2 * size, channels), BF16), ((size, 2 * inner), BF16), ((2, channels), F32)],
+        (scalars,), sums, expand_weight, gain_3, shift_3, pre_3, inputs, pool, counts,
+        key_weight, value_weight,
         flops=2 * size * channels * (rows + 4 * inner),
     )
-    kv_blocks = [kv_own] + [
+    shift_sums, _ = tie(shift_sums, kv_own)
+    shift_sums = trade(shift_sums)
+    kv = [kv_own] + [
         lax.ppermute(kv_own, "grp", flip(grp_count, step)) for step in range(1, grp_count)
     ]
     theta = dot(unit, query_weight).astype(BF16)
-    kv, probs, attended, pre_4, sums = call(
-        functools.partial(attend_kernel, grp_count),
+    probs, attended, pre_4, sums = call(
+        attend_kernel,
         [
-            ((grp_count * size, 2 * inner), BF16), ((rows, grp_count * size), F32),
-            ((rows, inner), BF16), wide_f32, ((copies, 3, channels), F32),
+            ((rows, grp_count * size), F32), ((rows, inner), BF16), wide_f32,
+            ((copies, 4, (inner + 2 * channels) // 4), F32),
         ],
-        (scalars,), theta, out_weight, cotangent, place, key_row, *kv_blocks,
+        (scalars,), theta, Stack(kv), place, key_row, out_weight, cotangent,
         flops=2 * rows * inner * (2 * grp_count * size + channels),
     )
     sums = trade(sums)
 
-    d_final, d_logits, stats_4, d_kv, *d_sent = call(
+    d_final, d_logits, mean_4, inv_4, gain_final_grad, shift_final_grad, d_kv, *d_sent = call(
         functools.partial(attend_back_kernel, grp_count),
         [
-            wide_bf16, ((rows, grp_count * size), BF16), ((3, channels), F32),
-            ((size, 2 * inner), F32),
+            wide_bf16, ((rows, grp_count * size), BF16),
         ]
+        + [((1, channels), F32)] * 4
+        + [((size, 2 * inner), F32)]
         + [((size, 2 * inner), BF16)] * (grp_count - 1),
-        (scalars,), sums, stats_3, pre_4, cotangent, gain_4, out_weight, probs, kv, theta, place, key_row,
+        (scalars,), sums, shift_sums, gain_4, place, key_row, out_weight, pre_4,
+        cotangent, Stack(kv), probs, theta,
         flops=2 * rows * inner * (3 * grp_count * size + channels),
     )
     d_received = [
         lax.ppermute(d_sent[step - 1], "grp", flip(grp_count, step)) for step in range(1, grp_count)
     ]
-    gain_final_grad, shift_final_grad = stats_4[2], stats_3[2]
     output = (
         unit.astype(F32)
-        + (pre_4 - stats_4[0]) * stats_4[1] * gain_final
+        + (pre_4 - mean_4) * inv_4 * gain_final
         + shift_final
     ).astype(BF16)
     half = deep * inner // LANE
     bundle_1 = Bundle(bits, 2 * half)
     d_unit_part, _ = bundle_1.add(
-        attend_grads_kernel, 0, 2 * half,
-        d_logits, kv, cotangent, query_weight, attended, d_final, unit,
+        functools.partial(attend_grads_kernel, grp_count), 0, 2 * half,
+        d_logits, cotangent, query_weight, attended, d_final, unit, *kv,
         extra=[wide_f32, ((rows, inner), BF16)],
+        scratch=[pltpu.VMEM((grp_count * size, inner), BF16)],
         flops=2 * rows * inner * (grp_count * size + 3 * channels),
     )
     d_pooled, d_summed, sums = call(
         functools.partial(summed_back_kernel, grp_count),
-        [((2 * size, 2 * inner), BF16), wide_f32, ((copies, 2, channels), F32)],
-        (scalars,), d_kv, d_unit_part, pre_3, inputs, stats_3, gain_3, shift_3, spread, counts,
-        key_weight, value_weight, *d_received,
+        [((2 * size, 2 * inner), BF16), wide_f32, ((copies, 8, channels // 4), F32)],
+        (scalars,), d_kv, counts, key_weight, value_weight, stats_3, gain_3,
+        shift_3, spread, d_unit_part, pre_3, inputs, *d_received,
         scratch=[pltpu.VMEM((2 * size, channels), BF16)],
         flops=4 * size * channels * (inner + rows),
     )
@@ -822,15 +910,16 @@
         pooled_grads_kernel, 2 * half, 2 * half, pooled, d_pooled,
         flops=8 * size * channels * inner,
     )
+    sums, bundle_1.send = tie(sums, bundle_1.send)
     bundle_1.begin()
-    sums, bundle_1.send = tie(sums, bundle_1.send)
-    d_third, d_act_2, sums, grads_3 = call(
+    d_third, d_act_2, sums, gain_third_grad, shift_third_grad = call(
         third_back_kernel,
-        [wide_bf16, narrow_f32, ((copies, 2, narrow), F32), ((2, channels), F32)],
-        (scalars,), sums, stats_3, gain_3, d_summed, pre_3, expand_weight, pre_2, stats_2, gain_2,
-        shift_2, place,
+        [wide_bf16, narrow_f32, (small, F32), ((1, channels), F32), ((1, channels), F32)],
+        (scalars,), sums, stats_3, gain_3, place, d_summed, pre_3, expand_weight,
+        pre_2, stats_2, gain_2, shift_2,
         flops=2 * rows * narrow * channels,
     )
+    sums, bundle_1.received = tie(sums, bundle_1.received)
     sums = trade(sums)
     tap_rows = wide * narrow // LANE
     expand_rows = narrow * deep // LANE
@@ -840,15 +929,17 @@
         flops=2 * rows * narrow * channels,
     )
     bundle_1.plane()
-    sums, bundle_2.send, bundle_1.parts[0][1] = tie(sums, bundle_2.send, bundle_1.parts[0][1])
-    d_second, d_act_1, sums, grads_2, last, first = call(
+    sums, _ = tie(sums, bundle_2.send)
+    sums = bundle_1.hold(sums)
+    bundle_1.turn()
+    d_second, d_act_1, sums, gain_second_grad, shift_second_grad, last, first = call(
         functools.partial(second_back_kernel, frames),
         [
-            ((rows, narrow), BF16), narrow_f32, ((copies, 2, narrow), F32), ((2, narrow), F32),
-            frame_f32, frame_f32,
+            ((rows, narrow), BF16), narrow_f32, (small, F32), ((1, narrow), F32), ((1, narrow), F32),
+            frame_bf16, frame_bf16,
         ],
-        (scalars,), sums, stats_2, gain_2, d_act_2, pre_2, space_weight, pre_1, stats_1, gain_1,
-        shift_1, place,
+        (scalars,), sums, stats_2, gain_2, d_act_2, pre_2, place, space_weight, pre_1, stats_1,
+        gain_1, shift_1,
         scratch=[pltpu.VMEM((rows + 2 * EDGE, narrow), F32)],
         flops=18 * rows * narrow * narrow,
     )
@@ -859,27 +950,37 @@
         space_grads_kernel, expand_rows, 9 * tap_rows, windows, d_second,
         flops=18 * rows * narrow * narrow,
     )
-    bundle_1.more()
-    sums, bundle_2.send, bundle_1.parts[0][1] = tie(sums, bundle_2.send, bundle_1.parts[0][1])
-    input_grad, d_taps, grads_1 = call(
+    (_, _, got_1), (_, _, got_2) = bundle_1.parts
+    sums, bundle_2.send, got_1, got_2 = tie(sums, bundle_2.send, got_1, got_2)
+    bundle_1.parts[0][2], bundle_1.parts[1][2] = got_1, got_2
+    input_grad, d_taps, gain_first_grad, shift_first_grad = call(
         functools.partial(first_back_kernel, frames),
-        [wide_f32, ((rows, 3 * narrow), BF16), ((2, narrow), F32)],
-        (scalars,), sums, stats_1, gain_1, d_act_1, pre_1, d_before, d_after, pre_before, pre_after,
-        time_weight, d_summed, place, near,
+        [wide_f32, ((rows, 3 * narrow), BF16), ((1, narrow), F32), ((1, narrow), F32)],
+        (scalars,), sums, stats_1, gain_1, d_act_1, pre_1, place, near, d_before, d_after,
+        pre_before, pre_after, time_weight, d_summed,
         scratch=[pltpu.VMEM((rows, narrow), F32), pltpu.VMEM((rows, narrow), F32)],
         flops=6 * rows * narrow * channels,
     )
 
+    bundle_1.after([d_taps, d_taps])
     bundle_2.add(
         time_grads_kernel, bundle_2.cut, 3 * deep * narrow // LANE, inputs, d_taps,
         flops=6 * rows * narrow * channels,
     )
     bundle_2.begin()
+    bundle_1.more()
+    bundle_2.plane()
+    bundle_2.turn()
     bundle_1.layer()
-    bundle_2.plane()
+    bundle_2.more(last=False)
+    bundle_1.got = bundle_2.hold(bundle_1.got)
+    bundle_2.turn()
+    bundle_1.exchange()
+    bundle_2.layer()
+    bundle_2.got, bundle_1.other = tie(bundle_2.got, bundle_1.other)
+    bundle_2.exchange()
     bundle_1.finish()
-    bundle_2.more()
-    bundle_2.layer()
+    bundle_2.other, bundle_1.other = tie(bundle_2.other, bundle_1.other)
     bundle_2.finish()
     if deep == LANE:
         out_grad, query_grad, key_grad, value_grad = bundle_1.outs(
@@ -912,9 +1013,9 @@
         time_all = columns(second, 0, deep, 3 * narrow)
         time_grad = jnp.stack([time_all[:, k * narrow : (k + 1) * narrow] for k in range(3)])
     return (
-        output, input_grad, time_grad, grads_1[0], grads_1[1], space_grad,
-        grads_2[0], grads_2[1], expand_grad, grads_3[0], grads_3[1],
-        query_grad, key_grad, value_grad, out_grad, gain_final_grad, shift_final_grad,
+        output, input_grad, time_grad, gain_first_grad[0], shift_first_grad[0], space_grad,
+        gain_second_grad[0], shift_second_grad[0], expand_grad, gain_third_grad[0], shift_third_grad[0],
+        query_grad, key_grad, value_grad, out_grad, gain_final_grad[0], shift_final_grad[0],
     )
 
 

time: 302 us -> 278 us (0.921)
  Pallas kernels: 100 us -> 85.3 us
  local copies, waits for them, and re-layouts: 25.9 us -> 14.3 us
  starting transfers between devices: 73.1 us -> 82.7 us
  waiting for transfers between devices: 89.3 us -> 81.6 us
    pallas_call x23 -> x17, Pallas kernels: 79.5 us -> 65.1 us  [call(): pl.pallas_call(body, out_shape=shapes, in_specs=[pl.BlockSpec(memory_spac...]
    unnamed x112 -> x100, local copies, waits for them, and re-layouts: 17.8 us -> 9.19 us
    ppermute x8, waiting for transfers between devices: 4.24 us -> 11.7 us  [turn(): self.parts[k].append(lax.ppermute(self.parts[k][0], 'pos', pairs))]
    all_to_all x7 -> x8, waiting for transfers between devices: 40.1 us -> 33.8 us  [trade(): return lax.all_to_all(copies, ('pos', 'grp'), 0, 0, tiled=True)]
    ppermute x4, starting transfers between devices: 5.4 us -> 11.5 us  [the longest x2 7.63 us: exchange(): lax.ppermute(self.low, 'grp', flip(self.grp_count, self.grp_count // 2))]
    all_to_all x7 -> x8, starting transfers between devices: 29.5 us -> 33.6 us  [trade(): return lax.all_to_all(copies, ('pos', 'grp'), 0, 0, tiled=True)]
    ppermute x3, waiting for transfers between devices: 14.5 us -> 10.7 us  [local(): lax.ppermute(kv_own, 'grp', flip(grp_count, step))]
    slice x5 -> x0, local copies, waits for them, and re-layouts: 3.66 us -> none  [the longest x2 1.92 us: local(): gain_final_grad, shift_final_grad = (stats_4[2], stats_3[2])]
  transfers between devices with their start and end apart: 35 -> 36, of which waited for: 16 -> 22; matrix products, arithmetic and copies ran while one was open for 6% -> 6% of each run, Pallas kernels for 17% -> 18%
where the time goes in v3:
time: 278 us; the launch traced here: 277 us
  Pallas kernels  85.3 us (31%)
  starting transfers between devices  82.7 us (30%)
  waiting for transfers between devices  81.6 us (29%)
  local copies, waits for them, and re-layouts  14.3 us (5%)
  other arithmetic  6.79 us (2%)
  matrix products  4.67 us (2%)
    pallas_call x17, Pallas kernels, call(): pl.pallas_call(body, out_shape=shapes, in_specs=[pl.BlockSpec(memory_spac...  65.1 us
    all_to_all x8, waiting for transfers between devices, trade(): return lax.all_to_all(copies, ('pos', 'grp'), 0, 0, tiled=True)  33.8 us
    all_to_all x8, starting transfers between devices, trade(): return lax.all_to_all(copies, ('pos', 'grp'), 0, 0, tiled=True)  33.6 us
    pallas_call x5, Pallas kernels, add(): pl.pallas_call(functools.partial(kernel, self.pos_count, start), out_shap...  20.3 us
    ppermute x2, waiting for transfers between devices, exchange(): lax.ppermute(self.low, 'grp', flip(self.grp_count, self.grp_count // 2))  11.8 us
    ppermute x8, waiting for transfers between devices, turn(): self.parts[k].append(lax.ppermute(self.parts[k][0], 'pos', pairs))  11.7 us
    ppermute x3, waiting for transfers between devices, local(): lax.ppermute(kv_own, 'grp', flip(grp_count, step))  10.7 us
    unnamed x100, local copies, waits for them, and re-layouts  9.19 us
  transfers between devices with their start and end apart: 36, of which 22 were waited for; matrix products, arithmetic and copies ran while one was open for 6% of the time, Pallas kernels for 18%

profile of v3, /device:TPU:0, one launch (start us, length us, event | category | flops | bytes accessed | tf_op | source)
XLA Modules:
  0.0 276.7 jit_solution(4233786806745333874)
XLA Ops:
  0.7 3.3 %shard_map.368 = (f32[392,256]{1,0:T(8,128)}, f32[392,256]{1,0:T(8,128)}, f32[196,256]{1,0:T(8,128)}, f32[196,256]{1,0:T(8,128)}) custom-call(bf16[392,1024]{1,0:T(8,128)(2,1)} %x.5, bf16[3,1024,256]{2,1,0:T(8,128)(2,1)} %refs_12_.1), custom_call_target="tpu_custom_call" | custom-call | flops 411041792 | bytes 3579904 | tf_op jit(solution)/shard_map/pallas_call | solution.py:98
  4.0 4.9 %collective-permute-start = (f32[196,256]{1,0:T(8,128)}, f32[196,256]{1,0:T(8,128)S(1)}, u32[]{:S(2)}, u32[]{:S(2)}) collective-permute-start(f32[196,256]{1,0:T(8,128)} %get-tuple-element.131), channel_id=1, source_target_pairs={{0,1},{1,2},{2,3},{4,5},{5,6},{6,7},{8,9},{9,10},{10,11},{12,13},{... | collective-permute-start | bytes 602120 | tf_op jit(solution)/shard_map/ppermute | solution.py:816
  10.2 2.2 fusion.refs_2_
  18.3 2.5 shard_map.369
  20.8 5.9 %all-to-all-start = ((f32[32,2,256]{2,1,0:T(2,128)}), f32[32,2,256]{2,1,0:T(2,128)S(1)}, u32[]{:S(2)}, u32[]{:S(2)}) async-start(f32[32,2,256]{2,1,0:T(2,128)} %get-tuple-element.133), calls=%async_computation | async-start | bytes 131072 | tf_op jit(solution)/shard_map/all_to_all | solution.py:49
  28.0 3.7 %collective-permute-start.2 = (bf16[196,256]{1,0:T(8,128)(2,1)}, bf16[196,256]{1,0:T(8,128)(2,1)S(1)}, u32[]{:S(2)}, u32[]{:S(2)}) collective-permute-start(bf16[196,256]{1,0:T(8,128)(2,1)} %get-tuple-element.136), channel_id=1, source_target_pairs={{0,1},{1,2},{2,3},{4,5},{5,6},{6,7},{8,9},{9,10},{10,11},{12,13},{... | collective-permute-start | bytes 301064 | tf_op jit(solution)/shard_map/ppermute | solution.py:825
  34.8 4.9 %shard_map.370 = (f32[392,256]{1,0:T(8,128)}, bf16[392,2304]{1,0:T(8,128)(2,1)}, f32[32,2,256]{2,1,0:T(2,128)}, f32[2,256]{1,0:T(2,128)}) custom-call(f32[5]{0:T(128)} %pad_maximum_fusion.3.refs_0_, f32[32,2,256]{2,1,0:T(2,128)} %copy-done.26, f32[392,256]{1,0:T(8,128)} %get-tuple-element.134.refs_2_.refs_8_.refs_5_, f32[1,256]{1,0:T(1,128)} %bitcast.45, ...), custom_call_target="tpu_custom_call" | custom-call | flops 462422016 | bytes 3930240 | tf_op jit(solution)/shard_map/pallas_call | solution.py:98
  39.7 5.6 %all-to-all-start.1 = ((f32[32,2,256]{2,1,0:T(2,128)}), f32[32,2,256]{2,1,0:T(2,128)S(1)}, u32[]{:S(2)}, u32[]{:S(2)}) async-start(f32[32,2,256]{2,1,0:T(2,128)} %get-tuple-element.135), calls=%async_computation.1 | async-start | bytes 131072 | tf_op jit(solution)/shard_map/all_to_all | solution.py:49
  45.5 7.3 %all-to-all-done.1.refs_1_ = f32[32,2,256]{2,1,0:T(2,128)S(1)} async-done(((f32[32,2,256]{2,1,0:T(2,128)}), f32[32,2,256]{2,1,0:T(2,128)S(1)}, u32[]{:S(2)}, u32[]{:S(2)}) %all-to-all-start.1) | async-done | bytes 65568 | tf_op jit(solution)/shard_map/all_to_all | solution.py:49
  53.4 3.0 %shard_map.371 = (bf16[392,256]{1,0:T(8,128)(2,1)}, f32[392,1024]{1,0:T(8,128)}, f32[32,2,640]{2,1,0:T(2,128)}, f32[2,256]{1,0:T(2,128)}) custom-call(f32[5]{0:T(128)} %pad_maximum_fusion.3.refs_0_, f32[32,2,256]{2,1,0:T(2,128)} %copy-done.27, f32[392,256]{1,0:T(8,128)} %get-tuple-element.139.refs_2_.refs_8_.refs_5_, f32[1,256]{1,0:T(1,128)} %bitcast.48, ...), custom_call_target="tpu_custom_call" | custom-call | flops 205520896 | bytes 2971776 | tf_op jit(solution)/shard_map/pallas_call | solution.py:98
  56.4 2.6 all-to-all-start.2
  60.3 7.6 %all-to-all-done.2.refs_1_ = f32[32,2,640]{2,1,0:T(2,128)S(1)} async-done(((f32[32,2,640]{2,1,0:T(2,128)}), f32[32,2,640]{2,1,0:T(2,128)S(1)}, u32[]{:S(2)}, u32[]{:S(2)}) %all-to-all-start.2) | async-done | bytes 163872 | tf_op jit(solution)/shard_map/all_to_all | solution.py:49
  68.5 4.8 %shard_map.372 = (bf16[392,1024]{1,0:T(8,128)(2,1)}, bf16[224,1024]{1,0:T(8,128)(2,1)}, bf16[112,1024]{1,0:T(8,128)(2,1)}, f32[2,1024]{1,0:T(2,128)}) custom-call(f32[5]{0:T(128)} %pad_maximum_fusion.3.refs_0_, f32[32,2,640]{2,1,0:T(2,128)} %copy-done.17, bf16[256,1024]{1,0:T(8,128)(2,1)} %refs_7_.2, f32[1,1024]{1,0:T(1,128)} %bitcast.38, ...), custom_call_target="tpu_custom_call" | custom-call | flops 559677440 | bytes 6789312 | tf_op jit(solution)/shard_map/pallas_call | solution.py:98
  75.1 2.6 collective-permute-start.6
  78.4 2.6 all-to-all-start.4
  81.0 2.5 convolution_convert_fusion.refs_1_.refs_14_
  84.8 9.4 %collective-permute-done.5.refs_4_.refs_11_.refs_2_ = bf16[112,1024]{1,0:T(8,128)(2,1)S(1)} collective-permute-done((bf16[112,1024]{1,0:T(8,128)(2,1)}, bf16[112,1024]{1,0:T(8,128)(2,1)S(1)}, u32[]{:S(2)}, u32[]{:S(2)}) %collective-permute-start.5) | collective-permute-done | bytes 229408 | tf_op jit(solution)/shard_map/ppermute | solution.py:857
  95.6 4.9 %shard_map.373 = (f32[392,448]{1,0:T(8,128)}, bf16[392,512]{1,0:T(8,128)(2,1)}, f32[392,1024]{1,0:T(8,128)}, f32[32,4,640]{2,1,0:T(4,128)}) custom-call(f32[5]{0:T(128)} %pad_maximum_fusion.3.refs_0_, bf16[392,512]{1,0:T(8,128)(2,1)} %convolution_convert_fusion.refs_1_.refs_14_, bf16[112,1024]{1,0:T(8,128)(2,1)} %get-tuple-element.143.refs_2_.refs_9_.refs_0_, ...), custom_call_target="tpu_custom_call" | custom-call | flops 770703360 | bytes 6217344 | tf_op jit(solution)/shard_map/pallas_call | solution.py:98
  100.5 5.6 %all-to-all-start.3 = ((f32[32,4,640]{2,1,0:T(4,128)}), f32[32,4,640]{2,1,0:T(4,128)S(1)}, u32[]{:S(2)}, u32[]{:S(2)}) async-start(f32[32,4,640]{2,1,0:T(4,128)} %get-tuple-element.145), calls=%async_computation.3 | async-start | bytes 655360 | tf_op jit(solution)/shard_map/all_to_all | solution.py:49
  106.9 10.0 %all-to-all-done.3.refs_1_ = f32[32,4,640]{2,1,0:T(4,128)S(1)} async-done(((f32[32,4,640]{2,1,0:T(4,128)}), f32[32,4,640]{2,1,0:T(4,128)S(1)}, u32[]{:S(2)}, u32[]{:S(2)}) %all-to-all-start.3) | async-done | bytes 327712 | tf_op jit(solution)/shard_map/all_to_all | solution.py:49
  117.6 5.8 %shard_map.374 = (bf16[392,1024]{1,0:T(8,128)(2,1)}, bf16[392,448]{1,0:T(8,128)(2,1)}, f32[1,1024]{1,0:T(1,128)}, f32[1,1024]{1,0:T(1,128)}, f32[1,1024]{1,0:T(1...) custom-call(f32[5]{0:T(128)} %pad_maximum_fusion.3.refs_0_, ...), custom_call_target="tpu_custom_call" | custom-call | flops 950534144 | bytes 8268416 | tf_op jit(solution)/shard_map/pallas_call | solution.py:98
  128.7 7.2 %shard_map.375 = (bf16[4,2048,128]{2,1,0:T(8,128)(2,1)}, bf16[4,2048,128]{2,1,0:T(8,128)(2,1)}, f32[392,1024]{1,0:T(8,128)}, bf16[392,512]{1,0:T(8,128)(2,1)}) custom-call(s32[5]{0:T(128)} %stack.57.bits.refs_0_, bf16[392,448]{1,0:T(8,128)(2,1)} %get-tuple-element.152.d_logits, bf16[392,1024]{1,0:T(8,128)(2,1)} %cot.1, bf16[1024,512]{1,0:T(8,128)(2,1)} %w.1, ...), custom_call_target="tpu_custom_call" | custom-call | flops 1412956160 | bytes 8272896 | tf_op jit(solution)/shard_map/pallas_call | solution.py:614
  135.9 8.8 %collective-permute-done.8.refs_13_ = bf16[112,1024]{1,0:T(8,128)(2,1)S(1)} collective-permute-done((bf16[112,1024]{1,0:T(8,128)(2,1)}, bf16[112,1024]{1,0:T(8,128)(2,1)S(1)}, u32[]{:S(2)}, u32[]{:S(2)}) %collective-permute-start.8) | collective-permute-done | bytes 229408 | tf_op jit(solution)/shard_map/ppermute | solution.py:884
  145.4 6.6 %shard_map.376 = (bf16[224,1024]{1,0:T(8,128)(2,1)}, f32[392,1024]{1,0:T(8,128)}, f32[32,8,256]{2,1,0:T(8,128)}) custom-call(f32[5]{0:T(128)} %pad_maximum_fusion.3.refs_0_, f32[112,1024]{1,0:T(8,128)} %get-tuple-element.150.refs_1_, f32[112,1]{1,0:T(8,128)} %copy.70.refs_8_.refs_2_, bf16[1024,512]{1,0:T(8,128)(2,1)} %refs_3_.1, bf16[1024,512]{1,0:T(8,128)(2,1)} %refs_4_.1, ...), custom_call_target="tpu_custom_call" | custom-call | flops 414711808 | bytes 9777088 | tf_op jit(solution)/shard_map/pallas_call | solution.py:98
  152.1 4.9 %all-to-all-start.5 = ((f32[32,8,256]{2,1,0:T(8,128)}), f32[32,8,256]{2,1,0:T(8,128)S(1)}, u32[]{:S(2)}, u32[]{:S(2)}) async-start(f32[32,8,256]{2,1,0:T(8,128)} %get-tuple-element.159), calls=%async_computation.5 | async-start | bytes 524288 | tf_op jit(solution)/shard_map/all_to_all | solution.py:49
  156.9 3.4 %shard_map.377 = (bf16[4,2048,128]{2,1,0:T(8,128)(2,1)}, bf16[4,2048,128]{2,1,0:T(8,128)(2,1)}) custom-call(s32[5]{0:T(128)} %stack.57.bits.refs_0_, bf16[4,2048,128]{2,1,0:T(8,128)(2,1)} %get-tuple-element.160.send_in, bf16[4,2048,128]{2,1,0:T(8,128)(2,1)} %get-tuple-element.161.keep_in, ...), custom_call_target="tpu_custom_call", output_to_operand_aliasing={{0}: (1, {}), {1}: (2, {})} | custom-call | flops 469762048 | bytes 4063232 | tf_op jit(solution)/shard_map/pallas_call | solution.py:614
  160.3 6.8 %all-to-all-done.5.refs_1_ = f32[32,8,256]{2,1,0:T(8,128)S(1)} async-done(((f32[32,8,256]{2,1,0:T(8,128)}), f32[32,8,256]{2,1,0:T(8,128)S(1)}, u32[]{:S(2)}, u32[]{:S(2)}) %all-to-all-start.5) | async-done | bytes 262176 | tf_op jit(solution)/shard_map/all_to_all | solution.py:49
  167.8 3.9 %shard_map.378 = (bf16[392,1024]{1,0:T(8,128)(2,1)}, f32[392,256]{1,0:T(8,128)}, f32[32,2,256]{2,1,0:T(2,128)}, f32[1,1024]{1,0:T(1,128)}, f32[1,1024]{1,0:T(1,128)}) custom-call(f32[5]{0:T(128)} %pad_maximum_fusion.3.refs_0_, f32[32,8,256]{2,1,0:T(8,128)} %copy-done.7, f32[2,1024]{1,0:T(2,128)} %get-tuple-element.151.refs_5_.refs_2_, f32[1,1024]{1,0:T(1,128)} %bitcast.40, ...), custom_call_target="tpu_custom_call" | custom-call | flops 205520896 | bytes 5699712 | tf_op jit(solution)/shard_map/pallas_call | solution.py:98
  171.7 2.7 all-to-all-start.6
  174.5 2.6 shard_map.379
  177.0 4.0 %shard_map.380 = (bf16[2,1024,128]{2,1,0:T(8,128)(2,1)}, bf16[2,1024,128]{2,1,0:T(8,128)(2,1)}, bf16[2,1024,128]{2,1,0:T(8,128)(2,1)}, bf16[2,1024,128]{2,1,0:T(8,128)(2,1)}) custom-call(s32[5]{0:T(128)} %stack.57.bits.refs_0_, bf16[4,2048,128]{2,1,0:T(8,128)(2,1)} %get-tuple-element.175.refs_1_, bf16[4,2048,128]{2,1,0:T(8,128)(2,1)} %copy-done.3), custom_call_target="tpu_custom_call" | custom-call | bytes 6291456 | tf_op jit(solution)/shard_map/pallas_call | solution.py:98
  184.4 4.2 %shard_map.381 = (bf16[392,256]{1,0:T(8,128)(2,1)}, f32[392,256]{1,0:T(8,128)}, f32[32,2,256]{2,1,0:T(2,128)}, f32[1,256]{1,0:T(1,128)}, f32[1,256]{1,0:T(1,128)...) custom-call(f32[5]{0:T(128)} %pad_maximum_fusion.3.refs_0_, f32[32,2,256]{2,1,0:T(2,128)} %copy-done.25, ...), custom_call_target="tpu_custom_call" | custom-call | flops 462422016 | bytes 3333248 | tf_op jit(solution)/shard_map/pallas_call | solution.py:98
  188.6 3.7 %all-to-all-start.7 = ((f32[32,2,256]{2,1,0:T(2,128)}), f32[32,2,256]{2,1,0:T(2,128)S(1)}, u32[]{:S(2)}, u32[]{:S(2)}) async-start(f32[32,2,256]{2,1,0:T(2,128)} %get-tuple-element.182), calls=%async_computation.7 | async-start | bytes 131072 | tf_op jit(solution)/shard_map/all_to_all | solution.py:49
  192.4 3.7 %collective-permute-start.13 = (bf16[196,256]{1,0:T(8,128)(2,1)}, bf16[196,256]{1,0:T(8,128)(2,1)S(1)}, u32[]{:S(2)}, u32[]{:S(2)}) collective-permute-start(bf16[196,256]{1,0:T(8,128)(2,1)} %get-tuple-element.191), channel_id=1, source_target_pairs={{0,1},{1,2},{2,3},{4,5},{5,6},{6,7},{8,9},{9,10},{10,11},{12,13},{... | collective-permute-start | bytes 301064 | tf_op jit(solution)/shard_map/ppermute | solution.py:947
  198.4 3.5 %shard_map.382 = (bf16[4,1664,128]{2,1,0:T(8,128)(2,1)}, bf16[4,1664,128]{2,1,0:T(8,128)(2,1)}) custom-call(s32[5]{0:T(128)} %stack.57.bits.refs_0_, bf16[4,1664,128]{2,1,0:T(8,128)(2,1)} %get-tuple-element.173.send_in, bf16[4,1664,128]{2,1,0:T(8,128)(2,1)} %get-tuple-element.183.keep_in, ...), custom_call_target="tpu_custom_call", output_to_operand_aliasing={{0}: (1, {}), {1}: (2, {})} | custom-call | flops 462422016 | bytes 3776512 | tf_op jit(solution)/shard_map/pallas_call | solution.py:614
  203.5 4.6 %shard_map.383 = (f32[392,1024]{1,0:T(8,128)}, bf16[392,768]{1,0:T(8,128)(2,1)}, f32[1,256]{1,0:T(1,128)}, f32[1,256]{1,0:T(1,128)}) custom-call(f32[5]{0:T(128)} %pad_maximum_fusion.3.refs_0_, f32[32,2,256]{2,1,0:T(2,128)} %copy-done.23, f32[2,256]{1,0:T(2,128)} %get-tuple-element.181.refs_9_.refs_2_, f32[1,256]{1,0:T(1,128)} %bitcast.47, ...), custom_call_target="tpu_custom_call" | custom-call | flops 616562688 | bytes 6668960 | tf_op jit(solution)/shard_map/pallas_call | solution.py:98
  208.1 3.7 %shard_map.384 = (bf16[4,1664,128]{2,1,0:T(8,128)(2,1)}, bf16[4,1664,128]{2,1,0:T(8,128)(2,1)}) custom-call(s32[5]{0:T(128)} %stack.57.bits.refs_0_, bf16[4,1664,128]{2,1,0:T(8,128)(2,1)} %get-tuple-element.196.send_in, bf16[4,1664,128]{2,1,0:T(8,128)(2,1)} %get-tuple-element.197.keep_in, ...), custom_call_target="tpu_custom_call", output_to_operand_aliasing={{0}: (1, {}), {1}: (2, {})} | custom-call | flops 616562688 | bytes 3764224 | tf_op jit(solution)/shard_map/pallas_call | solution.py:614
  211.8 2.7 shard_map.387
  218.6 3.6 %shard_map.385 = (bf16[2,832,128]{2,1,0:T(8,128)(2,1)}, bf16[2,832,128]{2,1,0:T(8,128)(2,1)}, bf16[2,832,128]{2,1,0:T(8,128)(2,1)}, bf16[2,832,128]{2,1,0:T(8,128)(2,1)}) custom-call(s32[5]{0:T(128)} %stack.57.bits.refs_0_, bf16[4,1664,128]{2,1,0:T(8,128)(2,1)} %get-tuple-element.199.refs_1_, bf16[4,1664,128]{2,1,0:T(8,128)(2,1)} %copy-done.4), custom_call_target="tpu_custom_call" | custom-call | bytes 5111808 | tf_op jit(solution)/shard_map/pallas_call | solution.py:98
  226.6 7.4 %collective-permute-done.16.refs_2_ = bf16[2,832,128]{2,1,0:T(8,128)(2,1)S(1)} collective-permute-done((bf16[2,832,128]{2,1,0:T(8,128)(2,1)}, bf16[2,832,128]{2,1,0:T(8,128)(2,1)S(1)}, u32[]{:S(2)}, u32[]{:S(2)}) %collective-permute-start.16) | collective-permute-done | bytes 426016 | tf_op jit(solution)/shard_map/ppermute | solution.py:651
  235.1 2.4 shard_map.386
  239.8 2.8 %collective-permute-start.24 = (bf16[1,1024,128]{2,1,0:T(8,128)(2,1)S(1)}, bf16[1,1024,128]{2,1,0:T(8,128)(2,1)S(1)}, u32[]{:S(2)}, u32[]{:S(2)}) collective-permute-start(bf16[1,1024,128]{2,1,0:T(8,128)(2,1)S(1)} %add_convert_fusion.2), channel_id=1, source_target_pairs={{0,2},{1,3},{2,0},{3,1},{4,6},{5,7},{6,4},{7,5},{8,10},{9,11},{10,... | collective-permute-start | bytes 786440 | tf_op jit(solution)/shard_map/ppermute | solution.py:698
  247.4 6.0 %collective-permute-done.24 = bf16[1,1024,128]{2,1,0:T(8,128)(2,1)S(1)} collective-permute-done((bf16[1,1024,128]{2,1,0:T(8,128)(2,1)S(1)}, bf16[1,1024,128]{2,1,0:T(8,128)(2,1)S(1)}, u32[]{:S(2)}, u32[]{:S(2)}) %collective-permute-start.24) | collective-permute-done | bytes 262176 | tf_op jit(solution)/shard_map/ppermute | solution.py:698
  253.4 2.3 collective-permute-done.23
  256.0 4.8 %collective-permute-start.25 = (bf16[1,832,128]{2,1,0:T(8,128)(2,1)S(1)}, bf16[1,832,128]{2,1,0:T(8,128)(2,1)S(1)}, u32[]{:S(2)}, u32[]{:S(2)}) collective-permute-start(bf16[1,832,128]{2,1,0:T(8,128)(2,1)S(1)} %add_convert_fusion.4), channel_id=1, source_target_pairs={{0,2},{1,3},{2,0},{3,1},{4,6},{5,7},{6,4},{7,5},{8,10},{9,11},{10,... | collective-permute-start | bytes 638984 | tf_op jit(solution)/shard_map/ppermute | solution.py:698
  260.8 5.8 %collective-permute-done.25 = bf16[1,832,128]{2,1,0:T(8,128)(2,1)S(1)} collective-permute-done((bf16[1,832,128]{2,1,0:T(8,128)(2,1)S(1)}, bf16[1,832,128]{2,1,0:T(8,128)(2,1)S(1)}, u32[]{:S(2)}, u32[]{:S(2)}) %collective-permute-start.25) | collective-permute-done | bytes 213024 | tf_op jit(solution)/shard_map/ppermute | solution.py:698
  266.8 3.4 %collective-permute-start.27 = (bf16[1,832,128]{2,1,0:T(8,128)(2,1)S(1)}, bf16[1,832,128]{2,1,0:T(8,128)(2,1)S(1)}, u32[]{:S(2)}, u32[]{:S(2)}) collective-permute-start(bf16[1,832,128]{2,1,0:T(8,128)(2,1)S(1)} %add_convert_fusion.3.refs_1_), channel_id=1, source_target_pairs={{0,1},{1,0},{2,3},{3,2},{4,5},{5,4},{6,7},{7,6},{8,9},{9,8},{10,11... | collective-permute-start | bytes 638984 | tf_op jit(solution)/shard_map/ppermute | solution.py:709
  271.5 2.0 shard_map.389
  (193 shorter events, 56.5 us)
Async XLA Ops:
  4.0 12.5 %collective-permute-start = (f32[196,256]{1,0:T(8,128)}, f32[196,256]{1,0:T(8,128)S(1)}, u32[]{:S(2)}, u32[]{:S(2)}) collective-permute-start(f32[196,256]{1,0:T(8,128)} %get-tuple-element.131), channel_id=1, source_target_pairs={{0,1},{1,2},{2,3},{4,5},{5,6},{6,7},{8,9},{9,10},{10,11},{12,13},{... | collective-permute-start | bytes 602120 | tf_op jit(solution)/shard_map/ppermute | solution.py:816
  8.9 8.6 %collective-permute-start.1 = (f32[196,256]{1,0:T(8,128)}, f32[196,256]{1,0:T(8,128)S(1)}, u32[]{:S(2)}, u32[]{:S(2)}) collective-permute-start(f32[196,256]{1,0:T(8,128)} %get-tuple-element.132), channel_id=1, source_target_pairs={{1,0},{2,1},{3,2},{5,4},{6,5},{7,6},{9,8},{10,9},{11,10},{13,12},{... | collective-permute-start | bytes 602120 | tf_op jit(solution)/shard_map/ppermute | solution.py:817
  18.2 27.1 %copy-start.1 = (bf16[392,1024]{1,0:T(8,128)(2,1)S(1)}, bf16[392,1024]{1,0:T(8,128)(2,1)}, u32[]{:S(2)}) copy-start(bf16[392,1024]{1,0:T(8,128)(2,1)} %cot.1) | copy-start | bytes 2408452
  20.8 13.4 %all-to-all-start = ((f32[32,2,256]{2,1,0:T(2,128)}), f32[32,2,256]{2,1,0:T(2,128)S(1)}, u32[]{:S(2)}, u32[]{:S(2)}) async-start(f32[32,2,256]{2,1,0:T(2,128)} %get-tuple-element.133), calls=%async_computation | async-start | bytes 131072 | tf_op jit(solution)/shard_map/all_to_all | solution.py:49
  28.0 17.4 %collective-permute-start.2 = (bf16[196,256]{1,0:T(8,128)(2,1)}, bf16[196,256]{1,0:T(8,128)(2,1)S(1)}, u32[]{:S(2)}, u32[]{:S(2)}) collective-permute-start(bf16[196,256]{1,0:T(8,128)(2,1)} %get-tuple-element.136), channel_id=1, source_target_pairs={{0,1},{1,2},{2,3},{4,5},{5,6},{6,7},{8,9},{9,10},{10,11},{12,13},{... | collective-permute-start | bytes 301064 | tf_op jit(solution)/shard_map/ppermute | solution.py:825
  31.7 13.8 %collective-permute-start.3 = (bf16[196,256]{1,0:T(8,128)(2,1)}, bf16[196,256]{1,0:T(8,128)(2,1)S(1)}, u32[]{:S(2)}, u32[]{:S(2)}) collective-permute-start(bf16[196,256]{1,0:T(8,128)(2,1)} %get-tuple-element.137), channel_id=1, source_target_pairs={{1,0},{2,1},{3,2},{5,4},{6,5},{7,6},{9,8},{10,9},{11,10},{13,12},{... | collective-permute-start | bytes 301064 | tf_op jit(solution)/shard_map/ppermute | solution.py:826
  39.7 19.3 %copy-start.45 = (f32[1,448]{1,0:T(1,128)S(1)}, f32[1,448]{1,0:T(1,128)}, u32[]{:S(2)}) copy-start(f32[1,448]{1,0:T(1,128)} %constant.79) | copy-start | bytes 5380
  39.7 19.9 %copy-start.28 = (f32[112,392]{1,0:T(8,128)S(1)}, f32[112,392]{1,0:T(8,128)}, u32[]{:S(2)}) copy-start(f32[112,392]{1,0:T(8,128)} %constant.68.clone) | copy-start | bytes 526852
  39.7 13.1 %all-to-all-start.1 = ((f32[32,2,256]{2,1,0:T(2,128)}), f32[32,2,256]{2,1,0:T(2,128)S(1)}, u32[]{:S(2)}, u32[]{:S(2)}) async-start(f32[32,2,256]{2,1,0:T(2,128)} %get-tuple-element.135), calls=%async_computation.1 | async-start | bytes 131072 | tf_op jit(solution)/shard_map/all_to_all | solution.py:49
  45.5 38.0 %copy-start.36 = (bf16[196,256]{1,0:T(8,128)(2,1)}, bf16[196,256]{1,0:T(8,128)(2,1)S(1)}, u32[]{:S(2)}) copy-start(bf16[196,256]{1,0:T(8,128)(2,1)S(1)} %collective-permute-done.2.refs_10_) | copy-start | bytes 301060
  45.5 38.0 %copy-start.37 = (bf16[196,256]{1,0:T(8,128)(2,1)}, bf16[196,256]{1,0:T(8,128)(2,1)S(1)}, u32[]{:S(2)}) copy-start(bf16[196,256]{1,0:T(8,128)(2,1)S(1)} %collective-permute-done.3.refs_11_) | copy-start | bytes 301060
  56.4 11.5 %all-to-all-start.2 = ((f32[32,2,640]{2,1,0:T(2,128)}), f32[32,2,640]{2,1,0:T(2,128)S(1)}, u32[]{:S(2)}, u32[]{:S(2)}) async-start(f32[32,2,640]{2,1,0:T(2,128)} %get-tuple-element.140), calls=%async_computation.2 | async-start | bytes 327680 | tf_op jit(solution)/shard_map/all_to_all | solution.py:49
  73.3 11.5 %collective-permute-start.4 = (bf16[112,1024]{1,0:T(8,128)(2,1)}, bf16[112,1024]{1,0:T(8,128)(2,1)S(1)}, u32[]{:S(2)}, u32[]{:S(2)}) collective-permute-start(bf16[112,1024]{1,0:T(8,128)(2,1)} %get-tuple-element.143.refs_2_.refs_9_.refs_0_), channel_id=1, source_target_pairs={{0,1},{1,0},{2,3},{3,2},{4,5},{5,4},{6,7},{7,6},{8,9},{9,8},{10,11... | collective-permute-start | bytes 688136 | tf_op jit(solution)/shard_map/ppermute | solution.py:857
  73.3 20.9 %collective-permute-start.5 = (bf16[112,1024]{1,0:T(8,128)(2,1)}, bf16[112,1024]{1,0:T(8,128)(2,1)S(1)}, u32[]{:S(2)}, u32[]{:S(2)}) collective-permute-start(bf16[112,1024]{1,0:T(8,128)(2,1)} %get-tuple-element.143.refs_2_.refs_9_.refs_0_), channel_id=1, source_target_pairs={{0,2},{1,3},{2,0},{3,1},{4,6},{5,7},{6,4},{7,5},{8,10},{9,11},{10,... | collective-permute-start | bytes 688136 | tf_op jit(solution)/shard_map/ppermute | solution.py:857
  75.1 19.1 %collective-permute-start.6 = (bf16[112,1024]{1,0:T(8,128)(2,1)}, bf16[112,1024]{1,0:T(8,128)(2,1)S(1)}, u32[]{:S(2)}, u32[]{:S(2)}) collective-permute-start(bf16[112,1024]{1,0:T(8,128)(2,1)} %get-tuple-element.143.refs_2_.refs_9_.refs_0_), channel_id=1, source_target_pairs={{0,3},{1,2},{2,1},{3,0},{4,7},{5,6},{6,5},{7,4},{8,11},{9,10},{10,... | collective-permute-start | bytes 688136 | tf_op jit(solution)/shard_map/ppermute | solution.py:857
  78.4 22.1 %all-to-all-start.4 = ((f32[32,2,512]{2,1,0:T(2,128)}), f32[32,2,512]{2,1,0:T(2,128)S(1)}, u32[]{:S(2)}, u32[]{:S(2)}) async-start(f32[32,2,512]{2,1,0:T(2,128)} %broadcast_in_dim.42), calls=%async_computation.4 | async-start | bytes 262144 | tf_op jit(solution)/shard_map/all_to_all | solution.py:49
  83.5 23.3 %copy-start.35 = (f32[392,112]{1,0:T(8,128)S(1)}, f32[392,112]{1,0:T(8,128)}, u32[]{:S(2)}) copy-start(f32[392,112]{1,0:T(8,128)} %constant.69.clone) | copy-start | bytes 526852
  100.5 16.4 %all-to-all-start.3 = ((f32[32,4,640]{2,1,0:T(4,128)}), f32[32,4,640]{2,1,0:T(4,128)S(1)}, u32[]{:S(2)}, u32[]{:S(2)}) async-start(f32[32,4,640]{2,1,0:T(4,128)} %get-tuple-element.145), calls=%async_computation.3 | async-start | bytes 655360 | tf_op jit(solution)/shard_map/all_to_all | solution.py:49
  123.4 12.4 %collective-permute-start.7 = (bf16[112,1024]{1,0:T(8,128)(2,1)}, bf16[112,1024]{1,0:T(8,128)(2,1)S(1)}, u32[]{:S(2)}, u32[]{:S(2)}) collective-permute-start(bf16[112,1024]{1,0:T(8,128)(2,1)} %get-tuple-element.156), channel_id=1, source_target_pairs={{0,1},{1,0},{2,3},{3,2},{4,5},{5,4},{6,7},{7,6},{8,9},{9,8},{10,11... | collective-permute-start | bytes 688136 | tf_op jit(solution)/shard_map/ppermute | solution.py:884
  125.2 19.5 %collective-permute-start.8 = (bf16[112,1024]{1,0:T(8,128)(2,1)}, bf16[112,1024]{1,0:T(8,128)(2,1)S(1)}, u32[]{:S(2)}, u32[]{:S(2)}) collective-permute-start(bf16[112,1024]{1,0:T(8,128)(2,1)} %get-tuple-element.157), channel_id=1, source_target_pairs={{0,2},{1,3},{2,0},{3,1},{4,6},{5,7},{6,4},{7,5},{8,10},{9,11},{10,... | collective-permute-start | bytes 688136 | tf_op jit(solution)/shard_map/ppermute | solution.py:884
  126.2 18.5 %collective-permute-start.9 = (bf16[112,1024]{1,0:T(8,128)(2,1)}, bf16[112,1024]{1,0:T(8,128)(2,1)S(1)}, u32[]{:S(2)}, u32[]{:S(2)}) collective-permute-start(bf16[112,1024]{1,0:T(8,128)(2,1)} %get-tuple-element.158), channel_id=1, source_target_pairs={{0,3},{1,2},{2,1},{3,0},{4,7},{5,6},{6,5},{7,4},{8,11},{9,10},{10,... | collective-permute-start | bytes 688136 | tf_op jit(solution)/shard_map/ppermute | solution.py:884
  152.1 15.1 %all-to-all-start.5 = ((f32[32,8,256]{2,1,0:T(8,128)}), f32[32,8,256]{2,1,0:T(8,128)S(1)}, u32[]{:S(2)}, u32[]{:S(2)}) async-start(f32[32,8,256]{2,1,0:T(8,128)} %get-tuple-element.159), calls=%async_computation.5 | async-start | bytes 524288 | tf_op jit(solution)/shard_map/all_to_all | solution.py:49
  167.1 4.6 %collective-permute-start.10 = (bf16[4,2048,128]{2,1,0:T(8,128)(2,1)}, bf16[4,2048,128]{2,1,0:T(8,128)(2,1)S(1)}, u32[]{:S(2)}, u32[]{:S(2)}) collective-permute-start(bf16[4,2048,128]{2,1,0:T(8,128)(2,1)} %get-tuple-element.169), channel_id=1, source_target_pairs={{0,4},{4,0},{8,12},{12,8},{16,20},{20,16},{24,28},{28,24},{1,5},{5... | collective-permute-start | bytes 6291464 | tf_op jit(solution)/shard_map/ppermute | solution.py:633
  171.7 10.2 %all-to-all-start.6 = ((f32[32,2,256]{2,1,0:T(2,128)}), f32[32,2,256]{2,1,0:T(2,128)S(1)}, u32[]{:S(2)}, u32[]{:S(2)}) async-start(f32[32,2,256]{2,1,0:T(2,128)} %get-tuple-element.170), calls=%async_computation.6 | async-start | bytes 131072 | tf_op jit(solution)/shard_map/all_to_all | solution.py:49
  182.0 19.9 %collective-permute-start.11 = (bf16[2,1024,128]{2,1,0:T(8,128)(2,1)}, bf16[2,1024,128]{2,1,0:T(8,128)(2,1)S(1)}, u32[]{:S(2)}, u32[]{:S(2)}) collective-permute-start(bf16[2,1024,128]{2,1,0:T(8,128)(2,1)} %get-tuple-element.187), channel_id=1, source_target_pairs={{0,8},{4,12},{8,0},{12,4},{16,24},{20,28},{24,16},{28,20},{1,9},{5... | collective-permute-start | bytes 1572872 | tf_op jit(solution)/shard_map/ppermute | solution.py:651
  182.9 19.0 %collective-permute-start.12 = (bf16[2,1024,128]{2,1,0:T(8,128)(2,1)}, bf16[2,1024,128]{2,1,0:T(8,128)(2,1)S(1)}, u32[]{:S(2)}, u32[]{:S(2)}) collective-permute-start(bf16[2,1024,128]{2,1,0:T(8,128)(2,1)} %get-tuple-element.188), channel_id=1, source_target_pairs={{0,16},{4,20},{8,24},{12,28},{16,0},{20,4},{24,8},{28,12},{1,17},{... | collective-permute-start | bytes 1572872 | tf_op jit(solution)/shard_map/ppermute | solution.py:651
  188.6 13.2 %all-to-all-start.7 = ((f32[32,2,256]{2,1,0:T(2,128)}), f32[32,2,256]{2,1,0:T(2,128)S(1)}, u32[]{:S(2)}, u32[]{:S(2)}) async-start(f32[32,2,256]{2,1,0:T(2,128)} %get-tuple-element.182), calls=%async_computation.7 | async-start | bytes 131072 | tf_op jit(solution)/shard_map/all_to_all | solution.py:49
  192.4 9.5 %collective-permute-start.13 = (bf16[196,256]{1,0:T(8,128)(2,1)}, bf16[196,256]{1,0:T(8,128)(2,1)S(1)}, u32[]{:S(2)}, u32[]{:S(2)}) collective-permute-start(bf16[196,256]{1,0:T(8,128)(2,1)} %get-tuple-element.191), channel_id=1, source_target_pairs={{0,1},{1,2},{2,3},{4,5},{5,6},{6,7},{8,9},{9,10},{10,11},{12,13},{... | collective-permute-start | bytes 301064 | tf_op jit(solution)/shard_map/ppermute | solution.py:947
  196.1 6.8 %collective-permute-start.14 = (bf16[196,256]{1,0:T(8,128)(2,1)}, bf16[196,256]{1,0:T(8,128)(2,1)S(1)}, u32[]{:S(2)}, u32[]{:S(2)}) collective-permute-start(bf16[196,256]{1,0:T(8,128)(2,1)} %get-tuple-element.192), channel_id=1, source_target_pairs={{1,0},{2,1},{3,2},{5,4},{6,5},{7,6},{9,8},{10,9},{11,10},{13,12},{... | collective-permute-start | bytes 301064 | tf_op jit(solution)/shard_map/ppermute | solution.py:948
  211.7 5.7 %collective-permute-start.15 = (bf16[4,1664,128]{2,1,0:T(8,128)(2,1)}, bf16[4,1664,128]{2,1,0:T(8,128)(2,1)S(1)}, u32[]{:S(2)}, u32[]{:S(2)}) collective-permute-start(bf16[4,1664,128]{2,1,0:T(8,128)(2,1)} %get-tuple-element.200), channel_id=1, source_target_pairs={{0,4},{4,0},{8,12},{12,8},{16,20},{20,16},{24,28},{28,24},{1,5},{5... | collective-permute-start | bytes 5111816 | tf_op jit(solution)/shard_map/ppermute | solution.py:633
  214.5 8.9 %collective-permute-start.18 = (bf16[1,1024,128]{2,1,0:T(8,128)(2,1)}, bf16[1,1024,128]{2,1,0:T(8,128)(2,1)S(1)}, u32[]{:S(2)}, u32[]{:S(2)}) collective-permute-start(bf16[1,1024,128]{2,1,0:T(8,128)(2,1)} %get-tuple-element.213), channel_id=1, source_target_pairs={{0,16},{4,20},{8,24},{12,28},{16,0},{20,4},{24,8},{28,12},{1,17},{... | collective-permute-start | bytes 786440 | tf_op jit(solution)/shard_map/ppermute | solution.py:651
  215.9 8.6 %collective-permute-start.19 = (bf16[1,1024,128]{2,1,0:T(8,128)(2,1)}, bf16[1,1024,128]{2,1,0:T(8,128)(2,1)S(1)}, u32[]{:S(2)}, u32[]{:S(2)}) collective-permute-start(bf16[1,1024,128]{2,1,0:T(8,128)(2,1)} %get-tuple-element.215), channel_id=1, source_target_pairs={{0,8},{4,12},{8,0},{12,4},{16,24},{20,28},{24,16},{28,20},{1,9},{5... | collective-permute-start | bytes 786440 | tf_op jit(solution)/shard_map/ppermute | solution.py:651
  222.2 11.9 %collective-permute-start.16 = (bf16[2,832,128]{2,1,0:T(8,128)(2,1)}, bf16[2,832,128]{2,1,0:T(8,128)(2,1)S(1)}, u32[]{:S(2)}, u32[]{:S(2)}) collective-permute-start(bf16[2,832,128]{2,1,0:T(8,128)(2,1)} %get-tuple-element.202), channel_id=1, source_target_pairs={{0,8},{4,12},{8,0},{12,4},{16,24},{20,28},{24,16},{28,20},{1,9},{5... | collective-permute-start | bytes 1277960 | tf_op jit(solution)/shard_map/ppermute | solution.py:651
  222.7 11.6 %collective-permute-start.17 = (bf16[2,832,128]{2,1,0:T(8,128)(2,1)}, bf16[2,832,128]{2,1,0:T(8,128)(2,1)S(1)}, u32[]{:S(2)}, u32[]{:S(2)}) collective-permute-start(bf16[2,832,128]{2,1,0:T(8,128)(2,1)} %get-tuple-element.204), channel_id=1, source_target_pairs={{0,16},{4,20},{8,24},{12,28},{16,0},{20,4},{24,8},{28,12},{1,17},{... | collective-permute-start | bytes 1277960 | tf_op jit(solution)/shard_map/ppermute | solution.py:651
  224.7 12.8 %collective-permute-start.20 = (bf16[1,1024,128]{2,1,0:T(8,128)(2,1)S(1)}, bf16[1,1024,128]{2,1,0:T(8,128)(2,1)S(1)}, u32[]{:S(2)}, u32[]{:S(2)}) collective-permute-start(bf16[1,1024,128]{2,1,0:T(8,128)(2,1)S(1)} %select_convert_fusion.1), channel_id=1, source_target_pairs={{0,1},{1,0},{2,3},{3,2},{4,5},{5,4},{6,7},{7,6},{8,9},{9,8},{10,11... | collective-permute-start | bytes 786440 | tf_op jit(solution)/shard_map/ppermute | solution.py:685
  237.5 6.4 %collective-permute-start.21 = (bf16[1,832,128]{2,1,0:T(8,128)(2,1)}, bf16[1,832,128]{2,1,0:T(8,128)(2,1)S(1)}, u32[]{:S(2)}, u32[]{:S(2)}) collective-permute-start(bf16[1,832,128]{2,1,0:T(8,128)(2,1)} %get-tuple-element.218), channel_id=1, source_target_pairs={{0,8},{4,12},{8,0},{12,4},{16,24},{20,28},{24,16},{28,20},{1,9},{5... | collective-permute-start | bytes 638984 | tf_op jit(solution)/shard_map/ppermute | solution.py:651
  239.1 6.2 %collective-permute-start.22 = (bf16[1,832,128]{2,1,0:T(8,128)(2,1)}, bf16[1,832,128]{2,1,0:T(8,128)(2,1)S(1)}, u32[]{:S(2)}, u32[]{:S(2)}) collective-permute-start(bf16[1,832,128]{2,1,0:T(8,128)(2,1)} %get-tuple-element.220), channel_id=1, source_target_pairs={{0,16},{4,20},{8,24},{12,28},{16,0},{20,4},{24,8},{28,12},{1,17},{... | collective-permute-start | bytes 638984 | tf_op jit(solution)/shard_map/ppermute | solution.py:651
  239.8 13.6 %collective-permute-start.24 = (bf16[1,1024,128]{2,1,0:T(8,128)(2,1)S(1)}, bf16[1,1024,128]{2,1,0:T(8,128)(2,1)S(1)}, u32[]{:S(2)}, u32[]{:S(2)}) collective-permute-start(bf16[1,1024,128]{2,1,0:T(8,128)(2,1)S(1)} %add_convert_fusion.2), channel_id=1, source_target_pairs={{0,2},{1,3},{2,0},{3,1},{4,6},{5,7},{6,4},{7,5},{8,10},{9,11},{10,... | collective-permute-start | bytes 786440 | tf_op jit(solution)/shard_map/ppermute | solution.py:698
  245.4 24.8 %copy-start.2 = (f32[392,1024]{1,0:T(8,128)S(1)}, f32[392,1024]{1,0:T(8,128)}, u32[]{:S(2)}) copy-start(f32[392,1024]{1,0:T(8,128)} %get-tuple-element.144.refs_7_) | copy-start | bytes 4816900
  245.4 24.8 %copy-start.16 = (bf16[392,1024]{1,0:T(8,128)(2,1)S(1)}, bf16[392,1024]{1,0:T(8,128)(2,1)}, u32[]{:S(2)}) copy-start(bf16[392,1024]{1,0:T(8,128)(2,1)} %get-tuple-element.142.unit) | copy-start | bytes 2408452
  245.4 24.8 %copy-start.41 = (f32[1024]{0:T(1024)S(1)}, f32[1024]{0:T(1024)}, u32[]{:S(2)}) copy-start(f32[1024]{0:T(1024)} %param.41) | copy-start | bytes 12292
  245.5 24.8 %copy-start.42 = (f32[1024]{0:T(1024)S(1)}, f32[1024]{0:T(1024)}, u32[]{:S(2)}) copy-start(f32[1024]{0:T(1024)} %param.42) | copy-start | bytes 12292
  245.5 24.8 %copy-start.43 = (f32[1,1024]{1,0:T(1,128)S(1)}, f32[1,1024]{1,0:T(1,128)}, u32[]{:S(2)}) copy-start(f32[1,1024]{1,0:T(1,128)} %get-tuple-element.148) | copy-start | bytes 12292
  245.5 24.8 %copy-start.44 = (f32[1,1024]{1,0:T(1,128)S(1)}, f32[1,1024]{1,0:T(1,128)}, u32[]{:S(2)}) copy-start(f32[1,1024]{1,0:T(1,128)} %get-tuple-element.149) | copy-start | bytes 12292
  245.5 10.2 %collective-permute-start.23 = (bf16[1,832,128]{2,1,0:T(8,128)(2,1)S(1)}, bf16[1,832,128]{2,1,0:T(8,128)(2,1)S(1)}, u32[]{:S(2)}, u32[]{:S(2)}) collective-permute-start(bf16[1,832,128]{2,1,0:T(8,128)(2,1)S(1)} %select_convert_fusion.2), channel_id=1, source_target_pairs={{0,1},{1,0},{2,3},{3,2},{4,5},{5,4},{6,7},{7,6},{8,9},{9,8},{10,11... | collective-permute-start | bytes 638984 | tf_op jit(solution)/shard_map/ppermute | solution.py:685
  255.7 11.0 %collective-permute-start.26 = (bf16[1,1024,128]{2,1,0:T(8,128)(2,1)S(1)}, bf16[1,1024,128]{2,1,0:T(8,128)(2,1)S(1)}, u32[]{:S(2)}, u32[]{:S(2)}) collective-permute-start(bf16[1,1024,128]{2,1,0:T(8,128)(2,1)S(1)} %add_convert_fusion.1.refs_1_), channel_id=1, source_target_pairs={{0,1},{1,0},{2,3},{3,2},{4,5},{5,4},{6,7},{7,6},{8,9},{9,8},{10,11... | collective-permute-start | bytes 786440 | tf_op jit(solution)/shard_map/ppermute | solution.py:709
  256.0 10.7 %collective-permute-start.25 = (bf16[1,832,128]{2,1,0:T(8,128)(2,1)S(1)}, bf16[1,832,128]{2,1,0:T(8,128)(2,1)S(1)}, u32[]{:S(2)}, u32[]{:S(2)}) collective-permute-start(bf16[1,832,128]{2,1,0:T(8,128)(2,1)S(1)} %add_convert_fusion.4), channel_id=1, source_target_pairs={{0,2},{1,3},{2,0},{3,1},{4,6},{5,7},{6,4},{7,5},{8,10},{9,11},{10,... | collective-permute-start | bytes 638984 | tf_op jit(solution)/shard_map/ppermute | solution.py:698
  266.8 7.2 %collective-permute-start.27 = (bf16[1,832,128]{2,1,0:T(8,128)(2,1)S(1)}, bf16[1,832,128]{2,1,0:T(8,128)(2,1)S(1)}, u32[]{:S(2)}, u32[]{:S(2)}) collective-permute-start(bf16[1,832,128]{2,1,0:T(8,128)(2,1)S(1)} %add_convert_fusion.3.refs_1_), channel_id=1, source_target_pairs={{0,1},{1,0},{2,3},{3,2},{4,5},{5,4},{6,7},{7,6},{8,9},{9,8},{10,11... | collective-permute-start | bytes 638984 | tf_op jit(solution)/shard_map/ppermute | solution.py:709
  (38 other events, 193.2 us)

commit v4 on v3

--- a/solution.py
+++ b/solution.py
@@ -56,51 +56,17 @@
     return lax.optimization_barrier((wanted,) + others)
 
 
-class Stack:
-    def __init__(self, arrays):
-        self.arrays = arrays
-
-
-def call(kernel, outs, scalars, *operands, scratch=(), flops=0):
+def call(kernel, outs, scalars, *arrays, scratch=(), flops=0):
     shapes = [jax.ShapeDtypeStruct(shape, kind) for shape, kind in outs]
-    arrays, plan, stacks = [], [], []
-    for operand in operands:
-        if isinstance(operand, Stack):
-            plan.append((len(arrays), len(operand.arrays)))
-            arrays += operand.arrays
-            one = operand.arrays[0]
-            stacks.append(pltpu.VMEM((len(operand.arrays) * one.shape[0],) + one.shape[1:], one.dtype))
-        else:
-            plan.append((len(arrays), 0))
-            arrays.append(operand)
-    count_s, count_a = len(scalars), len(arrays)
-
-    def body(*refs):
-        scalar_refs, refs = refs[:count_s], refs[count_s:]
-        in_refs, refs = refs[:count_a], refs[count_a:]
-        out_refs, refs = refs[: len(shapes)], refs[len(shapes) :]
-        user, stack_refs = refs[: len(scratch)], list(refs[len(scratch) :])
-        seen = []
-        for first, count in plan:
-            if count == 0:
-                seen.append(in_refs[first])
-                continue
-            stack = stack_refs.pop(0)
-            size = in_refs[first].shape[0]
-            for k in range(count):
-                stack[k * size : (k + 1) * size, :] = in_refs[first + k][...]
-            seen.append(stack)
-        kernel(*scalar_refs, *seen, *out_refs, *user)
-
     moved = sum(int(np.prod(s.shape)) * s.dtype.itemsize for s in shapes)
     moved += sum(a.size * a.dtype.itemsize for a in arrays)
     near = pl.BlockSpec(memory_space=pltpu.VMEM)
     return pl.pallas_call(
-        body,
+        kernel,
         out_shape=shapes,
-        in_specs=[pl.BlockSpec(memory_space=pltpu.SMEM)] * count_s + [near] * count_a,
+        in_specs=[pl.BlockSpec(memory_space=pltpu.SMEM)] * len(scalars) + [near] * len(arrays),
         out_specs=[near] * len(shapes),
-        scratch_shapes=list(scratch) + stacks,
+        scratch_shapes=list(scratch),
         compiler_params=pltpu.CompilerParams(vmem_limit_bytes=VMEM_BYTES),
         cost_estimate=pl.CostEstimate(flops=flops, bytes_accessed=moved, transcendentals=0),
     )(*scalars, *arrays)
@@ -161,6 +127,15 @@
     d_spread = -0.5 * gain * gain_grad * inv * inv
     d_mean = -gain * shift_grad * inv - 2.0 * mean * d_spread
     return gain * inv, d_mean / total, 2.0 * d_spread / total
+
+
+def pack_rows(value, rows, packed):
+    for k, c in enumerate(chunks(value.shape[1])):
+        packed[k * rows : (k + 1) * rows, :] = value[0:rows, c]
+
+
+def unpack_rows(packed, rows, size, k):
+    return packed[k * rows : k * rows + size, :]
 
 
 def border_kernel(x, w, tap_0, tap_2, up, down):
@@ -245,7 +220,7 @@
         emit(copies, width + c.start, column_sum(hidden * hidden * valid))
 
 
-def unit_kernel(sc, copies_in, w_expand, gain, shift, pre_3, x, pool, counts, w_key, w_value, unit, pooled, kv, stats):
+def unit_kernel(keys, sc, copies_in, w_expand, gain, shift, pre_3, x, pool, counts, w_key, w_value, unit, pooled, kv, stats, packed):
     total = sc[0]
     narrow, channels = w_expand.shape
     sums = collect(copies_in)
@@ -267,12 +242,21 @@
     for k, w in enumerate((w_key, w_value)):
         for c in chunks(inner, 2 * LANE):
             both = dot(pooled[...], w[:, c])
-            to = slice(k * inner + c.start, k * inner + c.stop)
-            kv[:, to] = ((both[:blocks] + both[blocks:]) / many).astype(BF16)
-
-
-def attend_kernel(sc, theta, kv, place, key_row, w, cot, probs, attended, pre_4, copies):
+            start = (k * inner + c.start) // LANE * keys
+            pack_rows((both[:blocks] + both[blocks:]) / many, keys, packed.at[start : start + 2 * keys])
+    kv[...] = packed[...].astype(BF16)
+
+
+def attend_kernel(slots, keys, sc, theta, place, key_row, w, cot, *refs):
+    blocks = refs[:slots]
+    kv, probs, attended, pre_4, copies, packed = refs[slots:]
     inner, channels = w.shape
+    size, lines = kv.shape[0] // slots, blocks[0].shape[0]
+    packed[lines:, :] = jnp.zeros((packed.shape[0] - lines, LANE), F32)
+    for k in range(slots):
+        packed[0:lines, :] = blocks[k][...].astype(F32)
+        for j, c in enumerate(chunks(2 * inner)):
+            kv[k * size : (k + 1) * size, c] = unpack_rows(packed, keys, size, j).astype(BF16)
     logits = dot_cols(theta[...], kv[:, 0:inner])
     allowed = place[:, 3:4] == key_row[0:1, :]
     scores = jnp.where(allowed, logits * TEMPER, key_row[1:2, :])
@@ -289,7 +273,8 @@
         emit(copies, inner + channels + c.start, column_sum(cot[:, c].astype(F32) * hidden))
 
 
-def attend_back_kernel(slots, sc, copies_in, shift_copies, gain, place, key_row, w, pre_4, cot, kv, probs, theta, d_final, d_logits, mean_out, inv_out, gain_out, shift_out, own, *sent):
+def attend_back_kernel(slots, keys, sc, copies_in, shift_copies, gain, place, key_row, w, pre_4, cot, kv, probs, theta, d_final, d_logits, mean_out, inv_out, gain_out, shift_out, own, *refs):
+    sent, packed = refs[:-1], refs[-1]
     total = sc[0]
     inner, channels = w.shape
     size = own.shape[0]
@@ -323,22 +308,28 @@
     own[:, inner:] = d_values[0:size]
     for k in range(1, slots):
         here = slice(k * size, (k + 1) * size)
-        sent[k - 1][:, 0:inner] = d_keys[here].astype(BF16)
-        sent[k - 1][:, inner:] = d_values[here].astype(BF16)
-
-
-def summed_back_kernel(slots, sc, own, counts, w_key, w_value, stats_3, gain, shift, spread, d_unit_part, pre_3, x, *refs):
+        half = inner // LANE * keys
+        pack_rows(d_keys[here], keys, packed.at[0:half])
+        pack_rows(d_values[here], keys, packed.at[half : 2 * half])
+        sent[k - 1][...] = packed[...].astype(BF16)
+
+
+def summed_back_kernel(slots, keys, sc, own, counts, w_key, w_value, stats_3, gain, shift, spread, d_unit_part, pre_3, x, *refs):
     received = refs[: slots - 1]
-    d_pooled, d_summed, copies, stacked = refs[slots - 1 :]
+    d_pooled, d_summed, copies, stacked, packed, low = refs[slots - 1 :]
     size, inner = own.shape[0], w_key.shape[1]
     channels = x.shape[1]
     many = jnp.maximum(counts[:, 0:1], 1.0)
-    whole = own[...]
-    for other in received:
-        whole = whole + other[...].astype(F32)
-    low = (whole / many).astype(BF16)
-    d_pooled[0:size, :] = low
-    d_pooled[size : 2 * size, :] = low
+    lines = received[0].shape[0]
+    others = received[0][...].astype(F32)
+    for other in received[1:]:
+        others = others + other[...].astype(F32)
+    packed[0:lines, :] = others
+    packed[lines:, :] = jnp.zeros((packed.shape[0] - lines, LANE), F32)
+    for k, c in enumerate(chunks(2 * inner)):
+        low[:, c] = ((own[:, c] + unpack_rows(packed, keys, size, k)) / many).astype(BF16)
+    d_pooled[0:size, :] = low[...]
+    d_pooled[size : 2 * size, :] = low[...]
     mean, inv = stats_3[0:1, :], stats_3[1:2, :]
     for c in chunks(channels, 2 * LANE):
         here = dot_cols(low[:, 0:inner], w_key[c, :]) + dot_cols(low[:, inner:], w_value[c, :])
@@ -470,14 +461,9 @@
     sent.wait()
 
 
-def attend_grads_kernel(slots, parts, start, bits, d_logits, cot, w, attended, d_final, unit, *refs):
-    blocks = refs[:slots]
-    send, keep, d_unit_part, d_theta, both, low, sems, keys = refs[slots:]
-    size = blocks[0].shape[0]
+def attend_grads_kernel(parts, start, bits, d_logits, cot, w, attended, d_final, unit, kv, send, keep, d_unit_part, d_theta, both, low, sems):
     inner, channels = attended.shape[1], unit.shape[1]
-    for k in range(slots):
-        keys[k * size : (k + 1) * size, :] = blocks[k][:, 0:inner]
-    d_theta[...] = dot(d_logits[...], keys[...]).astype(BF16)
+    d_theta[...] = dot(d_logits[...], kv[:, 0:inner]).astype(BF16)
     for c in chunks(channels, 2 * LANE):
         d_unit_part[:, c] = cot[:, c].astype(F32) + dot_cols(d_theta[...], w[c, :])
     wide = channels // parts
@@ -844,11 +830,14 @@
         flops=2 * rows * narrow * channels,
     )
     sums = trade(sums)
+    lines = own_keys * 2 * inner // LANE
+    packed_bf16 = ((lines, LANE), BF16)
     unit, pooled, kv_own, stats_3 = call(
-        unit_kernel,
-        [wide_bf16, ((2 * size, channels), BF16), ((size, 2 * inner), BF16), ((2, channels), F32)],
+        functools.partial(unit_kernel, own_keys),
+        [wide_bf16, ((2 * size, channels), BF16), packed_bf16, ((2, channels), F32)],
         (scalars,), sums, expand_weight, gain_3, shift_3, pre_3, inputs, pool, counts,
         key_weight, value_weight,
+        scratch=[pltpu.VMEM((lines, LANE), F32)],
         flops=2 * size * channels * (rows + 4 * inner),
     )
     shift_sums, _ = tie(shift_sums, kv_own)
@@ -857,27 +846,29 @@
         lax.ppermute(kv_own, "grp", flip(grp_count, step)) for step in range(1, grp_count)
     ]
     theta = dot(unit, query_weight).astype(BF16)
-    probs, attended, pre_4, sums = call(
-        attend_kernel,
+    kv_all, probs, attended, pre_4, sums = call(
+        functools.partial(attend_kernel, grp_count, own_keys),
         [
-            ((rows, grp_count * size), F32), ((rows, inner), BF16), wide_f32,
+            ((grp_count * size, 2 * inner), BF16), ((rows, grp_count * size), F32), ((rows, inner), BF16), wide_f32,
             ((copies, 4, (inner + 2 * channels) // 4), F32),
         ],
-        (scalars,), theta, Stack(kv), place, key_row, out_weight, cotangent,
+        (scalars,), theta, place, key_row, out_weight, cotangent, *kv,
+        scratch=[pltpu.VMEM((lines + 16, LANE), F32)],
         flops=2 * rows * inner * (2 * grp_count * size + channels),
     )
     sums = trade(sums)
 
     d_final, d_logits, mean_4, inv_4, gain_final_grad, shift_final_grad, d_kv, *d_sent = call(
-        functools.partial(attend_back_kernel, grp_count),
+        functools.partial(attend_back_kernel, grp_count, own_keys),
         [
             wide_bf16, ((rows, grp_count * size), BF16),
         ]
         + [((1, channels), F32)] * 4
         + [((size, 2 * inner), F32)]
-        + [((size, 2 * inner), BF16)] * (grp_count - 1),
+        + [packed_bf16] * (grp_count - 1),
         (scalars,), sums, shift_sums, gain_4, place, key_row, out_weight, pre_4,
-        cotangent, Stack(kv), probs, theta,
+        cotangent, kv_all, probs, theta,
+        scratch=[pltpu.VMEM((lines, LANE), F32)],
         flops=2 * rows * inner * (3 * grp_count * size + channels),
     )
     d_received = [
@@ -891,18 +882,20 @@
     half = deep * inner // LANE
     bundle_1 = Bundle(bits, 2 * half)
     d_unit_part, _ = bundle_1.add(
-        functools.partial(attend_grads_kernel, grp_count), 0, 2 * half,
-        d_logits, cotangent, query_weight, attended, d_final, unit, *kv,
+        attend_grads_kernel, 0, 2 * half,
+        d_logits, cotangent, query_weight, attended, d_final, unit, kv_all,
         extra=[wide_f32, ((rows, inner), BF16)],
-        scratch=[pltpu.VMEM((grp_count * size, inner), BF16)],
         flops=2 * rows * inner * (grp_count * size + 3 * channels),
     )
     d_pooled, d_summed, sums = call(
-        functools.partial(summed_back_kernel, grp_count),
+        functools.partial(summed_back_kernel, grp_count, own_keys),
         [((2 * size, 2 * inner), BF16), wide_f32, ((copies, 8, channels // 4), F32)],
         (scalars,), d_kv, counts, key_weight, value_weight, stats_3, gain_3,
         shift_3, spread, d_unit_part, pre_3, inputs, *d_received,
-        scratch=[pltpu.VMEM((2 * size, channels), BF16)],
+        scratch=[
+            pltpu.VMEM((2 * size, channels), BF16), pltpu.VMEM((lines + 16, LANE), F32),
+            pltpu.VMEM((size, 2 * inner), BF16),
+        ],
         flops=4 * size * channels * (inner + rows),
     )
     sums = trade(sums)

time: 278 us -> 273 us (0.982)
  waiting for transfers between devices: 81.6 us -> 77.9 us
  transfers between devices with their start and end apart: 36 -> 36, of which waited for: 22 -> 21; matrix products, arithmetic and copies ran while one was open for 6% -> 6% of each run, Pallas kernels for 18% -> 18%
where the time goes in v4:
time: 273 us; the launch traced here: 272 us
  Pallas kernels  85.3 us (31%)
  starting transfers between devices  81.4 us (30%)
  waiting for transfers between devices  77.9 us (29%)
  local copies, waits for them, and re-layouts  14.3 us (5%)
  other arithmetic  6.74 us (2%)
  matrix products  4.64 us (2%)
    pallas_call x17, Pallas kernels, call(): pl.pallas_call(kernel, out_shape=shapes, in_specs=[pl.BlockSpec(memory_sp...  65 us
    all_to_all x8, waiting for transfers between devices, trade(): return lax.all_to_all(copies, ('pos', 'grp'), 0, 0, tiled=True)  33.8 us
    all_to_all x8, starting transfers between devices, trade(): return lax.all_to_all(copies, ('pos', 'grp'), 0, 0, tiled=True)  32.3 us
    pallas_call x5, Pallas kernels, add(): pl.pallas_call(functools.partial(kernel, self.pos_count, start), out_shap...  20.2 us
    ppermute x2, waiting for transfers between devices, exchange(): lax.ppermute(self.low, 'grp', flip(self.grp_count, self.grp_count // 2))  11.8 us
    ppermute x8, waiting for transfers between devices, turn(): self.parts[k].append(lax.ppermute(self.parts[k][0], 'pos', pairs))  11.6 us
    unnamed x100, local copies, waits for them, and re-layouts  9.15 us
    ppermute x3, waiting for transfers between devices, local(): lax.ppermute(kv_own, 'grp', flip(grp_count, step))  8.89 us
  transfers between devices with their start and end apart: 36, of which 21 were waited for; matrix products, arithmetic and copies ran while one was open for 6% of the time, Pallas kernels for 18%

profile of v4, /device:TPU:0, one launch (start us, length us, event | category | flops | bytes accessed | tf_op | source)
XLA Modules:
  0.0 271.6 jit_solution(15687390659200196477)
XLA Ops:
  0.7 3.3 %shard_map.368 = (f32[392,256]{1,0:T(8,128)}, f32[392,256]{1,0:T(8,128)}, f32[196,256]{1,0:T(8,128)}, f32[196,256]{1,0:T(8,128)}) custom-call(bf16[392,1024]{1,0:T(8,128)(2,1)} %x.11, bf16[3,1024,256]{2,1,0:T(8,128)(2,1)} %w.15), custom_call_target="tpu_custom_call" | custom-call | flops 411041792 | bytes 3579904 | tf_op jit(solution)/shard_map/pallas_call | solution.py:64
  4.0 4.9 %collective-permute-start = (f32[196,256]{1,0:T(8,128)}, f32[196,256]{1,0:T(8,128)S(1)}, u32[]{:S(2)}, u32[]{:S(2)}) collective-permute-start(f32[196,256]{1,0:T(8,128)} %get-tuple-element.132), channel_id=1, source_target_pairs={{0,1},{1,2},{2,3},{4,5},{5,6},{6,7},{8,9},{9,10},{10,11},{12,13},{... | collective-permute-start | bytes 602120 | tf_op jit(solution)/shard_map/ppermute | solution.py:802
  10.2 2.2 fusion.tap_1
  18.3 2.5 shard_map.369
  20.8 5.8 %all-to-all-start = ((f32[32,2,256]{2,1,0:T(2,128)}), f32[32,2,256]{2,1,0:T(2,128)S(1)}, u32[]{:S(2)}, u32[]{:S(2)}) async-start(f32[32,2,256]{2,1,0:T(2,128)} %get-tuple-element.134), calls=%async_computation | async-start | bytes 131072 | tf_op jit(solution)/shard_map/all_to_all | solution.py:49
  28.0 3.7 %collective-permute-start.2 = (bf16[196,256]{1,0:T(8,128)(2,1)}, bf16[196,256]{1,0:T(8,128)(2,1)S(1)}, u32[]{:S(2)}, u32[]{:S(2)}) collective-permute-start(bf16[196,256]{1,0:T(8,128)(2,1)} %get-tuple-element.137), channel_id=1, source_target_pairs={{0,1},{1,2},{2,3},{4,5},{5,6},{6,7},{8,9},{9,10},{10,11},{12,13},{... | collective-permute-start | bytes 301064 | tf_op jit(solution)/shard_map/ppermute | solution.py:811
  34.7 4.9 %shard_map.370 = (f32[392,256]{1,0:T(8,128)}, bf16[392,2304]{1,0:T(8,128)(2,1)}, f32[32,2,256]{2,1,0:T(2,128)}, f32[2,256]{1,0:T(2,128)}) custom-call(f32[5]{0:T(128)} %pad_maximum_fusion.3.sc, f32[32,2,256]{2,1,0:T(2,128)} %copy-done.23, f32[392,256]{1,0:T(8,128)} %get-tuple-element.135.pre_1, f32[1,256]{1,0:T(1,128)} %bitcast.45, f32[1,256]{1,0:T(1,128)} %bitcast.51, ...), custom_call_target="tpu_custom_call" | custom-call | flops 462422016 | bytes 3930240 | tf_op jit(solution)/shard_map/pallas_call | solution.py:64
  39.7 5.6 %all-to-all-start.1 = ((f32[32,2,256]{2,1,0:T(2,128)}), f32[32,2,256]{2,1,0:T(2,128)S(1)}, u32[]{:S(2)}, u32[]{:S(2)}) async-start(f32[32,2,256]{2,1,0:T(2,128)} %get-tuple-element.136), calls=%async_computation.1 | async-start | bytes 131072 | tf_op jit(solution)/shard_map/all_to_all | solution.py:49
  45.5 7.3 %all-to-all-done.1.copies_in = f32[32,2,256]{2,1,0:T(2,128)S(1)} async-done(((f32[32,2,256]{2,1,0:T(2,128)}), f32[32,2,256]{2,1,0:T(2,128)S(1)}, u32[]{:S(2)}, u32[]{:S(2)}) %all-to-all-start.1) | async-done | bytes 65568 | tf_op jit(solution)/shard_map/all_to_all | solution.py:49
  53.4 3.0 %shard_map.371 = (bf16[392,256]{1,0:T(8,128)(2,1)}, f32[392,1024]{1,0:T(8,128)}, f32[32,2,640]{2,1,0:T(2,128)}, f32[2,256]{1,0:T(2,128)}) custom-call(f32[5]{0:T(128)} %pad_maximum_fusion.3.sc, f32[32,2,256]{2,1,0:T(2,128)} %copy-done.24, f32[392,256]{1,0:T(8,128)} %get-tuple-element.140.pre_2, f32[1,256]{1,0:T(1,128)} %bitcast.48, f32[1,256]{1,0:T(1,128)} %bitcast.57, ...), custom_call_target="tpu_custom_call" | custom-call | flops 205520896 | bytes 2971776 | tf_op jit(solution)/shard_map/pallas_call | solution.py:64
  56.4 2.6 all-to-all-start.2
  60.2 7.6 %all-to-all-done.2.copies_in = f32[32,2,640]{2,1,0:T(2,128)S(1)} async-done(((f32[32,2,640]{2,1,0:T(2,128)}), f32[32,2,640]{2,1,0:T(2,128)S(1)}, u32[]{:S(2)}, u32[]{:S(2)}) %all-to-all-start.2) | async-done | bytes 163872 | tf_op jit(solution)/shard_map/all_to_all | solution.py:49
  68.5 4.8 %shard_map.372 = (bf16[392,1024]{1,0:T(8,128)(2,1)}, bf16[224,1024]{1,0:T(8,128)(2,1)}, bf16[784,128]{1,0:T(8,128)(2,1)}, f32[2,1024]{1,0:T(2,128)}) custom-call(f32[5]{0:T(128)} %pad_maximum_fusion.3.sc, f32[32,2,640]{2,1,0:T(2,128)} %copy-done.14, bf16[256,1024]{1,0:T(8,128)(2,1)} %w.13, f32[1,1024]{1,0:T(1,128)} %bitcast.38, f32[1,1024]{1,0:T(1,128)} %bitcast.42, ...), custom_call_target="tpu_custom_call" | custom-call | flops 559677440 | bytes 6760640 | tf_op jit(solution)/shard_map/pallas_call | solution.py:64
  75.1 2.6 collective-permute-start.6
  78.3 2.6 all-to-all-start.4
  80.9 2.5 convolution_convert_fusion.theta
  83.4 8.9 %collective-permute-done.5.refs_2_ = bf16[784,128]{1,0:T(8,128)(2,1)S(1)} collective-permute-done((bf16[784,128]{1,0:T(8,128)(2,1)}, bf16[784,128]{1,0:T(8,128)(2,1)S(1)}, u32[]{:S(2)}, u32[]{:S(2)}) %collective-permute-start.5) | collective-permute-done | bytes 200736 | tf_op jit(solution)/shard_map/ppermute | solution.py:846
  93.7 4.9 %shard_map.373 = (bf16[448,1024]{1,0:T(8,128)(2,1)}, f32[392,448]{1,0:T(8,128)}, bf16[392,512]{1,0:T(8,128)(2,1)}, f32[392,1024]{1,0:T(8,128)}, f32[32,4,640]{2,1,0:T(4,128)}) custom-call(f32[5]{0:T(128)} %pad_maximum_fusion.3.sc, bf16[392,512]{1,0:T(8,128)(2,1)} %convolution_convert_fusion.theta, f32[392,4]{1,0:T(8,128)} %copy.67.place, ...), custom_call_target="tpu_custom_call" | custom-call | flops 770703360 | bytes 7020160 | tf_op jit(solution)/shard_map/pallas_call | solution.py:64
  98.6 5.0 %all-to-all-start.3 = ((f32[32,4,640]{2,1,0:T(4,128)}), f32[32,4,640]{2,1,0:T(4,128)S(1)}, u32[]{:S(2)}, u32[]{:S(2)}) async-start(f32[32,4,640]{2,1,0:T(4,128)} %get-tuple-element.146), calls=%async_computation.3 | async-start | bytes 655360 | tf_op jit(solution)/shard_map/all_to_all | solution.py:49
  104.4 10.0 %all-to-all-done.3.copies_in = f32[32,4,640]{2,1,0:T(4,128)S(1)} async-done(((f32[32,4,640]{2,1,0:T(4,128)}), f32[32,4,640]{2,1,0:T(4,128)S(1)}, u32[]{:S(2)}, u32[]{:S(2)}) %all-to-all-start.3) | async-done | bytes 327712 | tf_op jit(solution)/shard_map/all_to_all | solution.py:49
  115.1 5.7 %shard_map.374 = (bf16[392,1024]{1,0:T(8,128)(2,1)}, bf16[392,448]{1,0:T(8,128)(2,1)}, f32[1,1024]{1,0:T(1,128)}, f32[1,1024]{1,0:T(1,128)}, f32[1,1024]{1,0:T(1...) custom-call(f32[5]{0:T(128)} %pad_maximum_fusion.3.sc, ...), custom_call_target="tpu_custom_call" | custom-call | flops 950534144 | bytes 8182400 | tf_op jit(solution)/shard_map/pallas_call | solution.py:64
  126.0 7.2 %shard_map.375 = (bf16[4,2048,128]{2,1,0:T(8,128)(2,1)}, bf16[4,2048,128]{2,1,0:T(8,128)(2,1)}, f32[392,1024]{1,0:T(8,128)}, bf16[392,512]{1,0:T(8,128)(2,1)}) custom-call(s32[5]{0:T(128)} %stack.57.bits, bf16[392,448]{1,0:T(8,128)(2,1)} %get-tuple-element.154.d_logits, bf16[392,1024]{1,0:T(8,128)(2,1)} %cot.5, bf16[1024,512]{1,0:T(8,128)(2,1)} %w.12, ...), custom_call_target="tpu_custom_call" | custom-call | flops 1412956160 | bytes 8272896 | tf_op jit(solution)/shard_map/pallas_call | solution.py:600
  133.3 7.0 %collective-permute-done.8.refs_1_ = bf16[784,128]{1,0:T(8,128)(2,1)S(1)} collective-permute-done((bf16[784,128]{1,0:T(8,128)(2,1)}, bf16[784,128]{1,0:T(8,128)(2,1)S(1)}, u32[]{:S(2)}, u32[]{:S(2)}) %collective-permute-start.8) | collective-permute-done | bytes 200736 | tf_op jit(solution)/shard_map/ppermute | solution.py:875
  141.0 6.6 %shard_map.376 = (bf16[224,1024]{1,0:T(8,128)(2,1)}, f32[392,1024]{1,0:T(8,128)}, f32[32,8,256]{2,1,0:T(8,128)}) custom-call(f32[5]{0:T(128)} %pad_maximum_fusion.3.sc, f32[112,1024]{1,0:T(8,128)} %get-tuple-element.152.own, f32[112,1]{1,0:T(8,128)} %copy.70.counts, bf16[1024,512]{1,0:T(8,128)(2,1)} %w_key.3, bf16[1024,512]{1,0:T(8,128)(2,1)} %w_value.3, ...), custom_call_target="tpu_custom_call" | custom-call | flops 414711808 | bytes 9691072 | tf_op jit(solution)/shard_map/pallas_call | solution.py:64
  147.6 4.3 %all-to-all-start.5 = ((f32[32,8,256]{2,1,0:T(8,128)}), f32[32,8,256]{2,1,0:T(8,128)S(1)}, u32[]{:S(2)}, u32[]{:S(2)}) async-start(f32[32,8,256]{2,1,0:T(8,128)} %get-tuple-element.161), calls=%async_computation.5 | async-start | bytes 524288 | tf_op jit(solution)/shard_map/all_to_all | solution.py:49
  151.9 3.4 %shard_map.377 = (bf16[4,2048,128]{2,1,0:T(8,128)(2,1)}, bf16[4,2048,128]{2,1,0:T(8,128)(2,1)}) custom-call(s32[5]{0:T(128)} %stack.57.bits, bf16[4,2048,128]{2,1,0:T(8,128)(2,1)} %get-tuple-element.162.send_in, bf16[4,2048,128]{2,1,0:T(8,128)(2,1)} %get-tuple-element.163.keep_in, ...), custom_call_target="tpu_custom_call", output_to_operand_aliasing={{0}: (1, {}), {1}: (2, {})} | custom-call | flops 469762048 | bytes 4063232 | tf_op jit(solution)/shard_map/pallas_call | solution.py:600
  155.3 6.8 %all-to-all-done.5.copies_in = f32[32,8,256]{2,1,0:T(8,128)S(1)} async-done(((f32[32,8,256]{2,1,0:T(8,128)}), f32[32,8,256]{2,1,0:T(8,128)S(1)}, u32[]{:S(2)}, u32[]{:S(2)}) %all-to-all-start.5) | async-done | bytes 262176 | tf_op jit(solution)/shard_map/all_to_all | solution.py:49
  162.8 3.9 %shard_map.378 = (bf16[392,1024]{1,0:T(8,128)(2,1)}, f32[392,256]{1,0:T(8,128)}, f32[32,2,256]{2,1,0:T(2,128)}, f32[1,1024]{1,0:T(1,128)}, f32[1,1024]{1,0:T(1,128)}) custom-call(f32[5]{0:T(128)} %pad_maximum_fusion.3.sc, f32[32,8,256]{2,1,0:T(8,128)} %copy-done.7, f32[2,1024]{1,0:T(2,128)} %get-tuple-element.153.stats_3, f32[1,1024]{1,0:T(1,128)} %bitcast.40, ...), custom_call_target="tpu_custom_call" | custom-call | flops 205520896 | bytes 5699712 | tf_op jit(solution)/shard_map/pallas_call | solution.py:64
  166.7 2.7 %all-to-all-start.6 = ((f32[32,2,256]{2,1,0:T(2,128)}), f32[32,2,256]{2,1,0:T(2,128)S(1)}, u32[]{:S(2)}, u32[]{:S(2)}) async-start(f32[32,2,256]{2,1,0:T(2,128)} %get-tuple-element.172), calls=%async_computation.6 | async-start | bytes 131072 | tf_op jit(solution)/shard_map/all_to_all | solution.py:49
  169.4 2.6 shard_map.379
  172.0 4.0 %shard_map.380 = (bf16[2,1024,128]{2,1,0:T(8,128)(2,1)}, bf16[2,1024,128]{2,1,0:T(8,128)(2,1)}, bf16[2,1024,128]{2,1,0:T(8,128)(2,1)}, bf16[2,1024,128]{2,1,0:T(8,128)(2,1)}) custom-call(s32[5]{0:T(128)} %stack.57.bits, bf16[4,2048,128]{2,1,0:T(8,128)(2,1)} %get-tuple-element.177.keep_in, bf16[4,2048,128]{2,1,0:T(8,128)(2,1)} %copy-done.3), custom_call_target="tpu_custom_call" | custom-call | bytes 6291456 | tf_op jit(solution)/shard_map/pallas_call | solution.py:64
  179.4 4.2 %shard_map.381 = (bf16[392,256]{1,0:T(8,128)(2,1)}, f32[392,256]{1,0:T(8,128)}, f32[32,2,256]{2,1,0:T(2,128)}, f32[1,256]{1,0:T(1,128)}, f32[1,256]{1,0:T(1,128)...) custom-call(f32[5]{0:T(128)} %pad_maximum_fusion.3.sc, f32[32,2,256]{2,1,0:T(2,128)} %copy-done.22, ...), custom_call_target="tpu_custom_call" | custom-call | flops 462422016 | bytes 3333248 | tf_op jit(solution)/shard_map/pallas_call | solution.py:64
  183.6 3.7 %all-to-all-start.7 = ((f32[32,2,256]{2,1,0:T(2,128)}), f32[32,2,256]{2,1,0:T(2,128)S(1)}, u32[]{:S(2)}, u32[]{:S(2)}) async-start(f32[32,2,256]{2,1,0:T(2,128)} %get-tuple-element.184), calls=%async_computation.7 | async-start | bytes 131072 | tf_op jit(solution)/shard_map/all_to_all | solution.py:49
  187.3 3.7 %collective-permute-start.13 = (bf16[196,256]{1,0:T(8,128)(2,1)}, bf16[196,256]{1,0:T(8,128)(2,1)S(1)}, u32[]{:S(2)}, u32[]{:S(2)}) collective-permute-start(bf16[196,256]{1,0:T(8,128)(2,1)} %get-tuple-element.193), channel_id=1, source_target_pairs={{0,1},{1,2},{2,3},{4,5},{5,6},{6,7},{8,9},{9,10},{10,11},{12,13},{... | collective-permute-start | bytes 301064 | tf_op jit(solution)/shard_map/ppermute | solution.py:940
  193.3 3.5 %shard_map.382 = (bf16[4,1664,128]{2,1,0:T(8,128)(2,1)}, bf16[4,1664,128]{2,1,0:T(8,128)(2,1)}) custom-call(s32[5]{0:T(128)} %stack.57.bits, bf16[4,1664,128]{2,1,0:T(8,128)(2,1)} %get-tuple-element.175.send_in, bf16[4,1664,128]{2,1,0:T(8,128)(2,1)} %get-tuple-element.185.keep_in, ...), custom_call_target="tpu_custom_call", output_to_operand_aliasing={{0}: (1, {}), {1}: (2, {})} | custom-call | flops 462422016 | bytes 3776512 | tf_op jit(solution)/shard_map/pallas_call | solution.py:600
  198.4 4.6 %shard_map.383 = (f32[392,1024]{1,0:T(8,128)}, bf16[392,768]{1,0:T(8,128)(2,1)}, f32[1,256]{1,0:T(1,128)}, f32[1,256]{1,0:T(1,128)}) custom-call(f32[5]{0:T(128)} %pad_maximum_fusion.3.sc, f32[32,2,256]{2,1,0:T(2,128)} %copy-done.20, f32[2,256]{1,0:T(2,128)} %get-tuple-element.183.stats_1, f32[1,256]{1,0:T(1,128)} %bitcast.47, ...), custom_call_target="tpu_custom_call" | custom-call | flops 616562688 | bytes 6668960 | tf_op jit(solution)/shard_map/pallas_call | solution.py:64
  203.0 3.7 %shard_map.384 = (bf16[4,1664,128]{2,1,0:T(8,128)(2,1)}, bf16[4,1664,128]{2,1,0:T(8,128)(2,1)}) custom-call(s32[5]{0:T(128)} %stack.57.bits, bf16[4,1664,128]{2,1,0:T(8,128)(2,1)} %get-tuple-element.198.send_in, bf16[4,1664,128]{2,1,0:T(8,128)(2,1)} %get-tuple-element.199.keep_in, ...), custom_call_target="tpu_custom_call", output_to_operand_aliasing={{0}: (1, {}), {1}: (2, {})} | custom-call | flops 616562688 | bytes 3764224 | tf_op jit(solution)/shard_map/pallas_call | solution.py:600
  206.7 2.7 shard_map.387
  213.5 3.6 %shard_map.385 = (bf16[2,832,128]{2,1,0:T(8,128)(2,1)}, bf16[2,832,128]{2,1,0:T(8,128)(2,1)}, bf16[2,832,128]{2,1,0:T(8,128)(2,1)}, bf16[2,832,128]{2,1,0:T(8,128)(2,1)}) custom-call(s32[5]{0:T(128)} %stack.57.bits, bf16[4,1664,128]{2,1,0:T(8,128)(2,1)} %get-tuple-element.201.keep_in, bf16[4,1664,128]{2,1,0:T(8,128)(2,1)} %copy-done.4), custom_call_target="tpu_custom_call" | custom-call | bytes 5111808 | tf_op jit(solution)/shard_map/pallas_call | solution.py:64
  221.6 7.4 %collective-permute-done.16.received_1 = bf16[2,832,128]{2,1,0:T(8,128)(2,1)S(1)} collective-permute-done((bf16[2,832,128]{2,1,0:T(8,128)(2,1)}, bf16[2,832,128]{2,1,0:T(8,128)(2,1)S(1)}, u32[]{:S(2)}, u32[]{:S(2)}) %collective-permute-start.16) | collective-permute-done | bytes 426016 | tf_op jit(solution)/shard_map/ppermute | solution.py:637
  230.0 2.4 shard_map.386
  234.7 2.8 %collective-permute-start.24 = (bf16[1,1024,128]{2,1,0:T(8,128)(2,1)S(1)}, bf16[1,1024,128]{2,1,0:T(8,128)(2,1)S(1)}, u32[]{:S(2)}, u32[]{:S(2)}) collective-permute-start(bf16[1,1024,128]{2,1,0:T(8,128)(2,1)S(1)} %add_convert_fusion.2), channel_id=1, source_target_pairs={{0,2},{1,3},{2,0},{3,1},{4,6},{5,7},{6,4},{7,5},{8,10},{9,11},{10,... | collective-permute-start | bytes 786440 | tf_op jit(solution)/shard_map/ppermute | solution.py:684
  242.3 6.0 %collective-permute-done.24 = bf16[1,1024,128]{2,1,0:T(8,128)(2,1)S(1)} collective-permute-done((bf16[1,1024,128]{2,1,0:T(8,128)(2,1)S(1)}, bf16[1,1024,128]{2,1,0:T(8,128)(2,1)S(1)}, u32[]{:S(2)}, u32[]{:S(2)}) %collective-permute-start.24) | collective-permute-done | bytes 262176 | tf_op jit(solution)/shard_map/ppermute | solution.py:684
  248.3 2.2 collective-permute-done.23
  250.8 4.9 %collective-permute-start.25 = (bf16[1,832,128]{2,1,0:T(8,128)(2,1)S(1)}, bf16[1,832,128]{2,1,0:T(8,128)(2,1)S(1)}, u32[]{:S(2)}, u32[]{:S(2)}) collective-permute-start(bf16[1,832,128]{2,1,0:T(8,128)(2,1)S(1)} %add_convert_fusion.4), channel_id=1, source_target_pairs={{0,2},{1,3},{2,0},{3,1},{4,6},{5,7},{6,4},{7,5},{8,10},{9,11},{10,... | collective-permute-start | bytes 638984 | tf_op jit(solution)/shard_map/ppermute | solution.py:684
  255.7 5.8 %collective-permute-done.25 = bf16[1,832,128]{2,1,0:T(8,128)(2,1)S(1)} collective-permute-done((bf16[1,832,128]{2,1,0:T(8,128)(2,1)S(1)}, bf16[1,832,128]{2,1,0:T(8,128)(2,1)S(1)}, u32[]{:S(2)}, u32[]{:S(2)}) %collective-permute-start.25) | collective-permute-done | bytes 213024 | tf_op jit(solution)/shard_map/ppermute | solution.py:684
  261.7 3.4 %collective-permute-start.27 = (bf16[1,832,128]{2,1,0:T(8,128)(2,1)S(1)}, bf16[1,832,128]{2,1,0:T(8,128)(2,1)S(1)}, u32[]{:S(2)}, u32[]{:S(2)}) collective-permute-start(bf16[1,832,128]{2,1,0:T(8,128)(2,1)S(1)} %add_convert_fusion.3.mine), channel_id=1, source_target_pairs={{0,1},{1,0},{2,3},{3,2},{4,5},{5,4},{6,7},{7,6},{8,9},{9,8},{10,11... | collective-permute-start | bytes 638984 | tf_op jit(solution)/shard_map/ppermute | solution.py:695
  266.4 2.0 shard_map.389
  (193 shorter events, 55.1 us)
Async XLA Ops:
  4.0 12.4 %collective-permute-start = (f32[196,256]{1,0:T(8,128)}, f32[196,256]{1,0:T(8,128)S(1)}, u32[]{:S(2)}, u32[]{:S(2)}) collective-permute-start(f32[196,256]{1,0:T(8,128)} %get-tuple-element.132), channel_id=1, source_target_pairs={{0,1},{1,2},{2,3},{4,5},{5,6},{6,7},{8,9},{9,10},{10,11},{12,13},{... | collective-permute-start | bytes 602120 | tf_op jit(solution)/shard_map/ppermute | solution.py:802
  8.9 8.6 %collective-permute-start.1 = (f32[196,256]{1,0:T(8,128)}, f32[196,256]{1,0:T(8,128)S(1)}, u32[]{:S(2)}, u32[]{:S(2)}) collective-permute-start(f32[196,256]{1,0:T(8,128)} %get-tuple-element.133), channel_id=1, source_target_pairs={{1,0},{2,1},{3,2},{5,4},{6,5},{7,6},{9,8},{10,9},{11,10},{13,12},{... | collective-permute-start | bytes 602120 | tf_op jit(solution)/shard_map/ppermute | solution.py:803
  18.2 27.0 %copy-start.1 = (bf16[392,1024]{1,0:T(8,128)(2,1)S(1)}, bf16[392,1024]{1,0:T(8,128)(2,1)}, u32[]{:S(2)}) copy-start(bf16[392,1024]{1,0:T(8,128)(2,1)} %cot.5) | copy-start | bytes 2408452
  20.8 13.3 %all-to-all-start = ((f32[32,2,256]{2,1,0:T(2,128)}), f32[32,2,256]{2,1,0:T(2,128)S(1)}, u32[]{:S(2)}, u32[]{:S(2)}) async-start(f32[32,2,256]{2,1,0:T(2,128)} %get-tuple-element.134), calls=%async_computation | async-start | bytes 131072 | tf_op jit(solution)/shard_map/all_to_all | solution.py:49
  28.0 17.4 %collective-permute-start.2 = (bf16[196,256]{1,0:T(8,128)(2,1)}, bf16[196,256]{1,0:T(8,128)(2,1)S(1)}, u32[]{:S(2)}, u32[]{:S(2)}) collective-permute-start(bf16[196,256]{1,0:T(8,128)(2,1)} %get-tuple-element.137), channel_id=1, source_target_pairs={{0,1},{1,2},{2,3},{4,5},{5,6},{6,7},{8,9},{9,10},{10,11},{12,13},{... | collective-permute-start | bytes 301064 | tf_op jit(solution)/shard_map/ppermute | solution.py:811
  31.7 13.8 %collective-permute-start.3 = (bf16[196,256]{1,0:T(8,128)(2,1)}, bf16[196,256]{1,0:T(8,128)(2,1)S(1)}, u32[]{:S(2)}, u32[]{:S(2)}) collective-permute-start(bf16[196,256]{1,0:T(8,128)(2,1)} %get-tuple-element.138), channel_id=1, source_target_pairs={{1,0},{2,1},{3,2},{5,4},{6,5},{7,6},{9,8},{10,9},{11,10},{13,12},{... | collective-permute-start | bytes 301064 | tf_op jit(solution)/shard_map/ppermute | solution.py:812
  39.6 19.3 %copy-start.45 = (f32[1,448]{1,0:T(1,128)S(1)}, f32[1,448]{1,0:T(1,128)}, u32[]{:S(2)}) copy-start(f32[1,448]{1,0:T(1,128)} %constant.79) | copy-start | bytes 5380
  39.6 19.9 %copy-start.25 = (f32[112,392]{1,0:T(8,128)S(1)}, f32[112,392]{1,0:T(8,128)}, u32[]{:S(2)}) copy-start(f32[112,392]{1,0:T(8,128)} %constant.68.clone) | copy-start | bytes 526852
  39.7 13.1 %all-to-all-start.1 = ((f32[32,2,256]{2,1,0:T(2,128)}), f32[32,2,256]{2,1,0:T(2,128)S(1)}, u32[]{:S(2)}, u32[]{:S(2)}) async-start(f32[32,2,256]{2,1,0:T(2,128)} %get-tuple-element.136), calls=%async_computation.1 | async-start | bytes 131072 | tf_op jit(solution)/shard_map/all_to_all | solution.py:49
  45.4 38.0 %copy-start.36 = (bf16[196,256]{1,0:T(8,128)(2,1)}, bf16[196,256]{1,0:T(8,128)(2,1)S(1)}, u32[]{:S(2)}) copy-start(bf16[196,256]{1,0:T(8,128)(2,1)S(1)} %collective-permute-done.2.pre_before) | copy-start | bytes 301060
  45.5 38.0 %copy-start.37 = (bf16[196,256]{1,0:T(8,128)(2,1)}, bf16[196,256]{1,0:T(8,128)(2,1)S(1)}, u32[]{:S(2)}) copy-start(bf16[196,256]{1,0:T(8,128)(2,1)S(1)} %collective-permute-done.3.pre_after) | copy-start | bytes 301060
  56.4 11.5 %all-to-all-start.2 = ((f32[32,2,640]{2,1,0:T(2,128)}), f32[32,2,640]{2,1,0:T(2,128)S(1)}, u32[]{:S(2)}, u32[]{:S(2)}) async-start(f32[32,2,640]{2,1,0:T(2,128)} %get-tuple-element.141), calls=%async_computation.2 | async-start | bytes 327680 | tf_op jit(solution)/shard_map/all_to_all | solution.py:49
  73.3 10.2 %collective-permute-start.4 = (bf16[784,128]{1,0:T(8,128)(2,1)}, bf16[784,128]{1,0:T(8,128)(2,1)S(1)}, u32[]{:S(2)}, u32[]{:S(2)}) collective-permute-start(bf16[784,128]{1,0:T(8,128)(2,1)} %get-tuple-element.144.refs_0_), channel_id=1, source_target_pairs={{0,1},{1,0},{2,3},{3,2},{4,5},{5,4},{6,7},{7,6},{8,9},{9,8},{10,11... | collective-permute-start | bytes 602120 | tf_op jit(solution)/shard_map/ppermute | solution.py:846
  73.3 19.1 %collective-permute-start.5 = (bf16[784,128]{1,0:T(8,128)(2,1)}, bf16[784,128]{1,0:T(8,128)(2,1)S(1)}, u32[]{:S(2)}, u32[]{:S(2)}) collective-permute-start(bf16[784,128]{1,0:T(8,128)(2,1)} %get-tuple-element.144.refs_0_), channel_id=1, source_target_pairs={{0,2},{1,3},{2,0},{3,1},{4,6},{5,7},{6,4},{7,5},{8,10},{9,11},{10,... | collective-permute-start | bytes 602120 | tf_op jit(solution)/shard_map/ppermute | solution.py:846
  75.1 17.2 %collective-permute-start.6 = (bf16[784,128]{1,0:T(8,128)(2,1)}, bf16[784,128]{1,0:T(8,128)(2,1)S(1)}, u32[]{:S(2)}, u32[]{:S(2)}) collective-permute-start(bf16[784,128]{1,0:T(8,128)(2,1)} %get-tuple-element.144.refs_0_), channel_id=1, source_target_pairs={{0,3},{1,2},{2,1},{3,0},{4,7},{5,6},{6,5},{7,4},{8,11},{9,10},{10,... | collective-permute-start | bytes 602120 | tf_op jit(solution)/shard_map/ppermute | solution.py:846
  78.3 20.2 %all-to-all-start.4 = ((f32[32,2,512]{2,1,0:T(2,128)}), f32[32,2,512]{2,1,0:T(2,128)S(1)}, u32[]{:S(2)}, u32[]{:S(2)}) async-start(f32[32,2,512]{2,1,0:T(2,128)} %broadcast_in_dim.42), calls=%async_computation.4 | async-start | bytes 262144 | tf_op jit(solution)/shard_map/all_to_all | solution.py:49
  83.4 20.9 %copy-start.29 = (f32[392,112]{1,0:T(8,128)S(1)}, f32[392,112]{1,0:T(8,128)}, u32[]{:S(2)}) copy-start(f32[392,112]{1,0:T(8,128)} %constant.69.clone) | copy-start | bytes 526852
  98.6 15.8 %all-to-all-start.3 = ((f32[32,4,640]{2,1,0:T(4,128)}), f32[32,4,640]{2,1,0:T(4,128)S(1)}, u32[]{:S(2)}, u32[]{:S(2)}) async-start(f32[32,4,640]{2,1,0:T(4,128)} %get-tuple-element.146), calls=%async_computation.3 | async-start | bytes 655360 | tf_op jit(solution)/shard_map/all_to_all | solution.py:49
  120.9 12.4 %collective-permute-start.7 = (bf16[784,128]{1,0:T(8,128)(2,1)}, bf16[784,128]{1,0:T(8,128)(2,1)S(1)}, u32[]{:S(2)}, u32[]{:S(2)}) collective-permute-start(bf16[784,128]{1,0:T(8,128)(2,1)} %get-tuple-element.158), channel_id=1, source_target_pairs={{0,1},{1,0},{2,3},{3,2},{4,5},{5,4},{6,7},{7,6},{8,9},{9,8},{10,11... | collective-permute-start | bytes 602120 | tf_op jit(solution)/shard_map/ppermute | solution.py:875
  122.6 17.6 %collective-permute-start.8 = (bf16[784,128]{1,0:T(8,128)(2,1)}, bf16[784,128]{1,0:T(8,128)(2,1)S(1)}, u32[]{:S(2)}, u32[]{:S(2)}) collective-permute-start(bf16[784,128]{1,0:T(8,128)(2,1)} %get-tuple-element.159), channel_id=1, source_target_pairs={{0,2},{1,3},{2,0},{3,1},{4,6},{5,7},{6,4},{7,5},{8,10},{9,11},{10,... | collective-permute-start | bytes 602120 | tf_op jit(solution)/shard_map/ppermute | solution.py:875
  123.6 16.6 %collective-permute-start.9 = (bf16[784,128]{1,0:T(8,128)(2,1)}, bf16[784,128]{1,0:T(8,128)(2,1)S(1)}, u32[]{:S(2)}, u32[]{:S(2)}) collective-permute-start(bf16[784,128]{1,0:T(8,128)(2,1)} %get-tuple-element.160), channel_id=1, source_target_pairs={{0,3},{1,2},{2,1},{3,0},{4,7},{5,6},{6,5},{7,4},{8,11},{9,10},{10,... | collective-permute-start | bytes 602120 | tf_op jit(solution)/shard_map/ppermute | solution.py:875
  147.6 14.5 %all-to-all-start.5 = ((f32[32,8,256]{2,1,0:T(8,128)}), f32[32,8,256]{2,1,0:T(8,128)S(1)}, u32[]{:S(2)}, u32[]{:S(2)}) async-start(f32[32,8,256]{2,1,0:T(8,128)} %get-tuple-element.161), calls=%async_computation.5 | async-start | bytes 524288 | tf_op jit(solution)/shard_map/all_to_all | solution.py:49
  162.1 4.6 %collective-permute-start.10 = (bf16[4,2048,128]{2,1,0:T(8,128)(2,1)}, bf16[4,2048,128]{2,1,0:T(8,128)(2,1)S(1)}, u32[]{:S(2)}, u32[]{:S(2)}) collective-permute-start(bf16[4,2048,128]{2,1,0:T(8,128)(2,1)} %get-tuple-element.171), channel_id=1, source_target_pairs={{0,4},{4,0},{8,12},{12,8},{16,20},{20,16},{24,28},{28,24},{1,5},{5... | collective-permute-start | bytes 6291464 | tf_op jit(solution)/shard_map/ppermute | solution.py:619
  166.7 10.2 %all-to-all-start.6 = ((f32[32,2,256]{2,1,0:T(2,128)}), f32[32,2,256]{2,1,0:T(2,128)S(1)}, u32[]{:S(2)}, u32[]{:S(2)}) async-start(f32[32,2,256]{2,1,0:T(2,128)} %get-tuple-element.172), calls=%async_computation.6 | async-start | bytes 131072 | tf_op jit(solution)/shard_map/all_to_all | solution.py:49
  176.9 19.9 %collective-permute-start.11 = (bf16[2,1024,128]{2,1,0:T(8,128)(2,1)}, bf16[2,1024,128]{2,1,0:T(8,128)(2,1)S(1)}, u32[]{:S(2)}, u32[]{:S(2)}) collective-permute-start(bf16[2,1024,128]{2,1,0:T(8,128)(2,1)} %get-tuple-element.189), channel_id=1, source_target_pairs={{0,8},{4,12},{8,0},{12,4},{16,24},{20,28},{24,16},{28,20},{1,9},{5... | collective-permute-start | bytes 1572872 | tf_op jit(solution)/shard_map/ppermute | solution.py:637
  177.8 19.0 %collective-permute-start.12 = (bf16[2,1024,128]{2,1,0:T(8,128)(2,1)}, bf16[2,1024,128]{2,1,0:T(8,128)(2,1)S(1)}, u32[]{:S(2)}, u32[]{:S(2)}) collective-permute-start(bf16[2,1024,128]{2,1,0:T(8,128)(2,1)} %get-tuple-element.190), channel_id=1, source_target_pairs={{0,16},{4,20},{8,24},{12,28},{16,0},{20,4},{24,8},{28,12},{1,17},{... | collective-permute-start | bytes 1572872 | tf_op jit(solution)/shard_map/ppermute | solution.py:637
  183.6 13.2 %all-to-all-start.7 = ((f32[32,2,256]{2,1,0:T(2,128)}), f32[32,2,256]{2,1,0:T(2,128)S(1)}, u32[]{:S(2)}, u32[]{:S(2)}) async-start(f32[32,2,256]{2,1,0:T(2,128)} %get-tuple-element.184), calls=%async_computation.7 | async-start | bytes 131072 | tf_op jit(solution)/shard_map/all_to_all | solution.py:49
  187.3 9.5 %collective-permute-start.13 = (bf16[196,256]{1,0:T(8,128)(2,1)}, bf16[196,256]{1,0:T(8,128)(2,1)S(1)}, u32[]{:S(2)}, u32[]{:S(2)}) collective-permute-start(bf16[196,256]{1,0:T(8,128)(2,1)} %get-tuple-element.193), channel_id=1, source_target_pairs={{0,1},{1,2},{2,3},{4,5},{5,6},{6,7},{8,9},{9,10},{10,11},{12,13},{... | collective-permute-start | bytes 301064 | tf_op jit(solution)/shard_map/ppermute | solution.py:940
  191.0 6.8 %collective-permute-start.14 = (bf16[196,256]{1,0:T(8,128)(2,1)}, bf16[196,256]{1,0:T(8,128)(2,1)S(1)}, u32[]{:S(2)}, u32[]{:S(2)}) collective-permute-start(bf16[196,256]{1,0:T(8,128)(2,1)} %get-tuple-element.194), channel_id=1, source_target_pairs={{1,0},{2,1},{3,2},{5,4},{6,5},{7,6},{9,8},{10,9},{11,10},{13,12},{... | collective-permute-start | bytes 301064 | tf_op jit(solution)/shard_map/ppermute | solution.py:941
  206.7 5.7 %collective-permute-start.15 = (bf16[4,1664,128]{2,1,0:T(8,128)(2,1)}, bf16[4,1664,128]{2,1,0:T(8,128)(2,1)S(1)}, u32[]{:S(2)}, u32[]{:S(2)}) collective-permute-start(bf16[4,1664,128]{2,1,0:T(8,128)(2,1)} %get-tuple-element.202), channel_id=1, source_target_pairs={{0,4},{4,0},{8,12},{12,8},{16,20},{20,16},{24,28},{28,24},{1,5},{5... | collective-permute-start | bytes 5111816 | tf_op jit(solution)/shard_map/ppermute | solution.py:619
  209.4 8.9 %collective-permute-start.18 = (bf16[1,1024,128]{2,1,0:T(8,128)(2,1)}, bf16[1,1024,128]{2,1,0:T(8,128)(2,1)S(1)}, u32[]{:S(2)}, u32[]{:S(2)}) collective-permute-start(bf16[1,1024,128]{2,1,0:T(8,128)(2,1)} %get-tuple-element.215), channel_id=1, source_target_pairs={{0,16},{4,20},{8,24},{12,28},{16,0},{20,4},{24,8},{28,12},{1,17},{... | collective-permute-start | bytes 786440 | tf_op jit(solution)/shard_map/ppermute | solution.py:637
  210.9 8.6 %collective-permute-start.19 = (bf16[1,1024,128]{2,1,0:T(8,128)(2,1)}, bf16[1,1024,128]{2,1,0:T(8,128)(2,1)S(1)}, u32[]{:S(2)}, u32[]{:S(2)}) collective-permute-start(bf16[1,1024,128]{2,1,0:T(8,128)(2,1)} %get-tuple-element.217), channel_id=1, source_target_pairs={{0,8},{4,12},{8,0},{12,4},{16,24},{20,28},{24,16},{28,20},{1,9},{5... | collective-permute-start | bytes 786440 | tf_op jit(solution)/shard_map/ppermute | solution.py:637
  217.1 11.9 %collective-permute-start.16 = (bf16[2,832,128]{2,1,0:T(8,128)(2,1)}, bf16[2,832,128]{2,1,0:T(8,128)(2,1)S(1)}, u32[]{:S(2)}, u32[]{:S(2)}) collective-permute-start(bf16[2,832,128]{2,1,0:T(8,128)(2,1)} %get-tuple-element.204), channel_id=1, source_target_pairs={{0,8},{4,12},{8,0},{12,4},{16,24},{20,28},{24,16},{28,20},{1,9},{5... | collective-permute-start | bytes 1277960 | tf_op jit(solution)/shard_map/ppermute | solution.py:637
  217.7 11.6 %collective-permute-start.17 = (bf16[2,832,128]{2,1,0:T(8,128)(2,1)}, bf16[2,832,128]{2,1,0:T(8,128)(2,1)S(1)}, u32[]{:S(2)}, u32[]{:S(2)}) collective-permute-start(bf16[2,832,128]{2,1,0:T(8,128)(2,1)} %get-tuple-element.206), channel_id=1, source_target_pairs={{0,16},{4,20},{8,24},{12,28},{16,0},{20,4},{24,8},{28,12},{1,17},{... | collective-permute-start | bytes 1277960 | tf_op jit(solution)/shard_map/ppermute | solution.py:637
  219.7 12.8 %collective-permute-start.20 = (bf16[1,1024,128]{2,1,0:T(8,128)(2,1)S(1)}, bf16[1,1024,128]{2,1,0:T(8,128)(2,1)S(1)}, u32[]{:S(2)}, u32[]{:S(2)}) collective-permute-start(bf16[1,1024,128]{2,1,0:T(8,128)(2,1)S(1)} %select_convert_fusion.1), channel_id=1, source_target_pairs={{0,1},{1,0},{2,3},{3,2},{4,5},{5,4},{6,7},{7,6},{8,9},{9,8},{10,11... | collective-permute-start | bytes 786440 | tf_op jit(solution)/shard_map/ppermute | solution.py:671
  232.5 6.4 %collective-permute-start.21 = (bf16[1,832,128]{2,1,0:T(8,128)(2,1)}, bf16[1,832,128]{2,1,0:T(8,128)(2,1)S(1)}, u32[]{:S(2)}, u32[]{:S(2)}) collective-permute-start(bf16[1,832,128]{2,1,0:T(8,128)(2,1)} %get-tuple-element.220), channel_id=1, source_target_pairs={{0,8},{4,12},{8,0},{12,4},{16,24},{20,28},{24,16},{28,20},{1,9},{5... | collective-permute-start | bytes 638984 | tf_op jit(solution)/shard_map/ppermute | solution.py:637
  234.0 6.2 %collective-permute-start.22 = (bf16[1,832,128]{2,1,0:T(8,128)(2,1)}, bf16[1,832,128]{2,1,0:T(8,128)(2,1)S(1)}, u32[]{:S(2)}, u32[]{:S(2)}) collective-permute-start(bf16[1,832,128]{2,1,0:T(8,128)(2,1)} %get-tuple-element.222), channel_id=1, source_target_pairs={{0,16},{4,20},{8,24},{12,28},{16,0},{20,4},{24,8},{28,12},{1,17},{... | collective-permute-start | bytes 638984 | tf_op jit(solution)/shard_map/ppermute | solution.py:637
  234.7 13.6 %collective-permute-start.24 = (bf16[1,1024,128]{2,1,0:T(8,128)(2,1)S(1)}, bf16[1,1024,128]{2,1,0:T(8,128)(2,1)S(1)}, u32[]{:S(2)}, u32[]{:S(2)}) collective-permute-start(bf16[1,1024,128]{2,1,0:T(8,128)(2,1)S(1)} %add_convert_fusion.2), channel_id=1, source_target_pairs={{0,2},{1,3},{2,0},{3,1},{4,6},{5,7},{6,4},{7,5},{8,10},{9,11},{10,... | collective-permute-start | bytes 786440 | tf_op jit(solution)/shard_map/ppermute | solution.py:684
  240.3 24.8 %copy-start.2 = (f32[392,1024]{1,0:T(8,128)S(1)}, f32[392,1024]{1,0:T(8,128)}, u32[]{:S(2)}) copy-start(f32[392,1024]{1,0:T(8,128)} %get-tuple-element.145.pre_4) | copy-start | bytes 4816900
  240.3 24.8 %copy-start.13 = (bf16[392,1024]{1,0:T(8,128)(2,1)S(1)}, bf16[392,1024]{1,0:T(8,128)(2,1)}, u32[]{:S(2)}) copy-start(bf16[392,1024]{1,0:T(8,128)(2,1)} %get-tuple-element.143.unit) | copy-start | bytes 2408452
  240.4 24.8 %copy-start.41 = (f32[1024]{0:T(1024)S(1)}, f32[1024]{0:T(1024)}, u32[]{:S(2)}) copy-start(f32[1024]{0:T(1024)} %param.41) | copy-start | bytes 12292
  240.4 24.8 %copy-start.42 = (f32[1024]{0:T(1024)S(1)}, f32[1024]{0:T(1024)}, u32[]{:S(2)}) copy-start(f32[1024]{0:T(1024)} %param.42) | copy-start | bytes 12292
  240.4 24.7 %copy-start.43 = (f32[1,1024]{1,0:T(1,128)S(1)}, f32[1,1024]{1,0:T(1,128)}, u32[]{:S(2)}) copy-start(f32[1,1024]{1,0:T(1,128)} %get-tuple-element.150) | copy-start | bytes 12292
  240.4 24.7 %copy-start.44 = (f32[1,1024]{1,0:T(1,128)S(1)}, f32[1,1024]{1,0:T(1,128)}, u32[]{:S(2)}) copy-start(f32[1,1024]{1,0:T(1,128)} %get-tuple-element.151) | copy-start | bytes 12292
  240.4 10.1 %collective-permute-start.23 = (bf16[1,832,128]{2,1,0:T(8,128)(2,1)S(1)}, bf16[1,832,128]{2,1,0:T(8,128)(2,1)S(1)}, u32[]{:S(2)}, u32[]{:S(2)}) collective-permute-start(bf16[1,832,128]{2,1,0:T(8,128)(2,1)S(1)} %select_convert_fusion.2), channel_id=1, source_target_pairs={{0,1},{1,0},{2,3},{3,2},{4,5},{5,4},{6,7},{7,6},{8,9},{9,8},{10,11... | collective-permute-start | bytes 638984 | tf_op jit(solution)/shard_map/ppermute | solution.py:671
  250.6 11.0 %collective-permute-start.26 = (bf16[1,1024,128]{2,1,0:T(8,128)(2,1)S(1)}, bf16[1,1024,128]{2,1,0:T(8,128)(2,1)S(1)}, u32[]{:S(2)}, u32[]{:S(2)}) collective-permute-start(bf16[1,1024,128]{2,1,0:T(8,128)(2,1)S(1)} %add_convert_fusion.1.mine), channel_id=1, source_target_pairs={{0,1},{1,0},{2,3},{3,2},{4,5},{5,4},{6,7},{7,6},{8,9},{9,8},{10,11... | collective-permute-start | bytes 786440 | tf_op jit(solution)/shard_map/ppermute | solution.py:695
  250.8 10.7 %collective-permute-start.25 = (bf16[1,832,128]{2,1,0:T(8,128)(2,1)S(1)}, bf16[1,832,128]{2,1,0:T(8,128)(2,1)S(1)}, u32[]{:S(2)}, u32[]{:S(2)}) collective-permute-start(bf16[1,832,128]{2,1,0:T(8,128)(2,1)S(1)} %add_convert_fusion.4), channel_id=1, source_target_pairs={{0,2},{1,3},{2,0},{3,1},{4,6},{5,7},{6,4},{7,5},{8,10},{9,11},{10,... | collective-permute-start | bytes 638984 | tf_op jit(solution)/shard_map/ppermute | solution.py:684
  261.7 7.2 %collective-permute-start.27 = (bf16[1,832,128]{2,1,0:T(8,128)(2,1)S(1)}, bf16[1,832,128]{2,1,0:T(8,128)(2,1)S(1)}, u32[]{:S(2)}, u32[]{:S(2)}) collective-permute-start(bf16[1,832,128]{2,1,0:T(8,128)(2,1)S(1)} %add_convert_fusion.3.mine), channel_id=1, source_target_pairs={{0,1},{1,0},{2,3},{3,2},{4,5},{5,4},{6,7},{7,6},{8,9},{9,8},{10,11... | collective-permute-start | bytes 638984 | tf_op jit(solution)/shard_map/ppermute | solution.py:695
  (38 other events, 190.4 us)

commit v5 on v4

--- a/solution.py
+++ b/solution.py
@@ -398,34 +398,8 @@
     emit(copies, width, column_sum(d_here))
 
 
-def first_back_kernel(frames, sc, copies_in, stats_1, gain_1, d_act, pre_1, place, near, d_before, d_after, pre_before, pre_after, w, d_summed, input_grad, d_taps, gain_out, shift_out, whole, moved):
-    total = sc[0]
-    width = pre_1.shape[1]
-    sums = collect(copies_in)
-    gain_grad, shift_grad = part(sums, 0, width), part(sums, width, width)
-    gain_out[...] = gain_grad
-    shift_out[...] = shift_grad
-    scale, base, slope = back_terms(
-        gain_1[...], stats_1[0:1, :], stats_1[1:2, :], gain_grad, shift_grad, total
-    )
-    whole[...] = d_act[...] * scale + place[:, 0:1] * (base + pre_1[...] * slope)
-    d_taps[:, width : 2 * width] = whole[...].astype(BF16)
-    d_prev = d_before[...].astype(F32) * scale + near[:, 0:1] * (
-        base + pre_before[...].astype(F32) * slope
-    )
-    d_next = d_after[...].astype(F32) * scale + near[:, 1:2] * (
-        base + pre_after[...].astype(F32) * slope
-    )
-    for t in range(frames):
-        here = slice(t * AREA, (t + 1) * AREA)
-        ahead = d_next if t == frames - 1 else whole[(t + 1) * AREA : (t + 2) * AREA, :]
-        moved[here, :] = ahead * sc[1 + frames + t]
-    d_taps[:, 0:width] = moved[...].astype(BF16)
-    for t in range(frames):
-        here = slice(t * AREA, (t + 1) * AREA)
-        behind = d_prev if t == 0 else whole[(t - 1) * AREA : t * AREA, :]
-        moved[here, :] = behind * sc[1 + t]
-    d_taps[:, 2 * width :] = moved[...].astype(BF16)
+def input_back_kernel(d_taps, w, d_summed, input_grad):
+    width = w.shape[2]
     for c in chunks(d_summed.shape[1], 2 * LANE):
         value = d_summed[:, c]
         for tap in range(3):
@@ -503,7 +477,34 @@
     split_out(bits[0], start, both, low, send, keep, sems)
 
 
-def time_grads_kernel(parts, start, bits, send_in, keep_in, x, d_taps, send, keep, both, low, sems):
+def time_grads_kernel(frames, parts, start, bits, sc, send_in, keep_in, x, copies_in, stats_1, gain_1, d_act, pre_1, place, near, d_before, d_after, pre_before, pre_after, send, keep, d_taps, gain_out, shift_out, both, low, sems, whole, moved):
+    total = sc[0]
+    width = pre_1.shape[1]
+    sums = collect(copies_in)
+    gain_grad, shift_grad = part(sums, 0, width), part(sums, width, width)
+    gain_out[...] = gain_grad
+    shift_out[...] = shift_grad
+    scale, base, slope = back_terms(
+        gain_1[...], stats_1[0:1, :], stats_1[1:2, :], gain_grad, shift_grad, total
+    )
+    whole[...] = d_act[...] * scale + place[:, 0:1] * (base + pre_1[...] * slope)
+    d_taps[:, width : 2 * width] = whole[...].astype(BF16)
+    d_prev = d_before[...].astype(F32) * scale + near[:, 0:1] * (
+        base + pre_before[...].astype(F32) * slope
+    )
+    d_next = d_after[...].astype(F32) * scale + near[:, 1:2] * (
+        base + pre_after[...].astype(F32) * slope
+    )
+    for t in range(frames):
+        here = slice(t * AREA, (t + 1) * AREA)
+        ahead = d_next if t == frames - 1 else whole[(t + 1) * AREA : (t + 2) * AREA, :]
+        moved[here, :] = ahead * sc[1 + frames + t]
+    d_taps[:, 0:width] = moved[...].astype(BF16)
+    for t in range(frames):
+        here = slice(t * AREA, (t + 1) * AREA)
+        behind = d_prev if t == 0 else whole[(t - 1) * AREA : t * AREA, :]
+        moved[here, :] = behind * sc[1 + t]
+    d_taps[:, 2 * width :] = moved[...].astype(BF16)
     wide = x.shape[1] // parts
     for p in range(parts):
         put(both, p, 0, dot_rows(x[:, p * wide : (p + 1) * wide], d_taps[...]))
@@ -551,33 +552,32 @@
         out[:, c] = part[start + k * rows : start + (k + 1) * rows, :]
 
 
-def attend_outs_kernel(bit, bits, mine, other, out_grad, query_grad, key_grad, value_grad, first, second):
+def attend_outs_kernel(bit, bits, mine, other, out_grad, query_grad, key_grad, value_grad, both):
     swap = bits[bit] == 1
     here, there = mine[0].astype(F32), other[0].astype(F32)
-    first[...] = jnp.where(swap, there, here)
-    second[...] = jnp.where(swap, here, there)
-    unfold(first, 0, out_grad)
-    unfold(first, out_grad.shape[0], query_grad)
-    unfold(second, 0, key_grad)
-    unfold(second, first.shape[0] // 2, value_grad)
-
-
-def bottleneck_outs_kernel(bit, bits, mine, other, expand_grad, space_grad, time_grad, first, second):
+    cut = here.shape[0]
+    both[0:cut, :] = jnp.where(swap, there, here)
+    both[cut : 2 * cut, :] = jnp.where(swap, here, there)
+    unfold(both, 0, out_grad)
+    unfold(both, cut // 2, query_grad)
+    unfold(both, cut, key_grad)
+    unfold(both, cut + cut // 2, value_grad)
+
+
+def bottleneck_outs_kernel(bit, bits, mine, other, expand_grad, space_grad, time_grad, both):
     swap = bits[bit] == 1
     here, there = mine[0].astype(F32), other[0].astype(F32)
-    first[...] = jnp.where(swap, there, here)
-    second[...] = jnp.where(swap, here, there)
-    unfold(first, 0, expand_grad)
-    taps, deep, width = space_grad.shape
-    for tap in range(taps):
-        start = expand_grad.shape[0] + tap * deep * width // LANE
-        for k, c in enumerate(chunks(width)):
-            space_grad[tap, :, c] = first[start + k * deep : start + (k + 1) * deep, :]
-    taps, deep, width = time_grad.shape
-    for tap in range(taps):
-        for k, c in enumerate(chunks(width)):
-            start = (tap * width // LANE + k) * deep
-            time_grad[tap, :, c] = second[start : start + deep, :]
+    cut = here.shape[0]
+    both[0:cut, :] = jnp.where(swap, there, here)
+    both[cut : 2 * cut, :] = jnp.where(swap, here, there)
+    unfold(both, 0, expand_grad)
+    start = expand_grad.shape[0]
+    for grad in (space_grad, time_grad):
+        taps, deep, width = grad.shape
+        for tap in range(taps):
+            for c in chunks(width):
+                grad[tap, :, c] = both[start : start + deep, :]
+                start += deep
 
 
 class Bundle:
@@ -588,7 +588,7 @@
         self.grp_bits = self.grp_count.bit_length() - 1
         self.send = self.keep = None
 
-    def add(self, kernel, start, rows, *arrays, extra=(), scratch=(), flops=0):
+    def add(self, kernel, start, rows, *arrays, extra=(), scratch=(), scalars=(), flops=0):
         whole = (self.pos_count // 2, 2 * self.cut, LANE)
         half = (self.pos_count // 2, rows, LANE)
         held = () if self.send is None else (self.send, self.keep)
@@ -600,7 +600,7 @@
         self.send, self.keep, *rest = pl.pallas_call(
             functools.partial(kernel, self.pos_count, start),
             out_shape=shapes,
-            in_specs=[pl.BlockSpec(memory_space=pltpu.SMEM)]
+            in_specs=[pl.BlockSpec(memory_space=pltpu.SMEM)] * (1 + len(scalars))
             + [anywhere] * len(held)
             + [inside_vmem] * len(arrays),
             out_specs=[anywhere, anywhere] + [inside_vmem] * len(extra),
@@ -609,10 +609,10 @@
                 pltpu.SemaphoreType.DMA((2,)),
             ]
             + list(scratch),
-            input_output_aliases={1: 0, 2: 1} if held else {},
+            input_output_aliases={1 + len(scalars): 0, 2 + len(scalars): 1} if held else {},
             compiler_params=pltpu.CompilerParams(vmem_limit_bytes=VMEM_BYTES),
             cost_estimate=pl.CostEstimate(flops=flops, bytes_accessed=moved, transcendentals=0),
-        )(self.bits, *held, *arrays)
+        )(self.bits, *scalars, *held, *arrays)
         return rest
 
     def begin(self):
@@ -695,10 +695,9 @@
         self.other = lax.ppermute(final, "grp", flip(self.grp_count, 1))
 
     def outs(self, kernel, shapes):
-        part = pltpu.VMEM((self.cut, LANE), F32)
         return call(
             functools.partial(kernel, self.pos_bits), [(shape, F32) for shape in shapes],
-            (self.bits,), self.mine, self.other, scratch=[part, part],
+            (self.bits,), self.mine, self.other, scratch=[pltpu.VMEM((2 * self.cut, LANE), F32)],
         )
 
     def shares(self):
@@ -916,7 +915,9 @@
     sums = trade(sums)
     tap_rows = wide * narrow // LANE
     expand_rows = narrow * deep // LANE
-    bundle_2 = Bundle(bits, expand_rows + 9 * tap_rows)
+    time_start = expand_rows + 9 * tap_rows
+    cut = -(-(time_start + 3 * deep * narrow // LANE) // 32) * 16
+    bundle_2 = Bundle(bits, cut)
     bundle_2.add(
         expand_grads_kernel, 0, expand_rows, z_2, d_third,
         flops=2 * rows * narrow * channels,
@@ -946,25 +947,28 @@
     (_, _, got_1), (_, _, got_2) = bundle_1.parts
     sums, bundle_2.send, got_1, got_2 = tie(sums, bundle_2.send, got_1, got_2)
     bundle_1.parts[0][2], bundle_1.parts[1][2] = got_1, got_2
-    input_grad, d_taps, gain_first_grad, shift_first_grad = call(
-        functools.partial(first_back_kernel, frames),
-        [wide_f32, ((rows, 3 * narrow), BF16), ((1, narrow), F32), ((1, narrow), F32)],
-        (scalars,), sums, stats_1, gain_1, d_act_1, pre_1, place, near, d_before, d_after,
-        pre_before, pre_after, time_weight, d_summed,
+    d_taps, gain_first_grad, shift_first_grad = bundle_2.add(
+        functools.partial(time_grads_kernel, frames), time_start, 3 * deep * narrow // LANE,
+        inputs, sums, stats_1, gain_1, d_act_1, pre_1, place, near, d_before, d_after,
+        pre_before, pre_after,
+        extra=[((rows, 3 * narrow), BF16), ((1, narrow), F32), ((1, narrow), F32)],
         scratch=[pltpu.VMEM((rows, narrow), F32), pltpu.VMEM((rows, narrow), F32)],
+        scalars=(scalars,),
         flops=6 * rows * narrow * channels,
     )
 
     bundle_1.after([d_taps, d_taps])
-    bundle_2.add(
-        time_grads_kernel, bundle_2.cut, 3 * deep * narrow // LANE, inputs, d_taps,
-        flops=6 * rows * narrow * channels,
-    )
     bundle_2.begin()
     bundle_1.more()
     bundle_2.plane()
     bundle_2.turn()
+    d_taps, _ = tie(d_taps, bundle_2.parts[0][1])
+    (input_grad,) = call(
+        input_back_kernel, [wide_f32], (), d_taps, time_weight, d_summed,
+        flops=6 * rows * narrow * channels,
+    )
     bundle_1.layer()
+    bundle_2.after([input_grad])
     bundle_2.more(last=False)
     bundle_1.got = bundle_2.hold(bundle_1.got)
     bundle_2.turn()
@@ -998,12 +1002,12 @@
         query_grad = columns(first, half, deep, inner)
         key_grad = columns(second, 0, deep, inner)
         value_grad = columns(second, half, deep, inner)
-        first, second = bundle_2.shares()
-        expand_grad = folded(first, 0, narrow, deep)
+        both = jnp.concatenate(bundle_2.shares(), axis=0)
+        expand_grad = folded(both, 0, narrow, deep)
         space_grad = jnp.stack(
-            [columns(first, expand_rows + tap * tap_rows, wide, narrow) for tap in range(9)]
+            [columns(both, expand_rows + tap * tap_rows, wide, narrow) for tap in range(9)]
         )
-        time_all = columns(second, 0, deep, 3 * narrow)
+        time_all = columns(both, time_start, deep, 3 * narrow)
         time_grad = jnp.stack([time_all[:, k * narrow : (k + 1) * narrow] for k in range(3)])
     return (
         output, input_grad, time_grad, gain_first_grad[0], shift_first_grad[0], space_grad,

time: 273 us -> 269 us (0.985)
  waiting for transfers between devices: 77.9 us -> 72.7 us
    ppermute x8, waiting for transfers between devices: 11.6 us -> 7.05 us  [turn(): self.parts[k].append(lax.ppermute(self.parts[k][0], 'pos', pairs))]
  transfers between devices with their start and end apart: 36 -> 36, of which waited for: 21 -> 21; matrix products, arithmetic and copies ran while one was open for 6% -> 6% of each run, Pallas kernels for 18% -> 20%
where the time goes in v5:
time: 269 us; the launch traced here: 268 us
  Pallas kernels  86 us (32%)
  starting transfers between devices  82 us (30%)
  waiting for transfers between devices  72.7 us (27%)
  local copies, waits for them, and re-layouts  14.2 us (5%)
  other arithmetic  6.83 us (3%)
  matrix products  4.67 us (2%)
    pallas_call x17, Pallas kernels, call(): pl.pallas_call(kernel, out_shape=shapes, in_specs=[pl.BlockSpec(memory_sp...  64.3 us
    all_to_all x8, waiting for transfers between devices, trade(): return lax.all_to_all(copies, ('pos', 'grp'), 0, 0, tiled=True)  33.9 us
    all_to_all x8, starting transfers between devices, trade(): return lax.all_to_all(copies, ('pos', 'grp'), 0, 0, tiled=True)  32.4 us
    pallas_call x5, Pallas kernels, add(): pl.pallas_call(functools.partial(kernel, self.pos_count, start), out_shap...  21.7 us
    ppermute x2, waiting for transfers between devices, exchange(): lax.ppermute(self.low, 'grp', flip(self.grp_count, self.grp_count // 2))  11.9 us
    unnamed x100, local copies, waits for them, and re-layouts  9.12 us
    ppermute x3, waiting for transfers between devices, local(): lax.ppermute(kv_own, 'grp', flip(grp_count, step))  8.87 us
    ppermute x8, starting transfers between devices, turn(): self.parts[k].append(lax.ppermute(self.parts[k][0], 'pos', pairs))  8.53 us
  transfers between devices with their start and end apart: 36, of which 21 were waited for; matrix products, arithmetic and copies ran while one was open for 6% of the time, Pallas kernels for 20%

profile of v5, /device:TPU:0, one launch (start us, length us, event | category | flops | bytes accessed | tf_op | source)
XLA Modules:
  0.0 267.5 jit_solution(326616651713755438)
XLA Ops:
  0.7 3.3 %shard_map.368 = (f32[392,256]{1,0:T(8,128)}, f32[392,256]{1,0:T(8,128)}, f32[196,256]{1,0:T(8,128)}, f32[196,256]{1,0:T(8,128)}) custom-call(bf16[392,1024]{1,0:T(8,128)(2,1)} %x.11, bf16[3,1024,256]{2,1,0:T(8,128)(2,1)} %w.15), custom_call_target="tpu_custom_call" | custom-call | flops 411041792 | bytes 3579904 | tf_op jit(solution)/shard_map/pallas_call | solution.py:64
  4.0 4.9 %collective-permute-start = (f32[196,256]{1,0:T(8,128)}, f32[196,256]{1,0:T(8,128)S(1)}, u32[]{:S(2)}, u32[]{:S(2)}) collective-permute-start(f32[196,256]{1,0:T(8,128)} %get-tuple-element.133), channel_id=1, source_target_pairs={{0,1},{1,2},{2,3},{4,5},{5,6},{6,7},{8,9},{9,10},{10,11},{12,13},{... | collective-permute-start | bytes 602120 | tf_op jit(solution)/shard_map/ppermute | solution.py:801
  10.2 2.2 fusion.tap_1
  18.2 2.5 shard_map.369
  20.8 5.9 %all-to-all-start = ((f32[32,2,256]{2,1,0:T(2,128)}), f32[32,2,256]{2,1,0:T(2,128)S(1)}, u32[]{:S(2)}, u32[]{:S(2)}) async-start(f32[32,2,256]{2,1,0:T(2,128)} %get-tuple-element.135), calls=%async_computation | async-start | bytes 131072 | tf_op jit(solution)/shard_map/all_to_all | solution.py:49
  28.1 3.7 %collective-permute-start.2 = (bf16[196,256]{1,0:T(8,128)(2,1)}, bf16[196,256]{1,0:T(8,128)(2,1)S(1)}, u32[]{:S(2)}, u32[]{:S(2)}) collective-permute-start(bf16[196,256]{1,0:T(8,128)(2,1)} %get-tuple-element.138), channel_id=1, source_target_pairs={{0,1},{1,2},{2,3},{4,5},{5,6},{6,7},{8,9},{9,10},{10,11},{12,13},{... | collective-permute-start | bytes 301064 | tf_op jit(solution)/shard_map/ppermute | solution.py:810
  34.8 4.9 %shard_map.370 = (f32[392,256]{1,0:T(8,128)}, bf16[392,2304]{1,0:T(8,128)(2,1)}, f32[32,2,256]{2,1,0:T(2,128)}, f32[2,256]{1,0:T(2,128)}) custom-call(f32[5]{0:T(128)} %pad_maximum_fusion.3.sc, f32[32,2,256]{2,1,0:T(2,128)} %copy-done.23, f32[392,256]{1,0:T(8,128)} %get-tuple-element.136.pre_1, f32[1,256]{1,0:T(1,128)} %bitcast.45, f32[1,256]{1,0:T(1,128)} %bitcast.51, ...), custom_call_target="tpu_custom_call" | custom-call | flops 462422016 | bytes 3930240 | tf_op jit(solution)/shard_map/pallas_call | solution.py:64
  39.7 5.6 %all-to-all-start.1 = ((f32[32,2,256]{2,1,0:T(2,128)}), f32[32,2,256]{2,1,0:T(2,128)S(1)}, u32[]{:S(2)}, u32[]{:S(2)}) async-start(f32[32,2,256]{2,1,0:T(2,128)} %get-tuple-element.137), calls=%async_computation.1 | async-start | bytes 131072 | tf_op jit(solution)/shard_map/all_to_all | solution.py:49
  45.5 7.3 %all-to-all-done.1.copies_in = f32[32,2,256]{2,1,0:T(2,128)S(1)} async-done(((f32[32,2,256]{2,1,0:T(2,128)}), f32[32,2,256]{2,1,0:T(2,128)S(1)}, u32[]{:S(2)}, u32[]{:S(2)}) %all-to-all-start.1) | async-done | bytes 65568 | tf_op jit(solution)/shard_map/all_to_all | solution.py:49
  53.5 3.0 %shard_map.371 = (bf16[392,256]{1,0:T(8,128)(2,1)}, f32[392,1024]{1,0:T(8,128)}, f32[32,2,640]{2,1,0:T(2,128)}, f32[2,256]{1,0:T(2,128)}) custom-call(f32[5]{0:T(128)} %pad_maximum_fusion.3.sc, f32[32,2,256]{2,1,0:T(2,128)} %copy-done.24, f32[392,256]{1,0:T(8,128)} %get-tuple-element.141.pre_2, f32[1,256]{1,0:T(1,128)} %bitcast.48, f32[1,256]{1,0:T(1,128)} %bitcast.57, ...), custom_call_target="tpu_custom_call" | custom-call | flops 205520896 | bytes 2971776 | tf_op jit(solution)/shard_map/pallas_call | solution.py:64
  56.4 2.6 all-to-all-start.2
  60.3 7.6 %all-to-all-done.2.copies_in = f32[32,2,640]{2,1,0:T(2,128)S(1)} async-done(((f32[32,2,640]{2,1,0:T(2,128)}), f32[32,2,640]{2,1,0:T(2,128)S(1)}, u32[]{:S(2)}, u32[]{:S(2)}) %all-to-all-start.2) | async-done | bytes 163872 | tf_op jit(solution)/shard_map/all_to_all | solution.py:49
  68.6 4.8 %shard_map.372 = (bf16[392,1024]{1,0:T(8,128)(2,1)}, bf16[224,1024]{1,0:T(8,128)(2,1)}, bf16[784,128]{1,0:T(8,128)(2,1)}, f32[2,1024]{1,0:T(2,128)}) custom-call(f32[5]{0:T(128)} %pad_maximum_fusion.3.sc, f32[32,2,640]{2,1,0:T(2,128)} %copy-done.14, bf16[256,1024]{1,0:T(8,128)(2,1)} %w.13, f32[1,1024]{1,0:T(1,128)} %bitcast.38, f32[1,1024]{1,0:T(1,128)} %bitcast.42, ...), custom_call_target="tpu_custom_call" | custom-call | flops 559677440 | bytes 6760640 | tf_op jit(solution)/shard_map/pallas_call | solution.py:64
  75.2 2.6 collective-permute-start.6
  78.4 2.6 all-to-all-start.4
  81.0 2.5 convolution_convert_fusion.theta
  83.5 8.9 %collective-permute-done.5.refs_2_ = bf16[784,128]{1,0:T(8,128)(2,1)S(1)} collective-permute-done((bf16[784,128]{1,0:T(8,128)(2,1)}, bf16[784,128]{1,0:T(8,128)(2,1)S(1)}, u32[]{:S(2)}, u32[]{:S(2)}) %collective-permute-start.5) | collective-permute-done | bytes 200736 | tf_op jit(solution)/shard_map/ppermute | solution.py:845
  93.8 4.9 %shard_map.373 = (bf16[448,1024]{1,0:T(8,128)(2,1)}, f32[392,448]{1,0:T(8,128)}, bf16[392,512]{1,0:T(8,128)(2,1)}, f32[392,1024]{1,0:T(8,128)}, f32[32,4,640]{2,1,0:T(4,128)}) custom-call(f32[5]{0:T(128)} %pad_maximum_fusion.3.sc, bf16[392,512]{1,0:T(8,128)(2,1)} %convolution_convert_fusion.theta, f32[392,4]{1,0:T(8,128)} %copy.67.place, ...), custom_call_target="tpu_custom_call" | custom-call | flops 770703360 | bytes 7020160 | tf_op jit(solution)/shard_map/pallas_call | solution.py:64
  98.7 5.0 %all-to-all-start.3 = ((f32[32,4,640]{2,1,0:T(4,128)}), f32[32,4,640]{2,1,0:T(4,128)S(1)}, u32[]{:S(2)}, u32[]{:S(2)}) async-start(f32[32,4,640]{2,1,0:T(4,128)} %get-tuple-element.147), calls=%async_computation.3 | async-start | bytes 655360 | tf_op jit(solution)/shard_map/all_to_all | solution.py:49
  104.4 10.1 %all-to-all-done.3.copies_in = f32[32,4,640]{2,1,0:T(4,128)S(1)} async-done(((f32[32,4,640]{2,1,0:T(4,128)}), f32[32,4,640]{2,1,0:T(4,128)S(1)}, u32[]{:S(2)}, u32[]{:S(2)}) %all-to-all-start.3) | async-done | bytes 327712 | tf_op jit(solution)/shard_map/all_to_all | solution.py:49
  115.2 5.7 %shard_map.374 = (bf16[392,1024]{1,0:T(8,128)(2,1)}, bf16[392,448]{1,0:T(8,128)(2,1)}, f32[1,1024]{1,0:T(1,128)}, f32[1,1024]{1,0:T(1,128)}, f32[1,1024]{1,0:T(1...) custom-call(f32[5]{0:T(128)} %pad_maximum_fusion.3.sc, ...), custom_call_target="tpu_custom_call" | custom-call | flops 950534144 | bytes 8182400 | tf_op jit(solution)/shard_map/pallas_call | solution.py:64
  126.1 7.2 %shard_map.375 = (bf16[4,2048,128]{2,1,0:T(8,128)(2,1)}, bf16[4,2048,128]{2,1,0:T(8,128)(2,1)}, f32[392,1024]{1,0:T(8,128)}, bf16[392,512]{1,0:T(8,128)(2,1)}) custom-call(s32[5]{0:T(128)} %stack.57.bits, bf16[392,448]{1,0:T(8,128)(2,1)} %get-tuple-element.155.d_logits, bf16[392,1024]{1,0:T(8,128)(2,1)} %cot.5, bf16[1024,512]{1,0:T(8,128)(2,1)} %w.12, ...), custom_call_target="tpu_custom_call" | custom-call | flops 1412956160 | bytes 8272896 | tf_op jit(solution)/shard_map/pallas_call | solution.py:600
  133.4 6.9 %collective-permute-done.8.refs_1_ = bf16[784,128]{1,0:T(8,128)(2,1)S(1)} collective-permute-done((bf16[784,128]{1,0:T(8,128)(2,1)}, bf16[784,128]{1,0:T(8,128)(2,1)S(1)}, u32[]{:S(2)}, u32[]{:S(2)}) %collective-permute-start.8) | collective-permute-done | bytes 200736 | tf_op jit(solution)/shard_map/ppermute | solution.py:874
  141.0 6.6 %shard_map.376 = (bf16[224,1024]{1,0:T(8,128)(2,1)}, f32[392,1024]{1,0:T(8,128)}, f32[32,8,256]{2,1,0:T(8,128)}) custom-call(f32[5]{0:T(128)} %pad_maximum_fusion.3.sc, f32[112,1024]{1,0:T(8,128)} %get-tuple-element.153.own, f32[112,1]{1,0:T(8,128)} %copy.70.counts, bf16[1024,512]{1,0:T(8,128)(2,1)} %w_key.3, bf16[1024,512]{1,0:T(8,128)(2,1)} %w_value.3, ...), custom_call_target="tpu_custom_call" | custom-call | flops 414711808 | bytes 9691072 | tf_op jit(solution)/shard_map/pallas_call | solution.py:64
  147.7 4.3 %all-to-all-start.5 = ((f32[32,8,256]{2,1,0:T(8,128)}), f32[32,8,256]{2,1,0:T(8,128)S(1)}, u32[]{:S(2)}, u32[]{:S(2)}) async-start(f32[32,8,256]{2,1,0:T(8,128)} %get-tuple-element.162), calls=%async_computation.5 | async-start | bytes 524288 | tf_op jit(solution)/shard_map/all_to_all | solution.py:49
  152.0 3.3 %shard_map.377 = (bf16[4,2048,128]{2,1,0:T(8,128)(2,1)}, bf16[4,2048,128]{2,1,0:T(8,128)(2,1)}) custom-call(s32[5]{0:T(128)} %stack.57.bits, bf16[4,2048,128]{2,1,0:T(8,128)(2,1)} %get-tuple-element.163.send_in, bf16[4,2048,128]{2,1,0:T(8,128)(2,1)} %get-tuple-element.164.keep_in, ...), custom_call_target="tpu_custom_call", output_to_operand_aliasing={{0}: (1, {}), {1}: (2, {})} | custom-call | flops 469762048 | bytes 4063232 | tf_op jit(solution)/shard_map/pallas_call | solution.py:600
  155.3 6.8 %all-to-all-done.5.copies_in = f32[32,8,256]{2,1,0:T(8,128)S(1)} async-done(((f32[32,8,256]{2,1,0:T(8,128)}), f32[32,8,256]{2,1,0:T(8,128)S(1)}, u32[]{:S(2)}, u32[]{:S(2)}) %all-to-all-start.5) | async-done | bytes 262176 | tf_op jit(solution)/shard_map/all_to_all | solution.py:49
  162.9 3.9 %shard_map.378 = (bf16[392,1024]{1,0:T(8,128)(2,1)}, f32[392,256]{1,0:T(8,128)}, f32[32,2,256]{2,1,0:T(2,128)}, f32[1,1024]{1,0:T(1,128)}, f32[1,1024]{1,0:T(1,128)}) custom-call(f32[5]{0:T(128)} %pad_maximum_fusion.3.sc, f32[32,8,256]{2,1,0:T(8,128)} %copy-done.7, f32[2,1024]{1,0:T(2,128)} %get-tuple-element.154.stats_3, f32[1,1024]{1,0:T(1,128)} %bitcast.40, ...), custom_call_target="tpu_custom_call" | custom-call | flops 205520896 | bytes 5699712 | tf_op jit(solution)/shard_map/pallas_call | solution.py:64
  166.7 2.7 %all-to-all-start.6 = ((f32[32,2,256]{2,1,0:T(2,128)}), f32[32,2,256]{2,1,0:T(2,128)S(1)}, u32[]{:S(2)}, u32[]{:S(2)}) async-start(f32[32,2,256]{2,1,0:T(2,128)} %get-tuple-element.173), calls=%async_computation.6 | async-start | bytes 131072 | tf_op jit(solution)/shard_map/all_to_all | solution.py:49
  169.5 2.6 shard_map.379
  172.1 4.0 %shard_map.380 = (bf16[2,1024,128]{2,1,0:T(8,128)(2,1)}, bf16[2,1024,128]{2,1,0:T(8,128)(2,1)}, bf16[2,1024,128]{2,1,0:T(8,128)(2,1)}, bf16[2,1024,128]{2,1,0:T(8,128)(2,1)}) custom-call(s32[5]{0:T(128)} %stack.57.bits, bf16[4,2048,128]{2,1,0:T(8,128)(2,1)} %get-tuple-element.178.keep_in, bf16[4,2048,128]{2,1,0:T(8,128)(2,1)} %copy-done.3), custom_call_target="tpu_custom_call" | custom-call | bytes 6291456 | tf_op jit(solution)/shard_map/pallas_call | solution.py:64
  179.5 4.2 %shard_map.381 = (bf16[392,256]{1,0:T(8,128)(2,1)}, f32[392,256]{1,0:T(8,128)}, f32[32,2,256]{2,1,0:T(2,128)}, f32[1,256]{1,0:T(1,128)}, f32[1,256]{1,0:T(1,128)...) custom-call(f32[5]{0:T(128)} %pad_maximum_fusion.3.sc, f32[32,2,256]{2,1,0:T(2,128)} %copy-done.22, ...), custom_call_target="tpu_custom_call" | custom-call | flops 462422016 | bytes 3333248 | tf_op jit(solution)/shard_map/pallas_call | solution.py:64
  183.7 3.7 %all-to-all-start.7 = ((f32[32,2,256]{2,1,0:T(2,128)}), f32[32,2,256]{2,1,0:T(2,128)S(1)}, u32[]{:S(2)}, u32[]{:S(2)}) async-start(f32[32,2,256]{2,1,0:T(2,128)} %get-tuple-element.185), calls=%async_computation.7 | async-start | bytes 131072 | tf_op jit(solution)/shard_map/all_to_all | solution.py:49
  187.4 3.7 %collective-permute-start.13 = (bf16[196,256]{1,0:T(8,128)(2,1)}, bf16[196,256]{1,0:T(8,128)(2,1)S(1)}, u32[]{:S(2)}, u32[]{:S(2)}) collective-permute-start(bf16[196,256]{1,0:T(8,128)(2,1)} %get-tuple-element.196), channel_id=1, source_target_pairs={{0,1},{1,2},{2,3},{4,5},{5,6},{6,7},{8,9},{9,10},{10,11},{12,13},{... | collective-permute-start | bytes 301064 | tf_op jit(solution)/shard_map/ppermute | solution.py:941
  193.4 3.5 %shard_map.382 = (bf16[4,1600,128]{2,1,0:T(8,128)(2,1)}, bf16[4,1600,128]{2,1,0:T(8,128)(2,1)}) custom-call(s32[5]{0:T(128)} %stack.57.bits, bf16[4,1600,128]{2,1,0:T(8,128)(2,1)} %get-tuple-element.176.send_in, bf16[4,1600,128]{2,1,0:T(8,128)(2,1)} %get-tuple-element.186.keep_in, ...), custom_call_target="tpu_custom_call", output_to_operand_aliasing={{0}: (1, {}), {1}: (2, {})} | custom-call | flops 462422016 | bytes 3776512 | tf_op jit(solution)/shard_map/pallas_call | solution.py:600
  198.5 5.0 %shard_map.383 = (bf16[4,1600,128]{2,1,0:T(8,128)(2,1)}, bf16[4,1600,128]{2,1,0:T(8,128)(2,1)}, bf16[392,768]{1,0:T(8,128)(2,1)}, f32[1,256]{1,0:T(1,128)}, f32[1,256]{1,0:T(1,128)}) custom-call(s32[5]{0:T(128)} %stack.57.bits, f32[5]{0:T(128)} %pad_maximum_fusion.3.sc, ...), custom_call_target="tpu_custom_call", output_to_operand_aliasing={{0}: (2, {}), {1}: (3, {})} | custom-call | flops 616562688 | bytes 4442784 | tf_op jit(solution)/shard_map/pallas_call | solution.py:600
  203.6 2.7 shard_map.387
  210.4 3.5 %shard_map.384 = (bf16[2,800,128]{2,1,0:T(8,128)(2,1)}, bf16[2,800,128]{2,1,0:T(8,128)(2,1)}, bf16[2,800,128]{2,1,0:T(8,128)(2,1)}, bf16[2,800,128]{2,1,0:T(8,128)(2,1)}) custom-call(s32[5]{0:T(128)} %stack.57.bits, bf16[4,1600,128]{2,1,0:T(8,128)(2,1)} %get-tuple-element.201.keep_in, bf16[4,1600,128]{2,1,0:T(8,128)(2,1)} %copy-done.4), custom_call_target="tpu_custom_call" | custom-call | bytes 4915200 | tf_op jit(solution)/shard_map/pallas_call | solution.py:64
  218.4 4.1 %shard_map.385 = f32[392,1024]{1,0:T(8,128)} custom-call(bf16[392,768]{1,0:T(8,128)(2,1)} %get-tuple-element.204.d_taps, bf16[3,1024,256]{2,1,0:T(8,128)(2,1)} %w.15, f32[392,1024]{1,0:T(8,128)} %get-tuple-element.169.d_summed), custom_call_target="tpu_custom_call" | custom-call | flops 616562688 | bytes 5386240 | tf_op jit(solution)/shard_map/pallas_call | solution.py:64
  222.5 2.9 %collective-permute-done.16.received_1 = bf16[2,800,128]{2,1,0:T(8,128)(2,1)S(1)} collective-permute-done((bf16[2,800,128]{2,1,0:T(8,128)(2,1)}, bf16[2,800,128]{2,1,0:T(8,128)(2,1)S(1)}, u32[]{:S(2)}, u32[]{:S(2)}) %collective-permute-start.16) | collective-permute-done | bytes 409632 | tf_op jit(solution)/shard_map/ppermute | solution.py:637
  226.4 2.4 shard_map.386
  231.1 2.8 %collective-permute-start.24 = (bf16[1,1024,128]{2,1,0:T(8,128)(2,1)S(1)}, bf16[1,1024,128]{2,1,0:T(8,128)(2,1)S(1)}, u32[]{:S(2)}, u32[]{:S(2)}) collective-permute-start(bf16[1,1024,128]{2,1,0:T(8,128)(2,1)S(1)} %add_convert_fusion.2), channel_id=1, source_target_pairs={{0,2},{1,3},{2,0},{3,1},{4,6},{5,7},{6,4},{7,5},{8,10},{9,11},{10,... | collective-permute-start | bytes 786440 | tf_op jit(solution)/shard_map/ppermute | solution.py:684
  238.5 6.3 %collective-permute-done.24 = bf16[1,1024,128]{2,1,0:T(8,128)(2,1)S(1)} collective-permute-done((bf16[1,1024,128]{2,1,0:T(8,128)(2,1)S(1)}, bf16[1,1024,128]{2,1,0:T(8,128)(2,1)S(1)}, u32[]{:S(2)}, u32[]{:S(2)}) %collective-permute-start.24) | collective-permute-done | bytes 262176 | tf_op jit(solution)/shard_map/ppermute | solution.py:684
  246.8 5.0 %collective-permute-start.25 = (bf16[1,800,128]{2,1,0:T(8,128)(2,1)S(1)}, bf16[1,800,128]{2,1,0:T(8,128)(2,1)S(1)}, u32[]{:S(2)}, u32[]{:S(2)}) collective-permute-start(bf16[1,800,128]{2,1,0:T(8,128)(2,1)S(1)} %add_convert_fusion.4), channel_id=1, source_target_pairs={{0,2},{1,3},{2,0},{3,1},{4,6},{5,7},{6,4},{7,5},{8,10},{9,11},{10,... | collective-permute-start | bytes 614408 | tf_op jit(solution)/shard_map/ppermute | solution.py:684
  251.7 5.6 %collective-permute-done.25 = bf16[1,800,128]{2,1,0:T(8,128)(2,1)S(1)} collective-permute-done((bf16[1,800,128]{2,1,0:T(8,128)(2,1)S(1)}, bf16[1,800,128]{2,1,0:T(8,128)(2,1)S(1)}, u32[]{:S(2)}, u32[]{:S(2)}) %collective-permute-start.25) | collective-permute-done | bytes 204832 | tf_op jit(solution)/shard_map/ppermute | solution.py:684
  257.4 3.7 %collective-permute-start.27 = (bf16[1,800,128]{2,1,0:T(8,128)(2,1)S(1)}, bf16[1,800,128]{2,1,0:T(8,128)(2,1)S(1)}, u32[]{:S(2)}, u32[]{:S(2)}) collective-permute-start(bf16[1,800,128]{2,1,0:T(8,128)(2,1)S(1)} %add_convert_fusion.3.mine), channel_id=1, source_target_pairs={{0,1},{1,0},{2,3},{3,2},{4,5},{5,4},{6,7},{7,6},{8,9},{9,8},{10,11... | collective-permute-start | bytes 614408 | tf_op jit(solution)/shard_map/ppermute | solution.py:695
  262.5 2.0 shard_map.389
  265.6 2.0 shard_map.388
  (193 shorter events, 54.4 us)
Async XLA Ops:
  4.0 12.5 %collective-permute-start = (f32[196,256]{1,0:T(8,128)}, f32[196,256]{1,0:T(8,128)S(1)}, u32[]{:S(2)}, u32[]{:S(2)}) collective-permute-start(f32[196,256]{1,0:T(8,128)} %get-tuple-element.133), channel_id=1, source_target_pairs={{0,1},{1,2},{2,3},{4,5},{5,6},{6,7},{8,9},{9,10},{10,11},{12,13},{... | collective-permute-start | bytes 602120 | tf_op jit(solution)/shard_map/ppermute | solution.py:801
  8.9 8.6 %collective-permute-start.1 = (f32[196,256]{1,0:T(8,128)}, f32[196,256]{1,0:T(8,128)S(1)}, u32[]{:S(2)}, u32[]{:S(2)}) collective-permute-start(f32[196,256]{1,0:T(8,128)} %get-tuple-element.134), channel_id=1, source_target_pairs={{1,0},{2,1},{3,2},{5,4},{6,5},{7,6},{9,8},{10,9},{11,10},{13,12},{... | collective-permute-start | bytes 602120 | tf_op jit(solution)/shard_map/ppermute | solution.py:802
  18.2 27.1 %copy-start.1 = (bf16[392,1024]{1,0:T(8,128)(2,1)S(1)}, bf16[392,1024]{1,0:T(8,128)(2,1)}, u32[]{:S(2)}) copy-start(bf16[392,1024]{1,0:T(8,128)(2,1)} %cot.5) | copy-start | bytes 2408452
  20.8 13.4 %all-to-all-start = ((f32[32,2,256]{2,1,0:T(2,128)}), f32[32,2,256]{2,1,0:T(2,128)S(1)}, u32[]{:S(2)}, u32[]{:S(2)}) async-start(f32[32,2,256]{2,1,0:T(2,128)} %get-tuple-element.135), calls=%async_computation | async-start | bytes 131072 | tf_op jit(solution)/shard_map/all_to_all | solution.py:49
  28.1 17.4 %collective-permute-start.2 = (bf16[196,256]{1,0:T(8,128)(2,1)}, bf16[196,256]{1,0:T(8,128)(2,1)S(1)}, u32[]{:S(2)}, u32[]{:S(2)}) collective-permute-start(bf16[196,256]{1,0:T(8,128)(2,1)} %get-tuple-element.138), channel_id=1, source_target_pairs={{0,1},{1,2},{2,3},{4,5},{5,6},{6,7},{8,9},{9,10},{10,11},{12,13},{... | collective-permute-start | bytes 301064 | tf_op jit(solution)/shard_map/ppermute | solution.py:810
  31.8 13.7 %collective-permute-start.3 = (bf16[196,256]{1,0:T(8,128)(2,1)}, bf16[196,256]{1,0:T(8,128)(2,1)S(1)}, u32[]{:S(2)}, u32[]{:S(2)}) collective-permute-start(bf16[196,256]{1,0:T(8,128)(2,1)} %get-tuple-element.139), channel_id=1, source_target_pairs={{1,0},{2,1},{3,2},{5,4},{6,5},{7,6},{9,8},{10,9},{11,10},{13,12},{... | collective-permute-start | bytes 301064 | tf_op jit(solution)/shard_map/ppermute | solution.py:811
  39.7 19.3 %copy-start.45 = (f32[1,448]{1,0:T(1,128)S(1)}, f32[1,448]{1,0:T(1,128)}, u32[]{:S(2)}) copy-start(f32[1,448]{1,0:T(1,128)} %constant.79) | copy-start | bytes 5380
  39.7 19.9 %copy-start.25 = (f32[112,392]{1,0:T(8,128)S(1)}, f32[112,392]{1,0:T(8,128)}, u32[]{:S(2)}) copy-start(f32[112,392]{1,0:T(8,128)} %constant.68.clone) | copy-start | bytes 526852
  39.7 13.1 %all-to-all-start.1 = ((f32[32,2,256]{2,1,0:T(2,128)}), f32[32,2,256]{2,1,0:T(2,128)S(1)}, u32[]{:S(2)}, u32[]{:S(2)}) async-start(f32[32,2,256]{2,1,0:T(2,128)} %get-tuple-element.137), calls=%async_computation.1 | async-start | bytes 131072 | tf_op jit(solution)/shard_map/all_to_all | solution.py:49
  45.5 38.0 %copy-start.36 = (bf16[196,256]{1,0:T(8,128)(2,1)}, bf16[196,256]{1,0:T(8,128)(2,1)S(1)}, u32[]{:S(2)}) copy-start(bf16[196,256]{1,0:T(8,128)(2,1)S(1)} %collective-permute-done.2.pre_before) | copy-start | bytes 301060
  45.5 38.0 %copy-start.37 = (bf16[196,256]{1,0:T(8,128)(2,1)}, bf16[196,256]{1,0:T(8,128)(2,1)S(1)}, u32[]{:S(2)}) copy-start(bf16[196,256]{1,0:T(8,128)(2,1)S(1)} %collective-permute-done.3.pre_after) | copy-start | bytes 301060
  56.4 11.5 %all-to-all-start.2 = ((f32[32,2,640]{2,1,0:T(2,128)}), f32[32,2,640]{2,1,0:T(2,128)S(1)}, u32[]{:S(2)}, u32[]{:S(2)}) async-start(f32[32,2,640]{2,1,0:T(2,128)} %get-tuple-element.142), calls=%async_computation.2 | async-start | bytes 327680 | tf_op jit(solution)/shard_map/all_to_all | solution.py:49
  73.3 10.2 %collective-permute-start.4 = (bf16[784,128]{1,0:T(8,128)(2,1)}, bf16[784,128]{1,0:T(8,128)(2,1)S(1)}, u32[]{:S(2)}, u32[]{:S(2)}) collective-permute-start(bf16[784,128]{1,0:T(8,128)(2,1)} %get-tuple-element.145.refs_0_), channel_id=1, source_target_pairs={{0,1},{1,0},{2,3},{3,2},{4,5},{5,4},{6,7},{7,6},{8,9},{9,8},{10,11... | collective-permute-start | bytes 602120 | tf_op jit(solution)/shard_map/ppermute | solution.py:845
  73.3 19.0 %collective-permute-start.5 = (bf16[784,128]{1,0:T(8,128)(2,1)}, bf16[784,128]{1,0:T(8,128)(2,1)S(1)}, u32[]{:S(2)}, u32[]{:S(2)}) collective-permute-start(bf16[784,128]{1,0:T(8,128)(2,1)} %get-tuple-element.145.refs_0_), channel_id=1, source_target_pairs={{0,2},{1,3},{2,0},{3,1},{4,6},{5,7},{6,4},{7,5},{8,10},{9,11},{10,... | collective-permute-start | bytes 602120 | tf_op jit(solution)/shard_map/ppermute | solution.py:845
  75.2 17.2 %collective-permute-start.6 = (bf16[784,128]{1,0:T(8,128)(2,1)}, bf16[784,128]{1,0:T(8,128)(2,1)S(1)}, u32[]{:S(2)}, u32[]{:S(2)}) collective-permute-start(bf16[784,128]{1,0:T(8,128)(2,1)} %get-tuple-element.145.refs_0_), channel_id=1, source_target_pairs={{0,3},{1,2},{2,1},{3,0},{4,7},{5,6},{6,5},{7,4},{8,11},{9,10},{10,... | collective-permute-start | bytes 602120 | tf_op jit(solution)/shard_map/ppermute | solution.py:845
  78.4 20.2 %all-to-all-start.4 = ((f32[32,2,512]{2,1,0:T(2,128)}), f32[32,2,512]{2,1,0:T(2,128)S(1)}, u32[]{:S(2)}, u32[]{:S(2)}) async-start(f32[32,2,512]{2,1,0:T(2,128)} %broadcast_in_dim.42), calls=%async_computation.4 | async-start | bytes 262144 | tf_op jit(solution)/shard_map/all_to_all | solution.py:49
  83.5 20.8 %copy-start.29 = (f32[392,112]{1,0:T(8,128)S(1)}, f32[392,112]{1,0:T(8,128)}, u32[]{:S(2)}) copy-start(f32[392,112]{1,0:T(8,128)} %constant.69.clone) | copy-start | bytes 526852
  98.7 15.8 %all-to-all-start.3 = ((f32[32,4,640]{2,1,0:T(4,128)}), f32[32,4,640]{2,1,0:T(4,128)S(1)}, u32[]{:S(2)}, u32[]{:S(2)}) async-start(f32[32,4,640]{2,1,0:T(4,128)} %get-tuple-element.147), calls=%async_computation.3 | async-start | bytes 655360 | tf_op jit(solution)/shard_map/all_to_all | solution.py:49
  120.9 12.4 %collective-permute-start.7 = (bf16[784,128]{1,0:T(8,128)(2,1)}, bf16[784,128]{1,0:T(8,128)(2,1)S(1)}, u32[]{:S(2)}, u32[]{:S(2)}) collective-permute-start(bf16[784,128]{1,0:T(8,128)(2,1)} %get-tuple-element.159), channel_id=1, source_target_pairs={{0,1},{1,0},{2,3},{3,2},{4,5},{5,4},{6,7},{7,6},{8,9},{9,8},{10,11... | collective-permute-start | bytes 602120 | tf_op jit(solution)/shard_map/ppermute | solution.py:874
  122.7 17.6 %collective-permute-start.8 = (bf16[784,128]{1,0:T(8,128)(2,1)}, bf16[784,128]{1,0:T(8,128)(2,1)S(1)}, u32[]{:S(2)}, u32[]{:S(2)}) collective-permute-start(bf16[784,128]{1,0:T(8,128)(2,1)} %get-tuple-element.160), channel_id=1, source_target_pairs={{0,2},{1,3},{2,0},{3,1},{4,6},{5,7},{6,4},{7,5},{8,10},{9,11},{10,... | collective-permute-start | bytes 602120 | tf_op jit(solution)/shard_map/ppermute | solution.py:874
  123.7 16.6 %collective-permute-start.9 = (bf16[784,128]{1,0:T(8,128)(2,1)}, bf16[784,128]{1,0:T(8,128)(2,1)S(1)}, u32[]{:S(2)}, u32[]{:S(2)}) collective-permute-start(bf16[784,128]{1,0:T(8,128)(2,1)} %get-tuple-element.161), channel_id=1, source_target_pairs={{0,3},{1,2},{2,1},{3,0},{4,7},{5,6},{6,5},{7,4},{8,11},{9,10},{10,... | collective-permute-start | bytes 602120 | tf_op jit(solution)/shard_map/ppermute | solution.py:874
  147.7 14.5 %all-to-all-start.5 = ((f32[32,8,256]{2,1,0:T(8,128)}), f32[32,8,256]{2,1,0:T(8,128)S(1)}, u32[]{:S(2)}, u32[]{:S(2)}) async-start(f32[32,8,256]{2,1,0:T(8,128)} %get-tuple-element.162), calls=%async_computation.5 | async-start | bytes 524288 | tf_op jit(solution)/shard_map/all_to_all | solution.py:49
  162.2 4.6 %collective-permute-start.10 = (bf16[4,2048,128]{2,1,0:T(8,128)(2,1)}, bf16[4,2048,128]{2,1,0:T(8,128)(2,1)S(1)}, u32[]{:S(2)}, u32[]{:S(2)}) collective-permute-start(bf16[4,2048,128]{2,1,0:T(8,128)(2,1)} %get-tuple-element.172), channel_id=1, source_target_pairs={{0,4},{4,0},{8,12},{12,8},{16,20},{20,16},{24,28},{28,24},{1,5},{5... | collective-permute-start | bytes 6291464 | tf_op jit(solution)/shard_map/ppermute | solution.py:619
  166.7 10.2 %all-to-all-start.6 = ((f32[32,2,256]{2,1,0:T(2,128)}), f32[32,2,256]{2,1,0:T(2,128)S(1)}, u32[]{:S(2)}, u32[]{:S(2)}) async-start(f32[32,2,256]{2,1,0:T(2,128)} %get-tuple-element.173), calls=%async_computation.6 | async-start | bytes 131072 | tf_op jit(solution)/shard_map/all_to_all | solution.py:49
  177.0 19.9 %collective-permute-start.11 = (bf16[2,1024,128]{2,1,0:T(8,128)(2,1)}, bf16[2,1024,128]{2,1,0:T(8,128)(2,1)S(1)}, u32[]{:S(2)}, u32[]{:S(2)}) collective-permute-start(bf16[2,1024,128]{2,1,0:T(8,128)(2,1)} %get-tuple-element.190), channel_id=1, source_target_pairs={{0,8},{4,12},{8,0},{12,4},{16,24},{20,28},{24,16},{28,20},{1,9},{5... | collective-permute-start | bytes 1572872 | tf_op jit(solution)/shard_map/ppermute | solution.py:637
  177.9 19.0 %collective-permute-start.12 = (bf16[2,1024,128]{2,1,0:T(8,128)(2,1)}, bf16[2,1024,128]{2,1,0:T(8,128)(2,1)S(1)}, u32[]{:S(2)}, u32[]{:S(2)}) collective-permute-start(bf16[2,1024,128]{2,1,0:T(8,128)(2,1)} %get-tuple-element.191), channel_id=1, source_target_pairs={{0,16},{4,20},{8,24},{12,28},{16,0},{20,4},{24,8},{28,12},{1,17},{... | collective-permute-start | bytes 1572872 | tf_op jit(solution)/shard_map/ppermute | solution.py:637
  183.7 13.2 %all-to-all-start.7 = ((f32[32,2,256]{2,1,0:T(2,128)}), f32[32,2,256]{2,1,0:T(2,128)S(1)}, u32[]{:S(2)}, u32[]{:S(2)}) async-start(f32[32,2,256]{2,1,0:T(2,128)} %get-tuple-element.185), calls=%async_computation.7 | async-start | bytes 131072 | tf_op jit(solution)/shard_map/all_to_all | solution.py:49
  187.4 9.5 %collective-permute-start.13 = (bf16[196,256]{1,0:T(8,128)(2,1)}, bf16[196,256]{1,0:T(8,128)(2,1)S(1)}, u32[]{:S(2)}, u32[]{:S(2)}) collective-permute-start(bf16[196,256]{1,0:T(8,128)(2,1)} %get-tuple-element.196), channel_id=1, source_target_pairs={{0,1},{1,2},{2,3},{4,5},{5,6},{6,7},{8,9},{9,10},{10,11},{12,13},{... | collective-permute-start | bytes 301064 | tf_op jit(solution)/shard_map/ppermute | solution.py:941
  191.1 6.8 %collective-permute-start.14 = (bf16[196,256]{1,0:T(8,128)(2,1)}, bf16[196,256]{1,0:T(8,128)(2,1)S(1)}, u32[]{:S(2)}, u32[]{:S(2)}) collective-permute-start(bf16[196,256]{1,0:T(8,128)(2,1)} %get-tuple-element.197), channel_id=1, source_target_pairs={{1,0},{2,1},{3,2},{5,4},{6,5},{7,6},{9,8},{10,9},{11,10},{13,12},{... | collective-permute-start | bytes 301064 | tf_op jit(solution)/shard_map/ppermute | solution.py:942
  203.5 5.7 %collective-permute-start.15 = (bf16[4,1600,128]{2,1,0:T(8,128)(2,1)}, bf16[4,1600,128]{2,1,0:T(8,128)(2,1)S(1)}, u32[]{:S(2)}, u32[]{:S(2)}) collective-permute-start(bf16[4,1600,128]{2,1,0:T(8,128)(2,1)} %get-tuple-element.202), channel_id=1, source_target_pairs={{0,4},{4,0},{8,12},{12,8},{16,20},{20,16},{24,28},{28,24},{1,5},{5... | collective-permute-start | bytes 4915208 | tf_op jit(solution)/shard_map/ppermute | solution.py:619
  206.3 8.9 %collective-permute-start.18 = (bf16[1,1024,128]{2,1,0:T(8,128)(2,1)}, bf16[1,1024,128]{2,1,0:T(8,128)(2,1)S(1)}, u32[]{:S(2)}, u32[]{:S(2)}) collective-permute-start(bf16[1,1024,128]{2,1,0:T(8,128)(2,1)} %get-tuple-element.217), channel_id=1, source_target_pairs={{0,16},{4,20},{8,24},{12,28},{16,0},{20,4},{24,8},{28,12},{1,17},{... | collective-permute-start | bytes 786440 | tf_op jit(solution)/shard_map/ppermute | solution.py:637
  207.7 8.6 %collective-permute-start.19 = (bf16[1,1024,128]{2,1,0:T(8,128)(2,1)}, bf16[1,1024,128]{2,1,0:T(8,128)(2,1)S(1)}, u32[]{:S(2)}, u32[]{:S(2)}) collective-permute-start(bf16[1,1024,128]{2,1,0:T(8,128)(2,1)} %get-tuple-element.219), channel_id=1, source_target_pairs={{0,8},{4,12},{8,0},{12,4},{16,24},{20,28},{24,16},{28,20},{1,9},{5... | collective-permute-start | bytes 786440 | tf_op jit(solution)/shard_map/ppermute | solution.py:637
  213.9 11.5 %collective-permute-start.16 = (bf16[2,800,128]{2,1,0:T(8,128)(2,1)}, bf16[2,800,128]{2,1,0:T(8,128)(2,1)S(1)}, u32[]{:S(2)}, u32[]{:S(2)}) collective-permute-start(bf16[2,800,128]{2,1,0:T(8,128)(2,1)} %get-tuple-element.205), channel_id=1, source_target_pairs={{0,8},{4,12},{8,0},{12,4},{16,24},{20,28},{24,16},{28,20},{1,9},{5... | collective-permute-start | bytes 1228808 | tf_op jit(solution)/shard_map/ppermute | solution.py:637
  214.4 11.2 %collective-permute-start.17 = (bf16[2,800,128]{2,1,0:T(8,128)(2,1)}, bf16[2,800,128]{2,1,0:T(8,128)(2,1)S(1)}, u32[]{:S(2)}, u32[]{:S(2)}) collective-permute-start(bf16[2,800,128]{2,1,0:T(8,128)(2,1)} %get-tuple-element.208), channel_id=1, source_target_pairs={{0,16},{4,20},{8,24},{12,28},{16,0},{20,4},{24,8},{28,12},{1,17},{... | collective-permute-start | bytes 1228808 | tf_op jit(solution)/shard_map/ppermute | solution.py:637
  216.5 12.3 %collective-permute-start.20 = (bf16[1,1024,128]{2,1,0:T(8,128)(2,1)S(1)}, bf16[1,1024,128]{2,1,0:T(8,128)(2,1)S(1)}, u32[]{:S(2)}, u32[]{:S(2)}) collective-permute-start(bf16[1,1024,128]{2,1,0:T(8,128)(2,1)S(1)} %select_convert_fusion.1), channel_id=1, source_target_pairs={{0,1},{1,0},{2,3},{3,2},{4,5},{5,4},{6,7},{7,6},{8,9},{9,8},{10,11... | collective-permute-start | bytes 786440 | tf_op jit(solution)/shard_map/ppermute | solution.py:671
  228.8 6.2 %collective-permute-start.21 = (bf16[1,800,128]{2,1,0:T(8,128)(2,1)}, bf16[1,800,128]{2,1,0:T(8,128)(2,1)S(1)}, u32[]{:S(2)}, u32[]{:S(2)}) collective-permute-start(bf16[1,800,128]{2,1,0:T(8,128)(2,1)} %get-tuple-element.222), channel_id=1, source_target_pairs={{0,8},{4,12},{8,0},{12,4},{16,24},{20,28},{24,16},{28,20},{1,9},{5... | collective-permute-start | bytes 614408 | tf_op jit(solution)/shard_map/ppermute | solution.py:637
  230.3 6.1 %collective-permute-start.22 = (bf16[1,800,128]{2,1,0:T(8,128)(2,1)}, bf16[1,800,128]{2,1,0:T(8,128)(2,1)S(1)}, u32[]{:S(2)}, u32[]{:S(2)}) collective-permute-start(bf16[1,800,128]{2,1,0:T(8,128)(2,1)} %get-tuple-element.224), channel_id=1, source_target_pairs={{0,16},{4,20},{8,24},{12,28},{16,0},{20,4},{24,8},{28,12},{1,17},{... | collective-permute-start | bytes 614408 | tf_op jit(solution)/shard_map/ppermute | solution.py:637
  231.1 13.8 %collective-permute-start.24 = (bf16[1,1024,128]{2,1,0:T(8,128)(2,1)S(1)}, bf16[1,1024,128]{2,1,0:T(8,128)(2,1)S(1)}, u32[]{:S(2)}, u32[]{:S(2)}) collective-permute-start(bf16[1,1024,128]{2,1,0:T(8,128)(2,1)S(1)} %add_convert_fusion.2), channel_id=1, source_target_pairs={{0,2},{1,3},{2,0},{3,1},{4,6},{5,7},{6,4},{7,5},{8,10},{9,11},{10,... | collective-permute-start | bytes 786440 | tf_op jit(solution)/shard_map/ppermute | solution.py:684
  236.4 24.8 %copy-start.2 = (f32[392,1024]{1,0:T(8,128)S(1)}, f32[392,1024]{1,0:T(8,128)}, u32[]{:S(2)}) copy-start(f32[392,1024]{1,0:T(8,128)} %get-tuple-element.146.pre_4) | copy-start | bytes 4816900
  236.4 24.8 %copy-start.13 = (bf16[392,1024]{1,0:T(8,128)(2,1)S(1)}, bf16[392,1024]{1,0:T(8,128)(2,1)}, u32[]{:S(2)}) copy-start(bf16[392,1024]{1,0:T(8,128)(2,1)} %get-tuple-element.144.unit) | copy-start | bytes 2408452
  236.4 24.8 %copy-start.41 = (f32[1024]{0:T(1024)S(1)}, f32[1024]{0:T(1024)}, u32[]{:S(2)}) copy-start(f32[1024]{0:T(1024)} %param.41) | copy-start | bytes 12292
  236.4 24.7 %copy-start.42 = (f32[1024]{0:T(1024)S(1)}, f32[1024]{0:T(1024)}, u32[]{:S(2)}) copy-start(f32[1024]{0:T(1024)} %param.42) | copy-start | bytes 12292
  236.4 24.7 %copy-start.43 = (f32[1,1024]{1,0:T(1,128)S(1)}, f32[1,1024]{1,0:T(1,128)}, u32[]{:S(2)}) copy-start(f32[1,1024]{1,0:T(1,128)} %get-tuple-element.151) | copy-start | bytes 12292
  236.4 24.7 %copy-start.44 = (f32[1,1024]{1,0:T(1,128)S(1)}, f32[1,1024]{1,0:T(1,128)}, u32[]{:S(2)}) copy-start(f32[1,1024]{1,0:T(1,128)} %get-tuple-element.152) | copy-start | bytes 12292
  236.6 9.9 %collective-permute-start.23 = (bf16[1,800,128]{2,1,0:T(8,128)(2,1)S(1)}, bf16[1,800,128]{2,1,0:T(8,128)(2,1)S(1)}, u32[]{:S(2)}, u32[]{:S(2)}) collective-permute-start(bf16[1,800,128]{2,1,0:T(8,128)(2,1)S(1)} %select_convert_fusion.2), channel_id=1, source_target_pairs={{0,1},{1,0},{2,3},{3,2},{4,5},{5,4},{6,7},{7,6},{8,9},{9,8},{10,11... | collective-permute-start | bytes 614408 | tf_op jit(solution)/shard_map/ppermute | solution.py:671
  246.5 10.8 %collective-permute-start.26 = (bf16[1,1024,128]{2,1,0:T(8,128)(2,1)S(1)}, bf16[1,1024,128]{2,1,0:T(8,128)(2,1)S(1)}, u32[]{:S(2)}, u32[]{:S(2)}) collective-permute-start(bf16[1,1024,128]{2,1,0:T(8,128)(2,1)S(1)} %add_convert_fusion.1.mine), channel_id=1, source_target_pairs={{0,1},{1,0},{2,3},{3,2},{4,5},{5,4},{6,7},{7,6},{8,9},{9,8},{10,11... | collective-permute-start | bytes 786440 | tf_op jit(solution)/shard_map/ppermute | solution.py:695
  246.8 10.5 %collective-permute-start.25 = (bf16[1,800,128]{2,1,0:T(8,128)(2,1)S(1)}, bf16[1,800,128]{2,1,0:T(8,128)(2,1)S(1)}, u32[]{:S(2)}, u32[]{:S(2)}) collective-permute-start(bf16[1,800,128]{2,1,0:T(8,128)(2,1)S(1)} %add_convert_fusion.4), channel_id=1, source_target_pairs={{0,2},{1,3},{2,0},{3,1},{4,6},{5,7},{6,4},{7,5},{8,10},{9,11},{10,... | collective-permute-start | bytes 614408 | tf_op jit(solution)/shard_map/ppermute | solution.py:684
  257.4 7.5 %collective-permute-start.27 = (bf16[1,800,128]{2,1,0:T(8,128)(2,1)S(1)}, bf16[1,800,128]{2,1,0:T(8,128)(2,1)S(1)}, u32[]{:S(2)}, u32[]{:S(2)}) collective-permute-start(bf16[1,800,128]{2,1,0:T(8,128)(2,1)S(1)} %add_convert_fusion.3.mine), channel_id=1, source_target_pairs={{0,1},{1,0},{2,3},{3,2},{4,5},{5,4},{6,7},{7,6},{8,9},{9,8},{10,11... | collective-permute-start | bytes 614408 | tf_op jit(solution)/shard_map/ppermute | solution.py:695
  (38 other events, 191.6 us)

commit v6 on v5

--- a/solution.py
+++ b/solution.py
@@ -178,7 +178,23 @@
     padded[EDGE : EDGE + rows, :] = value
 
 
-def second_kernel(sc, copies_in, pre_1, gain, shift, place, w, pre_2, windows, copies, stats, padded):
+def fill_windows(value, place, padded, windows):
+    rows, width = value.shape
+    fill_padded(padded, value.astype(F32))
+    for tap in range(9):
+        down, right = tap // 3 - 1, tap % 3 - 1
+        start = EDGE + down * SIDE + right
+        window = padded[start : start + rows, :]
+        if tap != 4:
+            window = window * inside(place, down, right)
+        windows[:, tap * width : (tap + 1) * width] = window.astype(BF16)
+
+
+def windows_kernel(z_1, place, windows, padded):
+    fill_windows(z_1[...], place, padded, windows)
+
+
+def second_kernel(sc, copies_in, pre_1, gain, shift, place, w, pre_2, z_1, copies, stats, padded, windows):
     rows, width = pre_1.shape
     total = sc[0]
     sums = collect(copies_in)
@@ -186,14 +202,9 @@
     stats[0:1, :] = mean
     stats[1:2, :] = inv
     act = (pre_1[...] - mean) * inv * gain[...] + shift[...]
-    fill_padded(padded, (act * jax.nn.sigmoid(act)).astype(BF16).astype(F32))
-    for tap in range(9):
-        down, right = tap // 3 - 1, tap % 3 - 1
-        start = EDGE + down * SIDE + right
-        window = padded[start : start + rows, :]
-        if tap != 4:
-            window = window * inside(place, down, right)
-        windows[:, tap * width : (tap + 1) * width] = window.astype(BF16)
+    low = (act * jax.nn.sigmoid(act)).astype(BF16)
+    z_1[...] = low
+    fill_windows(low, place, padded, windows)
     pre_2[...] = dot(windows[...], w[...])
     valid = place[:, 0:1]
     for c in chunks(width):
@@ -249,7 +260,7 @@
 
 def attend_kernel(slots, keys, sc, theta, place, key_row, w, cot, *refs):
     blocks = refs[:slots]
-    kv, probs, attended, pre_4, copies, packed = refs[slots:]
+    kv, probs, attended, copies, packed = refs[slots:]
     inner, channels = w.shape
     size, lines = kv.shape[0] // slots, blocks[0].shape[0]
     packed[lines:, :] = jnp.zeros((packed.shape[0] - lines, LANE), F32)
@@ -268,7 +279,6 @@
     emit(copies, 0, column_sum(attended[...].astype(F32) * valid))
     for c in chunks(channels, 2 * LANE):
         hidden = dot(attended[...], w[:, c])
-        pre_4[:, c] = hidden
         emit(copies, inner + c.start, column_sum(hidden * hidden * valid))
         emit(copies, inner + channels + c.start, column_sum(cot[:, c].astype(F32) * hidden))
 
@@ -467,17 +477,7 @@
     split_out(bits[0], start, both, low, send, keep, sems)
 
 
-def space_grads_kernel(parts, start, bits, send_in, keep_in, windows, d_second, send, keep, both, low, sems):
-    width = d_second.shape[1]
-    wide = width // parts
-    for tap in range(9):
-        grad = dot_rows(windows[:, tap * width : (tap + 1) * width], d_second[...])
-        for p in range(parts):
-            put(both, p, tap * wide * width // LANE, grad[p * wide : (p + 1) * wide, :])
-    split_out(bits[0], start, both, low, send, keep, sems)
-
-
-def time_grads_kernel(frames, parts, start, bits, sc, send_in, keep_in, x, copies_in, stats_1, gain_1, d_act, pre_1, place, near, d_before, d_after, pre_before, pre_after, send, keep, d_taps, gain_out, shift_out, both, low, sems, whole, moved):
+def time_grads_kernel(frames, parts, start, bits, sc, send_in, keep_in, windows, d_second, x, copies_in, stats_1, gain_1, d_act, pre_1, place, near, d_before, d_after, pre_before, pre_after, send, keep, d_taps, gain_out, shift_out, both, low, sems, whole, moved):
     total = sc[0]
     width = pre_1.shape[1]
     sums = collect(copies_in)
@@ -505,9 +505,14 @@
         behind = d_prev if t == 0 else whole[(t - 1) * AREA : t * AREA, :]
         moved[here, :] = behind * sc[1 + t]
     d_taps[:, 2 * width :] = moved[...].astype(BF16)
+    step = width // parts
+    for tap in range(9):
+        grad = dot_rows(windows[:, tap * width : (tap + 1) * width], d_second[...])
+        for p in range(parts):
+            put(both, p, tap * step * width // LANE, grad[p * step : (p + 1) * step, :])
     wide = x.shape[1] // parts
     for p in range(parts):
-        put(both, p, 0, dot_rows(x[:, p * wide : (p + 1) * wide], d_taps[...]))
+        put(both, p, 9 * step * width // LANE, dot_rows(x[:, p * wide : (p + 1) * wide], d_taps[...]))
     split_out(bits[0], start, both, low, send, keep, sems)
 
 
@@ -809,15 +814,22 @@
     sums = trade(sums)
     pre_before = lax.ppermute(last, "grp", up)
     pre_after = lax.ppermute(first, "grp", down)
-    pre_2, windows, sums, stats_1 = call(
+    pre_2, z_1, sums, stats_1 = call(
         second_kernel,
-        [narrow_f32, ((rows, 9 * narrow), BF16), (small, F32), ((2, narrow), F32)],
+        [narrow_f32, ((rows, narrow), BF16), (small, F32), ((2, narrow), F32)],
         (scalars,), sums, pre_1, gain_1, shift_1, place,
         space_weight.reshape(9 * narrow, narrow),
+        scratch=[
+            pltpu.VMEM((rows + 2 * EDGE, narrow), F32), pltpu.VMEM((rows, 9 * narrow), BF16),
+        ],
+        flops=18 * rows * narrow * narrow,
+    )
+    sums = trade(sums)
+    (windows,) = call(
+        windows_kernel, [((rows, 9 * narrow), BF16)], (), z_1, place,
         scratch=[pltpu.VMEM((rows + 2 * EDGE, narrow), F32)],
-        flops=18 * rows * narrow * narrow,
-    )
-    sums = trade(sums)
+    )
+    sums, windows = tie(sums, windows)
     sums, pre_before, pre_after = tie(sums, pre_before, pre_after)
     z_2, pre_3, sums, stats_2 = call(
         third_kernel,
@@ -845,10 +857,10 @@
         lax.ppermute(kv_own, "grp", flip(grp_count, step)) for step in range(1, grp_count)
     ]
     theta = dot(unit, query_weight).astype(BF16)
-    kv_all, probs, attended, pre_4, sums = call(
+    kv_all, probs, attended, sums = call(
         functools.partial(attend_kernel, grp_count, own_keys),
         [
-            ((grp_count * size, 2 * inner), BF16), ((rows, grp_count * size), F32), ((rows, inner), BF16), wide_f32,
+            ((grp_count * size, 2 * inner), BF16), ((rows, grp_count * size), F32), ((rows, inner), BF16),
             ((copies, 4, (inner + 2 * channels) // 4), F32),
         ],
         (scalars,), theta, place, key_row, out_weight, cotangent, *kv,
@@ -856,6 +868,7 @@
         flops=2 * rows * inner * (2 * grp_count * size + channels),
     )
     sums = trade(sums)
+    pre_4 = dot(attended, out_weight)
 
     d_final, d_logits, mean_4, inv_4, gain_final_grad, shift_final_grad, d_kv, *d_sent = call(
         functools.partial(attend_back_kernel, grp_count, own_keys),
@@ -940,16 +953,14 @@
     sums = trade(sums)
     d_before = lax.ppermute(last, "grp", up)
     d_after = lax.ppermute(first, "grp", down)
-    bundle_2.add(
-        space_grads_kernel, expand_rows, 9 * tap_rows, windows, d_second,
-        flops=18 * rows * narrow * narrow,
-    )
     (_, _, got_1), (_, _, got_2) = bundle_1.parts
-    sums, bundle_2.send, got_1, got_2 = tie(sums, bundle_2.send, got_1, got_2)
+    sums, got_1, got_2 = tie(sums, got_1, got_2)
     bundle_1.parts[0][2], bundle_1.parts[1][2] = got_1, got_2
+    bundle_1.more(last=False)
+    sums = bundle_1.hold(sums)
     d_taps, gain_first_grad, shift_first_grad = bundle_2.add(
-        functools.partial(time_grads_kernel, frames), time_start, 3 * deep * narrow // LANE,
-        inputs, sums, stats_1, gain_1, d_act_1, pre_1, place, near, d_before, d_after,
+        functools.partial(time_grads_kernel, frames), expand_rows,
+        9 * tap_rows + 3 * deep * narrow // LANE, windows, d_second, inputs, sums, stats_1, gain_1, d_act_1, pre_1, place, near, d_before, d_after,
         pre_before, pre_after,
         extra=[((rows, 3 * narrow), BF16), ((1, narrow), F32), ((1, narrow), F32)],
         scratch=[pltpu.VMEM((rows, narrow), F32), pltpu.VMEM((rows, narrow), F32)],
@@ -957,9 +968,8 @@
         flops=6 * rows * narrow * channels,
     )
 
-    bundle_1.after([d_taps, d_taps])
     bundle_2.begin()
-    bundle_1.more()
+    bundle_1.turn()
     bundle_2.plane()
     bundle_2.turn()
     d_taps, _ = tie(d_taps, bundle_2.parts[0][1])

time: 269 us -> 268 us (level)
  waiting for transfers between devices: 72.7 us -> 67 us
  matrix products: 4.67 us -> 7.44 us
    all_to_all x8, waiting for transfers between devices: 33.9 us -> 28.4 us  [trade(): return lax.all_to_all(copies, ('pos', 'grp'), 0, 0, tiled=True)]
    pallas_call x17 -> x18, Pallas kernels: 64.3 us -> 67.4 us  [call(): pl.pallas_call(kernel, out_shape=shapes, in_specs=[pl.BlockSpec(memory_sp...]
    dot_general x2 -> x3, matrix products: 4.67 us -> 7.44 us  [dot(): return jnp.dot(left, right, preferred_element_type=F32)]
    pallas_call x5 -> x4, Pallas kernels: 21.7 us -> 19.9 us  [add(): pl.pallas_call(functools.partial(kernel, self.pos_count, start), out_shap...]
    unnamed x100 -> x106, local copies, waits for them, and re-layouts: 9.12 us -> 10.1 us
  transfers between devices with their start and end apart: 36 -> 36, of which waited for: 21 -> 20; matrix products, arithmetic and copies ran while one was open for 6% -> 7% of each run, Pallas kernels for 20% -> 20%
where the time goes in v6:
time: 268 us; the launch traced here: 266 us
  Pallas kernels  87.3 us (33%)
  starting transfers between devices  81.4 us (30%)
  waiting for transfers between devices  67 us (25%)
  local copies, waits for them, and re-layouts  15.2 us (6%)
  matrix products  7.44 us (3%)
  other arithmetic  6.79 us (3%)
    pallas_call x18, Pallas kernels, call(): pl.pallas_call(kernel, out_shape=shapes, in_specs=[pl.BlockSpec(memory_sp...  67.4 us
    all_to_all x8, starting transfers between devices, trade(): return lax.all_to_all(copies, ('pos', 'grp'), 0, 0, tiled=True)  32.3 us
    all_to_all x8, waiting for transfers between devices, trade(): return lax.all_to_all(copies, ('pos', 'grp'), 0, 0, tiled=True)  28.4 us
    pallas_call x4, Pallas kernels, add(): pl.pallas_call(functools.partial(kernel, self.pos_count, start), out_shap...  19.9 us
    ppermute x2, waiting for transfers between devices, exchange(): lax.ppermute(self.low, 'grp', flip(self.grp_count, self.grp_count // 2))  12.8 us
    unnamed x106, local copies, waits for them, and re-layouts  10.1 us
    ppermute x8, starting transfers between devices, turn(): self.parts[k].append(lax.ppermute(self.parts[k][0], 'pos', pairs))  9.04 us
    ppermute x3, waiting for transfers between devices, local(): lax.ppermute(kv_own, 'grp', flip(grp_count, step))  8.89 us
  transfers between devices with their start and end apart: 36, of which 20 were waited for; matrix products, arithmetic and copies ran while one was open for 7% of the time, Pallas kernels for 20%

profile of v6, /device:TPU:0, one launch (start us, length us, event | category | flops | bytes accessed | tf_op | source)
XLA Modules:
  0.0 266.5 jit_solution(13883277833122110056)
XLA Ops:
  0.7 3.3 %shard_map.368 = (f32[392,256]{1,0:T(8,128)}, f32[392,256]{1,0:T(8,128)}, f32[196,256]{1,0:T(8,128)}, f32[196,256]{1,0:T(8,128)}) custom-call(bf16[392,1024]{1,0:T(8,128)(2,1)} %x.11, bf16[3,1024,256]{2,1,0:T(8,128)(2,1)} %w.15), custom_call_target="tpu_custom_call" | custom-call | flops 411041792 | bytes 3579904 | tf_op jit(solution)/shard_map/pallas_call | solution.py:64
  4.0 4.9 %collective-permute-start = (f32[196,256]{1,0:T(8,128)}, f32[196,256]{1,0:T(8,128)S(1)}, u32[]{:S(2)}, u32[]{:S(2)}) collective-permute-start(f32[196,256]{1,0:T(8,128)} %get-tuple-element.132), channel_id=1, source_target_pairs={{0,1},{1,2},{2,3},{4,5},{5,6},{6,7},{8,9},{9,10},{10,11},{12,13},{... | collective-permute-start | bytes 602120 | tf_op jit(solution)/shard_map/ppermute | solution.py:806
  10.2 2.2 fusion.tap_1
  18.2 2.5 shard_map.369
  20.8 5.9 %all-to-all-start = ((f32[32,2,256]{2,1,0:T(2,128)}), f32[32,2,256]{2,1,0:T(2,128)S(1)}, u32[]{:S(2)}, u32[]{:S(2)}) async-start(f32[32,2,256]{2,1,0:T(2,128)} %get-tuple-element.134), calls=%async_computation | async-start | bytes 131072 | tf_op jit(solution)/shard_map/all_to_all | solution.py:49
  28.1 3.7 %collective-permute-start.2 = (bf16[196,256]{1,0:T(8,128)(2,1)}, bf16[196,256]{1,0:T(8,128)(2,1)S(1)}, u32[]{:S(2)}, u32[]{:S(2)}) collective-permute-start(bf16[196,256]{1,0:T(8,128)(2,1)} %get-tuple-element.139), channel_id=1, source_target_pairs={{0,1},{1,2},{2,3},{4,5},{5,6},{6,7},{8,9},{9,10},{10,11},{12,13},{... | collective-permute-start | bytes 301064 | tf_op jit(solution)/shard_map/ppermute | solution.py:815
  34.8 4.4 %shard_map.370 = (f32[392,256]{1,0:T(8,128)}, bf16[392,256]{1,0:T(8,128)(2,1)}, f32[32,2,256]{2,1,0:T(2,128)}, f32[2,256]{1,0:T(2,128)}) custom-call(f32[5]{0:T(128)} %pad_maximum_fusion.3.sc, f32[32,2,256]{2,1,0:T(2,128)} %copy-done.24, f32[392,256]{1,0:T(8,128)} %get-tuple-element.135.pre_1, f32[1,256]{1,0:T(1,128)} %bitcast.47, f32[1,256]{1,0:T(1,128)} %bitcast.53, ...), custom_call_target="tpu_custom_call" | custom-call | flops 462422016 | bytes 2324608 | tf_op jit(solution)/shard_map/pallas_call | solution.py:64
  39.2 5.6 %all-to-all-start.1 = ((f32[32,2,256]{2,1,0:T(2,128)}), f32[32,2,256]{2,1,0:T(2,128)S(1)}, u32[]{:S(2)}, u32[]{:S(2)}) async-start(f32[32,2,256]{2,1,0:T(2,128)} %get-tuple-element.136), calls=%async_computation.1 | async-start | bytes 131072 | tf_op jit(solution)/shard_map/all_to_all | solution.py:49
  45.0 4.1 %shard_map.371.windows = bf16[392,2304]{1,0:T(8,128)(2,1)} custom-call(bf16[392,256]{1,0:T(8,128)(2,1)} %get-tuple-element.137.z_1, f32[392,4]{1,0:T(8,128)} %copy.66.place), custom_call_target="tpu_custom_call" | custom-call | bytes 2013312 | tf_op jit(solution)/shard_map/pallas_call | solution.py:64
  49.0 3.3 %all-to-all-done.1.copies_in = f32[32,2,256]{2,1,0:T(2,128)S(1)} async-done(((f32[32,2,256]{2,1,0:T(2,128)}), f32[32,2,256]{2,1,0:T(2,128)S(1)}, u32[]{:S(2)}, u32[]{:S(2)}) %all-to-all-start.1) | async-done | bytes 65568 | tf_op jit(solution)/shard_map/all_to_all | solution.py:49
  52.9 3.0 %shard_map.372 = (bf16[392,256]{1,0:T(8,128)(2,1)}, f32[392,1024]{1,0:T(8,128)}, f32[32,2,640]{2,1,0:T(2,128)}, f32[2,256]{1,0:T(2,128)}) custom-call(f32[5]{0:T(128)} %pad_maximum_fusion.3.sc, f32[32,2,256]{2,1,0:T(2,128)} %copy-done.25, f32[392,256]{1,0:T(8,128)} %get-tuple-element.142.pre_2, f32[1,256]{1,0:T(1,128)} %bitcast.50, f32[1,256]{1,0:T(1,128)} %bitcast.59, ...), custom_call_target="tpu_custom_call" | custom-call | flops 205520896 | bytes 2971776 | tf_op jit(solution)/shard_map/pallas_call | solution.py:64
  55.9 2.6 all-to-all-start.2
  59.7 7.6 %all-to-all-done.2.copies_in = f32[32,2,640]{2,1,0:T(2,128)S(1)} async-done(((f32[32,2,640]{2,1,0:T(2,128)}), f32[32,2,640]{2,1,0:T(2,128)S(1)}, u32[]{:S(2)}, u32[]{:S(2)}) %all-to-all-start.2) | async-done | bytes 163872 | tf_op jit(solution)/shard_map/all_to_all | solution.py:49
  68.0 4.8 %shard_map.373 = (bf16[392,1024]{1,0:T(8,128)(2,1)}, bf16[224,1024]{1,0:T(8,128)(2,1)}, bf16[784,128]{1,0:T(8,128)(2,1)}, f32[2,1024]{1,0:T(2,128)}) custom-call(f32[5]{0:T(128)} %pad_maximum_fusion.3.sc, f32[32,2,640]{2,1,0:T(2,128)} %copy-done.15, bf16[256,1024]{1,0:T(8,128)(2,1)} %w.13, f32[1,1024]{1,0:T(1,128)} %bitcast.40, f32[1,1024]{1,0:T(1,128)} %bitcast.44, ...), custom_call_target="tpu_custom_call" | custom-call | flops 559677440 | bytes 6760640 | tf_op jit(solution)/shard_map/pallas_call | solution.py:64
  74.7 2.5 collective-permute-start.6
  77.9 2.6 all-to-all-start.4
  80.5 2.5 convolution_convert_fusion.theta
  83.0 8.9 %collective-permute-done.5.refs_2_ = bf16[784,128]{1,0:T(8,128)(2,1)S(1)} collective-permute-done((bf16[784,128]{1,0:T(8,128)(2,1)}, bf16[784,128]{1,0:T(8,128)(2,1)S(1)}, u32[]{:S(2)}, u32[]{:S(2)}) %collective-permute-start.5) | collective-permute-done | bytes 200736 | tf_op jit(solution)/shard_map/ppermute | solution.py:857
  93.3 4.4 %shard_map.374 = (bf16[448,1024]{1,0:T(8,128)(2,1)}, f32[392,448]{1,0:T(8,128)}, bf16[392,512]{1,0:T(8,128)(2,1)}, f32[32,4,640]{2,1,0:T(4,128)}) custom-call(f32[5]{0:T(128)} %pad_maximum_fusion.3.sc, bf16[392,512]{1,0:T(8,128)(2,1)} %convolution_convert_fusion.theta, f32[392,4]{1,0:T(8,128)} %copy.66.place, f32[2,448]{1,0:T(2,128)} %pad_maximum_fusion.2.key_row, ...), custom_call_target="tpu_custom_call" | custom-call | flops 770703360 | bytes 5414528 | tf_op jit(solution)/shard_map/pallas_call | solution.py:64
  97.7 5.0 %all-to-all-start.3 = ((f32[32,4,640]{2,1,0:T(4,128)}), f32[32,4,640]{2,1,0:T(4,128)S(1)}, u32[]{:S(2)}, u32[]{:S(2)}) async-start(f32[32,4,640]{2,1,0:T(4,128)} %get-tuple-element.148), calls=%async_computation.3 | async-start | bytes 655360 | tf_op jit(solution)/shard_map/all_to_all | solution.py:49
  103.5 2.8 %fusion.5.pre_4 = f32[392,1024]{1,0:T(8,128)} fusion(bf16[392,512]{1,0:T(8,128)(2,1)} %get-tuple-element.147.attended, bf16[512,1024]{1,0:T(8,128)(2,1)S(1)} %copy-done.2), kind=kOutput, calls=%fused_computation.40 | convolution fusion | flops 411041792 | bytes 3055616 | tf_op jit(solution)/shard_map/dot_general | solution.py:30
  106.3 7.2 %all-to-all-done.3.copies_in = f32[32,4,640]{2,1,0:T(4,128)S(1)} async-done(((f32[32,4,640]{2,1,0:T(4,128)}), f32[32,4,640]{2,1,0:T(4,128)S(1)}, u32[]{:S(2)}, u32[]{:S(2)}) %all-to-all-start.3) | async-done | bytes 327712 | tf_op jit(solution)/shard_map/all_to_all | solution.py:49
  114.2 5.8 %shard_map.375 = (bf16[392,1024]{1,0:T(8,128)(2,1)}, bf16[392,448]{1,0:T(8,128)(2,1)}, f32[1,1024]{1,0:T(1,128)}, f32[1,1024]{1,0:T(1,128)}, f32[1,1024]{1,0:T(1...) custom-call(f32[5]{0:T(128)} %pad_maximum_fusion.3.sc, ...), custom_call_target="tpu_custom_call" | custom-call | flops 950534144 | bytes 8182400 | tf_op jit(solution)/shard_map/pallas_call | solution.py:64
  125.2 7.2 %shard_map.376 = (bf16[4,2048,128]{2,1,0:T(8,128)(2,1)}, bf16[4,2048,128]{2,1,0:T(8,128)(2,1)}, f32[392,1024]{1,0:T(8,128)}, bf16[392,512]{1,0:T(8,128)(2,1)}) custom-call(s32[5]{0:T(128)} %stack.57.bits, bf16[392,448]{1,0:T(8,128)(2,1)} %get-tuple-element.157.d_logits, bf16[392,1024]{1,0:T(8,128)(2,1)} %cot.5, bf16[1024,512]{1,0:T(8,128)(2,1)} %w.12, ...), custom_call_target="tpu_custom_call" | custom-call | flops 1412956160 | bytes 8272896 | tf_op jit(solution)/shard_map/pallas_call | solution.py:605
  132.4 6.9 %collective-permute-done.8.refs_1_ = bf16[784,128]{1,0:T(8,128)(2,1)S(1)} collective-permute-done((bf16[784,128]{1,0:T(8,128)(2,1)}, bf16[784,128]{1,0:T(8,128)(2,1)S(1)}, u32[]{:S(2)}, u32[]{:S(2)}) %collective-permute-start.8) | collective-permute-done | bytes 200736 | tf_op jit(solution)/shard_map/ppermute | solution.py:887
  140.1 6.6 %shard_map.377 = (bf16[224,1024]{1,0:T(8,128)(2,1)}, f32[392,1024]{1,0:T(8,128)}, f32[32,8,256]{2,1,0:T(8,128)}) custom-call(f32[5]{0:T(128)} %pad_maximum_fusion.3.sc, f32[112,1024]{1,0:T(8,128)} %get-tuple-element.155.own, f32[112,1]{1,0:T(8,128)} %copy.70.counts, bf16[1024,512]{1,0:T(8,128)(2,1)} %w_key.3, bf16[1024,512]{1,0:T(8,128)(2,1)} %w_value.3, ...), custom_call_target="tpu_custom_call" | custom-call | flops 414711808 | bytes 9691072 | tf_op jit(solution)/shard_map/pallas_call | solution.py:64
  146.7 4.3 %all-to-all-start.5 = ((f32[32,8,256]{2,1,0:T(8,128)}), f32[32,8,256]{2,1,0:T(8,128)S(1)}, u32[]{:S(2)}, u32[]{:S(2)}) async-start(f32[32,8,256]{2,1,0:T(8,128)} %get-tuple-element.163), calls=%async_computation.5 | async-start | bytes 524288 | tf_op jit(solution)/shard_map/all_to_all | solution.py:49
  151.0 3.4 %shard_map.378 = (bf16[4,2048,128]{2,1,0:T(8,128)(2,1)}, bf16[4,2048,128]{2,1,0:T(8,128)(2,1)}) custom-call(s32[5]{0:T(128)} %stack.57.bits, bf16[4,2048,128]{2,1,0:T(8,128)(2,1)} %get-tuple-element.164.send_in, bf16[4,2048,128]{2,1,0:T(8,128)(2,1)} %get-tuple-element.165.keep_in, ...), custom_call_target="tpu_custom_call", output_to_operand_aliasing={{0}: (1, {}), {1}: (2, {})} | custom-call | flops 469762048 | bytes 4063232 | tf_op jit(solution)/shard_map/pallas_call | solution.py:605
  154.4 6.8 %all-to-all-done.5.copies_in = f32[32,8,256]{2,1,0:T(8,128)S(1)} async-done(((f32[32,8,256]{2,1,0:T(8,128)}), f32[32,8,256]{2,1,0:T(8,128)S(1)}, u32[]{:S(2)}, u32[]{:S(2)}) %all-to-all-start.5) | async-done | bytes 262176 | tf_op jit(solution)/shard_map/all_to_all | solution.py:49
  161.9 3.9 %shard_map.379 = (bf16[392,1024]{1,0:T(8,128)(2,1)}, f32[392,256]{1,0:T(8,128)}, f32[32,2,256]{2,1,0:T(2,128)}, f32[1,1024]{1,0:T(1,128)}, f32[1,1024]{1,0:T(1,128)}) custom-call(f32[5]{0:T(128)} %pad_maximum_fusion.3.sc, f32[32,8,256]{2,1,0:T(8,128)} %copy-done.8, f32[2,1024]{1,0:T(2,128)} %get-tuple-element.156.stats_3, f32[1,1024]{1,0:T(1,128)} %bitcast.42, ...), custom_call_target="tpu_custom_call" | custom-call | flops 205520896 | bytes 5699712 | tf_op jit(solution)/shard_map/pallas_call | solution.py:64
  165.8 2.7 %all-to-all-start.6 = ((f32[32,2,256]{2,1,0:T(2,128)}), f32[32,2,256]{2,1,0:T(2,128)S(1)}, u32[]{:S(2)}, u32[]{:S(2)}) async-start(f32[32,2,256]{2,1,0:T(2,128)} %get-tuple-element.178), calls=%async_computation.6 | async-start | bytes 131072 | tf_op jit(solution)/shard_map/all_to_all | solution.py:49
  168.5 2.6 shard_map.380
  171.1 4.0 %shard_map.381 = (bf16[2,1024,128]{2,1,0:T(8,128)(2,1)}, bf16[2,1024,128]{2,1,0:T(8,128)(2,1)}, bf16[2,1024,128]{2,1,0:T(8,128)(2,1)}, bf16[2,1024,128]{2,1,0:T(8,128)(2,1)}) custom-call(s32[5]{0:T(128)} %stack.57.bits, bf16[4,2048,128]{2,1,0:T(8,128)(2,1)} %get-tuple-element.180.keep_in, bf16[4,2048,128]{2,1,0:T(8,128)(2,1)} %copy-done.4), custom_call_target="tpu_custom_call" | custom-call | bytes 6291456 | tf_op jit(solution)/shard_map/pallas_call | solution.py:64
  178.4 4.2 %shard_map.382 = (bf16[392,256]{1,0:T(8,128)(2,1)}, f32[392,256]{1,0:T(8,128)}, f32[32,2,256]{2,1,0:T(2,128)}, f32[1,256]{1,0:T(1,128)}, f32[1,256]{1,0:T(1,128)...) custom-call(f32[5]{0:T(128)} %pad_maximum_fusion.3.sc, f32[32,2,256]{2,1,0:T(2,128)} %copy-done.23, ...), custom_call_target="tpu_custom_call" | custom-call | flops 462422016 | bytes 3333248 | tf_op jit(solution)/shard_map/pallas_call | solution.py:64
  182.6 3.7 %all-to-all-start.7 = ((f32[32,2,256]{2,1,0:T(2,128)}), f32[32,2,256]{2,1,0:T(2,128)S(1)}, u32[]{:S(2)}, u32[]{:S(2)}) async-start(f32[32,2,256]{2,1,0:T(2,128)} %get-tuple-element.188), calls=%async_computation.7 | async-start | bytes 131072 | tf_op jit(solution)/shard_map/all_to_all | solution.py:49
  186.4 3.7 %collective-permute-start.13 = (bf16[196,256]{1,0:T(8,128)(2,1)}, bf16[196,256]{1,0:T(8,128)(2,1)S(1)}, u32[]{:S(2)}, u32[]{:S(2)}) collective-permute-start(bf16[196,256]{1,0:T(8,128)(2,1)} %get-tuple-element.200), channel_id=1, source_target_pairs={{0,1},{1,2},{2,3},{4,5},{5,6},{6,7},{8,9},{9,10},{10,11},{12,13},{... | collective-permute-start | bytes 301064 | tf_op jit(solution)/shard_map/ppermute | solution.py:954
  194.8 2.7 shard_map.383
  198.1 6.8 %shard_map.384 = (bf16[4,1600,128]{2,1,0:T(8,128)(2,1)}, bf16[4,1600,128]{2,1,0:T(8,128)(2,1)}, bf16[392,768]{1,0:T(8,128)(2,1)}, f32[1,256]{1,0:T(1,128)}, f32[1,256]{1,0:T(1,128)}) custom-call(s32[5]{0:T(128)} %stack.57.bits, f32[5]{0:T(128)} %pad_maximum_fusion.3.sc, ...), custom_call_target="tpu_custom_call", output_to_operand_aliasing={{0}: (2, {}), {1}: (3, {})} | custom-call | flops 616562688 | bytes 8219296 | tf_op jit(solution)/shard_map/pallas_call | solution.py:605
  209.9 3.5 %shard_map.385 = (bf16[2,800,128]{2,1,0:T(8,128)(2,1)}, bf16[2,800,128]{2,1,0:T(8,128)(2,1)}, bf16[2,800,128]{2,1,0:T(8,128)(2,1)}, bf16[2,800,128]{2,1,0:T(8,128)(2,1)}) custom-call(s32[5]{0:T(128)} %stack.57.bits, bf16[4,1600,128]{2,1,0:T(8,128)(2,1)} %get-tuple-element.205.keep_in, bf16[4,1600,128]{2,1,0:T(8,128)(2,1)} %copy-done.5), custom_call_target="tpu_custom_call" | custom-call | bytes 4915200 | tf_op jit(solution)/shard_map/pallas_call | solution.py:64
  217.7 4.1 %shard_map.386 = f32[392,1024]{1,0:T(8,128)} custom-call(bf16[392,768]{1,0:T(8,128)(2,1)} %get-tuple-element.208.d_taps, bf16[3,1024,256]{2,1,0:T(8,128)(2,1)} %w.15, f32[392,1024]{1,0:T(8,128)} %get-tuple-element.170.d_summed), custom_call_target="tpu_custom_call" | custom-call | flops 616562688 | bytes 5386240 | tf_op jit(solution)/shard_map/pallas_call | solution.py:64
  221.8 3.3 %collective-permute-done.16.received_1 = bf16[2,800,128]{2,1,0:T(8,128)(2,1)S(1)} collective-permute-done((bf16[2,800,128]{2,1,0:T(8,128)(2,1)}, bf16[2,800,128]{2,1,0:T(8,128)(2,1)S(1)}, u32[]{:S(2)}, u32[]{:S(2)}) %collective-permute-start.16) | collective-permute-done | bytes 409632 | tf_op jit(solution)/shard_map/ppermute | solution.py:642
  226.3 2.4 shard_map.387
  231.0 2.9 %collective-permute-start.24 = (bf16[1,1024,128]{2,1,0:T(8,128)(2,1)S(1)}, bf16[1,1024,128]{2,1,0:T(8,128)(2,1)S(1)}, u32[]{:S(2)}, u32[]{:S(2)}) collective-permute-start(bf16[1,1024,128]{2,1,0:T(8,128)(2,1)S(1)} %add_convert_fusion.2), channel_id=1, source_target_pairs={{0,2},{1,3},{2,0},{3,1},{4,6},{5,7},{6,4},{7,5},{8,10},{9,11},{10,... | collective-permute-start | bytes 786440 | tf_op jit(solution)/shard_map/ppermute | solution.py:689
  237.6 7.1 %collective-permute-done.24 = bf16[1,1024,128]{2,1,0:T(8,128)(2,1)S(1)} collective-permute-done((bf16[1,1024,128]{2,1,0:T(8,128)(2,1)S(1)}, bf16[1,1024,128]{2,1,0:T(8,128)(2,1)S(1)}, u32[]{:S(2)}, u32[]{:S(2)}) %collective-permute-start.24) | collective-permute-done | bytes 262176 | tf_op jit(solution)/shard_map/ppermute | solution.py:689
  246.1 4.8 %collective-permute-start.25 = (bf16[1,800,128]{2,1,0:T(8,128)(2,1)S(1)}, bf16[1,800,128]{2,1,0:T(8,128)(2,1)S(1)}, u32[]{:S(2)}, u32[]{:S(2)}) collective-permute-start(bf16[1,800,128]{2,1,0:T(8,128)(2,1)S(1)} %add_convert_fusion.4), channel_id=1, source_target_pairs={{0,2},{1,3},{2,0},{3,1},{4,6},{5,7},{6,4},{7,5},{8,10},{9,11},{10,... | collective-permute-start | bytes 614408 | tf_op jit(solution)/shard_map/ppermute | solution.py:689
  250.9 5.7 %collective-permute-done.25 = bf16[1,800,128]{2,1,0:T(8,128)(2,1)S(1)} collective-permute-done((bf16[1,800,128]{2,1,0:T(8,128)(2,1)S(1)}, bf16[1,800,128]{2,1,0:T(8,128)(2,1)S(1)}, u32[]{:S(2)}, u32[]{:S(2)}) %collective-permute-start.25) | collective-permute-done | bytes 204832 | tf_op jit(solution)/shard_map/ppermute | solution.py:689
  256.8 3.3 %collective-permute-start.27 = (bf16[1,800,128]{2,1,0:T(8,128)(2,1)S(1)}, bf16[1,800,128]{2,1,0:T(8,128)(2,1)S(1)}, u32[]{:S(2)}, u32[]{:S(2)}) collective-permute-start(bf16[1,800,128]{2,1,0:T(8,128)(2,1)S(1)} %add_convert_fusion.3.mine), channel_id=1, source_target_pairs={{0,1},{1,0},{2,3},{3,2},{4,5},{5,4},{6,7},{7,6},{8,9},{9,8},{10,11... | collective-permute-start | bytes 614408 | tf_op jit(solution)/shard_map/ppermute | solution.py:700
  261.4 2.0 shard_map.389
  (200 shorter events, 57.6 us)
Async XLA Ops:
  4.0 12.5 %collective-permute-start = (f32[196,256]{1,0:T(8,128)}, f32[196,256]{1,0:T(8,128)S(1)}, u32[]{:S(2)}, u32[]{:S(2)}) collective-permute-start(f32[196,256]{1,0:T(8,128)} %get-tuple-element.132), channel_id=1, source_target_pairs={{0,1},{1,2},{2,3},{4,5},{5,6},{6,7},{8,9},{9,10},{10,11},{12,13},{... | collective-permute-start | bytes 602120 | tf_op jit(solution)/shard_map/ppermute | solution.py:806
  8.9 8.6 %collective-permute-start.1 = (f32[196,256]{1,0:T(8,128)}, f32[196,256]{1,0:T(8,128)S(1)}, u32[]{:S(2)}, u32[]{:S(2)}) collective-permute-start(f32[196,256]{1,0:T(8,128)} %get-tuple-element.133), channel_id=1, source_target_pairs={{1,0},{2,1},{3,2},{5,4},{6,5},{7,6},{9,8},{10,9},{11,10},{13,12},{... | collective-permute-start | bytes 602120 | tf_op jit(solution)/shard_map/ppermute | solution.py:807
  18.2 26.5 %copy-start.3 = (bf16[392,1024]{1,0:T(8,128)(2,1)S(1)}, bf16[392,1024]{1,0:T(8,128)(2,1)}, u32[]{:S(2)}) copy-start(bf16[392,1024]{1,0:T(8,128)(2,1)} %cot.5) | copy-start | bytes 2408452
  20.8 13.4 %all-to-all-start = ((f32[32,2,256]{2,1,0:T(2,128)}), f32[32,2,256]{2,1,0:T(2,128)S(1)}, u32[]{:S(2)}, u32[]{:S(2)}) async-start(f32[32,2,256]{2,1,0:T(2,128)} %get-tuple-element.134), calls=%async_computation | async-start | bytes 131072 | tf_op jit(solution)/shard_map/all_to_all | solution.py:49
  28.1 24.2 %collective-permute-start.2 = (bf16[196,256]{1,0:T(8,128)(2,1)}, bf16[196,256]{1,0:T(8,128)(2,1)S(1)}, u32[]{:S(2)}, u32[]{:S(2)}) collective-permute-start(bf16[196,256]{1,0:T(8,128)(2,1)} %get-tuple-element.139), channel_id=1, source_target_pairs={{0,1},{1,2},{2,3},{4,5},{5,6},{6,7},{8,9},{9,10},{10,11},{12,13},{... | collective-permute-start | bytes 301064 | tf_op jit(solution)/shard_map/ppermute | solution.py:815
  31.7 20.5 %collective-permute-start.3 = (bf16[196,256]{1,0:T(8,128)(2,1)}, bf16[196,256]{1,0:T(8,128)(2,1)S(1)}, u32[]{:S(2)}, u32[]{:S(2)}) collective-permute-start(bf16[196,256]{1,0:T(8,128)(2,1)} %get-tuple-element.140), channel_id=1, source_target_pairs={{1,0},{2,1},{3,2},{5,4},{6,5},{7,6},{9,8},{10,9},{11,10},{13,12},{... | collective-permute-start | bytes 301064 | tf_op jit(solution)/shard_map/ppermute | solution.py:816
  39.2 13.1 %all-to-all-start.1 = ((f32[32,2,256]{2,1,0:T(2,128)}), f32[32,2,256]{2,1,0:T(2,128)S(1)}, u32[]{:S(2)}, u32[]{:S(2)}) async-start(f32[32,2,256]{2,1,0:T(2,128)} %get-tuple-element.136), calls=%async_computation.1 | async-start | bytes 131072 | tf_op jit(solution)/shard_map/all_to_all | solution.py:49
  52.3 20.5 %copy-start.37 = (bf16[196,256]{1,0:T(8,128)(2,1)}, bf16[196,256]{1,0:T(8,128)(2,1)S(1)}, u32[]{:S(2)}) copy-start(bf16[196,256]{1,0:T(8,128)(2,1)S(1)} %collective-permute-done.2.pre_before) | copy-start | bytes 301060
  52.3 20.5 %copy-start.38 = (bf16[196,256]{1,0:T(8,128)(2,1)}, bf16[196,256]{1,0:T(8,128)(2,1)S(1)}, u32[]{:S(2)}) copy-start(bf16[196,256]{1,0:T(8,128)(2,1)S(1)} %collective-permute-done.3.pre_after) | copy-start | bytes 301060
  55.9 11.5 %all-to-all-start.2 = ((f32[32,2,640]{2,1,0:T(2,128)}), f32[32,2,640]{2,1,0:T(2,128)S(1)}, u32[]{:S(2)}, u32[]{:S(2)}) async-start(f32[32,2,640]{2,1,0:T(2,128)} %get-tuple-element.143), calls=%async_computation.2 | async-start | bytes 327680 | tf_op jit(solution)/shard_map/all_to_all | solution.py:49
  72.8 10.2 %collective-permute-start.4 = (bf16[784,128]{1,0:T(8,128)(2,1)}, bf16[784,128]{1,0:T(8,128)(2,1)S(1)}, u32[]{:S(2)}, u32[]{:S(2)}) collective-permute-start(bf16[784,128]{1,0:T(8,128)(2,1)} %get-tuple-element.146.refs_0_), channel_id=1, source_target_pairs={{0,1},{1,0},{2,3},{3,2},{4,5},{5,4},{6,7},{7,6},{8,9},{9,8},{10,11... | collective-permute-start | bytes 602120 | tf_op jit(solution)/shard_map/ppermute | solution.py:857
  72.9 19.0 %collective-permute-start.5 = (bf16[784,128]{1,0:T(8,128)(2,1)}, bf16[784,128]{1,0:T(8,128)(2,1)S(1)}, u32[]{:S(2)}, u32[]{:S(2)}) collective-permute-start(bf16[784,128]{1,0:T(8,128)(2,1)} %get-tuple-element.146.refs_0_), channel_id=1, source_target_pairs={{0,2},{1,3},{2,0},{3,1},{4,6},{5,7},{6,4},{7,5},{8,10},{9,11},{10,... | collective-permute-start | bytes 602120 | tf_op jit(solution)/shard_map/ppermute | solution.py:857
  74.7 17.2 %collective-permute-start.6 = (bf16[784,128]{1,0:T(8,128)(2,1)}, bf16[784,128]{1,0:T(8,128)(2,1)S(1)}, u32[]{:S(2)}, u32[]{:S(2)}) collective-permute-start(bf16[784,128]{1,0:T(8,128)(2,1)} %get-tuple-element.146.refs_0_), channel_id=1, source_target_pairs={{0,3},{1,2},{2,1},{3,0},{4,7},{5,6},{6,5},{7,4},{8,11},{9,10},{10,... | collective-permute-start | bytes 602120 | tf_op jit(solution)/shard_map/ppermute | solution.py:857
  77.9 19.8 %all-to-all-start.4 = ((f32[32,2,512]{2,1,0:T(2,128)}), f32[32,2,512]{2,1,0:T(2,128)S(1)}, u32[]{:S(2)}, u32[]{:S(2)}) async-start(f32[32,2,512]{2,1,0:T(2,128)} %broadcast_in_dim.42), calls=%async_computation.4 | async-start | bytes 262144 | tf_op jit(solution)/shard_map/all_to_all | solution.py:49
  83.0 20.3 %copy-start.30 = (f32[392,112]{1,0:T(8,128)S(1)}, f32[392,112]{1,0:T(8,128)}, u32[]{:S(2)}) copy-start(f32[392,112]{1,0:T(8,128)} %constant.69.clone) | copy-start | bytes 526852
  83.0 20.5 %copy-start.2 = (bf16[512,1024]{1,0:T(8,128)(2,1)S(1)}, bf16[512,1024]{1,0:T(8,128)(2,1)}, u32[]{:S(2)}) copy-start(bf16[512,1024]{1,0:T(8,128)(2,1)} %w.11) | copy-start | bytes 3145732
  97.7 15.8 %all-to-all-start.3 = ((f32[32,4,640]{2,1,0:T(4,128)}), f32[32,4,640]{2,1,0:T(4,128)S(1)}, u32[]{:S(2)}, u32[]{:S(2)}) async-start(f32[32,4,640]{2,1,0:T(4,128)} %get-tuple-element.148), calls=%async_computation.3 | async-start | bytes 655360 | tf_op jit(solution)/shard_map/all_to_all | solution.py:49
  120.0 12.4 %collective-permute-start.7 = (bf16[784,128]{1,0:T(8,128)(2,1)}, bf16[784,128]{1,0:T(8,128)(2,1)S(1)}, u32[]{:S(2)}, u32[]{:S(2)}) collective-permute-start(bf16[784,128]{1,0:T(8,128)(2,1)} %get-tuple-element.160), channel_id=1, source_target_pairs={{0,1},{1,0},{2,3},{3,2},{4,5},{5,4},{6,7},{7,6},{8,9},{9,8},{10,11... | collective-permute-start | bytes 602120 | tf_op jit(solution)/shard_map/ppermute | solution.py:887
  121.7 17.6 %collective-permute-start.8 = (bf16[784,128]{1,0:T(8,128)(2,1)}, bf16[784,128]{1,0:T(8,128)(2,1)S(1)}, u32[]{:S(2)}, u32[]{:S(2)}) collective-permute-start(bf16[784,128]{1,0:T(8,128)(2,1)} %get-tuple-element.161), channel_id=1, source_target_pairs={{0,2},{1,3},{2,0},{3,1},{4,6},{5,7},{6,4},{7,5},{8,10},{9,11},{10,... | collective-permute-start | bytes 602120 | tf_op jit(solution)/shard_map/ppermute | solution.py:887
  122.7 16.6 %collective-permute-start.9 = (bf16[784,128]{1,0:T(8,128)(2,1)}, bf16[784,128]{1,0:T(8,128)(2,1)S(1)}, u32[]{:S(2)}, u32[]{:S(2)}) collective-permute-start(bf16[784,128]{1,0:T(8,128)(2,1)} %get-tuple-element.162), channel_id=1, source_target_pairs={{0,3},{1,2},{2,1},{3,0},{4,7},{5,6},{6,5},{7,4},{8,11},{9,10},{10,... | collective-permute-start | bytes 602120 | tf_op jit(solution)/shard_map/ppermute | solution.py:887
  146.7 14.5 %all-to-all-start.5 = ((f32[32,8,256]{2,1,0:T(8,128)}), f32[32,8,256]{2,1,0:T(8,128)S(1)}, u32[]{:S(2)}, u32[]{:S(2)}) async-start(f32[32,8,256]{2,1,0:T(8,128)} %get-tuple-element.163), calls=%async_computation.5 | async-start | bytes 524288 | tf_op jit(solution)/shard_map/all_to_all | solution.py:49
  161.2 4.6 %collective-permute-start.10 = (bf16[4,2048,128]{2,1,0:T(8,128)(2,1)}, bf16[4,2048,128]{2,1,0:T(8,128)(2,1)S(1)}, u32[]{:S(2)}, u32[]{:S(2)}) collective-permute-start(bf16[4,2048,128]{2,1,0:T(8,128)(2,1)} %get-tuple-element.177), channel_id=1, source_target_pairs={{0,4},{4,0},{8,12},{12,8},{16,20},{20,16},{24,28},{28,24},{1,5},{5... | collective-permute-start | bytes 6291464 | tf_op jit(solution)/shard_map/ppermute | solution.py:624
  165.8 10.2 %all-to-all-start.6 = ((f32[32,2,256]{2,1,0:T(2,128)}), f32[32,2,256]{2,1,0:T(2,128)S(1)}, u32[]{:S(2)}, u32[]{:S(2)}) async-start(f32[32,2,256]{2,1,0:T(2,128)} %get-tuple-element.178), calls=%async_computation.6 | async-start | bytes 131072 | tf_op jit(solution)/shard_map/all_to_all | solution.py:49
  176.0 17.8 %collective-permute-start.11 = (bf16[2,1024,128]{2,1,0:T(8,128)(2,1)}, bf16[2,1024,128]{2,1,0:T(8,128)(2,1)S(1)}, u32[]{:S(2)}, u32[]{:S(2)}) collective-permute-start(bf16[2,1024,128]{2,1,0:T(8,128)(2,1)} %get-tuple-element.189), channel_id=1, source_target_pairs={{0,8},{4,12},{8,0},{12,4},{16,24},{20,28},{24,16},{28,20},{1,9},{5... | collective-permute-start | bytes 1572872 | tf_op jit(solution)/shard_map/ppermute | solution.py:642
  176.9 16.9 %collective-permute-start.12 = (bf16[2,1024,128]{2,1,0:T(8,128)(2,1)}, bf16[2,1024,128]{2,1,0:T(8,128)(2,1)S(1)}, u32[]{:S(2)}, u32[]{:S(2)}) collective-permute-start(bf16[2,1024,128]{2,1,0:T(8,128)(2,1)} %get-tuple-element.190), channel_id=1, source_target_pairs={{0,16},{4,20},{8,24},{12,28},{16,0},{20,4},{24,8},{28,12},{1,17},{... | collective-permute-start | bytes 1572872 | tf_op jit(solution)/shard_map/ppermute | solution.py:642
  182.6 11.2 %all-to-all-start.7 = ((f32[32,2,256]{2,1,0:T(2,128)}), f32[32,2,256]{2,1,0:T(2,128)S(1)}, u32[]{:S(2)}, u32[]{:S(2)}) async-start(f32[32,2,256]{2,1,0:T(2,128)} %get-tuple-element.188), calls=%async_computation.7 | async-start | bytes 131072 | tf_op jit(solution)/shard_map/all_to_all | solution.py:49
  186.4 11.1 %collective-permute-start.13 = (bf16[196,256]{1,0:T(8,128)(2,1)}, bf16[196,256]{1,0:T(8,128)(2,1)S(1)}, u32[]{:S(2)}, u32[]{:S(2)}) collective-permute-start(bf16[196,256]{1,0:T(8,128)(2,1)} %get-tuple-element.200), channel_id=1, source_target_pairs={{0,1},{1,2},{2,3},{4,5},{5,6},{6,7},{8,9},{9,10},{10,11},{12,13},{... | collective-permute-start | bytes 301064 | tf_op jit(solution)/shard_map/ppermute | solution.py:954
  190.1 7.4 %collective-permute-start.14 = (bf16[196,256]{1,0:T(8,128)(2,1)}, bf16[196,256]{1,0:T(8,128)(2,1)S(1)}, u32[]{:S(2)}, u32[]{:S(2)}) collective-permute-start(bf16[196,256]{1,0:T(8,128)(2,1)} %get-tuple-element.201), channel_id=1, source_target_pairs={{1,0},{2,1},{3,2},{5,4},{6,5},{7,6},{9,8},{10,9},{11,10},{13,12},{... | collective-permute-start | bytes 301064 | tf_op jit(solution)/shard_map/ppermute | solution.py:955
  204.9 3.8 %collective-permute-start.15 = (bf16[4,1600,128]{2,1,0:T(8,128)(2,1)}, bf16[4,1600,128]{2,1,0:T(8,128)(2,1)S(1)}, u32[]{:S(2)}, u32[]{:S(2)}) collective-permute-start(bf16[4,1600,128]{2,1,0:T(8,128)(2,1)} %get-tuple-element.206), channel_id=1, source_target_pairs={{0,4},{4,0},{8,12},{12,8},{16,20},{20,16},{24,28},{28,24},{1,5},{5... | collective-permute-start | bytes 4915208 | tf_op jit(solution)/shard_map/ppermute | solution.py:624
  205.0 10.6 %collective-permute-start.18 = (bf16[1,1024,128]{2,1,0:T(8,128)(2,1)S(1)}, bf16[1,1024,128]{2,1,0:T(8,128)(2,1)S(1)}, u32[]{:S(2)}, u32[]{:S(2)}) collective-permute-start(bf16[1,1024,128]{2,1,0:T(8,128)(2,1)S(1)} %copy-done.52), channel_id=1, source_target_pairs={{0,16},{4,20},{8,24},{12,28},{16,0},{20,4},{24,8},{28,12},{1,17},{... | collective-permute-start | bytes 786440 | tf_op jit(solution)/shard_map/ppermute | solution.py:642
  205.9 9.7 %collective-permute-start.19 = (bf16[1,1024,128]{2,1,0:T(8,128)(2,1)S(1)}, bf16[1,1024,128]{2,1,0:T(8,128)(2,1)S(1)}, u32[]{:S(2)}, u32[]{:S(2)}) collective-permute-start(bf16[1,1024,128]{2,1,0:T(8,128)(2,1)S(1)} %copy-done.51), channel_id=1, source_target_pairs={{0,8},{4,12},{8,0},{12,4},{16,24},{20,28},{24,16},{28,20},{1,9},{5... | collective-permute-start | bytes 786440 | tf_op jit(solution)/shard_map/ppermute | solution.py:642
  213.3 11.7 %collective-permute-start.16 = (bf16[2,800,128]{2,1,0:T(8,128)(2,1)}, bf16[2,800,128]{2,1,0:T(8,128)(2,1)S(1)}, u32[]{:S(2)}, u32[]{:S(2)}) collective-permute-start(bf16[2,800,128]{2,1,0:T(8,128)(2,1)} %get-tuple-element.209), channel_id=1, source_target_pairs={{0,8},{4,12},{8,0},{12,4},{16,24},{20,28},{24,16},{28,20},{1,9},{5... | collective-permute-start | bytes 1228808 | tf_op jit(solution)/shard_map/ppermute | solution.py:642
  214.1 11.4 %collective-permute-start.17 = (bf16[2,800,128]{2,1,0:T(8,128)(2,1)}, bf16[2,800,128]{2,1,0:T(8,128)(2,1)S(1)}, u32[]{:S(2)}, u32[]{:S(2)}) collective-permute-start(bf16[2,800,128]{2,1,0:T(8,128)(2,1)} %get-tuple-element.212), channel_id=1, source_target_pairs={{0,16},{4,20},{8,24},{12,28},{16,0},{20,4},{24,8},{28,12},{1,17},{... | collective-permute-start | bytes 1228808 | tf_op jit(solution)/shard_map/ppermute | solution.py:642
  215.8 13.0 %collective-permute-start.20 = (bf16[1,1024,128]{2,1,0:T(8,128)(2,1)S(1)}, bf16[1,1024,128]{2,1,0:T(8,128)(2,1)S(1)}, u32[]{:S(2)}, u32[]{:S(2)}) collective-permute-start(bf16[1,1024,128]{2,1,0:T(8,128)(2,1)S(1)} %select_convert_fusion.1), channel_id=1, source_target_pairs={{0,1},{1,0},{2,3},{3,2},{4,5},{5,4},{6,7},{7,6},{8,9},{9,8},{10,11... | collective-permute-start | bytes 786440 | tf_op jit(solution)/shard_map/ppermute | solution.py:676
  228.7 6.2 %collective-permute-start.21 = (bf16[1,800,128]{2,1,0:T(8,128)(2,1)}, bf16[1,800,128]{2,1,0:T(8,128)(2,1)S(1)}, u32[]{:S(2)}, u32[]{:S(2)}) collective-permute-start(bf16[1,800,128]{2,1,0:T(8,128)(2,1)} %get-tuple-element.220), channel_id=1, source_target_pairs={{0,8},{4,12},{8,0},{12,4},{16,24},{20,28},{24,16},{28,20},{1,9},{5... | collective-permute-start | bytes 614408 | tf_op jit(solution)/shard_map/ppermute | solution.py:642
  230.0 6.0 %collective-permute-start.22 = (bf16[1,800,128]{2,1,0:T(8,128)(2,1)}, bf16[1,800,128]{2,1,0:T(8,128)(2,1)S(1)}, u32[]{:S(2)}, u32[]{:S(2)}) collective-permute-start(bf16[1,800,128]{2,1,0:T(8,128)(2,1)} %get-tuple-element.222), channel_id=1, source_target_pairs={{0,16},{4,20},{8,24},{12,28},{16,0},{20,4},{24,8},{28,12},{1,17},{... | collective-permute-start | bytes 614408 | tf_op jit(solution)/shard_map/ppermute | solution.py:642
  231.0 13.7 %collective-permute-start.24 = (bf16[1,1024,128]{2,1,0:T(8,128)(2,1)S(1)}, bf16[1,1024,128]{2,1,0:T(8,128)(2,1)S(1)}, u32[]{:S(2)}, u32[]{:S(2)}) collective-permute-start(bf16[1,1024,128]{2,1,0:T(8,128)(2,1)S(1)} %add_convert_fusion.2), channel_id=1, source_target_pairs={{0,2},{1,3},{2,0},{3,1},{4,6},{5,7},{6,4},{7,5},{8,10},{9,11},{10,... | collective-permute-start | bytes 786440 | tf_op jit(solution)/shard_map/ppermute | solution.py:689
  236.0 24.1 %copy-start = (f32[392,1024]{1,0:T(8,128)S(1)}, f32[392,1024]{1,0:T(8,128)}, u32[]{:S(2)}) copy-start(f32[392,1024]{1,0:T(8,128)} %fusion.5.pre_4) | copy-start | bytes 4816900
  236.0 24.1 %copy-start.14 = (bf16[392,1024]{1,0:T(8,128)(2,1)S(1)}, bf16[392,1024]{1,0:T(8,128)(2,1)}, u32[]{:S(2)}) copy-start(bf16[392,1024]{1,0:T(8,128)(2,1)} %get-tuple-element.145.unit) | copy-start | bytes 2408452
  236.0 24.1 %copy-start.42 = (f32[1024]{0:T(1024)S(1)}, f32[1024]{0:T(1024)}, u32[]{:S(2)}) copy-start(f32[1024]{0:T(1024)} %param.41) | copy-start | bytes 12292
  236.0 24.1 %copy-start.43 = (f32[1024]{0:T(1024)S(1)}, f32[1024]{0:T(1024)}, u32[]{:S(2)}) copy-start(f32[1024]{0:T(1024)} %param.42) | copy-start | bytes 12292
  236.0 24.1 %copy-start.44 = (f32[1,1024]{1,0:T(1,128)S(1)}, f32[1,1024]{1,0:T(1,128)}, u32[]{:S(2)}) copy-start(f32[1,1024]{1,0:T(1,128)} %get-tuple-element.152) | copy-start | bytes 12292
  236.1 24.1 %copy-start.45 = (f32[1,1024]{1,0:T(1,128)S(1)}, f32[1,1024]{1,0:T(1,128)}, u32[]{:S(2)}) copy-start(f32[1,1024]{1,0:T(1,128)} %get-tuple-element.153) | copy-start | bytes 12292
  236.2 9.6 %collective-permute-start.23 = (bf16[1,800,128]{2,1,0:T(8,128)(2,1)S(1)}, bf16[1,800,128]{2,1,0:T(8,128)(2,1)S(1)}, u32[]{:S(2)}, u32[]{:S(2)}) collective-permute-start(bf16[1,800,128]{2,1,0:T(8,128)(2,1)S(1)} %select_convert_fusion.2), channel_id=1, source_target_pairs={{0,1},{1,0},{2,3},{3,2},{4,5},{5,4},{6,7},{7,6},{8,9},{9,8},{10,11... | collective-permute-start | bytes 614408 | tf_op jit(solution)/shard_map/ppermute | solution.py:676
  245.9 15.5 %copy-start.7 = (bf16[1,1024,128]{2,1,0:T(8,128)(2,1)}, bf16[1,1024,128]{2,1,0:T(8,128)(2,1)S(1)}, u32[]{:S(2)}) copy-start(bf16[1,1024,128]{2,1,0:T(8,128)(2,1)S(1)} %add_convert_fusion.1.mine) | copy-start | bytes 786436
  245.9 10.8 %collective-permute-start.26 = (bf16[1,1024,128]{2,1,0:T(8,128)(2,1)S(1)}, bf16[1,1024,128]{2,1,0:T(8,128)(2,1)S(1)}, u32[]{:S(2)}, u32[]{:S(2)}) collective-permute-start(bf16[1,1024,128]{2,1,0:T(8,128)(2,1)S(1)} %add_convert_fusion.1.mine), channel_id=1, source_target_pairs={{0,1},{1,0},{2,3},{3,2},{4,5},{5,4},{6,7},{7,6},{8,9},{9,8},{10,11... | collective-permute-start | bytes 786440 | tf_op jit(solution)/shard_map/ppermute | solution.py:700
  246.1 10.4 %collective-permute-start.25 = (bf16[1,800,128]{2,1,0:T(8,128)(2,1)S(1)}, bf16[1,800,128]{2,1,0:T(8,128)(2,1)S(1)}, u32[]{:S(2)}, u32[]{:S(2)}) collective-permute-start(bf16[1,800,128]{2,1,0:T(8,128)(2,1)S(1)} %add_convert_fusion.4), channel_id=1, source_target_pairs={{0,2},{1,3},{2,0},{3,1},{4,6},{5,7},{6,4},{7,5},{8,10},{9,11},{10,... | collective-permute-start | bytes 614408 | tf_op jit(solution)/shard_map/ppermute | solution.py:689
  256.8 7.0 %collective-permute-start.27 = (bf16[1,800,128]{2,1,0:T(8,128)(2,1)S(1)}, bf16[1,800,128]{2,1,0:T(8,128)(2,1)S(1)}, u32[]{:S(2)}, u32[]{:S(2)}) collective-permute-start(bf16[1,800,128]{2,1,0:T(8,128)(2,1)S(1)} %add_convert_fusion.3.mine), channel_id=1, source_target_pairs={{0,1},{1,0},{2,3},{3,2},{4,5},{5,4},{6,7},{7,6},{8,9},{9,8},{10,11... | collective-permute-start | bytes 614408 | tf_op jit(solution)/shard_map/ppermute | solution.py:700
  (41 other events, 199.6 us)
